TPU v7x, 32 devices: a whole 2x2x4 slice. The times are simulated.
32 devices in a mesh: dp: 8 (over z, y), mp: 4 (over x, core).
Axes of the slice: x: 2, y: 2, z: 4, core: 2. Of those that a mesh axis runs over, the one named last changes fastest.
Arguments:
- tokens: bfloat16 [16384, 1024], P('dp'), may hold values from -6 to 6
- cotangent: float32 [16384, 1024], P('dp'), may hold values from -6 to 6
- lengths: int32 [8], P('dp'), may hold values from 409 to 2048, as said below
- qkv_weight: float32 [1024, 3, 1024], P('dp', None, 'mp'), may hold values from -0.1875 to 0.1875
- qkv_first: float32 [1024, 3, 1024], P('dp', None, 'mp')
- qkv_second: float32 [1024, 3, 1024], P('dp', None, 'mp'), as said below
- out_weight: float32 [1024, 1024], P('mp', 'dp'), may hold values from -0.5 to 0.5
- out_first: float32 [1024, 1024], P('mp', 'dp')
- out_second: float32 [1024, 1024], P('mp', 'dp'), as said below
- up_weight: float32 [1024, 4, 1024], P('dp', None, 'mp'), may hold values from -0.1875 to 0.1875
- up_first: float32 [1024, 4, 1024], P('dp', None, 'mp')
- up_second: float32 [1024, 4, 1024], P('dp', None, 'mp'), as said below
- down_weight: float32 [4, 1024, 1024], P(None, 'mp', 'dp'), may hold values from -0.09375 to 0.09375
- down_first: float32 [4, 1024, 1024], P(None, 'mp', 'dp')
- down_second: float32 [4, 1024, 1024], P(None, 'mp', 'dp'), as said below
- row_vectors: float32 [6, 1024], replicated, as said below
- row_first: float32 [6, 1024], replicated
- row_second: float32 [6, 1024], replicated, as said below
- col_bias: float32 [6, 1024], P(None, 'mp'), may hold values from -4 to 4
- col_first: float32 [6, 1024], P(None, 'mp')
- col_second: float32 [6, 1024], P(None, 'mp'), as said below
Outputs:
- outputs: float32 [16384, 1024], P('dp')
- input_grad: float32 [16384, 1024], P('dp')
- rms_stats: float32 [3], replicated
- qkv_first_new: float32 [1024, 3, 1024], P('dp', None, 'mp')
- qkv_second_new: float32 [1024, 3, 1024], P('dp', None, 'mp')
- qkv_weight_new: float32 [1024, 3, 1024], P('dp', None, 'mp')
- out_first_new: float32 [1024, 1024], P('mp', 'dp')
- out_second_new: float32 [1024, 1024], P('mp', 'dp')
- out_weight_new: float32 [1024, 1024], P('mp', 'dp')
- up_first_new: float32 [1024, 4, 1024], P('dp', None, 'mp')
- up_second_new: float32 [1024, 4, 1024], P('dp', None, 'mp')
- up_weight_new: float32 [1024, 4, 1024], P('dp', None, 'mp')
- down_first_new: float32 [4, 1024, 1024], P(None, 'mp', 'dp')
- down_second_new: float32 [4, 1024, 1024], P(None, 'mp', 'dp')
- down_weight_new: float32 [4, 1024, 1024], P(None, 'mp', 'dp')
- row_first_new: float32 [6, 1024], replicated
- row_second_new: float32 [6, 1024], replicated
- row_vectors_new: float32 [6, 1024], replicated
- col_first_new: float32 [6, 1024], P(None, 'mp')
- col_second_new: float32 [6, 1024], P(None, 'mp')
- col_bias_new: float32 [6, 1024], P(None, 'mp')
Inputs may be any that keep to these rules, and one draw needn't show every extreme that they name: lengths of the valid prefixes; some sequence is full. `qkv_second`: every entry is positive. `out_second`: every entry is positive. `up_second`: every entry is positive. `down_second`: every entry is positive. `row_second`: every entry is positive. `col_second`: every entry is positive. `row_vectors`: gains of the norms near one in rows 0 and 3, biases in the other rows.
All inputs are finite; a program needn't handle non-finite values.
Results may differ from a plain program's by a relative error of at most 0.018.
Values may be sent and summed in bfloat16 or wider, within the bound.
No kernel may reach another device: no remote copies, remote signals or barrier semaphores. Data moves between devices by JAX's collectives and lax.ppermute only.
A program may use at most 192 MiB of HBM per device.

v0:
```python
import jax
import jax.numpy as jnp
from jax import lax
from jax.sharding import PartitionSpec as P

HEADS = 16
HEAD_DIM = 64
STEP = 5


norm_eps = 1e-05
masked_score = -1e30
first_decay = 0.5
second_decay = 0.5
matrix_rate = 0.03
vector_rate = 0.4
weight_decay = 0.1
adam_eps = 1e-08


def layer_norm(values_in, gain, shift):
    average = jnp.mean(values_in, axis=-1, keepdims=True)
    centred = values_in - average
    variance = jnp.mean(centred * centred, axis=-1, keepdims=True)
    return centred * lax.rsqrt(variance + norm_eps) * gain + shift


def gelu_tanh(hidden):
    return (
        0.5
        * hidden
        * (1.0 + jnp.tanh(0.7978845608028654 * (hidden + 0.044715 * hidden * hidden * hidden)))
    )


def adamw(weight, moment_one, moment_two, gradient, learn_rate, decay_rate):
    moment_one = first_decay * moment_one + (1.0 - first_decay) * gradient
    moment_two = second_decay * moment_two + (1.0 - second_decay) * gradient * gradient
    correct_one = 1.0 - first_decay**STEP
    correct_two = 1.0 - second_decay**STEP
    direction = moment_one / correct_one / (jnp.sqrt(moment_two / correct_two) + adam_eps)
    return (moment_one, moment_two, weight - learn_rate * (direction + decay_rate * weight))


def scores_block(query_block, key_rows, first_row, length, slopes, score_scale):
    scores = (
        jnp.einsum("qhd,khd->hqk", query_block, key_rows, preferred_element_type=jnp.float32)
        * score_scale
    )
    rows_at = first_row + jnp.arange(query_block.shape[0])
    cols_at = jnp.arange(key_rows.shape[0])
    offset = (cols_at[None, :] - rows_at[:, None]).astype(jnp.float32)
    scores = scores + slopes[:, None, None] * offset[None]
    allowed = (cols_at[None, :] <= rows_at[:, None]) & (cols_at[None, :] < length)
    return jnp.where(allowed[None], scores, masked_score)


def attend_forward(element, slopes, score_scale, block_rows):
    queries, key_rows, values, length = element
    block_count = queries.shape[0] // block_rows

    def single_block(block_index):
        first_row = block_index * block_rows
        query_block = lax.dynamic_slice_in_dim(queries, first_row, block_rows, 0)
        scores = scores_block(query_block, key_rows, first_row, length, slopes, score_scale)
        highest = jnp.max(scores, axis=-1, keepdims=True)
        exponent = jnp.exp(scores - highest)
        summed = jnp.sum(exponent, axis=-1, keepdims=True)
        probabilities = (exponent / summed).astype(jnp.bfloat16)
        result = jnp.einsum(
            "hqk,khd->qhd", probabilities, values, preferred_element_type=jnp.float32
        )
        return (result.astype(jnp.bfloat16), (highest + jnp.log(summed))[:, :, 0])

    return lax.map(single_block, jnp.arange(block_count))


def attend_backward(element, slopes, score_scale, block_rows):
    queries, key_rows, values, grad_rows, log_sums, length = element
    span = queries.shape[0]
    block_count = span // block_rows

    def single_block(running, block_index):
        key_grad, value_grad = running
        first_row = block_index * block_rows
        query_block = lax.dynamic_slice_in_dim(queries, first_row, block_rows, 0)
        grad_block = lax.dynamic_slice_in_dim(grad_rows, first_row, block_rows, 0)
        scores = scores_block(query_block, key_rows, first_row, length, slopes, score_scale)
        probabilities = jnp.exp(scores - log_sums[block_index][:, :, None])
        prob_grad = jnp.einsum(
            "qhd,khd->hqk", grad_block, values, preferred_element_type=jnp.float32
        )
        inner_sum = jnp.sum(probabilities * prob_grad, axis=-1, keepdims=True)
        score_grad = (probabilities * (prob_grad - inner_sum)).astype(jnp.bfloat16)
        query_grad = (
            jnp.einsum("hqk,khd->qhd", score_grad, key_rows, preferred_element_type=jnp.float32)
            * score_scale
        )
        key_grad = (
            key_grad
            + jnp.einsum(
                "hqk,qhd->khd", score_grad, query_block, preferred_element_type=jnp.float32
            )
            * score_scale
        )
        value_grad = value_grad + jnp.einsum(
            "hqk,qhd->khd",
            probabilities.astype(jnp.bfloat16),
            grad_block,
            preferred_element_type=jnp.float32,
        )
        return ((key_grad, value_grad), query_grad)

    start_zero = jnp.zeros(key_rows.shape, jnp.float32)
    (key_grad, value_grad), query_grad = lax.scan(
        single_block, (start_zero, start_zero), jnp.arange(block_count)
    )
    return (query_grad.reshape(span, key_rows.shape[1], key_rows.shape[2]), key_grad, value_grad)


def body(
    tokens,
    cotangent,
    lengths,
    qkv_weight,
    qkv_first,
    qkv_second,
    out_weight,
    out_first,
    out_second,
    up_weight,
    up_first,
    up_second,
    down_weight,
    down_first,
    down_second,
    row_vectors,
    row_first,
    row_second,
    col_bias,
    col_first,
    col_second,
):
    qkv_w, out_w, up_w, down_w = (
        lax.all_gather(qkv_weight.astype(jnp.bfloat16), "dp", axis=0, tiled=True),
        lax.all_gather(out_weight.astype(jnp.bfloat16), "dp", axis=1, tiled=True),
        lax.all_gather(up_weight.astype(jnp.bfloat16), "dp", axis=0, tiled=True),
        lax.all_gather(down_weight.astype(jnp.bfloat16), "dp", axis=2, tiled=True),
    )
    row_count = tokens.shape[0]
    model_width = tokens.shape[1]
    seq_count = lengths.shape[0]
    span = row_count // seq_count
    local_heads = qkv_w.shape[2] // HEAD_DIM
    block_rows = min(512, span)
    score_scale = HEAD_DIM ** (-0.5)
    head_ids = lax.axis_index("mp") * local_heads + jnp.arange(local_heads)
    slopes = jnp.exp2(-8.0 * (head_ids.astype(jnp.float32) + 1.0) / HEADS)
    share = row_count // lax.axis_size("mp")
    share_start = lax.axis_index("mp") * share
    inputs = tokens.astype(jnp.float32)
    normed_one = layer_norm(inputs, row_vectors[0], row_vectors[1])
    normed_low = normed_one.astype(jnp.bfloat16)
    projected = jnp.einsum("td,dkc->tkc", normed_low, qkv_w, preferred_element_type=jnp.float32)
    queries = (projected[:, 0] + col_bias[0]).astype(jnp.bfloat16)
    key_rows = projected[:, 1].astype(jnp.bfloat16)
    values = (projected[:, 2] + col_bias[1]).astype(jnp.bfloat16)
    head_shape = (seq_count, span, local_heads, HEAD_DIM)
    queries = queries.reshape(head_shape)
    key_rows = key_rows.reshape(head_shape)
    values = values.reshape(head_shape)

    def forward_seq(element):
        return attend_forward(element, slopes, score_scale, block_rows)

    attended, log_sums = lax.map(forward_seq, (queries, key_rows, values, lengths))
    attended = attended.reshape(row_count, local_heads * HEAD_DIM)
    places = jnp.arange(span)
    valid_all = (places[None, :] < lengths[:, None]).reshape(row_count).astype(jnp.float32)[:, None]
    branch_a = (
        lax.psum_scatter(
            jnp.dot(attended, out_w, preferred_element_type=jnp.float32),
            "mp",
            scatter_dimension=0,
            tiled=True,
        )
        + row_vectors[2]
    )
    inputs_here = lax.dynamic_slice_in_dim(inputs, share_start, share, 0)
    cotangent_here = lax.dynamic_slice_in_dim(cotangent, share_start, share, 0)
    valid_rows = lax.dynamic_slice_in_dim(valid_all, share_start, share, 0)
    resid = inputs_here + branch_a
    normed_two, norm_two_back = jax.vjp(layer_norm, resid, row_vectors[3], row_vectors[4])
    normed_two_low = lax.all_gather(normed_two.astype(jnp.bfloat16), "mp", axis=0, tiled=True)
    hidden = (
        jnp.einsum("td,dkc->tkc", normed_two_low, up_w, preferred_element_type=jnp.float32)
        + col_bias[2:]
    )
    active, gelu_back = jax.vjp(gelu_tanh, hidden)
    active_low = active.astype(jnp.bfloat16)
    branch_m = (
        lax.psum_scatter(
            jnp.einsum(
                "tkc,kcd->td", active_low, down_w, preferred_element_type=jnp.float32
            ).astype(jnp.bfloat16),
            "mp",
            scatter_dimension=0,
            tiled=True,
        ).astype(jnp.float32)
        + row_vectors[5]
    )
    outputs = resid + branch_m
    stat_terms = jnp.stack(
        [
            jnp.sum(valid_rows * outputs * outputs),
            jnp.sum(valid_rows * branch_a * branch_a),
            jnp.sum(valid_rows * branch_m * branch_m),
            jnp.sum(valid_rows),
        ]
    )
    grad_m = cotangent.astype(jnp.bfloat16)
    down_grad = jnp.einsum("tkc,td->kcd", active_low, grad_m, preferred_element_type=jnp.float32)
    active_grad = jnp.einsum("td,kcd->tkc", grad_m, down_w, preferred_element_type=jnp.float32)
    hidden_grad = gelu_back(active_grad)[0].astype(jnp.bfloat16)
    up_grad = jnp.einsum(
        "td,tkc->dkc", normed_two_low, hidden_grad, preferred_element_type=jnp.float32
    )
    normed_two_grad = lax.psum_scatter(
        jnp.einsum("tkc,dkc->td", hidden_grad, up_w, preferred_element_type=jnp.float32),
        "mp",
        scatter_dimension=0,
        tiled=True,
    )
    resid_part, gain_two_grad, shift_two_grad = norm_two_back(normed_two_grad)
    resid_grad = cotangent_here + resid_part
    grad_a_here = resid_grad.astype(jnp.bfloat16)
    grad_a = lax.all_gather(grad_a_here, "mp", axis=0, tiled=True)
    out_grad = jnp.einsum("tc,td->cd", attended, grad_a, preferred_element_type=jnp.float32)
    attended_grad = jnp.einsum(
        "td,cd->tc", grad_a, out_w, preferred_element_type=jnp.float32
    ).astype(jnp.bfloat16)

    def backward_seq(element):
        return attend_backward(element, slopes, score_scale, block_rows)

    query_grad, key_grad, value_grad = lax.map(
        backward_seq,
        (queries, key_rows, values, attended_grad.reshape(head_shape), log_sums, lengths),
    )
    qkv_grad = (
        jnp.stack([query_grad, key_grad, value_grad], axis=2)
        .astype(jnp.bfloat16)
        .reshape(row_count, 3, local_heads * HEAD_DIM)
    )
    qkv_wgrad = jnp.einsum("td,tkc->dkc", normed_low, qkv_grad, preferred_element_type=jnp.float32)
    qkv_shard, out_shard, up_shard, down_shard = (
        lax.psum_scatter(
            qkv_wgrad.astype(jnp.bfloat16), "dp", scatter_dimension=0, tiled=True
        ).astype(jnp.float32),
        lax.psum_scatter(
            out_grad.astype(jnp.bfloat16), "dp", scatter_dimension=1, tiled=True
        ).astype(jnp.float32),
        lax.psum_scatter(
            up_grad.astype(jnp.bfloat16), "dp", scatter_dimension=0, tiled=True
        ).astype(jnp.float32),
        lax.psum_scatter(
            down_grad.astype(jnp.bfloat16), "dp", scatter_dimension=2, tiled=True
        ).astype(jnp.float32),
    )
    _, norm_one_back = jax.vjp(layer_norm, inputs_here, row_vectors[0], row_vectors[1])
    normed_one_grad = lax.psum_scatter(
        jnp.einsum("tkc,dkc->td", qkv_grad, qkv_w, preferred_element_type=jnp.float32).astype(
            jnp.bfloat16
        ),
        "mp",
        scatter_dimension=0,
        tiled=True,
    ).astype(jnp.float32)
    input_part, gain_one_grad, shift_one_grad = norm_one_back(normed_one_grad)
    input_grad = resid_grad + input_part
    grad_m_here = cotangent_here.astype(jnp.bfloat16)
    row_grads = jnp.stack(
        [
            gain_one_grad,
            shift_one_grad,
            jnp.sum(grad_a_here.astype(jnp.float32), axis=0),
            gain_two_grad,
            shift_two_grad,
            jnp.sum(grad_m_here.astype(jnp.float32), axis=0),
        ]
    )
    outputs, input_grad, row_pieces, stat_pieces = (
        lax.all_gather(outputs.astype(jnp.bfloat16), "mp", axis=0, tiled=True).astype(
            outputs.dtype
        ),
        lax.all_gather(input_grad.astype(jnp.bfloat16), "mp", axis=0, tiled=True).astype(
            input_grad.dtype
        ),
        lax.all_gather(row_grads[None].astype(jnp.bfloat16), "mp", axis=0, tiled=True).astype(
            jnp.float32
        ),
        lax.all_gather(stat_terms[None].astype(jnp.bfloat16), "mp", axis=0, tiled=True).astype(
            jnp.float32
        ),
    )
    row_grads = jnp.sum(row_pieces, axis=0)
    stat_terms = jnp.sum(stat_pieces, axis=0)
    col_head = jnp.stack(
        [
            jnp.sum(qkv_grad[:, 0].astype(jnp.float32), axis=0),
            jnp.sum(qkv_grad[:, 2].astype(jnp.float32), axis=0),
        ]
    )
    col_grads = jnp.concatenate(
        [col_head, jnp.sum(hidden_grad.astype(jnp.float32), axis=0)], axis=0
    )
    row_total, col_total, stat_total = lax.psum((row_grads, col_grads, stat_terms), "dp")
    rms_stats = jnp.sqrt(stat_total[:3] / (stat_total[3] * model_width))
    qkv_new = adamw(qkv_weight, qkv_first, qkv_second, qkv_shard, matrix_rate, weight_decay)
    out_new = adamw(out_weight, out_first, out_second, out_shard, matrix_rate, weight_decay)
    up_new = adamw(up_weight, up_first, up_second, up_shard, matrix_rate, weight_decay)
    down_new = adamw(down_weight, down_first, down_second, down_shard, matrix_rate, weight_decay)
    row_new = adamw(row_vectors, row_first, row_second, row_total, vector_rate, 0.0)
    col_new = adamw(col_bias, col_first, col_second, col_total, vector_rate, 0.0)
    return (
        outputs,
        input_grad,
        rms_stats,
        qkv_new[0],
        qkv_new[1],
        qkv_new[2],
        out_new[0],
        out_new[1],
        out_new[2],
        up_new[0],
        up_new[1],
        up_new[2],
        down_new[0],
        down_new[1],
        down_new[2],
        row_new[0],
        row_new[1],
        row_new[2],
        col_new[0],
        col_new[1],
        col_new[2],
    )


def solution(mesh):
    in_specs = (
        P("dp", None),
        P("dp", None),
        P("dp"),
        P("dp", None, "mp"),
        P("dp", None, "mp"),
        P("dp", None, "mp"),
        P("mp", "dp"),
        P("mp", "dp"),
        P("mp", "dp"),
        P("dp", None, "mp"),
        P("dp", None, "mp"),
        P("dp", None, "mp"),
        P(None, "mp", "dp"),
        P(None, "mp", "dp"),
        P(None, "mp", "dp"),
        P(),
        P(),
        P(),
        P(None, "mp"),
        P(None, "mp"),
        P(None, "mp"),
    )
    out_specs = (
        P("dp", None),
        P("dp", None),
        P(),
        P("dp", None, "mp"),
        P("dp", None, "mp"),
        P("dp", None, "mp"),
        P("mp", "dp"),
        P("mp", "dp"),
        P("mp", "dp"),
        P("dp", None, "mp"),
        P("dp", None, "mp"),
        P("dp", None, "mp"),
        P(None, "mp", "dp"),
        P(None, "mp", "dp"),
        P(None, "mp", "dp"),
        P(),
        P(),
        P(),
        P(None, "mp"),
        P(None, "mp"),
        P(None, "mp"),
    )
    return jax.shard_map(body, mesh=mesh, in_specs=in_specs, out_specs=out_specs, check_vma=False)
```

profile of v0, /device:TPU:0, one launch (start us, length us, event | category | flops | bytes accessed | tf_op | source)
XLA Modules:
  0.0 1243.7 jit_solution(10739516356983932014)
XLA Ops:
  16.5 31.4 %all_gather.31 = bf16[256,1024]{1,0:T(8,128)(2,1)} all-gather(bf16[256,128]{1,0:T(8,128)(2,1)S(1)} %convert_element_type.187), channel_id=1, replica_groups=mesh['dp'=8,'mp'=4] {'dp'}, dimensions={1}, use_global_device_ids=true | all-gather | bytes 589824 | tf_op jit(solution)/shard_map/all_gather | solution.py:146
  47.9 14.8 %all-gather.9.cloned.1.call-done = bf16[1024,3,256]{0,2,1:T(8,128)(2,1)} async-done(((bf16[128,3,256]{0,2,1:T(8,128)(2,1)}), bf16[1024,3,256]{0,2,1:T(8,128)(2,1)}) %all-gather.9.cloned.1.call-update) | async-done | bytes 1572880 | tf_op jit(solution)/shard_map/all_gather | solution.py:145
  62.7 6.1 fusion.73
  71.1 96.0 %while.48 = (s32[]{:T(128)}, bf16[4,512,4,64]{1,3,2,0:T(8,128)(2,1)}, f32[4,4,512]{2,1,0:T(4,128)S(1)}, s32[4]{0:T(128)S(1)}, s32[]{:T(128)}, /*index=5*/bf16[20...) while((s32[]{:T(128)}, ...), condition=%wide.region_5.6_spmd.clone, body=%wide.region_2.5_spmd.clone.sunk | while | flops 1153565184 | bytes 90777904 | solution.py:75
  74.3 6.4 fusion.147
  80.7 5.8 fusion.148
  86.5 8.6 fusion.149
  98.2 6.3 fusion.147
  104.5 5.8 fusion.148
  110.3 8.6 fusion.149
  122.0 6.3 fusion.147
  128.4 5.8 fusion.148
  134.2 8.6 fusion.149
  145.8 6.3 fusion.147
  152.2 5.8 fusion.148
  158.0 8.6 fusion.149
  170.5 4.7 fusion.102
  177.1 8.0 convert_element_type.180
  185.1 60.6 %reduce-scatter.13.cloned.1.call-done = f32[512,1024]{1,0:T(8,128)} async-done(((f32[2048,1024]{1,0:T(8,128)}), f32[512,1024]{1,0:T(8,128)}) %reduce-scatter.13.cloned.1.call-update) | async-done | bytes 2097168 | tf_op jit(solution)/shard_map/reduce_scatter | solution.py:181
  251.7 46.2 %all-gather.13.cloned.1.call-done = bf16[1024,4,256]{2,0,1:T(8,128)(2,1)} async-done(((bf16[128,4,256]{2,0,1:T(8,128)(2,1)}), bf16[1024,4,256]{2,0,1:T(8,128)(2,1)}) %all-gather.13.cloned.1.call-update) | async-done | bytes 2097168 | tf_op jit(solution)/shard_map/all_gather | solution.py:147
  298.0 35.1 %all-gather.11.cloned.1.call-done = bf16[2048,1024]{1,0:T(8,128)(2,1)} async-done(((bf16[512,1024]{1,0:T(8,128)(2,1)}), bf16[2048,1024]{1,0:T(8,128)(2,1)}) %all-gather.11.cloned.1.call-update) | async-done | bytes 4194320 | tf_op jit(solution)/shard_map/all_gather | solution.py:194
  333.0 6.9 fusion.51
  343.3 9.4 fusion.68
  360.5 68.0 %reduce-scatter.27.cloned.1.call-done = bf16[128,1024]{1,0:T(8,128)(2,1)} async-done(((bf16[1024,1024]{1,0:T(8,128)(2,1)}), bf16[128,1024]{1,0:T(8,128)(2,1)}) %reduce-scatter.27.cloned.1.call-update) | async-done | bytes 262160
  432.6 50.1 %all-gather.15.cloned.1.call-done = bf16[4,256,1024]{2,1,0:T(8,128)(2,1)} async-done(((bf16[4,256,128]{2,1,0:T(8,128)(2,1)}), bf16[4,256,1024]{2,1,0:T(8,128)(2,1)}) %all-gather.15.cloned.1.call-update) | async-done | bytes 2097168 | tf_op jit(solution)/shard_map/all_gather | solution.py:148
  482.7 11.7 bitcast_convert_fusion.1
  494.6 16.3 %convert_reduce_fusion = (f32[4,256]{1,0:T(4,128)}, bf16[2048,4,256]{2,0,1:T(8,128)(2,1)S(1)}) fusion(bf16[4,256,1024]{2,1,0:T(8,128)(2,1)} %all-gather.15.cloned.1.call-done, f32[2048,1024]{1,0:T(8,128)} %param.26, f32[2048,4,256]{2,0,1:T(8,128)} %copy-done.54, f32[4,256]{1,0:T(4,128)S(1)} %slice.56), kind=kOutput, calls=%fused_computation.64 | convolution fusion | flops 4353686528 | bytes 23076864 | tf_op jit(solution)/shard_map/td,kcd->tkc/dot_general | solution.py:223
  512.9 7.0 convolution_bitcast_fusion
  520.7 16.6 %reduce-scatter.15.cloned.1.call-done = bf16[512,1024]{1,0:T(8,128)(2,1)} async-done(((bf16[2048,1024]{1,0:T(8,128)(2,1)}), bf16[512,1024]{1,0:T(8,128)(2,1)}) %reduce-scatter.15.cloned.1.call-update) | async-done | bytes 1048592 | tf_op jit(solution)/shard_map/reduce_scatter | solution.py:202
  537.3 74.9 %reduce-scatter.17.cloned.1.call-done = f32[512,1024]{1,0:T(8,128)} async-done(((f32[2048,1024]{1,0:T(8,128)}), f32[512,1024]{1,0:T(8,128)}) %reduce-scatter.17.cloned.1.call-update) | async-done | bytes 2097168 | tf_op jit(solution)/shard_map/reduce_scatter | solution.py:228
  612.2 5.8 multiply_reduce_fusion.2
  624.2 34.6 %all-gather.19.cloned.1.call-done = bf16[2048,1024]{1,0:T(8,128)(2,1)} async-done(((bf16[512,1024]{1,0:T(8,128)(2,1)}), bf16[2048,1024]{1,0:T(8,128)(2,1)}) %all-gather.19.cloned.1.call-update) | async-done | bytes 4194320 | tf_op jit(solution)/shard_map/all_gather | solution.py:237
  663.2 222.7 %while.49 = (s32[]{:T(128)}, f32[2048,4,64]{0,2,1:T(8,128)}, f32[2048,4,64]{0,2,1:T(8,128)}, bf16[4,512,4,64]{1,3,2,0:T(8,128)(2,1)}, s32[4]{0:T(128)S(1)}, /*in...) while((s32[]{:T(128)}, f32[2048,4,64]{0,2,1:T(8,128)}, ...), condition=%wide.region_15.16_spmd.clone, body=%wide.region_13.15_spmd.clone.sunk | while | flops 2737439232 | bytes 216582512 | solution.py:115
  668.5 9.1 fusion.159
  677.5 13.9 %multiply_reduce_fusion.7 = (f32[4,512]{1,0:T(4,128)S(1)}, f32[4,512,2048]{2,1,0:T(8,128)}) fusion(f32[4,512,2048]{2,1,0:T(8,128)} %fusion.159, f32[4,512]{1,0:T(4,128)S(1)} %dynamic-slice_bitcast_fusion.2, f32[512,2048]{1,0:T(8,128)S(1)} %subtract_convert_fusion.5, f32[4]{0:T(128)S(1)} %multiply_exponential_fusion.5, ...), kind=kOutput, calls=%fused_computation.24.clone.1 | convolution fusion | flops 566228992 | bytes 40124436 | tf_op jit(solution)/shard_map/while/body/eval_jaxpr/while/body/eval_jaxpr/qhd,khd->hqk/dot_general | solution.py:47
  691.5 11.5 multiply_convert_fusion.5
  722.9 9.1 fusion.159
  731.9 13.9 %multiply_reduce_fusion.7 = (f32[4,512]{1,0:T(4,128)S(1)}, f32[4,512,2048]{2,1,0:T(8,128)}) fusion(f32[4,512,2048]{2,1,0:T(8,128)} %fusion.159, f32[4,512]{1,0:T(4,128)S(1)} %dynamic-slice_bitcast_fusion.2, f32[512,2048]{1,0:T(8,128)S(1)} %subtract_convert_fusion.5, f32[4]{0:T(128)S(1)} %multiply_exponential_fusion.5, ...), kind=kOutput, calls=%fused_computation.24.clone.1 | convolution fusion | flops 566228992 | bytes 40124436 | tf_op jit(solution)/shard_map/while/body/eval_jaxpr/while/body/eval_jaxpr/qhd,khd->hqk/dot_general | solution.py:47
  745.9 11.5 multiply_convert_fusion.5
  761.2 4.6 fusion.162
  769.2 4.6 fusion.161
  778.7 9.1 fusion.159
  787.8 13.9 %multiply_reduce_fusion.7 = (f32[4,512]{1,0:T(4,128)S(1)}, f32[4,512,2048]{2,1,0:T(8,128)}) fusion(f32[4,512,2048]{2,1,0:T(8,128)} %fusion.159, f32[4,512]{1,0:T(4,128)S(1)} %dynamic-slice_bitcast_fusion.2, f32[512,2048]{1,0:T(8,128)S(1)} %subtract_convert_fusion.5, f32[4]{0:T(128)S(1)} %multiply_exponential_fusion.5, ...), kind=kOutput, calls=%fused_computation.24.clone.1 | convolution fusion | flops 566228992 | bytes 40124436 | tf_op jit(solution)/shard_map/while/body/eval_jaxpr/while/body/eval_jaxpr/qhd,khd->hqk/dot_general | solution.py:47
  801.7 11.5 multiply_convert_fusion.5
  817.1 4.6 fusion.162
  825.1 4.6 fusion.161
  834.6 9.1 fusion.159
  843.7 13.9 %multiply_reduce_fusion.7 = (f32[4,512]{1,0:T(4,128)S(1)}, f32[4,512,2048]{2,1,0:T(8,128)}) fusion(f32[4,512,2048]{2,1,0:T(8,128)} %fusion.159, f32[4,512]{1,0:T(4,128)S(1)} %dynamic-slice_bitcast_fusion.2, f32[512,2048]{1,0:T(8,128)S(1)} %subtract_convert_fusion.5, f32[4]{0:T(128)S(1)} %multiply_exponential_fusion.5, ...), kind=kOutput, calls=%fused_computation.24.clone.1 | convolution fusion | flops 566228992 | bytes 40124436 | tf_op jit(solution)/shard_map/while/body/eval_jaxpr/while/body/eval_jaxpr/qhd,khd->hqk/dot_general | solution.py:47
  857.6 11.5 multiply_convert_fusion.5
  873.0 4.6 fusion.162
  881.0 4.6 fusion.161
  896.9 7.5 bitcast_convert_fusion
  904.5 9.5 fusion.65
  921.5 8.3 convolution_convert_fusion.1
  929.9 19.2 %reduce-scatter.19.cloned.1.call-done = bf16[512,1024]{1,0:T(8,128)(2,1)} async-done(((bf16[2048,1024]{1,0:T(8,128)(2,1)}), bf16[512,1024]{1,0:T(8,128)(2,1)}) %reduce-scatter.19.cloned.1.call-update) | async-done | bytes 1048592 | tf_op jit(solution)/shard_map/reduce_scatter | solution.py:271
  959.4 61.7 %reduce-scatter.23.cloned.1.call-done = bf16[128,4,256]{2,0,1:T(8,128)(2,1)} async-done(((bf16[1024,4,256]{2,0,1:T(8,128)(2,1)}), bf16[128,4,256]{2,0,1:T(8,128)(2,1)}) %reduce-scatter.23.cloned.1.call-update) | async-done | bytes 262160 | tf_op jit(solution)/shard_map/reduce_scatter | solution.py:263
  1029.0 5.0 all-gather
  1035.8 20.1 %all-gather.17.cloned.1.call-done = bf16[2048,1024]{1,0:T(8,128)(2,1)} async-done(((bf16[512,1024]{1,0:T(8,128)(2,1)}), bf16[2048,1024]{1,0:T(8,128)(2,1)}) %all-gather.17.cloned.1.call-update) | async-done | bytes 4194320 | tf_op jit(solution)/shard_map/all_gather | solution.py:293
  1056.0 6.6 convert_element_type.195
  1063.2 58.1 %reduce-scatter.25.cloned.1.call-done = bf16[128,256]{1,0:T(8,128)(2,1)} async-done(((bf16[1024,256]{1,0:T(8,128)(2,1)}), bf16[128,256]{1,0:T(8,128)(2,1)}) %reduce-scatter.25.cloned.1.call-update) | async-done | bytes 65552
  1125.7 5.2 all_gather.39
  1130.9 58.6 %reduce-scatter.21.cloned.1.call-done = bf16[128,3,256]{2,0,1:T(8,128)(2,1)} async-done(((bf16[1024,3,256]{2,0,1:T(8,128)(2,1)}), bf16[128,3,256]{2,0,1:T(8,128)(2,1)}) %reduce-scatter.21.cloned.1.call-update) | async-done | bytes 196624 | tf_op jit(solution)/shard_map/reduce_scatter | solution.py:257
  1191.9 35.4 %all-reduce = (f32[4]{0:T(128)S(1)}, f32[6,1024]{1,0:T(8,128)S(1)}, f32[6,256]{1,0:T(8,128)S(1)}) all-reduce(f32[4]{0:T(128)S(1)} %copy-done.52, f32[6,1024]{1,0:T(8,128)S(1)} %convert_reduce_fusion.4, f32[6,256]{1,0:T(8,128)S(1)} %pad_maximum_fusion.3), channel_id=1, replica_groups=mesh['dp'=8,'mp'=4] {'dp'}, use_global_device_ids=true, to_apply=%region_26.27 | all-reduce | flops 7684 | bytes 61472 | tf_op jit(solution)/shard_map/psum | solution.py:317
  1230.3 6.6 convert_element_type.203
  (298 shorter events, 154.5 us)
Async XLA Ops:
  7.2 55.5 %all-gather.9.cloned.1.call-start = ((), (), s32[]{:S(2)}) async-start(), calls=%async_computation.8 | async-start | bytes 1769472 | tf_op jit(solution)/shard_map/all_gather | solution.py:145
  9.1 236.6 %reduce-scatter.13.cloned.1.call-start = ((), (), s32[]{:S(2)}) async-start(), calls=%async_computation.9 | async-start | bytes 10485760 | tf_op jit(solution)/shard_map/reduce_scatter | solution.py:181
  11.0 4.8 copy-start.24
  14.5 54.3 %copy-start.30 = (f32[2048]{0:T(1024)}, f32[2048]{0:T(1024)S(1)}, u32[]{:S(2)}) copy-start(f32[2048]{0:T(1024)S(1)} %broadcast_multiply_fusion) | copy-start | bytes 24580
  15.9 52.9 %copy-start.45 = (f32[2048]{0:T(1024)}, f32[2048]{0:T(1024)S(1)}, u32[]{:S(2)}) copy-start(f32[2048]{0:T(1024)S(1)} %add_rsqrt_fusion) | copy-start | bytes 24580
  16.5 52.3 %copy-start.26 = (f32[1,1024]{1,0:T(1,128)}, f32[1,1024]{1,0:T(1,128)S(1)}, u32[]{:S(2)}) copy-start(f32[1,1024]{1,0:T(1,128)S(1)} %get-tuple-element.417) | copy-start | bytes 12292
  16.5 52.3 %copy-start.49 = (f32[1,1024]{1,0:T(1,128)}, f32[1,1024]{1,0:T(1,128)S(1)}, u32[]{:S(2)}) copy-start(f32[1,1024]{1,0:T(1,128)S(1)} %get-tuple-element.416) | copy-start | bytes 12292
  74.3 6.4 copy-start.1
  98.1 6.4 copy-start.1
  122.0 6.4 copy-start.1
  145.8 6.4 copy-start.1
  175.2 122.8 %all-gather.13.cloned.1.call-start = ((), (), s32[]{:S(2)}) async-start(), calls=%async_computation.11 | async-start | bytes 2359296 | tf_op jit(solution)/shard_map/all_gather | solution.py:147
  177.0 156.0 %all-gather.11.cloned.1.call-start = ((), (), s32[]{:S(2)}) async-start(), calls=%async_computation.10 | async-start | bytes 5242880 | tf_op jit(solution)/shard_map/all_gather | solution.py:194
  177.0 68.6 %copy-start.29 = (f32[1,1024]{1,0:T(1,128)S(1)}, f32[1,1024]{1,0:T(1,128)}, u32[]{:S(2)}) copy-start(f32[1,1024]{1,0:T(1,128)} %get-tuple-element.415) | copy-start | bytes 12292
  251.6 176.9 %reduce-scatter.27.cloned.1.call-start = ((), (), s32[]{:S(2)}) async-start(), calls=%async_computation.22 | async-start | bytes 2359296
  357.0 73.0 %copy-start.22 = (f32[4,256,128]{2,1,0:T(8,128)S(1)}, f32[4,256,128]{2,1,0:T(8,128)}, u32[]{:S(2)}) copy-start(f32[4,256,128]{2,1,0:T(8,128)} %param.37) | copy-start | bytes 1572868
  357.0 73.0 %copy-start.23 = (f32[4,256,128]{2,1,0:T(8,128)S(1)}, f32[4,256,128]{2,1,0:T(8,128)}, u32[]{:S(2)}) copy-start(f32[4,256,128]{2,1,0:T(8,128)} %param.39) | copy-start | bytes 1572868
  360.5 122.2 %all-gather.15.cloned.1.call-start = ((), (), s32[]{:S(2)}) async-start(), calls=%async_computation.12 | async-start | bytes 2359296 | tf_op jit(solution)/shard_map/all_gather | solution.py:148
  432.5 104.8 %reduce-scatter.15.cloned.1.call-start = ((), (), s32[]{:S(2)}) async-start(), calls=%async_computation.13 | async-start | bytes 5242880 | tf_op jit(solution)/shard_map/reduce_scatter | solution.py:202
  494.4 117.7 %reduce-scatter.17.cloned.1.call-start = ((), (), s32[]{:S(2)}) async-start(), calls=%async_computation.15 | async-start | bytes 10485760 | tf_op jit(solution)/shard_map/reduce_scatter | solution.py:228
  494.6 18.3 %copy-start.53 = (bf16[1024,4,256]{2,0,1:T(8,128)(2,1)S(1)}, bf16[1024,4,256]{2,0,1:T(8,128)(2,1)}, u32[]{:S(2)}) copy-start(bf16[1024,4,256]{2,0,1:T(8,128)(2,1)} %all-gather.13.cloned.1.call-done) | copy-start | bytes 6291460
  519.9 92.2 %copy-start.38 = (f32[1,1024]{1,0:T(1,128)S(1)}, f32[1,1024]{1,0:T(1,128)}, u32[]{:S(2)}) copy-start(f32[1,1024]{1,0:T(1,128)} %get-tuple-element.412) | copy-start | bytes 12292
  520.0 138.8 %all-gather.19.cloned.1.call-start = ((), (), s32[]{:S(2)}) async-start(), calls=%async_computation.16 | async-start | bytes 5242880 | tf_op jit(solution)/shard_map/all_gather | solution.py:237
  612.2 5.8 copy-start.4
  612.2 5.8 copy-start.14
  618.7 44.6 %copy-start.36 = (f32[512]{0:T(512)}, f32[512]{0:T(512)S(1)}, u32[]{:S(2)}) copy-start(f32[512]{0:T(512)S(1)} %negate_multiply_fusion.1) | copy-start | bytes 6148
  624.1 39.1 %copy-start.6 = (bf16[2048,4,64]{0,2,1:T(8,128)(2,1)S(1)}, bf16[2048,4,64]{0,2,1:T(8,128)(2,1)}, u32[]{:S(2)}) copy-start(bf16[2048,4,64]{0,2,1:T(8,128)(2,1)} %get-tuple-element.668) | copy-start | bytes 3145732
  624.1 324.9 %reduce-scatter.19.cloned.1.call-start = ((), (), s32[]{:S(2)}) async-start(), calls=%async_computation.17 | async-start | bytes 5242880 | tf_op jit(solution)/shard_map/reduce_scatter | solution.py:271
  691.5 15.4 %copy-start = (f32[4,512,2048]{2,1,0:T(8,128)S(1)}, f32[4,512,2048]{2,1,0:T(8,128)}, u32[]{:S(2)}) copy-start(f32[4,512,2048]{2,1,0:T(8,128)} %get-tuple-element.558) | copy-start | bytes 50331652 | tf_op jit(solution)/shard_map/while/body/eval_jaxpr/while
  745.9 15.4 %copy-start = (f32[4,512,2048]{2,1,0:T(8,128)S(1)}, f32[4,512,2048]{2,1,0:T(8,128)}, u32[]{:S(2)}) copy-start(f32[4,512,2048]{2,1,0:T(8,128)} %get-tuple-element.558) | copy-start | bytes 50331652 | tf_op jit(solution)/shard_map/while/body/eval_jaxpr/while
  801.7 15.4 %copy-start = (f32[4,512,2048]{2,1,0:T(8,128)S(1)}, f32[4,512,2048]{2,1,0:T(8,128)}, u32[]{:S(2)}) copy-start(f32[4,512,2048]{2,1,0:T(8,128)} %get-tuple-element.558) | copy-start | bytes 50331652 | tf_op jit(solution)/shard_map/while/body/eval_jaxpr/while
  857.6 15.4 %copy-start = (f32[4,512,2048]{2,1,0:T(8,128)S(1)}, f32[4,512,2048]{2,1,0:T(8,128)}, u32[]{:S(2)}) copy-start(f32[4,512,2048]{2,1,0:T(8,128)} %get-tuple-element.558) | copy-start | bytes 50331652 | tf_op jit(solution)/shard_map/while/body/eval_jaxpr/while
  886.0 6.4 copy-start.2
  892.5 11.9 copy-start.10
  904.4 10.2 copy-start.16
  904.4 116.7 %reduce-scatter.23.cloned.1.call-start = ((), (), s32[]{:S(2)}) async-start(), calls=%async_computation.20 | async-start | bytes 2359296 | tf_op jit(solution)/shard_map/reduce_scatter | solution.py:263
  913.9 142.1 %all-gather.17.cloned.1.call-start = ((), (), s32[]{:S(2)}) async-start(), calls=%async_computation.14 | async-start | bytes 5242880 | tf_op jit(solution)/shard_map/all_gather | solution.py:293
  914.5 6.9 copy-start.21
  914.5 6.9 copy-start.27
  914.5 6.9 copy-start.31
  914.6 6.9 copy-start.46
  914.6 6.9 copy-start.50
  914.6 206.7 %reduce-scatter.25.cloned.1.call-start = ((), (), s32[]{:S(2)}) async-start(), calls=%async_computation.21 | async-start | bytes 589824
  921.2 8.7 copy-start.40
  921.2 268.3 %reduce-scatter.21.cloned.1.call-start = ((), (), s32[]{:S(2)}) async-start(), calls=%async_computation.19 | async-start | bytes 1769472 | tf_op jit(solution)/shard_map/reduce_scatter | solution.py:257
  929.8 25.5 %copy-start.8 = (f32[512,1024]{1,0:T(8,128)S(1)}, f32[512,1024]{1,0:T(8,128)}, u32[]{:S(2)}) copy-start(f32[512,1024]{1,0:T(8,128)} %copy-done.7) | copy-start | bytes 6291460
  929.8 25.5 %copy-start.37 = (f32[512]{0:T(512)S(1)}, f32[512]{0:T(512)}, u32[]{:S(2)}) copy-start(f32[512]{0:T(512)} %copy-done.36) | copy-start | bytes 6148
  929.8 300.5 %all-gather.21.cloned.1.call-start = ((), (), s32[]{:S(2)}) async-start(), calls=%async_computation.18 | async-start | bytes 5242880 | tf_op jit(solution)/shard_map/all_gather | solution.py:296
  949.1 6.2 copy-start.9
  958.8 75.3 %copy-start.48 = (bf16[1024]{0:T(1024)(128)(2,1)S(1)}, bf16[1024]{0:T(1024)(128)(2,1)}, u32[]{:S(2)}) copy-start(bf16[1024]{0:T(1024)(128)(2,1)} %get-tuple-element.325) | copy-start | bytes 6148
  958.8 75.3 %copy-start.47 = (bf16[1024]{0:T(1024)(128)(2,1)S(1)}, bf16[1024]{0:T(1024)(128)(2,1)}, u32[]{:S(2)}) copy-start(bf16[1024]{0:T(1024)(128)(2,1)} %get-tuple-element.327) | copy-start | bytes 6148
  958.8 75.3 %copy-start.42 = (bf16[1024]{0:T(1024)(128)(2,1)S(1)}, bf16[1024]{0:T(1024)(128)(2,1)}, u32[]{:S(2)}) copy-start(bf16[1024]{0:T(1024)(128)(2,1)} %get-tuple-element.396) | copy-start | bytes 6148
  958.8 75.9 %copy-start.41 = (bf16[1024]{0:T(1024)(128)(2,1)S(1)}, bf16[1024]{0:T(1024)(128)(2,1)}, u32[]{:S(2)}) copy-start(bf16[1024]{0:T(1024)(128)(2,1)} %get-tuple-element.406) | copy-start | bytes 6148
  1035.8 26.8 %copy-start.13 = (bf16[2048,1,256]{0,2,1:T(8,128)(2,1)S(1)}, bf16[2048,1,256]{0,2,1:T(8,128)(2,1)}, u32[]{:S(2)}) copy-start(bf16[2048,1,256]{0,2,1:T(8,128)(2,1)} %copy-done.12) | copy-start | bytes 3145732
  1035.8 27.1 %copy-start.11 = (bf16[2048,4,64]{0,2,1:T(8,128)(2,1)S(1)}, bf16[2048,4,64]{0,2,1:T(8,128)(2,1)}, u32[]{:S(2)}) copy-start(bf16[2048,4,64]{0,2,1:T(8,128)(2,1)} %copy-done.10) | copy-start | bytes 3145732
  1056.0 7.2 copy-start.51
  1062.6 126.9 %copy-start.19 = (f32[128,3,256]{2,0,1:T(8,128)S(1)}, f32[128,3,256]{2,0,1:T(8,128)}, u32[]{:S(2)}) copy-start(f32[128,3,256]{2,0,1:T(8,128)} %param.28) | copy-start | bytes 1179652
  1062.6 166.4 %copy-start.35 = (f32[6,256]{1,0:T(8,128)S(1)}, f32[6,256]{1,0:T(8,128)}, u32[]{:S(2)}) copy-start(f32[6,256]{1,0:T(8,128)} %param.43) | copy-start | bytes 18436
  1062.9 129.0 %copy-start.52 = (f32[4]{0:T(128)S(1)}, f32[4]{0:T(128)}, u32[]{:S(2)}) copy-start(f32[4]{0:T(128)} %convert_reduce_fusion.5) | copy-start | bytes 52
  1062.9 166.2 %copy-start.43 = (f32[6,256]{1,0:T(8,128)S(1)}, f32[6,256]{1,0:T(8,128)}, u32[]{:S(2)}) copy-start(f32[6,256]{1,0:T(8,128)} %param.45) | copy-start | bytes 18436
  1062.9 166.2 %copy-start.44 = (f32[6,256]{1,0:T(8,128)S(1)}, f32[6,256]{1,0:T(8,128)}, u32[]{:S(2)}) copy-start(f32[6,256]{1,0:T(8,128)} %param.44) | copy-start | bytes 18436
  1062.9 166.8 %copy-start.25 = (f32[6,1024]{1,0:T(8,128)S(1)}, f32[6,1024]{1,0:T(8,128)}, u32[]{:S(2)}) copy-start(f32[6,1024]{1,0:T(8,128)} %param.40) | copy-start | bytes 73732
  1062.9 166.8 %copy-start.32 = (f32[6,1024]{1,0:T(8,128)S(1)}, f32[6,1024]{1,0:T(8,128)}, u32[]{:S(2)}) copy-start(f32[6,1024]{1,0:T(8,128)} %param.42) | copy-start | bytes 73732
  1062.9 166.8 %copy-start.33 = (f32[6,1024]{1,0:T(8,128)S(1)}, f32[6,1024]{1,0:T(8,128)}, u32[]{:S(2)}) copy-start(f32[6,1024]{1,0:T(8,128)} %param.41) | copy-start | bytes 73732
  (13 other events, 34.6 us)
Sparse Core Ops, SparseCore 0:
  10.6 51.9 all-gather.8
  175.3 70.3 reduce-scatter.12
  248.6 49.2 all-gather.12
  300.0 32.9 all-gather.10
  360.6 67.9 reduce-scatter.26
  432.6 50.0 all-gather.14
  494.5 42.6 reduce-scatter.14
  540.4 71.6 reduce-scatter.16
  624.3 34.4 all-gather.18
  904.5 44.5 reduce-scatter.18
  952.6 68.4 reduce-scatter.22
  1022.5 33.4 all-gather.16
  1059.3 61.8 reduce-scatter.24
  1124.9 64.5 reduce-scatter.20
  1191.5 33.4 all-gather.20
where the time goes:
time: 1250 us; the launch traced here: 1240 us
  waiting for transfers between devices  619 us (50%)
  matrix products  297 us (24%)
  other arithmetic  153 us (12%)
  blocking collectives  77 us (6%)
  local copies, waits for them, and re-layouts  65.5 us (5%)
  between operations  16.1 us (1%)
  loops' own time  14.8 us (1%)
    unnamed x17, waiting for transfers between devices  127 us
    dot_general x8, matrix products, scores_block(): jnp.einsum('qhd,khd->hqk', query_block, key_rows, preferred_element_type=...  81.2 us
    reduce_scatter x1, waiting for transfers between devices, body(): lax.psum_scatter(jnp.einsum('tkc,dkc->td', hidden_grad, up_w, preferred_e...  74.9 us
    reduce_scatter x1, waiting for transfers between devices, body(): lax.psum_scatter(up_grad.astype(jnp.bfloat16), 'dp', scatter_dimension=0,...  61.7 us
    reduce_scatter x1, waiting for transfers between devices, body(): lax.psum_scatter(jnp.dot(attended, out_w, preferred_element_type=jnp.floa...  60.6 us
    reduce_scatter x1, waiting for transfers between devices, body(): lax.psum_scatter(qkv_wgrad.astype(jnp.bfloat16), 'dp', scatter_dimension=...  58.6 us
    all_gather x1, waiting for transfers between devices, body(): lax.all_gather(down_weight.astype(jnp.bfloat16), 'dp', axis=2, tiled=True)  50.1 us
    all_gather x1, waiting for transfers between devices, body(): lax.all_gather(up_weight.astype(jnp.bfloat16), 'dp', axis=0, tiled=True)  46.2 us
  transfers between devices with their start and end apart: 15, of which 14 were waited for; matrix products, arithmetic and copies ran while one was open for 8% of the time, Pallas kernels for 0%

commit v1 on v0

v1 whole, which is shorter than its diff:
```python
import functools

import jax
import jax.numpy as jnp
from jax import lax
from jax.experimental import pallas as pl
from jax.experimental.pallas import tpu as pltpu
from jax.sharding import PartitionSpec as P

HEADS = 16
HEAD_DIM = 64
STEP = 5

norm_eps = 1e-05
masked_score = -1e30
first_decay = 0.5
second_decay = 0.5
matrix_rate = 0.03
vector_rate = 0.4
weight_decay = 0.1
adam_eps = 1e-08
gelu_scale = 0.7978845608028654
gelu_cubic = 0.044715

F32 = jnp.float32
BF = jnp.bfloat16
NN = (((1,), (0,)), ((), ()))
NT = (((1,), (1,)), ((), ()))
TN = (((0,), (0,)), ((), ()))
MIB = 2**20


def dot(a, b, dims=NN):
    return lax.dot_general(a, b, dims, preferred_element_type=F32)


def adamw(weight, moment_one, moment_two, gradient, learn_rate, decay_rate):
    moment_one = first_decay * moment_one + (1.0 - first_decay) * gradient
    moment_two = second_decay * moment_two + (1.0 - second_decay) * gradient * gradient
    correct_one = 1.0 - first_decay**STEP
    correct_two = 1.0 - second_decay**STEP
    direction = moment_one / correct_one / (jnp.sqrt(moment_two / correct_two) + adam_eps)
    return (moment_one, moment_two, weight - learn_rate * (direction + decay_rate * weight))


def to_core(x):
    return lax.ppermute(x, "mp", [(i, i ^ 1) for i in range(lax.axis_size("mp"))])


def to_chip(x):
    return lax.ppermute(x, "mp", [(i, i ^ 2) for i in range(lax.axis_size("mp"))])


def to_all(x):
    return lax.all_to_all(x, "mp", split_axis=0, concat_axis=0, tiled=True)


def ring_order(n):
    return [0, 2, 4, 6, 7, 5, 3, 1] if n == 8 else list(range(n))


def ring_perms(n):
    order = ring_order(n)
    up = [(order[p], order[(p + 1) % n]) for p in range(n)]
    down = [(order[p], order[(p - 1) % n]) for p in range(n)]
    return up, down


def ring_index(n):
    order = ring_order(n)
    place = jnp.array([order.index(i) for i in range(n)], jnp.int32)[lax.axis_index("dp")]
    return jnp.array(order, jnp.int32)[(place + jnp.arange(n)) % n]


class Gather:
    def __init__(self, piece):
        self.n = lax.axis_size("dp")
        self.perms = ring_perms(self.n)
        self.pieces = [piece] + [None] * (self.n - 1)
        self.up = self.down = piece
        self.done = 0

    def hop(self, *gates):
        if self.done == self.n // 2:
            return
        self.done += 1
        self.up = self.pieces[self.n - self.done] = lax.ppermute(after(self.up, *gates), "dp", self.perms[0])
        if self.done <= (self.n - 1) // 2:
            self.down = self.pieces[self.done] = lax.ppermute(after(self.down, *gates), "dp", self.perms[1])

    def finish(self):
        while self.done < self.n // 2:
            self.hop()
        return self.pieces


class Reduce:
    def __init__(self, total, index):
        self.n = lax.axis_size("dp")
        self.perms = ring_perms(self.n)
        self.total, self.index = total, index
        self.rows = total.shape[0] // self.n
        self.up = self.down = None
        self.done = 0

    def block(self, k):
        return lax.dynamic_slice_in_dim(self.total, self.index[k % self.n] * self.rows, self.rows, 0)

    def add(self, x, k):
        if x is None:
            return self.block(k)
        return (x.astype(F32) + self.block(k).astype(F32)).astype(BF)

    def hop(self, *gates):
        ups, downs = self.n // 2, (self.n - 1) // 2
        if self.done == ups:
            return
        up = after(self.add(self.up, ups - self.done), *gates)
        if self.done < downs:
            down = after(self.add(self.down, self.done - downs), *gates)
            self.down = lax.ppermute(down, "dp", self.perms[1])
        self.up = lax.ppermute(up, "dp", self.perms[0])
        self.done += 1

    def finish(self):
        while self.done < self.n // 2:
            self.hop()
        return self.block(0).astype(F32) + self.up.astype(F32) + self.down.astype(F32)


def after(x, *others):
    return lax.optimization_barrier((x, *others))[0] if others else x


def cost(flops, nbytes):
    return pl.CostEstimate(flops=int(flops), bytes_accessed=int(nbytes), transcendentals=0)


def whole(shape):
    return pl.BlockSpec(shape, lambda *_: (0,) * len(shape), pipeline_mode=pl.Buffered(1))


def assemble_kernel(index_ref, pieces, out_ref, at):
    rows, cols = pieces[0].shape
    for k, piece in enumerate(pieces):
        row = pl.multiple_of(index_ref[k] * rows, rows)
        out_ref[pl.ds(row, rows), at : at + cols] = piece[...]


def assemble(index, *groups):
    n = len(groups[0])
    shapes = [group[0].shape for group in groups]
    shape = (n * shapes[0][0], sum(cols for _, cols in shapes))

    def kernel(index_ref, *refs):
        at = 0
        for k, (_, cols) in enumerate(shapes):
            assemble_kernel(index_ref, refs[k * n : (k + 1) * n], refs[-1], at)
            at += cols

    return pl.pallas_call(
        kernel,
        out_shape=jax.ShapeDtypeStruct(shape, BF),
        grid=(1,),
        in_specs=[pl.BlockSpec(memory_space=pltpu.SMEM)]
        + [whole(piece.shape) for group in groups for piece in group],
        out_specs=whole(shape),
        compiler_params=pltpu.CompilerParams(vmem_limit_bytes=16 * MIB),
        cost_estimate=cost(0, 4 * shape[0] * shape[1]),
        name="assemble",
    )(index, *[piece for group in groups for piece in group])


def split3(x):
    hi = x.astype(BF).astype(F32)
    rest = x - hi
    mid = rest.astype(BF).astype(F32)
    return hi, mid, rest - mid


def put3(base, lane, first, x):
    hi, mid, lo = split3(x)
    return jnp.where(
        lane == first,
        hi,
        jnp.where(lane == first + 1, mid, jnp.where(lane == first + 2, lo, base)),
    )


def project_kernel(index_ref, slope_ref, length_ref, n_ref, bias_ref, *refs, heads):
    *pieces, q_ref, k_ref, v_ref, w_ref = refs

    @pl.when(pl.program_id(0) == 0)
    def _():
        assemble_kernel(index_ref, pieces, w_ref, 0)

    rows = n_ref.shape[0]
    width = heads * HEAD_DIM
    out = dot(n_ref[...], w_ref[...])
    query = (out[:, :width] + bias_ref[0:1, :]).astype(BF).astype(F32) * (HEAD_DIM**-0.5)
    key = out[:, width : 2 * width]
    value = out[:, 2 * width :] + bias_ref[1:2, :]
    lane = lax.broadcasted_iota(jnp.int32, (rows, 128), 1)
    at = lax.broadcasted_iota(jnp.int32, (rows, 128), 0) + pl.program_id(0) * rows
    ones = ((lane >= 64) & (lane < 67)).astype(F32)
    more = ((lane >= 67) & (lane < 70)).astype(F32)
    seen = at < length_ref[0]
    zero = jnp.zeros((rows, 64), F32)
    for h in range(heads):
        cols = slice(h * HEAD_DIM, (h + 1) * HEAD_DIM)
        slope = jnp.where(seen, at.astype(F32) * slope_ref[h], masked_score)
        q_ref[h] = (jnp.concatenate([query[:, cols], zero], axis=1) + ones).astype(BF)
        wide = jnp.concatenate([key[:, cols], zero], axis=1) + more
        k_ref[h] = put3(wide, lane, 64, slope).astype(BF)
        v_ref[h] = (jnp.concatenate([value[:, cols], zero], axis=1) + ones).astype(BF)


def project(normed, index, pieces, col_bias, slopes, length):
    span, depth = normed.shape
    cols = pieces[0].shape[1]
    heads = slopes.shape[0]
    tile = 256
    shape = jax.ShapeDtypeStruct((heads, span, 128), BF)
    return pl.pallas_call(
        functools.partial(project_kernel, heads=heads),
        out_shape=(shape,) * 3 + (jax.ShapeDtypeStruct((depth, cols), BF),),
        grid=(span // tile,),
        in_specs=[pl.BlockSpec(memory_space=pltpu.SMEM)] * 3
        + [pl.BlockSpec((tile, depth), lambda i: (i, 0)), whole(col_bias.shape)]
        + [whole(piece.shape) for piece in pieces],
        out_specs=[pl.BlockSpec((heads, tile, 128), lambda i: (0, i, 0))] * 3
        + [whole((depth, cols))],
        compiler_params=pltpu.CompilerParams(vmem_limit_bytes=40 * MIB),
        cost_estimate=cost(2 * span * depth * cols, 12 * MIB),
        name="project",
    )(index, slopes, length, normed, col_bias, *pieces)


def attend_forward_kernel(q_ref, k_ref, v_ref, o_ref, qb_ref, send_ref, *, bq, span):
    lane = lax.broadcasted_iota(jnp.int32, (bq, 128), 1)
    row = lax.broadcasted_iota(jnp.int32, (bq, bq), 0)
    causal = row >= lax.broadcasted_iota(jnp.int32, (bq, bq), 1)
    for i in range(span // bq):
        outs = []
        here = pl.ds(i * bq, bq)
        for h in range(2):
            q = q_ref[h, here, :]
            near = jnp.where(causal, dot(q, k_ref[h, here, :], NT), masked_score)
            highest = jnp.max(near, axis=1, keepdims=True)
            if i:
                before = pl.ds(0, i * bq)
                far = dot(q, k_ref[h, before, :], NT)
                highest = jnp.maximum(highest, jnp.max(far, axis=1, keepdims=True))
            acc = dot(jnp.exp(near - highest).astype(BF), v_ref[h, here, :])
            if i:
                acc = acc + dot(jnp.exp(far - highest).astype(BF), v_ref[h, before, :])
            total = acc[:, 64:65]
            outs.append((acc[:, :64] * (1.0 / total)).astype(BF))
            log_sum = highest + jnp.log(total)
            qb_ref[h, here, :] = put3(q.astype(F32), lane, 67, -log_sum).astype(BF)
        o_ref[here, :] = jnp.concatenate(outs, axis=1)
    half = span // 2
    for j in range(4):
        send_ref[j] = o_ref[pl.ds(j % 2 * half, half), :]


def pair_spec(span, pair):
    return pl.BlockSpec((2, span, 128), lambda i: (pair, 0, 0), pipeline_mode=pl.Buffered(1))


def attend_forward(q, k, v, pair):
    span = q.shape[1]
    shapes = [(span, 128), (2, span, 128), (4, span // 2, 128)]
    return pl.pallas_call(
        functools.partial(attend_forward_kernel, bq=min(512, span), span=span),
        out_shape=[jax.ShapeDtypeStruct(x, BF) for x in shapes],
        grid=(1,),
        in_specs=[pair_spec(span, pair)] * 3,
        out_specs=[whole(x) for x in shapes],
        compiler_params=pltpu.CompilerParams(vmem_limit_bytes=50 * MIB),
        cost_estimate=cost(12e9, 5 * MIB),
        name="attend_forward",
    )(q, k, v)


def attend_backward_kernel(half_ref, q_ref, k_ref, v_ref, o_ref, *refs, bk, span, chunks):
    partials, (d_ref, sib_ref, sum_ref, do_ref, doa_ref, dq_ref) = refs[:-6], refs[-6:]
    half = span // 2
    rows = half // chunks
    for c, part in enumerate(partials):
        for side in range(2):
            total = part[side].astype(F32) + part[2 + side].astype(F32)
            do_ref[pl.ds(side * half + c * rows, rows), :] = total.astype(BF)
    lane = lax.broadcasted_iota(jnp.int32, (span, 128), 1)
    row = lax.broadcasted_iota(jnp.int32, (bk, bk), 0)
    causal = row <= lax.broadcasted_iota(jnp.int32, (bk, bk), 1)
    grad = do_ref[...].astype(F32)
    prod = grad * o_ref[...].astype(F32)
    for h in range(2):
        cols = slice(h * HEAD_DIM, (h + 1) * HEAD_DIM)
        delta = jnp.sum(prod[:, cols], axis=1, keepdims=True)
        base = jnp.concatenate([grad[:, cols], jnp.zeros((span, 64), F32)], axis=1)
        doa_ref[h] = put3(base, lane, 64, -delta).astype(BF)
    dq_ref[...] = jnp.zeros_like(dq_ref)
    value_sums = jnp.zeros((1, 128), F32)
    for j in range(span // bk):
        dks, dvs = [], []
        here = pl.ds(j * bk, bk)
        rest = pl.ds(j * bk, span - j * bk)
        for h in range(2):
            k = k_ref[h, here, :]
            q = q_ref[h, rest, :]
            do = doa_ref[h, rest, :]
            p = jnp.exp(dot(k, q, NT))
            near = jnp.where(causal, p[:, :bk], 0.0)
            p = jnp.concatenate([near, p[:, bk:]], axis=1) if rest.size > bk else near
            ds = (p * dot(v_ref[h, here, :], do, NT)).astype(BF)
            dvs.append(dot(p.astype(BF), do)[:, :64])
            dks.append(dot(ds, q)[:, :64])
            dq_ref[h, :, rest] += dot(k[:, :64], ds, TN)
        d_ref[1, here, :] = jnp.concatenate(dks, axis=1).astype(BF)
        value_grad = jnp.concatenate(dvs, axis=1).astype(BF)
        d_ref[2, here, :] = value_grad
        value_sums += jnp.sum(value_grad.astype(F32), axis=0, keepdims=True)
    dq = jnp.concatenate([dq_ref[0], dq_ref[1]], axis=0).T * (HEAD_DIM**-0.5)
    dq = dq.astype(BF)
    d_ref[0] = dq
    sum_ref[0:1, :] = jnp.sum(dq.astype(F32), axis=0, keepdims=True)
    sum_ref[1:2, :] = value_sums
    for kind in range(3):
        sib_ref[kind] = d_ref[kind, pl.ds(pl.multiple_of((1 - half_ref[0]) * half, half), half), :]


def attend_backward(scalars, qb, k, v, o, partials, pair):
    span = qb.shape[1]
    chunks = len(partials)
    part = pl.BlockSpec((4, span // 2 // chunks, 128), lambda i: (0, 0, pair), pipeline_mode=pl.Buffered(1))
    shapes = [((3, span, 128), BF), ((3, span // 2, 128), BF), ((2, 128), F32)]
    return pl.pallas_call(
        functools.partial(attend_backward_kernel, bk=min(256, span), span=span, chunks=chunks),
        out_shape=[jax.ShapeDtypeStruct(*x) for x in shapes],
        grid=(1,),
        in_specs=[
            pl.BlockSpec(memory_space=pltpu.SMEM),
            pair_spec(span, 0),
            pair_spec(span, pair),
            pair_spec(span, pair),
            whole((span, 128)),
        ]
        + [part] * chunks,
        out_specs=[whole(x[0]) for x in shapes],
        scratch_shapes=[
            pltpu.VMEM((span, 128), BF),
            pltpu.VMEM((2, span, 128), BF),
            pltpu.VMEM((2, 64, span), F32),
        ],
        compiler_params=pltpu.CompilerParams(vmem_limit_bytes=50 * MIB),
        cost_estimate=cost(18e9, 6 * MIB),
        name="attend_backward",
    )(scalars, qb, k, v, o, *partials)


def norm_parts(x):
    average = jnp.mean(x, axis=-1, keepdims=True)
    centred = x - average
    variance = jnp.mean(centred * centred, axis=-1, keepdims=True)
    scale = lax.rsqrt(variance + norm_eps)
    return centred * scale, scale


def norm_back(grad, unit, scale, gain):
    weighted = grad * gain
    mean_one = jnp.mean(weighted, axis=-1, keepdims=True)
    mean_two = jnp.mean(weighted * unit, axis=-1, keepdims=True)
    return scale * (weighted - mean_one - unit * mean_two)


def middle_kernel(
    scalar_ref,
    o0_ref,
    o1_ref,
    tokens_ref,
    cot_ref,
    first_own_ref,
    first_sib_ref,
    late_own_ref,
    late_sib_ref,
    row_ref,
    bias_ref,
    *refs,
    chunk,
):
    (resid_ref, n2_ref, g_ref, du_ref, da_ref, dr_ref, mlp_ref, do_ref, sum_ref,
     up_sum_ref, out_w) = refs[-11:]
    step = pl.program_id(0)
    tile, depth = tokens_ref.shape

    @pl.when(step == 0)
    def _():
        for k, ref in enumerate((first_own_ref, first_sib_ref)):
            for chip in range(2):
                for pair in range(2):
                    at = (pair * 4 + (scalar_ref[3] ^ (k + 2 * chip))) * 128
                    cols = slice(256 * chip + 128 * pair, 256 * chip + 128 * (pair + 1))
                    out_w[:, pl.ds(pl.multiple_of(at, 128), 128)] = ref[:, cols]
        sum_ref[...] = jnp.zeros_like(sum_ref)
        up_sum_ref[...] = jnp.zeros_like(up_sum_ref)

    heads = jnp.concatenate([ref[j] for ref in (o0_ref, o1_ref) for j in range(4)], axis=1)
    branch = dot(heads, out_w[...], NT) + row_ref[2:3, :]
    resid = tokens_ref[...].astype(F32) + branch
    resid_ref[...] = resid
    at = lax.broadcasted_iota(jnp.int32, (tile, 1), 0) + (
        scalar_ref[0] * scalar_ref[1] + (chunk * pl.num_programs(0) + step) * tile
    )
    valid = (at < scalar_ref[2]).astype(F32)
    unit, scale = norm_parts(resid)
    n2 = (unit * row_ref[3:4, :] + row_ref[4:5, :]).astype(BF)
    n2_ref[...] = n2
    cot = cot_ref[...]
    dm = cot.astype(BF)
    mlp = None
    hid = late_own_ref.shape[1] // 2
    for half, late in enumerate((late_own_ref, late_sib_ref)):
        up, down = late.at[:, :hid], late.at[:, hid:]
        cols = slice(half * hid, (half + 1) * hid)
        u = dot(n2, up[...]) + bias_ref[half : half + 1, :]
        square = u * u
        t = jnp.tanh(gelu_scale * (u + gelu_cubic * square * u))
        plus = 0.5 * (1.0 + t)
        g = (u * plus).astype(BF)
        slope = plus + (0.5 * gelu_scale) * u * (1.0 - t * t) * (1.0 + 3.0 * gelu_cubic * square)
        du_wide = (dot(dm, down[...]) * slope).astype(BF)
        g_ref[:, cols] = g
        du_ref[:, cols] = du_wide
        up_sum_ref[half : half + 1, :] += jnp.sum(du_wide.astype(F32), axis=0, keepdims=True)
        m = dot(g, down[...], NT)
        d = dot(du_wide, up[...], NT)
        mlp, dn2 = (m, d) if mlp is None else (mlp + m, dn2 + d)
    mlp_ref[...] = mlp.astype(BF)
    dr = norm_back(dn2, unit, scale, row_ref[3:4, :]) + 0.5 * cot
    dr_ref[...] = dr
    da = dr.astype(BF)
    da_ref[...] = da
    do = dot(da, out_w[...]).astype(BF)
    for j in range(4):
        do_ref[j] = jnp.concatenate([do[:, 128 * (j + 4 * p) : 128 * (j + 4 * p + 1)] for p in range(2)], axis=1)
    for k, x in enumerate(
        (dn2 * unit, dn2, da.astype(F32), 0.5 * dm.astype(F32), valid * branch * branch)
    ):
        sum_ref[k : k + 1, :] += jnp.sum(x, axis=0, keepdims=True)


def middle(chunk, chunks, scalars, heads_in, tokens, cotangent, weights, row_vectors, up_bias, before):
    depth = tokens.shape[1]
    half = tokens.shape[0] // 2
    tile = 256
    steps = half // chunks // tile
    hidden = weights[2].shape[1]
    own = lambda i, s: (chunk * steps + i, 0)
    absolute = lambda i, s: (s[0] * (half // tile) + chunk * steps + i, 0)
    part = lambda i, s: (i, 0)
    kept = [(depth, F32), (depth, BF), (hidden, BF), (hidden, BF), (depth, BF), (depth, F32)]
    n_in = 10
    return pl.pallas_call(
        functools.partial(middle_kernel, chunk=chunk),
        out_shape=[jax.ShapeDtypeStruct((half, w), t) for w, t in kept]
        + [
            jax.ShapeDtypeStruct((half // chunks, depth), BF),
            jax.ShapeDtypeStruct((4, half // chunks, 256), BF),
        ]
        + [jax.ShapeDtypeStruct((8, depth), F32), jax.ShapeDtypeStruct((2, hidden // 2), F32)],
        grid_spec=pltpu.PrefetchScalarGridSpec(
            num_scalar_prefetch=1,
            grid=(steps,),
            in_specs=[pl.BlockSpec((4, tile, 128), lambda i, s: (0, *own(i, s)))] * 2
            + [pl.BlockSpec((tile, depth), absolute)] * 2
            + [whole(w.shape) for w in weights]
            + [whole(row_vectors.shape), whole(up_bias.shape)]
            + [pl.BlockSpec(memory_space=pl.ANY)] * len(before),
            out_specs=[pl.BlockSpec((tile, w), own) for w, _ in kept]
            + [
                pl.BlockSpec((tile, depth), part),
                pl.BlockSpec((4, tile, 256), lambda i, s: (0, i, 0)),
            ]
            + [whole((8, depth)), whole((2, hidden // 2))],
            scratch_shapes=[
                pltpu.VMEM((depth, 1024), BF),
            ],
        ),
        input_output_aliases={n_in + 1 + k: k for k in range(len(before))},
        compiler_params=pltpu.CompilerParams(vmem_limit_bytes=56 * MIB),
        cost_estimate=cost(21e9 / chunks, 24 * MIB),
        name="middle",
    )(scalars, *heads_in, tokens, cotangent, *weights, row_vectors, up_bias, *before)


def last_kernel(
    scalar_ref, o0_ref, o1_ref, s0_ref, s1_ref, w_own_ref, w_sib_ref, tokens_ref, dr_ref, row_ref, ig_ref, sum_ref,
):
    @pl.when(pl.program_id(0) == 0)
    def _():
        sum_ref[...] = jnp.zeros_like(sum_ref)

    def side(x, y):
        return jnp.concatenate([r[k] for k in range(3) for r in (x, y)], axis=1)

    dn1 = dot(side(o0_ref, o1_ref), w_own_ref[...], NT) + dot(side(s0_ref, s1_ref), w_sib_ref[...], NT)
    unit, scale = norm_parts(tokens_ref[...].astype(F32))
    ig_ref[...] = (dr_ref[...] + norm_back(dn1, unit, scale, row_ref[0:1, :])).astype(BF)
    sum_ref[0:1, :] += jnp.sum(dn1 * unit, axis=0, keepdims=True)
    sum_ref[1:2, :] += jnp.sum(dn1, axis=0, keepdims=True)


def last(chunk, chunks, scalars, own, sibling, w_own, w_sib, tokens, dr, row_vectors):
    depth = tokens.shape[1]
    half = tokens.shape[0] // 2
    tile = 256
    steps = half // chunks // tile
    absolute = lambda i, s: (s[0] * (half // tile) + chunk * steps + i, 0)
    return pl.pallas_call(
        last_kernel,
        out_shape=[
            jax.ShapeDtypeStruct((half // chunks, depth), BF),
            jax.ShapeDtypeStruct((8, depth), F32),
        ],
        grid_spec=pltpu.PrefetchScalarGridSpec(
            num_scalar_prefetch=1,
            grid=(steps,),
            in_specs=[pl.BlockSpec((3, tile, 128), lambda i, s: (0,) + absolute(i, s))] * 2
            + [pl.BlockSpec((3, tile, 128), lambda i, s: (0, chunk * steps + i, 0))] * 2
            + [whole(w_own.shape), whole(w_sib.shape)]
            + [
                pl.BlockSpec((tile, depth), absolute),
                pl.BlockSpec((tile, depth), lambda i, s: (chunk * steps + i, 0)),
                whole(row_vectors.shape),
            ],
            out_specs=[pl.BlockSpec((tile, depth), lambda i, s: (i, 0)), whole((8, depth))],
        ),
        compiler_params=pltpu.CompilerParams(vmem_limit_bytes=40 * MIB),
        cost_estimate=cost(3.2e9 / chunks, 10 * MIB),
        name="last",
    )(scalars, *own, *sibling, w_own, w_sib, tokens, dr, row_vectors)


def weight_grads_kernel(half_ref, n2_ref, cot_ref, da_ref, du_ref, g_ref, a0_ref, a1_ref, b0_ref, b1_ref, *refs):
    out_ref = refs[-1]
    o_refs = [r.at[0] for r in (a0_ref, a1_ref, b0_ref, b1_ref)]
    hidden = du_ref.shape[1]
    parts = [
        (n2_ref[...], [du_ref]),
        (cot_ref[...].astype(BF), [g_ref]),
        (da_ref[...], o_refs),
    ]
    at = 0
    for left, rights in parts:
        right = jnp.concatenate([r[...] for r in rights], axis=1) if len(rights) > 1 else rights[0][...]
        cols = slice(at, at + right.shape[1])
        at += right.shape[1]
        value = dot(left, right, TN)
        if len(refs) > 1:
            value = value + refs[0][:, cols].astype(F32)
        out_ref[:, cols] = value.astype(BF)


def weight_grads(side, scalars, n2, cotangent, da, du, g, heads_in, more=()):
    half, depth = n2.shape
    hidden = du.shape[1] // 2
    cols = 2 * hidden + 4 * 128
    tile = 256
    left = pl.BlockSpec((half, tile), lambda i, s: (0, i))
    right = lambda w: pl.BlockSpec((half, w), lambda i, s: (0, side), pipeline_mode=pl.Buffered(1))
    rows = pl.BlockSpec((tile, cols), lambda i, s: (i, 0))
    return pl.pallas_call(
        weight_grads_kernel,
        out_shape=jax.ShapeDtypeStruct((depth, cols), BF),
        grid_spec=pltpu.PrefetchScalarGridSpec(
            num_scalar_prefetch=1,
            grid=(depth // tile,),
            in_specs=[left, pl.BlockSpec((half, tile), lambda i, s: (s[0], i)), left]
            + [right(hidden), right(hidden)]
            + [
                pl.BlockSpec((1, half, 128), lambda i, s, flip=flip: (s[3] ^ flip, 0, 0), pipeline_mode=pl.Buffered(1))
                for flip in (side, side, side + 2, side + 2)
            ]
            + [rows] * len(more),
            out_specs=rows,
        ),
        compiler_params=pltpu.CompilerParams(vmem_limit_bytes=50 * MIB),
        cost_estimate=cost(2 * half * depth * cols, 18 * MIB),
        name="weight_grads",
    )(scalars, n2, cotangent, da, du, g, *heads_in, *heads_in, *more)


def finish_kernel(half_ref, *refs, steps):
    out_ref = refs[-1]
    for k, ref in enumerate(refs[:-1]):

        @pl.when(pl.program_id(0) // steps == k)
        def _():
            out_ref[...] = ref[...].astype(F32)


def finish(scalars, own, other):
    chunks = len(own)
    rows, depth = own[0].shape
    tile = 256
    steps = rows // tile
    span = lambda k: pl.BlockSpec((tile, depth), lambda i, s: (jnp.clip(i - k * steps, 0, steps - 1), 0))

    def out_index(i, s):
        first = i < chunks * steps
        return (jnp.where(first, s[0], 1 - s[0]) * chunks * steps + i - jnp.where(first, 0, chunks * steps), 0)

    return pl.pallas_call(
        functools.partial(finish_kernel, steps=steps),
        out_shape=jax.ShapeDtypeStruct((2 * chunks * rows, depth), F32),
        grid_spec=pltpu.PrefetchScalarGridSpec(
            num_scalar_prefetch=1,
            grid=(2 * chunks * steps,),
            in_specs=[span(k) for k in range(2 * chunks)],
            out_specs=pl.BlockSpec((tile, depth), out_index),
        ),
        compiler_params=pltpu.CompilerParams(vmem_limit_bytes=24 * MIB),
        cost_estimate=cost(0, 12 * chunks * rows * depth),
        name="finish",
    )(scalars, *own, *other)


def body(
    tokens,
    cotangent,
    lengths,
    qkv_weight,
    qkv_first,
    qkv_second,
    out_weight,
    out_first,
    out_second,
    up_weight,
    up_first,
    up_second,
    down_weight,
    down_first,
    down_second,
    row_vectors,
    row_first,
    row_second,
    col_bias,
    col_first,
    col_second,
):
    span, depth = tokens.shape
    half = span // 2
    share = qkv_weight.shape[0]
    n_dp = lax.axis_size("dp")
    device = lax.axis_index("mp")
    core = device % 2
    heads = qkv_weight.shape[2] // HEAD_DIM
    width = heads * HEAD_DIM
    hidden = up_weight.shape[1] * up_weight.shape[2]
    head_ids = device * heads + jnp.arange(heads)
    slopes = jnp.exp2(-8.0 * (head_ids.astype(F32) + 1.0) / HEADS)
    scalars = jnp.stack([core.astype(jnp.int32), jnp.int32(half), lengths[0], device.astype(jnp.int32)])

    index = ring_index(n_dp)
    out_piece = out_weight.astype(BF).T
    out_piece = jnp.concatenate([out_piece, to_chip(out_piece)], axis=1)
    qkv_ring = Gather(qkv_weight.astype(BF).reshape(share, 3 * width))
    out_ring = Gather(out_piece)
    up_ring = Gather(up_weight.astype(BF).reshape(share, hidden))
    down_ring = Gather(down_weight.astype(BF).reshape(hidden, share).T)
    gate = []
    for _ in range(n_dp // 2):
        gate.append(qkv_ring.up)
        qkv_ring.hop()
        out_ring.hop()
    up_bias = col_bias[2:].reshape(1, hidden)
    up_bias = jnp.concatenate([up_bias, to_core(up_bias)], axis=0)
    up_ring.hop(gate[-1])
    down_ring.hop(qkv_ring.up)

    unit_one, _ = norm_parts(tokens.astype(F32))
    normed = (unit_one * row_vectors[0] + row_vectors[1]).astype(BF)
    normed = after(normed, out_ring.up, out_ring.down, up_bias)
    q, k, v, qkv_w = project(normed, index, qkv_ring.finish(), col_bias, slopes, lengths)
    outs, heads_in = [], []
    for pair in range(2):
        ready = (up_ring.up,) if pair == 0 else (up_ring.up, down_ring.up)
        if pair == 0:
            up_ring.hop(q)
        q = after(q, *ready)
        o, qb, send = attend_forward(q, k, v, pair)
        outs.append((o, qb))
        heads_in.append(to_all(send))
        down_ring.hop(send)
        up_ring.hop(send)
    qkv_sib = to_core(qkv_w)
    out_w = assemble(index, out_ring.finish())
    late_w = assemble(index, up_ring.finish(), down_ring.finish())
    out_sib, late_sib = to_core(out_w), to_core(late_w)

    weights = (out_w, out_sib, late_w, late_sib)
    chunks = 2
    before, mlps, partials, sums, up_sums = (), [], [], 0.0, 0.0
    for chunk in range(chunks):
        got = middle(
            chunk,
            chunks,
            scalars,
            heads_in,
            tokens,
            cotangent,
            weights,
            row_vectors,
            up_bias,
            before,
        )
        before = got[:6]
        mlps.append(got[6])
        partials.append(to_all(got[7]))
        sums, up_sums = sums + got[8], up_sums + got[9]
    resid, n2, g, du, da, dr = before
    mlp_far = [to_chip(after(m, partials[-1])) for m in mlps]
    grad_args = (scalars, n2, cotangent, da, du, g)
    other_grads = weight_grads(1, *grad_args, heads_in)
    got_grads = to_core(other_grads)

    parts, part_sums, siblings = [], [], []
    for pair in range(2):
        o, qb = outs[pair]
        d, d_sib, s = attend_backward(scalars, after(qb, other_grads), k, v, o, partials, pair)
        parts.append(d)
        part_sums.append(s)
        siblings.append(to_core(d_sib))
        if pair == 0:
            total = weight_grads(0, *grad_args, heads_in, (after(got_grads, s),))
            middle_ring = Reduce(total, index)
            middle_ring.hop()
            outs[1] = (outs[1][0], after(outs[1][1], total))
    middle_ring.hop(part_sums[1])
    lasts = [
        last(c, chunks, scalars, parts, siblings, qkv_w, qkv_sib, tokens, dr, row_vectors)
        for c in range(chunks)
    ]
    last_sums = sum(x[1] for x in lasts)
    last_far = [to_chip(x[0]) for x in lasts]
    mlp_far = [after(f, lasts[-1][1]) for f in mlp_far]
    middle_ring.hop(lasts[-1][1])

    qkv_grad = jnp.concatenate([parts[p][kind] for kind in range(3) for p in range(2)], axis=1)
    qkv_wgrad = dot(normed, after(qkv_grad, lasts[-1][1]), TN).astype(BF)
    qkv_shard = Reduce(qkv_wgrad, index).finish().reshape(qkv_weight.shape)
    mid_shard = middle_ring.finish()
    up_shard = mid_shard[:, :hidden].reshape(up_weight.shape)
    down_shard = mid_shard[:, hidden : 2 * hidden].T.reshape(down_weight.shape)
    out_mine = mid_shard[:, 2 * hidden : 2 * hidden + width]
    out_theirs = to_chip(mid_shard[:, 2 * hidden + width :].astype(BF))
    out_shard = (out_mine + out_theirs.astype(F32)).T

    valid = ((core * half + jnp.arange(half)) < lengths[0]).astype(F32)[:, None]
    stat_out, stat_m, own_low = 0.0, 0.0, []
    for chunk, (m, f) in enumerate(zip(mlps, mlp_far)):
        rows = slice(chunk * half // chunks, (chunk + 1) * half // chunks)
        branch_m = m.astype(F32) + f.astype(F32) + row_vectors[5]
        outputs_own = resid[rows] + branch_m
        stat_out += jnp.sum(valid[rows] * outputs_own * outputs_own)
        stat_m += jnp.sum(valid[rows] * branch_m * branch_m)
        own_low.append(outputs_own.astype(BF))
    outputs = finish(scalars, own_low, [to_core(x) for x in own_low])

    summed = [(x[0].astype(F32) + f.astype(F32)).astype(BF) for x, f in zip(lasts, last_far)]
    input_grad = finish(scalars, summed, [to_core(x) for x in summed])

    stats = jnp.stack([stat_out, jnp.sum(sums[4]), stat_m, jnp.sum(valid)])
    small = jnp.concatenate(
        [
            last_sums[0:2],
            sums[2:3],
            sums[0:2],
            sums[3:4],
            jnp.pad(stats, (0, depth - 4))[None],
            jnp.pad(
                jnp.concatenate([part_sums[p][kind] for kind in range(2) for p in range(2)]),
                (0, depth - 2 * width),
            )[None],
            up_sums,
        ],
        axis=0,
    )
    every = lax.all_gather(small, ("dp", "mp"), axis=0, tiled=False)
    every = every.reshape(n_dp, -1, *small.shape)
    row_stat = jnp.sum(every[:, :, :7], axis=(0, 1))
    row_total, stat_total = row_stat[:6], row_stat[6]
    col_all = jnp.sum(every[:, :, 7:], axis=0)
    mine = lax.dynamic_index_in_dim(col_all, device, 0, keepdims=False)
    theirs = lax.dynamic_index_in_dim(col_all, device ^ 1, 0, keepdims=False)
    col_total = jnp.concatenate(
        [mine[0, : 2 * width].reshape(2, width), (mine[1] + theirs[2]).reshape(-1, width)], axis=0
    )
    rms_stats = jnp.sqrt(stat_total[:3] / (stat_total[3] * depth))

    qkv_new = adamw(qkv_weight, qkv_first, qkv_second, qkv_shard, matrix_rate, weight_decay)
    out_new = adamw(out_weight, out_first, out_second, out_shard, matrix_rate, weight_decay)
    up_new = adamw(up_weight, up_first, up_second, up_shard, matrix_rate, weight_decay)
    down_new = adamw(down_weight, down_first, down_second, down_shard, matrix_rate, weight_decay)
    row_new = adamw(row_vectors, row_first, row_second, row_total, vector_rate, 0.0)
    col_new = adamw(col_bias, col_first, col_second, col_total, vector_rate, 0.0)
    return (
        outputs,
        input_grad,
        rms_stats,
        *qkv_new,
        *out_new,
        *up_new,
        *down_new,
        *row_new,
        *col_new,
    )


def solution(mesh):
    matrices = [P("dp", None, "mp"), P("mp", "dp"), P("dp", None, "mp"), P(None, "mp", "dp")]
    vectors = [P(), P(None, "mp")]
    groups = [spec for spec in matrices + vectors for _ in range(3)]
    return jax.shard_map(
        body,
        mesh=mesh,
        in_specs=(P("dp", None), P("dp", None), P("dp"), *groups),
        out_specs=(P("dp", None), P("dp", None), P(), *groups),
        check_vma=False,
    )
```

time: 1250 us -> 456 us (0.36)
  waiting for transfers between devices: 619 us -> 82.5 us
  matrix products: 297 us -> 5.74 us
  Pallas kernels: 0 us -> 160 us
  other arithmetic: 153 us -> 42.9 us
  starting transfers between devices: 0.96 us -> 71.2 us
  blocking collectives: 77 us -> 17.7 us
  local copies, waits for them, and re-layouts: 65.5 us -> 44.2 us
  loops' own time: 14.8 us -> 0 us
    reduce_scatter x6 -> x0, waiting for transfers between devices: 291 us -> none  [the longest x1 74.9 us: body(): lax.psum_scatter(jnp.einsum('tkc,dkc->td', hidden_grad, up_w, preferred_e...]
    dot_general x40 -> x1, matrix products: 297 us -> 5.74 us  [dot(): return lax.dot_general(a, b, dims, preferred_element_type=F32)]
    all_gather x7 -> x1, waiting for transfers between devices: 201 us -> 0.01 us  [body(): every = lax.all_gather(small, ('dp', 'mp'), axis=0, tiled=False)]
    pallas_call x0 -> x15, Pallas kernels: none -> 160 us  [the longest x2 45 us: middle(): pl.pallas_call(functools.partial(middle_kernel, chunk=chunk), out_shape=[...]
    unnamed x17 -> x1, waiting for transfers between devices: 127 us -> 0.02 us
    convert_element_type x20 -> x12, other arithmetic: 77.3 us -> 15.7 us  [the longest x6 7.23 us: add(): return (x.astype(F32) + self.block(k).astype(F32)).astype(BF)]
    ppermute x0 -> x59, starting transfers between devices: none -> 60.2 us  [the longest x16 27 us: hop(): lax.ppermute(after(self.up, *gates), 'dp', self.perms[0])]
    ppermute x0 -> x59, waiting for transfers between devices: none -> 51.7 us  [the longest x8 15.7 us: hop(): self.up = lax.ppermute(up, 'dp', self.perms[0])]
  transfers between devices with their start and end apart: 15 -> 63, of which waited for: 14 -> 17; matrix products, arithmetic and copies ran while one was open for 8% -> 15% of each run, Pallas kernels for 0% -> 22%
where the time goes in v1:
time: 456 us; the launch traced here: 449 us
  Pallas kernels  160 us (35%)
  waiting for transfers between devices  82.5 us (18%)
  starting transfers between devices  71.2 us (16%)
  local copies, waits for them, and re-layouts  44.2 us (10%)
  other arithmetic  42.9 us (9%)
  between operations  24.3 us (5%)
  blocking collectives  17.7 us (4%)
  matrix products  5.74 us (1%)
    pallas_call x2, Pallas kernels, middle(): pl.pallas_call(functools.partial(middle_kernel, chunk=chunk), out_shape=[...  45 us
    pallas_call x2, Pallas kernels, attend_backward(): pl.pallas_call(functools.partial(attend_backward_kernel, bk=min(256, span...  33.5 us
    all_to_all x3, waiting for transfers between devices, to_all(): return lax.all_to_all(x, 'mp', split_axis=0, concat_axis=0, tiled=True)  30.8 us
    unnamed x153, local copies, waits for them, and re-layouts  28.7 us
    ppermute x16, starting transfers between devices, hop(): lax.ppermute(after(self.up, *gates), 'dp', self.perms[0])  27 us
    pallas_call x2, Pallas kernels, weight_grads(): pl.pallas_call(weight_grads_kernel, out_shape=jax.ShapeDtypeStruct((depth...  24.2 us
    pallas_call x2, Pallas kernels, attend_forward(): pl.pallas_call(functools.partial(attend_forward_kernel, bq=min(512, span)...  21 us
    all_to_all x1, blocking collectives, to_all(): return lax.all_to_all(x, 'mp', split_axis=0, concat_axis=0, tiled=True)  17.7 us
  transfers between devices with their start and end apart: 63, of which 17 were waited for; matrix products, arithmetic and copies ran while one was open for 15% of the time, Pallas kernels for 22%

profile of v1, /device:TPU:0, one launch (start us, length us, event | category | flops | bytes accessed | tf_op | source)
XLA Modules:
  0.0 448.9 jit_solution(7683283804439916411)
XLA Ops:
  8.5 3.1 collective-permute-start.12
  12.6 2.0 collective-permute-start
  15.4 3.0 convert_reduce_fusion
  21.1 1.6 collective-permute-start.1
  23.2 3.4 collective-permute-done.1.refs_7_
  29.7 3.0 fusion.5.n_ref
  38.0 1.7 collective-permute-done.6.refs_2_
  40.1 3.7 collective-permute-done.10.refs_2_
  45.9 1.6 collective-permute-start.15
  52.8 2.0 collective-permute-done.15.refs_4_
  57.6 2.2 copy-done.11
  62.6 7.8 %project.1 = (bf16[4,2048,128]{2,1,0:T(8,128)(2,1)S(1)}, bf16[4,2048,128]{2,1,0:T(8,128)(2,1)S(1)}, bf16[4,2048,128]{2,1,0:T(8,128)(2,1)S(1)}, bf16[1024,768]{1,0:T(8,128)(2,1)S(1)}) custom-call(s32[8]{0:T(128)S(1)} %gather_fusion, f32[4]{0:T(128)S(1)} %multiply_exponential_fusion.slope_ref, s32[1]{0:T(128)} %copy.113.length_ref, ...), custom_call_target="tpu_custom_call" | custom-call | flops 3221225472 | bytes 12582912 | tf_op jit(solution)/shard_map/project/pallas_call | solution.py:224
  75.5 2.1 collective-permute-start.17
  77.6 11.0 %attend_forward.2 = (bf16[2048,128]{1,0:T(8,128)(2,1)S(1)}, bf16[2,2048,128]{2,1,0:T(8,128)(2,1)S(1)}, bf16[4,1024,128]{2,1,0:T(8,128)(2,1)}) custom-call(bf16[4,2048,128]{2,1,0:T(8,128)(2,1)} %copy-done.29, bf16[4,2048,128]{2,1,0:T(8,128)(2,1)} %copy-done.27, bf16[4,2048,128]{2,1,0:T(8,128)(2,1)} %copy-done.28), custom_call_target="tpu_custom_call" | custom-call | flops 12000000000 | bytes 5242880 | tf_op jit(solution)/shard_map/attend_forward/pallas_call | solution.py:274
  94.6 2.2 collective-permute-done.20.refs_14_
  96.8 2.8 collective-permute-done.18.refs_5_
  99.6 10.0 %attend_forward.3 = (bf16[2048,128]{1,0:T(8,128)(2,1)S(1)}, bf16[2,2048,128]{2,1,0:T(8,128)(2,1)S(1)}, bf16[4,1024,128]{2,1,0:T(8,128)(2,1)S(1)}) custom-call(bf16[4,2048,128]{2,1,0:T(8,128)(2,1)} %copy-done.29, bf16[4,2048,128]{2,1,0:T(8,128)(2,1)} %copy-done.27, bf16[4,2048,128]{2,1,0:T(8,128)(2,1)} %copy-done.28), custom_call_target="tpu_custom_call" | custom-call | flops 12000000000 | bytes 5242880 | tf_op jit(solution)/shard_map/attend_forward/pallas_call | solution.py:274
  114.5 2.3 collective-permute-done.29.refs_13_
  118.3 2.8 collective-permute-done.28.refs_11_
  121.1 2.0 collective-permute-done.30.refs_12_
  123.1 2.8 assemble.3.late_own_ref
  126.0 3.5 all-to-all-start
  130.7 13.2 %all-to-all-done.o0_ref.a0_ref.b0_ref = bf16[4,1024,128]{2,1,0:T(8,128)(2,1)S(1)} async-done(((bf16[4,1024,128]{2,1,0:T(8,128)(2,1)}), bf16[4,1024,128]{2,1,0:T(8,128)(2,1)S(1)}, u32[]{:S(2)}, u32[]{:S(2)}) %all-to-all-start) | async-done | bytes 1048608 | tf_op jit(solution)/shard_map/all_to_all | solution.py:55
  144.0 3.7 all-to-all-start.1
  148.3 13.8 %all-to-all-done.1.o1_ref.a1_ref.b1_ref = bf16[4,1024,128]{2,1,0:T(8,128)(2,1)S(1)} async-done(((bf16[4,1024,128]{2,1,0:T(8,128)(2,1)}), bf16[4,1024,128]{2,1,0:T(8,128)(2,1)S(1)}, u32[]{:S(2)}, u32[]{:S(2)}) %all-to-all-start.1) | async-done | bytes 1048608 | tf_op jit(solution)/shard_map/all_to_all | solution.py:55
  163.1 22.2 %middle.2 = (f32[1024,1024]{1,0:T(8,128)}, bf16[1024,1024]{1,0:T(8,128)(2,1)}, bf16[1024,2048]{1,0:T(8,128)(2,1)}, bf16[1024,2048]{1,0:T(8,128)(2,1)}, bf16[1024...) custom-call(s32[4]{0:T(128)} %pad_add_fusion.scalar_ref.half_ref, ...), custom_call_target="tpu_custom_call" | custom-call | flops 10499999744 | bytes 25165824 | tf_op jit(solution)/shard_map/middle/pallas_call | solution.py:465
  185.3 22.8 %middle.3 = (f32[1024,1024]{1,0:T(8,128)}, bf16[1024,1024]{1,0:T(8,128)(2,1)}, bf16[1024,2048]{1,0:T(8,128)(2,1)}, bf16[1024,2048]{1,0:T(8,128)(2,1)}, bf16[1024...) custom-call(s32[4]{0:T(128)} %pad_add_fusion.scalar_ref.half_ref, ...), custom_call_target="tpu_custom_call", output_to_operand_aliasing={{0}: (11, {}), {1}: (12, {}), {2}: (13, {}), {3}: (14, {}),... | custom-call | flops 10499999744 | bytes 25165824 | tf_op jit(solution)/shard_map/middle/pallas_call | solution.py:465
  208.2 11.7 %weight_grads.2 = bf16[1024,2560]{1,0:T(8,128)(2,1)} custom-call(s32[4]{0:T(128)S(1)} %copy-done.19, bf16[1024,1024]{1,0:T(8,128)(2,1)} %get-tuple-element.118.n2_ref, f32[2048,1024]{1,0:T(8,128)} %cot_ref.7, bf16[1024,1024]{1,0:T(8,128)(2,1)} %get-tuple-element.119.da_ref, bf16[1024,2048]{1,0:T(8,128)(2,1)} %get-tuple-element.120.du_ref, ...), custom_call_target="tpu_custom_call" | custom-call | flops 5368709120 | bytes 18874368 | tf_op jit(solution)/shard_map/weight_grads/pallas_call | solution.py:574
  219.9 17.7 %all_to_all.20.refs_1_ = bf16[4,512,256]{2,1,0:T(8,128)(2,1)} all-to-all(bf16[4,512,256]{2,1,0:T(8,128)(2,1)S(1)} %copy-done.50), channel_id=1, replica_groups=mesh['dp'=8,'mp'=4] {'mp'}, dimensions={0} | all-to-all | bytes 2097152 | tf_op jit(solution)/shard_map/all_to_all | solution.py:55
  237.7 3.5 all-to-all-start.3
  250.7 1.7 collective-permute-start.32
  252.4 3.7 all-to-all-done.3.refs_0_
  258.3 16.9 %attend_backward.2 = (bf16[3,2048,128]{2,1,0:T(8,128)(2,1)}, bf16[3,1024,128]{2,1,0:T(8,128)(2,1)}, f32[2,128]{1,0:T(2,128)S(1)}) custom-call(s32[4]{0:T(128)S(1)} %copy-done.19, bf16[2,2048,128]{2,1,0:T(8,128)(2,1)S(1)} %copy-done.31, bf16[4,2048,128]{2,1,0:T(8,128)(2,1)} %copy-done.27, bf16[4,2048,128]{2,1,0:T(8,128)(2,1)} %copy-done.28, ...), custom_call_target="tpu_custom_call" | custom-call | flops 17999998976 | bytes 6291456 | tf_op jit(solution)/shard_map/attend_backward/pallas_call | solution.py:339
  276.6 12.6 %weight_grads.3 = bf16[1024,2560]{1,0:T(8,128)(2,1)} custom-call(s32[4]{0:T(128)S(1)} %copy-done.19, bf16[1024,1024]{1,0:T(8,128)(2,1)} %get-tuple-element.118.n2_ref, f32[2048,1024]{1,0:T(8,128)} %cot_ref.7, bf16[1024,1024]{1,0:T(8,128)(2,1)} %get-tuple-element.119.da_ref, bf16[1024,2048]{1,0:T(8,128)(2,1)} %get-tuple-element.120.du_ref, ...), custom_call_target="tpu_custom_call" | custom-call | flops 5368709120 | bytes 18874368 | tf_op jit(solution)/shard_map/weight_grads/pallas_call | solution.py:574
  289.2 16.6 %attend_backward.3 = (bf16[3,2048,128]{2,1,0:T(8,128)(2,1)}, bf16[3,1024,128]{2,1,0:T(8,128)(2,1)S(1)}, f32[2,128]{1,0:T(2,128)S(1)}) custom-call(s32[4]{0:T(128)S(1)} %copy-done.19, bf16[2,2048,128]{2,1,0:T(8,128)(2,1)S(1)} %copy-done.33, bf16[4,2048,128]{2,1,0:T(8,128)(2,1)} %copy-done.27, bf16[4,2048,128]{2,1,0:T(8,128)(2,1)} %copy-done.28, ...), custom_call_target="tpu_custom_call" | custom-call | flops 17999998976 | bytes 6291456 | tf_op jit(solution)/shard_map/attend_backward/pallas_call | solution.py:339
  307.7 1.6 copy-done.56
  310.3 1.9 constant_dynamic-slice_fusion.3
  315.1 5.5 %last.2 = (bf16[512,1024]{1,0:T(8,128)(2,1)S(1)}, f32[8,1024]{1,0:T(8,128)S(1)}) custom-call(s32[4]{0:T(128)S(1)} %copy-done.19, bf16[3,2048,128]{2,1,0:T(8,128)(2,1)S(1)} %copy-done.6, bf16[3,2048,128]{2,1,0:T(8,128)(2,1)S(1)} %copy-done.7, bf16[3,1024,128]{2,1,0:T(8,128)(2,1)S(1)} %collective-permute-done.34.s0_ref, ...), custom_call_target="tpu_custom_call" | custom-call | flops 1600000000 | bytes 10485760 | tf_op jit(solution)/shard_map/last/pallas_call | solution.py:521
  320.6 5.7 %convolution_convert_fusion = bf16[1024,768]{0,1:T(8,128)(2,1)S(1)} fusion(bf16[2048,1024]{1,0:T(8,128)(2,1)S(1)} %copy-done.12, bf16[2048,768]{1,0:T(8,128)(2,1)} %bitcast_dynamic-update-slice_fusion), kind=kOutput, calls=%fused_computation.23 | convolution fusion | flops 3222011904 | bytes 8912896 | tf_op jit(solution)/shard_map/dot_general | solution.py:34
  326.5 1.6 collective-permute-start.44
  328.1 2.6 collective-permute-done.51
  331.9 1.6 collective-permute-start.52
  334.0 1.7 collective-permute-start.41
  335.7 5.1 %last.3 = (bf16[512,1024]{1,0:T(8,128)(2,1)S(1)}, f32[8,1024]{1,0:T(8,128)S(1)}) custom-call(s32[4]{0:T(128)S(1)} %copy-done.19, bf16[3,2048,128]{2,1,0:T(8,128)(2,1)S(1)} %copy-done.6, bf16[3,2048,128]{2,1,0:T(8,128)(2,1)S(1)} %copy-done.7, bf16[3,1024,128]{2,1,0:T(8,128)(2,1)S(1)} %collective-permute-done.34.s0_ref, ...), custom_call_target="tpu_custom_call" | custom-call | flops 1600000000 | bytes 10485760 | tf_op jit(solution)/shard_map/last/pallas_call | solution.py:521
  342.6 9.8 %collective-permute-done.45 = bf16[128,768]{0,1:T(8,128)(2,1)S(1)} collective-permute-done((bf16[128,768]{0,1:T(8,128)(2,1)S(1)}, bf16[128,768]{0,1:T(8,128)(2,1)S(1)}, u32[]{:S(2)}, u32[]{:S(2)}) %collective-permute-start.45) | collective-permute-done | bytes 196640 | tf_op jit(solution)/shard_map/ppermute | solution.py:122
  354.6 2.9 add_convert_fusion.5
  359.5 1.6 collective-permute-done.49
  364.1 4.2 fusion.7
  373.5 3.4 collective-permute-done.47
  376.9 2.2 collective-permute-start.40
  379.1 1.9 convert_add_fusion.1
  381.1 1.9 copy.87
  383.6 2.0 add_convert_fusion.4
  385.9 1.7 collective-permute-start.54
  388.9 1.7 add_convert_fusion.refs_1_
  390.6 11.4 %collective-permute-done.40 = bf16[512,1024]{1,0:T(8,128)(2,1)} collective-permute-done((bf16[512,1024]{1,0:T(8,128)(2,1)}, bf16[512,1024]{1,0:T(8,128)(2,1)}, u32[]{:S(2)}, u32[]{:S(2)}) %collective-permute-start.40) | collective-permute-done | bytes 1048608 | tf_op jit(solution)/shard_map/ppermute | solution.py:51
  402.0 2.6 add_convert_fusion.1.refs_0_
  405.1 7.0 %finish.2 = f32[2048,1024]{1,0:T(8,128)} custom-call(s32[4]{0:T(128)S(1)} %copy-done.19, bf16[512,1024]{1,0:T(8,128)(2,1)S(1)} %get-tuple-element.241.refs_0_, bf16[512,1024]{1,0:T(8,128)(2,1)S(1)} %get-tuple-element.240.refs_1_, bf16[512,1024]{1,0:T(8,128)(2,1)} %collective-permute-done.38.refs_2_, bf16[512,1024]{1,0:T(8,128)(2,1)S(1)} %collective-permute-done.39.refs_3_), custom_call_target="tpu_custom_call" | custom-call | bytes 12582912 | tf_op jit(solution)/shard_map/finish/pallas_call | solution.py:615
  414.5 2.0 copy.99
  416.6 2.1 reshape.170
  418.6 2.0 collective-permute-start.58
  420.7 3.2 multiply_subtract_fusion.1
  427.7 7.8 %finish.3 = f32[2048,1024]{1,0:T(8,128)} custom-call(s32[4]{0:T(128)S(1)} %copy-done.19, bf16[512,1024]{1,0:T(8,128)(2,1)} %add_convert_fusion.1.refs_0_, bf16[512,1024]{1,0:T(8,128)(2,1)S(1)} %add_convert_fusion.refs_1_, bf16[512,1024]{1,0:T(8,128)(2,1)} %collective-permute-done.42.refs_2_, bf16[512,1024]{1,0:T(8,128)(2,1)} %collective-permute-done.43.refs_3_), custom_call_target="tpu_custom_call" | custom-call | bytes 12582912 | tf_op jit(solution)/shard_map/finish/pallas_call | solution.py:615
  435.6 1.8 slice_reduce_fusion.1
  (301 shorter events, 87.2 us)
Async XLA Ops:
  8.5 19.6 %collective-permute-start.12 = (bf16[128,768]{1,0:T(8,128)(2,1)S(1)}, bf16[128,768]{1,0:T(8,128)(2,1)S(1)}, u32[]{:S(2)}, u32[]{:S(2)}) collective-permute-start(bf16[128,768]{1,0:T(8,128)(2,1)S(1)} %copy.85.refs_0_), channel_id=1, source_target_pairs={{0,8},{8,16},{16,24},{24,28},{28,20},{20,12},{12,4},{4,0},{1,9},{9... | collective-permute-start | bytes 589832 | tf_op jit(solution)/shard_map/ppermute | solution.py:87
  11.6 22.1 %collective-permute-start.9 = (bf16[128,768]{1,0:T(8,128)(2,1)S(1)}, bf16[128,768]{1,0:T(8,128)(2,1)S(1)}, u32[]{:S(2)}, u32[]{:S(2)}) collective-permute-start(bf16[128,768]{1,0:T(8,128)(2,1)S(1)} %copy.85.refs_0_), channel_id=1, source_target_pairs={{0,4},{8,0},{16,8},{24,16},{28,24},{20,28},{12,20},{4,12},{1,5},{9... | collective-permute-start | bytes 589832 | tf_op jit(solution)/shard_map/ppermute | solution.py:89
  12.6 8.4 %collective-permute-start = (bf16[128,256]{1,0:T(8,128)(2,1)S(1)}, bf16[128,256]{1,0:T(8,128)(2,1)S(1)}, u32[]{:S(2)}, u32[]{:S(2)}) collective-permute-start(bf16[128,256]{1,0:T(8,128)(2,1)S(1)} %convert_bitcast_fusion), channel_id=1, source_target_pairs={{0,2},{1,3},{2,0},{3,1},{4,6},{5,7},{6,4},{7,5},{8,10},{9,11},{10,... | collective-permute-start | bytes 196616 | tf_op jit(solution)/shard_map/ppermute | solution.py:51
  15.3 34.8 %collective-permute-start.8 = (f32[1,1024]{1,0:T(1,128)S(1)}, f32[1,1024]{1,0:T(1,128)S(1)}, u32[]{:S(2)}, u32[]{:S(2)}) collective-permute-start(f32[1,1024]{1,0:T(1,128)S(1)} %bitcast.94), channel_id=1, source_target_pairs={{0,1},{1,0},{2,3},{3,2},{4,5},{5,4},{6,7},{7,6},{8,9},{9,8},{10,11... | collective-permute-start | bytes 12296 | tf_op jit(solution)/shard_map/ppermute | solution.py:47
  21.1 5.4 %collective-permute-start.1 = (bf16[128,512]{1,0:T(8,128)(2,1)S(1)}, bf16[128,512]{1,0:T(8,128)(2,1)S(1)}, u32[]{:S(2)}, u32[]{:S(2)}) collective-permute-start(bf16[128,512]{1,0:T(8,128)(2,1)S(1)} %pad_maximum_fusion.refs_0_), channel_id=1, source_target_pairs={{0,8},{8,16},{16,24},{24,28},{28,20},{20,12},{12,4},{4,0},{1,9},{9... | collective-permute-start | bytes 393224 | tf_op jit(solution)/shard_map/ppermute | solution.py:87
  22.7 10.5 %collective-permute-start.5 = (bf16[128,512]{1,0:T(8,128)(2,1)S(1)}, bf16[128,512]{1,0:T(8,128)(2,1)S(1)}, u32[]{:S(2)}, u32[]{:S(2)}) collective-permute-start(bf16[128,512]{1,0:T(8,128)(2,1)S(1)} %pad_maximum_fusion.refs_0_), channel_id=1, source_target_pairs={{0,4},{8,0},{16,8},{24,16},{28,24},{20,28},{12,20},{4,12},{1,5},{9... | collective-permute-start | bytes 393224 | tf_op jit(solution)/shard_map/ppermute | solution.py:89
  26.5 7.6 %collective-permute-start.2 = (bf16[128,512]{1,0:T(8,128)(2,1)S(1)}, bf16[128,512]{1,0:T(8,128)(2,1)S(1)}, u32[]{:S(2)}, u32[]{:S(2)}) collective-permute-start(bf16[128,512]{1,0:T(8,128)(2,1)S(1)} %collective-permute-done.1.refs_7_), channel_id=1, source_target_pairs={{0,8},{8,16},{16,24},{24,28},{28,20},{20,12},{12,4},{4,0},{1,9},{9... | collective-permute-start | bytes 393224 | tf_op jit(solution)/shard_map/ppermute | solution.py:87
  28.1 7.6 %collective-permute-start.13 = (bf16[128,768]{1,0:T(8,128)(2,1)S(1)}, bf16[128,768]{1,0:T(8,128)(2,1)S(1)}, u32[]{:S(2)}, u32[]{:S(2)}) collective-permute-start(bf16[128,768]{1,0:T(8,128)(2,1)S(1)} %collective-permute-done.12.refs_7_), channel_id=1, source_target_pairs={{0,8},{8,16},{16,24},{24,28},{28,20},{20,12},{12,4},{4,0},{1,9},{9... | collective-permute-start | bytes 589832 | tf_op jit(solution)/shard_map/ppermute | solution.py:87
  33.2 6.4 %collective-permute-start.6 = (bf16[128,512]{1,0:T(8,128)(2,1)S(1)}, bf16[128,512]{1,0:T(8,128)(2,1)S(1)}, u32[]{:S(2)}, u32[]{:S(2)}) collective-permute-start(bf16[128,512]{1,0:T(8,128)(2,1)S(1)} %collective-permute-done.5.refs_1_), channel_id=1, source_target_pairs={{0,4},{8,0},{16,8},{24,16},{28,24},{20,28},{12,20},{4,12},{1,5},{9... | collective-permute-start | bytes 393224 | tf_op jit(solution)/shard_map/ppermute | solution.py:89
  33.7 10.1 %collective-permute-start.10 = (bf16[128,768]{1,0:T(8,128)(2,1)S(1)}, bf16[128,768]{1,0:T(8,128)(2,1)}, u32[]{:S(2)}, u32[]{:S(2)}) collective-permute-start(bf16[128,768]{1,0:T(8,128)(2,1)S(1)} %collective-permute-done.9.refs_1_), channel_id=1, source_target_pairs={{0,4},{8,0},{16,8},{24,16},{28,24},{20,28},{12,20},{4,12},{1,5},{9... | collective-permute-start | bytes 589832 | tf_op jit(solution)/shard_map/ppermute | solution.py:89
  34.2 10.1 %collective-permute-start.3 = (bf16[128,512]{1,0:T(8,128)(2,1)S(1)}, bf16[128,512]{1,0:T(8,128)(2,1)S(1)}, u32[]{:S(2)}, u32[]{:S(2)}) collective-permute-start(bf16[128,512]{1,0:T(8,128)(2,1)S(1)} %collective-permute-done.2.refs_6_), channel_id=1, source_target_pairs={{0,8},{8,16},{16,24},{24,28},{28,20},{20,12},{12,4},{4,0},{1,9},{9... | collective-permute-start | bytes 393224 | tf_op jit(solution)/shard_map/ppermute | solution.py:87
  35.7 10.1 %collective-permute-start.14 = (bf16[128,768]{1,0:T(8,128)(2,1)S(1)}, bf16[128,768]{1,0:T(8,128)(2,1)S(1)}, u32[]{:S(2)}, u32[]{:S(2)}) collective-permute-start(bf16[128,768]{1,0:T(8,128)(2,1)S(1)} %collective-permute-done.13.refs_6_), channel_id=1, source_target_pairs={{0,8},{8,16},{16,24},{24,28},{28,20},{20,12},{12,4},{4,0},{1,9},{9... | collective-permute-start | bytes 589832 | tf_op jit(solution)/shard_map/ppermute | solution.py:87
  39.7 12.6 %collective-permute-start.7 = (bf16[128,512]{1,0:T(8,128)(2,1)S(1)}, bf16[128,512]{1,0:T(8,128)(2,1)S(1)}, u32[]{:S(2)}, u32[]{:S(2)}) collective-permute-start(bf16[128,512]{1,0:T(8,128)(2,1)S(1)} %collective-permute-done.6.refs_2_), channel_id=1, source_target_pairs={{0,4},{8,0},{16,8},{24,16},{28,24},{20,28},{12,20},{4,12},{1,5},{9... | collective-permute-start | bytes 393224 | tf_op jit(solution)/shard_map/ppermute | solution.py:89
  43.8 13.7 %collective-permute-start.11 = (bf16[128,768]{1,0:T(8,128)(2,1)}, bf16[128,768]{1,0:T(8,128)(2,1)}, u32[]{:S(2)}, u32[]{:S(2)}) collective-permute-start(bf16[128,768]{1,0:T(8,128)(2,1)} %collective-permute-done.10.refs_2_), channel_id=1, source_target_pairs={{0,4},{8,0},{16,8},{24,16},{28,24},{20,28},{12,20},{4,12},{1,5},{9... | collective-permute-start | bytes 589832 | tf_op jit(solution)/shard_map/ppermute | solution.py:89
  44.3 8.5 %collective-permute-start.4 = (bf16[128,512]{1,0:T(8,128)(2,1)S(1)}, bf16[128,512]{1,0:T(8,128)(2,1)S(1)}, u32[]{:S(2)}, u32[]{:S(2)}) collective-permute-start(bf16[128,512]{1,0:T(8,128)(2,1)S(1)} %collective-permute-done.3.refs_5_), channel_id=1, source_target_pairs={{0,8},{8,16},{16,24},{24,28},{28,20},{20,12},{12,4},{4,0},{1,9},{9... | collective-permute-start | bytes 393224 | tf_op jit(solution)/shard_map/ppermute | solution.py:87
  45.9 9.0 %collective-permute-start.15 = (bf16[128,768]{1,0:T(8,128)(2,1)S(1)}, bf16[128,768]{1,0:T(8,128)(2,1)S(1)}, u32[]{:S(2)}, u32[]{:S(2)}) collective-permute-start(bf16[128,768]{1,0:T(8,128)(2,1)S(1)} %collective-permute-done.14.refs_5_), channel_id=1, source_target_pairs={{0,8},{8,16},{16,24},{24,28},{28,20},{20,12},{12,4},{4,0},{1,9},{9... | collective-permute-start | bytes 589832 | tf_op jit(solution)/shard_map/ppermute | solution.py:87
  50.8 24.7 %collective-permute-start.16 = (bf16[128,1024]{1,0:T(8,128)(2,1)S(1)}, bf16[128,1024]{1,0:T(8,128)(2,1)S(1)}, u32[]{:S(2)}, u32[]{:S(2)}) collective-permute-start(bf16[128,1024]{1,0:T(8,128)(2,1)S(1)} %bitcast.77), channel_id=1, source_target_pairs={{0,8},{8,16},{16,24},{24,28},{28,20},{20,12},{12,4},{4,0},{1,9},{9... | collective-permute-start | bytes 786440 | tf_op jit(solution)/shard_map/ppermute | solution.py:87
  52.3 41.2 %collective-permute-start.22 = (bf16[128,1024]{1,0:T(8,128)(2,1)S(1)}, bf16[128,1024]{1,0:T(8,128)(2,1)S(1)}, u32[]{:S(2)}, u32[]{:S(2)}) collective-permute-start(bf16[128,1024]{1,0:T(8,128)(2,1)S(1)} %bitcast.78), channel_id=1, source_target_pairs={{0,4},{8,0},{16,8},{24,16},{28,24},{20,28},{12,20},{4,12},{1,5},{9... | collective-permute-start | bytes 786440 | tf_op jit(solution)/shard_map/ppermute | solution.py:89
  55.5 34.9 %collective-permute-start.19 = (bf16[128,1024]{1,0:T(8,128)(2,1)S(1)}, bf16[128,1024]{1,0:T(8,128)(2,1)S(1)}, u32[]{:S(2)}, u32[]{:S(2)}) collective-permute-start(bf16[128,1024]{1,0:T(8,128)(2,1)S(1)} %bitcast.80), channel_id=1, source_target_pairs={{0,8},{8,16},{16,24},{24,28},{28,20},{20,12},{12,4},{4,0},{1,9},{9... | collective-permute-start | bytes 786440 | tf_op jit(solution)/shard_map/ppermute | solution.py:87
  57.1 36.9 %collective-permute-start.26 = (bf16[128,1024]{1,0:T(8,128)(2,1)S(1)}, bf16[128,1024]{1,0:T(8,128)(2,1)S(1)}, u32[]{:S(2)}, u32[]{:S(2)}) collective-permute-start(bf16[128,1024]{1,0:T(8,128)(2,1)S(1)} %bitcast.81), channel_id=1, source_target_pairs={{0,4},{8,0},{16,8},{24,16},{28,24},{20,28},{12,20},{4,12},{1,5},{9... | collective-permute-start | bytes 786440 | tf_op jit(solution)/shard_map/ppermute | solution.py:89
  75.5 16.5 %collective-permute-start.17 = (bf16[128,1024]{1,0:T(8,128)(2,1)S(1)}, bf16[128,1024]{1,0:T(8,128)(2,1)S(1)}, u32[]{:S(2)}, u32[]{:S(2)}) collective-permute-start(bf16[128,1024]{1,0:T(8,128)(2,1)S(1)} %collective-permute-done.16.refs_7_), channel_id=1, source_target_pairs={{0,8},{8,16},{16,24},{24,28},{28,20},{20,12},{12,4},{4,0},{1,9},{9... | collective-permute-start | bytes 786440 | tf_op jit(solution)/shard_map/ppermute | solution.py:87
  90.4 6.4 %collective-permute-start.20 = (bf16[128,1024]{1,0:T(8,128)(2,1)S(1)}, bf16[128,1024]{1,0:T(8,128)(2,1)S(1)}, u32[]{:S(2)}, u32[]{:S(2)}) collective-permute-start(bf16[128,1024]{1,0:T(8,128)(2,1)S(1)} %collective-permute-done.19.refs_15_), channel_id=1, source_target_pairs={{0,8},{8,16},{16,24},{24,28},{28,20},{20,12},{12,4},{4,0},{1,9},{9... | collective-permute-start | bytes 786440 | tf_op jit(solution)/shard_map/ppermute | solution.py:87
  92.0 7.6 %collective-permute-start.18 = (bf16[128,1024]{1,0:T(8,128)(2,1)S(1)}, bf16[128,1024]{1,0:T(8,128)(2,1)S(1)}, u32[]{:S(2)}, u32[]{:S(2)}) collective-permute-start(bf16[128,1024]{1,0:T(8,128)(2,1)S(1)} %collective-permute-done.17.refs_6_), channel_id=1, source_target_pairs={{0,8},{8,16},{16,24},{24,28},{28,20},{20,12},{12,4},{4,0},{1,9},{9... | collective-permute-start | bytes 786440 | tf_op jit(solution)/shard_map/ppermute | solution.py:87
  93.5 18.5 %collective-permute-start.23 = (bf16[128,1024]{1,0:T(8,128)(2,1)S(1)}, bf16[128,1024]{1,0:T(8,128)(2,1)S(1)}, u32[]{:S(2)}, u32[]{:S(2)}) collective-permute-start(bf16[128,1024]{1,0:T(8,128)(2,1)S(1)} %collective-permute-done.22.refs_1_), channel_id=1, source_target_pairs={{0,4},{8,0},{16,8},{24,16},{28,24},{20,28},{12,20},{4,12},{1,5},{9... | collective-permute-start | bytes 786440 | tf_op jit(solution)/shard_map/ppermute | solution.py:89
  94.0 18.4 %collective-permute-start.27 = (bf16[128,1024]{1,0:T(8,128)(2,1)S(1)}, bf16[128,1024]{1,0:T(8,128)(2,1)S(1)}, u32[]{:S(2)}, u32[]{:S(2)}) collective-permute-start(bf16[128,1024]{1,0:T(8,128)(2,1)S(1)} %collective-permute-done.26.refs_9_), channel_id=1, source_target_pairs={{0,4},{8,0},{16,8},{24,16},{28,24},{20,28},{12,20},{4,12},{1,5},{9... | collective-permute-start | bytes 786440 | tf_op jit(solution)/shard_map/ppermute | solution.py:89
  110.4 6.4 %collective-permute-start.29 = (bf16[128,1024]{1,0:T(8,128)(2,1)S(1)}, bf16[128,1024]{1,0:T(8,128)(2,1)S(1)}, u32[]{:S(2)}, u32[]{:S(2)}) collective-permute-start(bf16[128,1024]{1,0:T(8,128)(2,1)S(1)} %collective-permute-done.20.refs_14_), channel_id=1, source_target_pairs={{0,8},{8,16},{16,24},{24,28},{28,20},{20,12},{12,4},{4,0},{1,9},{9... | collective-permute-start | bytes 786440 | tf_op jit(solution)/shard_map/ppermute | solution.py:87
  111.9 6.4 %collective-permute-start.24 = (bf16[128,1024]{1,0:T(8,128)(2,1)S(1)}, bf16[128,1024]{1,0:T(8,128)(2,1)S(1)}, u32[]{:S(2)}, u32[]{:S(2)}) collective-permute-start(bf16[128,1024]{1,0:T(8,128)(2,1)S(1)} %collective-permute-done.23.refs_2_), channel_id=1, source_target_pairs={{0,4},{8,0},{16,8},{24,16},{28,24},{20,28},{12,20},{4,12},{1,5},{9... | collective-permute-start | bytes 786440 | tf_op jit(solution)/shard_map/ppermute | solution.py:89
  112.4 8.7 %collective-permute-start.28 = (bf16[128,1024]{1,0:T(8,128)(2,1)S(1)}, bf16[128,1024]{1,0:T(8,128)(2,1)S(1)}, u32[]{:S(2)}, u32[]{:S(2)}) collective-permute-start(bf16[128,1024]{1,0:T(8,128)(2,1)S(1)} %collective-permute-done.27.refs_10_), channel_id=1, source_target_pairs={{0,4},{8,0},{16,8},{24,16},{28,24},{20,28},{12,20},{4,12},{1,5},{9... | collective-permute-start | bytes 786440 | tf_op jit(solution)/shard_map/ppermute | solution.py:89
  112.9 8.2 %collective-permute-start.25 = (bf16[128,1024]{1,0:T(8,128)(2,1)S(1)}, bf16[128,1024]{1,0:T(8,128)(2,1)S(1)}, u32[]{:S(2)}, u32[]{:S(2)}) collective-permute-start(bf16[128,1024]{1,0:T(8,128)(2,1)S(1)} %collective-permute-done.18.refs_5_), channel_id=1, source_target_pairs={{0,8},{8,16},{16,24},{24,28},{28,20},{20,12},{12,4},{4,0},{1,9},{9... | collective-permute-start | bytes 786440 | tf_op jit(solution)/shard_map/ppermute | solution.py:87
  116.8 6.4 %collective-permute-start.30 = (bf16[128,1024]{1,0:T(8,128)(2,1)S(1)}, bf16[128,1024]{1,0:T(8,128)(2,1)S(1)}, u32[]{:S(2)}, u32[]{:S(2)}) collective-permute-start(bf16[128,1024]{1,0:T(8,128)(2,1)S(1)} %collective-permute-done.29.refs_13_), channel_id=1, source_target_pairs={{0,8},{8,16},{16,24},{24,28},{28,20},{20,12},{12,4},{4,0},{1,9},{9... | collective-permute-start | bytes 786440 | tf_op jit(solution)/shard_map/ppermute | solution.py:87
  126.0 36.1 %collective-permute-start.31 = (bf16[1024,2048]{1,0:T(8,128)(2,1)}, bf16[1024,2048]{1,0:T(8,128)(2,1)}, u32[]{:S(2)}, u32[]{:S(2)}) collective-permute-start(bf16[1024,2048]{1,0:T(8,128)(2,1)} %assemble.3.late_own_ref), channel_id=1, source_target_pairs={{0,1},{1,0},{2,3},{3,2},{4,5},{5,4},{6,7},{7,6},{8,9},{9,8},{10,11... | collective-permute-start | bytes 12582920 | tf_op jit(solution)/shard_map/ppermute | solution.py:47
  126.0 18.0 %all-to-all-start = ((bf16[4,1024,128]{2,1,0:T(8,128)(2,1)}), bf16[4,1024,128]{2,1,0:T(8,128)(2,1)S(1)}, u32[]{:S(2)}, u32[]{:S(2)}) async-start(bf16[4,1024,128]{2,1,0:T(8,128)(2,1)} %get-tuple-element.94), calls=%async_computation | async-start | bytes 2097152 | tf_op jit(solution)/shard_map/all_to_all | solution.py:55
  130.2 18.1 %collective-permute-start.21 = (bf16[1024,512]{1,0:T(8,128)(2,1)S(1)}, bf16[1024,512]{1,0:T(8,128)(2,1)}, u32[]{:S(2)}, u32[]{:S(2)}) collective-permute-start(bf16[1024,512]{1,0:T(8,128)(2,1)S(1)} %assemble.2.first_own_ref), channel_id=1, source_target_pairs={{0,1},{1,0},{2,3},{3,2},{4,5},{5,4},{6,7},{7,6},{8,9},{9,8},{10,11... | collective-permute-start | bytes 3145736 | tf_op jit(solution)/shard_map/ppermute | solution.py:47
  144.0 18.1 %all-to-all-start.1 = ((bf16[4,1024,128]{2,1,0:T(8,128)(2,1)}), bf16[4,1024,128]{2,1,0:T(8,128)(2,1)S(1)}, u32[]{:S(2)}, u32[]{:S(2)}) async-start(bf16[4,1024,128]{2,1,0:T(8,128)(2,1)} %copy-done.17), calls=%async_computation.1 | async-start | bytes 2097152 | tf_op jit(solution)/shard_map/all_to_all | solution.py:55
  219.9 56.7 %collective-permute-start.33 = (bf16[1024,2560]{1,0:T(8,128)(2,1)}, bf16[1024,2560]{1,0:T(8,128)(2,1)}, u32[]{:S(2)}, u32[]{:S(2)}) collective-permute-start(bf16[1024,2560]{1,0:T(8,128)(2,1)} %weight_grads.2), channel_id=1, source_target_pairs={{0,1},{1,0},{2,3},{3,2},{4,5},{5,4},{6,7},{7,6},{8,9},{9,8},{10,11... | collective-permute-start | bytes 15728648 | tf_op jit(solution)/shard_map/ppermute | solution.py:47
  237.7 18.4 %all-to-all-start.3 = ((bf16[4,512,256]{2,1,0:T(8,128)(2,1)}), bf16[4,512,256]{2,1,0:T(8,128)(2,1)S(1)}, u32[]{:S(2)}, u32[]{:S(2)}) async-start(bf16[4,512,256]{2,1,0:T(8,128)(2,1)} %get-tuple-element.124), calls=%async_computation.3 | async-start | bytes 2097152 | tf_op jit(solution)/shard_map/all_to_all | solution.py:55
  241.2 194.4 %all-gather.4.cloned.1.call-start = ((), (), s32[]{:S(2)}) async-start(), calls=%async_computation.4 | async-start | bytes 2162688 | tf_op jit(solution)/shard_map/all_gather | solution.py:791
  249.6 63.5 %collective-permute-start.36 = (bf16[1024,768]{1,0:T(8,128)(2,1)}, bf16[1024,768]{1,0:T(8,128)(2,1)}, u32[]{:S(2)}, u32[]{:S(2)}) collective-permute-start(bf16[1024,768]{1,0:T(8,128)(2,1)} %copy-done.8), channel_id=1, source_target_pairs={{0,1},{1,0},{2,3},{3,2},{4,5},{5,4},{6,7},{7,6},{8,9},{9,8},{10,11... | collective-permute-start | bytes 4718600 | tf_op jit(solution)/shard_map/ppermute | solution.py:47
  250.7 82.8 %collective-permute-start.32 = (bf16[512,1024]{1,0:T(8,128)(2,1)}, bf16[512,1024]{1,0:T(8,128)(2,1)}, u32[]{:S(2)}, u32[]{:S(2)}) collective-permute-start(bf16[512,1024]{1,0:T(8,128)(2,1)} %get-tuple-element.116), channel_id=1, source_target_pairs={{0,2},{1,3},{2,0},{3,1},{4,6},{5,7},{6,4},{7,5},{8,10},{9,11},{10,... | collective-permute-start | bytes 3145736 | tf_op jit(solution)/shard_map/ppermute | solution.py:51
  275.3 39.4 %collective-permute-start.34 = (bf16[3,1024,128]{2,1,0:T(8,128)(2,1)}, bf16[3,1024,128]{2,1,0:T(8,128)(2,1)S(1)}, u32[]{:S(2)}, u32[]{:S(2)}) collective-permute-start(bf16[3,1024,128]{2,1,0:T(8,128)(2,1)} %get-tuple-element.133), channel_id=1, source_target_pairs={{0,1},{1,0},{2,3},{3,2},{4,5},{5,4},{6,7},{7,6},{8,9},{9,8},{10,11... | collective-permute-start | bytes 2359304 | tf_op jit(solution)/shard_map/ppermute | solution.py:47
  275.3 58.2 %collective-permute-start.37 = (bf16[512,1024]{1,0:T(8,128)(2,1)}, bf16[512,1024]{1,0:T(8,128)(2,1)}, u32[]{:S(2)}, u32[]{:S(2)}) collective-permute-start(bf16[512,1024]{1,0:T(8,128)(2,1)} %get-tuple-element.140), channel_id=1, source_target_pairs={{0,2},{1,3},{2,0},{3,1},{4,6},{5,7},{6,4},{7,5},{8,10},{9,11},{10,... | collective-permute-start | bytes 3145736 | tf_op jit(solution)/shard_map/ppermute | solution.py:51
  305.8 9.4 %collective-permute-start.35 = (bf16[3,1024,128]{2,1,0:T(8,128)(2,1)S(1)}, bf16[3,1024,128]{2,1,0:T(8,128)(2,1)S(1)}, u32[]{:S(2)}, u32[]{:S(2)}) collective-permute-start(bf16[3,1024,128]{2,1,0:T(8,128)(2,1)S(1)} %get-tuple-element.134), channel_id=1, source_target_pairs={{0,1},{1,0},{2,3},{3,2},{4,5},{5,4},{6,7},{7,6},{8,9},{9,8},{10,11... | collective-permute-start | bytes 2359304 | tf_op jit(solution)/shard_map/ppermute | solution.py:47
  313.1 17.6 %collective-permute-start.51 = (bf16[128,2560]{1,0:T(8,128)(2,1)S(1)}, bf16[128,2560]{1,0:T(8,128)(2,1)S(1)}, u32[]{:S(2)}, u32[]{:S(2)}) collective-permute-start(bf16[128,2560]{1,0:T(8,128)(2,1)S(1)} %get-tuple-element.246), channel_id=1, source_target_pairs={{0,8},{8,16},{16,24},{24,28},{28,20},{20,12},{12,4},{4,0},{1,9},{9... | collective-permute-start | bytes 1966088 | tf_op jit(solution)/shard_map/ppermute | solution.py:122
  314.6 39.9 %collective-permute-start.55 = (bf16[128,2560]{1,0:T(8,128)(2,1)S(1)}, bf16[128,2560]{1,0:T(8,128)(2,1)S(1)}, u32[]{:S(2)}, u32[]{:S(2)}) collective-permute-start(bf16[128,2560]{1,0:T(8,128)(2,1)S(1)} %get-tuple-element.247), channel_id=1, source_target_pairs={{0,4},{8,0},{16,8},{24,16},{28,24},{20,28},{12,20},{4,12},{1,5},{9... | collective-permute-start | bytes 1966088 | tf_op jit(solution)/shard_map/ppermute | solution.py:121
  326.4 34.8 %copy-start.44 = (bf16[1024,768]{0,1:T(8,128)(2,1)}, bf16[1024,768]{0,1:T(8,128)(2,1)S(1)}, u32[]{:S(2)}) copy-start(bf16[1024,768]{0,1:T(8,128)(2,1)S(1)} %convolution_convert_fusion) | copy-start | bytes 4718596
  326.5 14.4 %collective-permute-start.44 = (bf16[128,768]{0,1:T(8,128)(2,1)S(1)}, bf16[128,768]{0,1:T(8,128)(2,1)S(1)}, u32[]{:S(2)}, u32[]{:S(2)}) collective-permute-start(bf16[128,768]{0,1:T(8,128)(2,1)S(1)} %get-tuple-element.252), channel_id=1, source_target_pairs={{0,8},{8,16},{16,24},{24,28},{28,20},{20,12},{12,4},{4,0},{1,9},{9... | collective-permute-start | bytes 589832 | tf_op jit(solution)/shard_map/ppermute | solution.py:122
  331.9 22.7 %collective-permute-start.52 = (bf16[128,2560]{1,0:T(8,128)(2,1)S(1)}, bf16[128,2560]{1,0:T(8,128)(2,1)S(1)}, u32[]{:S(2)}, u32[]{:S(2)}) collective-permute-start(bf16[128,2560]{1,0:T(8,128)(2,1)S(1)} %add_convert_fusion.6), channel_id=1, source_target_pairs={{0,8},{8,16},{16,24},{24,28},{28,20},{20,12},{12,4},{4,0},{1,9},{9... | collective-permute-start | bytes 1966088 | tf_op jit(solution)/shard_map/ppermute | solution.py:122
  333.5 9.1 %collective-permute-start.48 = (bf16[128,768]{0,1:T(8,128)(2,1)S(1)}, bf16[128,768]{0,1:T(8,128)(2,1)S(1)}, u32[]{:S(2)}, u32[]{:S(2)}) collective-permute-start(bf16[128,768]{0,1:T(8,128)(2,1)S(1)} %get-tuple-element.253), channel_id=1, source_target_pairs={{0,4},{8,0},{16,8},{24,16},{28,24},{20,28},{12,20},{4,12},{1,5},{9... | collective-permute-start | bytes 589832 | tf_op jit(solution)/shard_map/ppermute | solution.py:121
  334.0 51.9 %collective-permute-start.41 = (bf16[512,1024]{1,0:T(8,128)(2,1)S(1)}, bf16[512,1024]{1,0:T(8,128)(2,1)}, u32[]{:S(2)}, u32[]{:S(2)}) collective-permute-start(bf16[512,1024]{1,0:T(8,128)(2,1)S(1)} %get-tuple-element.143), channel_id=1, source_target_pairs={{0,2},{1,3},{2,0},{3,1},{4,6},{5,7},{6,4},{7,5},{8,10},{9,11},{10,... | collective-permute-start | bytes 3145736 | tf_op jit(solution)/shard_map/ppermute | solution.py:51
  341.0 11.4 %collective-permute-start.45 = (bf16[128,768]{0,1:T(8,128)(2,1)S(1)}, bf16[128,768]{0,1:T(8,128)(2,1)S(1)}, u32[]{:S(2)}, u32[]{:S(2)}) collective-permute-start(bf16[128,768]{0,1:T(8,128)(2,1)S(1)} %add_convert_fusion.11), channel_id=1, source_target_pairs={{0,8},{8,16},{16,24},{24,28},{28,20},{20,12},{12,4},{4,0},{1,9},{9... | collective-permute-start | bytes 589832 | tf_op jit(solution)/shard_map/ppermute | solution.py:122
  352.5 7.1 %collective-permute-start.46 = (bf16[128,768]{0,1:T(8,128)(2,1)S(1)}, bf16[128,768]{0,1:T(8,128)(2,1)S(1)}, u32[]{:S(2)}, u32[]{:S(2)}) collective-permute-start(bf16[128,768]{0,1:T(8,128)(2,1)S(1)} %get-tuple-element.250), channel_id=1, source_target_pairs={{0,8},{8,16},{16,24},{24,28},{28,20},{20,12},{12,4},{4,0},{1,9},{9... | collective-permute-start | bytes 589832 | tf_op jit(solution)/shard_map/ppermute | solution.py:122
  354.1 7.1 %collective-permute-start.49 = (bf16[128,768]{0,1:T(8,128)(2,1)S(1)}, bf16[128,768]{0,1:T(8,128)(2,1)S(1)}, u32[]{:S(2)}, u32[]{:S(2)}) collective-permute-start(bf16[128,768]{0,1:T(8,128)(2,1)S(1)} %get-tuple-element.251), channel_id=1, source_target_pairs={{0,4},{8,0},{16,8},{24,16},{28,24},{20,28},{12,20},{4,12},{1,5},{9... | collective-permute-start | bytes 589832 | tf_op jit(solution)/shard_map/ppermute | solution.py:121
  357.5 25.5 %collective-permute-start.56 = (bf16[128,2560]{1,0:T(8,128)(2,1)}, bf16[128,2560]{1,0:T(8,128)(2,1)}, u32[]{:S(2)}, u32[]{:S(2)}) collective-permute-start(bf16[128,2560]{1,0:T(8,128)(2,1)} %get-tuple-element.153), channel_id=1, source_target_pairs={{0,4},{8,0},{16,8},{24,16},{28,24},{20,28},{12,20},{4,12},{1,5},{9... | collective-permute-start | bytes 1966088 | tf_op jit(solution)/shard_map/ppermute | solution.py:121
  357.9 25.6 %collective-permute-start.53 = (bf16[128,2560]{1,0:T(8,128)(2,1)}, bf16[128,2560]{1,0:T(8,128)(2,1)}, u32[]{:S(2)}, u32[]{:S(2)}) collective-permute-start(bf16[128,2560]{1,0:T(8,128)(2,1)} %get-tuple-element.152), channel_id=1, source_target_pairs={{0,8},{8,16},{16,24},{24,28},{28,20},{20,12},{12,4},{4,0},{1,9},{9... | collective-permute-start | bytes 1966088 | tf_op jit(solution)/shard_map/ppermute | solution.py:122
  362.0 14.9 %collective-permute-start.47 = (bf16[128,768]{0,1:T(8,128)(2,1)}, bf16[128,768]{0,1:T(8,128)(2,1)}, u32[]{:S(2)}, u32[]{:S(2)}) collective-permute-start(bf16[128,768]{0,1:T(8,128)(2,1)} %get-tuple-element.248), channel_id=1, source_target_pairs={{0,8},{8,16},{16,24},{24,28},{28,20},{20,12},{12,4},{4,0},{1,9},{9... | collective-permute-start | bytes 589832 | tf_op jit(solution)/shard_map/ppermute | solution.py:122
  363.4 15.7 %collective-permute-start.50 = (bf16[128,768]{0,1:T(8,128)(2,1)}, bf16[128,768]{0,1:T(8,128)(2,1)}, u32[]{:S(2)}, u32[]{:S(2)}) collective-permute-start(bf16[128,768]{0,1:T(8,128)(2,1)} %get-tuple-element.249), channel_id=1, source_target_pairs={{0,4},{8,0},{16,8},{24,16},{28,24},{20,28},{12,20},{4,12},{1,5},{9... | collective-permute-start | bytes 589832 | tf_op jit(solution)/shard_map/ppermute | solution.py:121
  376.9 25.1 %collective-permute-start.40 = (bf16[512,1024]{1,0:T(8,128)(2,1)}, bf16[512,1024]{1,0:T(8,128)(2,1)}, u32[]{:S(2)}, u32[]{:S(2)}) collective-permute-start(bf16[512,1024]{1,0:T(8,128)(2,1)} %copy-done.15), channel_id=1, source_target_pairs={{0,2},{1,3},{2,0},{3,1},{4,6},{5,7},{6,4},{7,5},{8,10},{9,11},{10,... | collective-permute-start | bytes 3145736 | tf_op jit(solution)/shard_map/ppermute | solution.py:51
  379.1 25.5 %collective-permute-start.38 = (bf16[512,1024]{1,0:T(8,128)(2,1)S(1)}, bf16[512,1024]{1,0:T(8,128)(2,1)}, u32[]{:S(2)}, u32[]{:S(2)}) collective-permute-start(bf16[512,1024]{1,0:T(8,128)(2,1)S(1)} %get-tuple-element.241.refs_0_), channel_id=1, source_target_pairs={{0,1},{1,0},{2,3},{3,2},{4,5},{5,4},{6,7},{7,6},{8,9},{9,8},{10,11... | collective-permute-start | bytes 3145736 | tf_op jit(solution)/shard_map/ppermute | solution.py:47
  383.0 22.1 %collective-permute-start.39 = (bf16[512,1024]{1,0:T(8,128)(2,1)S(1)}, bf16[512,1024]{1,0:T(8,128)(2,1)S(1)}, u32[]{:S(2)}, u32[]{:S(2)}) collective-permute-start(bf16[512,1024]{1,0:T(8,128)(2,1)S(1)} %get-tuple-element.240.refs_1_), channel_id=1, source_target_pairs={{0,1},{1,0},{2,3},{3,2},{4,5},{5,4},{6,7},{7,6},{8,9},{9,8},{10,11... | collective-permute-start | bytes 3145736 | tf_op jit(solution)/shard_map/ppermute | solution.py:47
  385.6 26.6 %collective-permute-start.57 = (bf16[128,2560]{1,0:T(8,128)(2,1)S(1)}, bf16[128,2560]{1,0:T(8,128)(2,1)S(1)}, u32[]{:S(2)}, u32[]{:S(2)}) collective-permute-start(bf16[128,2560]{1,0:T(8,128)(2,1)S(1)} %get-tuple-element.154), channel_id=1, source_target_pairs={{0,4},{8,0},{16,8},{24,16},{28,24},{20,28},{12,20},{4,12},{1,5},{9... | collective-permute-start | bytes 1966088 | tf_op jit(solution)/shard_map/ppermute | solution.py:121
  385.9 26.2 %collective-permute-start.54 = (bf16[128,2560]{1,0:T(8,128)(2,1)S(1)}, bf16[128,2560]{1,0:T(8,128)(2,1)S(1)}, u32[]{:S(2)}, u32[]{:S(2)}) collective-permute-start(bf16[128,2560]{1,0:T(8,128)(2,1)S(1)} %get-tuple-element.242), channel_id=1, source_target_pairs={{0,8},{8,16},{16,24},{24,28},{28,20},{20,12},{12,4},{4,0},{1,9},{9... | collective-permute-start | bytes 1966088 | tf_op jit(solution)/shard_map/ppermute | solution.py:122
  402.0 25.7 %collective-permute-start.43 = (bf16[512,1024]{1,0:T(8,128)(2,1)S(1)}, bf16[512,1024]{1,0:T(8,128)(2,1)}, u32[]{:S(2)}, u32[]{:S(2)}) collective-permute-start(bf16[512,1024]{1,0:T(8,128)(2,1)S(1)} %add_convert_fusion.refs_1_), channel_id=1, source_target_pairs={{0,1},{1,0},{2,3},{3,2},{4,5},{5,4},{6,7},{7,6},{8,9},{9,8},{10,11... | collective-permute-start | bytes 3145736 | tf_op jit(solution)/shard_map/ppermute | solution.py:47
  404.6 23.1 %collective-permute-start.42 = (bf16[512,1024]{1,0:T(8,128)(2,1)}, bf16[512,1024]{1,0:T(8,128)(2,1)}, u32[]{:S(2)}, u32[]{:S(2)}) collective-permute-start(bf16[512,1024]{1,0:T(8,128)(2,1)} %add_convert_fusion.1.refs_0_), channel_id=1, source_target_pairs={{0,1},{1,0},{2,3},{3,2},{4,5},{5,4},{6,7},{7,6},{8,9},{9,8},{10,11... | collective-permute-start | bytes 3145736 | tf_op jit(solution)/shard_map/ppermute | solution.py:47
  418.6 6.7 %collective-permute-start.58 = (bf16[128,256]{1,0:T(8,128)(2,1)S(1)}, bf16[128,256]{1,0:T(8,128)(2,1)S(1)}, u32[]{:S(2)}, u32[]{:S(2)}) collective-permute-start(bf16[128,256]{1,0:T(8,128)(2,1)S(1)} %slice.254), channel_id=1, source_target_pairs={{0,2},{1,3},{2,0},{3,1},{4,6},{5,7},{6,4},{7,5},{8,10},{9,11},{10,... | collective-permute-start | bytes 196616 | tf_op jit(solution)/shard_map/ppermute | solution.py:51
  (69 other events, 730.0 us)
Sparse Core Ops, SparseCore 0:
  373.7 55.6 all-gather.3

commit v2 on v1

--- a/solution.py
+++ b/solution.py
@@ -73,9 +73,10 @@
 
 
 class Gather:
-    def __init__(self, piece):
+    def __init__(self, piece, turn=1):
         self.n = lax.axis_size("dp")
-        self.perms = ring_perms(self.n)
+        self.perms = ring_perms(self.n)[::turn]
+        self.turn = turn
         self.pieces = [piece] + [None] * (self.n - 1)
         self.up = self.down = piece
         self.done = 0
@@ -84,9 +85,9 @@
         if self.done == self.n // 2:
             return
         self.done += 1
-        self.up = self.pieces[self.n - self.done] = lax.ppermute(after(self.up, *gates), "dp", self.perms[0])
+        self.up = self.pieces[-self.turn * self.done % self.n] = lax.ppermute(after(self.up, *gates), "dp", self.perms[0])
         if self.done <= (self.n - 1) // 2:
-            self.down = self.pieces[self.done] = lax.ppermute(after(self.down, *gates), "dp", self.perms[1])
+            self.down = self.pieces[self.turn * self.done % self.n] = lax.ppermute(after(self.down, *gates), "dp", self.perms[1])
 
     def finish(self):
         while self.done < self.n // 2:
@@ -95,16 +96,17 @@
 
 
 class Reduce:
-    def __init__(self, total, index):
+    def __init__(self, total, index, turn=1):
         self.n = lax.axis_size("dp")
-        self.perms = ring_perms(self.n)
+        self.perms = ring_perms(self.n)[::turn]
+        self.turn = turn
         self.total, self.index = total, index
         self.rows = total.shape[0] // self.n
         self.up = self.down = None
         self.done = 0
 
     def block(self, k):
-        return lax.dynamic_slice_in_dim(self.total, self.index[k % self.n] * self.rows, self.rows, 0)
+        return lax.dynamic_slice_in_dim(self.total, self.index[self.turn * k % self.n] * self.rows, self.rows, 0)
 
     def add(self, x, k):
         if x is None:
@@ -145,30 +147,6 @@
     for k, piece in enumerate(pieces):
         row = pl.multiple_of(index_ref[k] * rows, rows)
         out_ref[pl.ds(row, rows), at : at + cols] = piece[...]
-
-
-def assemble(index, *groups):
-    n = len(groups[0])
-    shapes = [group[0].shape for group in groups]
-    shape = (n * shapes[0][0], sum(cols for _, cols in shapes))
-
-    def kernel(index_ref, *refs):
-        at = 0
-        for k, (_, cols) in enumerate(shapes):
-            assemble_kernel(index_ref, refs[k * n : (k + 1) * n], refs[-1], at)
-            at += cols
-
-    return pl.pallas_call(
-        kernel,
-        out_shape=jax.ShapeDtypeStruct(shape, BF),
-        grid=(1,),
-        in_specs=[pl.BlockSpec(memory_space=pltpu.SMEM)]
-        + [whole(piece.shape) for group in groups for piece in group],
-        out_specs=whole(shape),
-        compiler_params=pltpu.CompilerParams(vmem_limit_bytes=16 * MIB),
-        cost_estimate=cost(0, 4 * shape[0] * shape[1]),
-        name="assemble",
-    )(index, *[piece for group in groups for piece in group])
 
 
 def split3(x):
@@ -381,8 +359,6 @@
     o1_ref,
     tokens_ref,
     cot_ref,
-    first_own_ref,
-    first_sib_ref,
     late_own_ref,
     late_sib_ref,
     row_ref,
@@ -390,14 +366,13 @@
     *refs,
     chunk,
 ):
-    (resid_ref, n2_ref, g_ref, du_ref, da_ref, dr_ref, mlp_ref, do_ref, sum_ref,
-     up_sum_ref, out_w) = refs[-11:]
+    (*mlp_refs, resid_ref, send_ref, g_ref, du_ref, da_ref, do_ref, sum_ref, up_sum_ref, out_w) = refs
     step = pl.program_id(0)
     tile, depth = tokens_ref.shape
 
     @pl.when(step == 0)
     def _():
-        for k, ref in enumerate((first_own_ref, first_sib_ref)):
+        for k, ref in enumerate((late_own_ref, late_sib_ref)):
             for chip in range(2):
                 for pair in range(2):
                     at = (pair * 4 + (scalar_ref[3] ^ (k + 2 * chip))) * 128
@@ -409,21 +384,20 @@
     heads = jnp.concatenate([ref[j] for ref in (o0_ref, o1_ref) for j in range(4)], axis=1)
     branch = dot(heads, out_w[...], NT) + row_ref[2:3, :]
     resid = tokens_ref[...].astype(F32) + branch
-    resid_ref[...] = resid
+    resid_ref[...] = resid.astype(BF)
     at = lax.broadcasted_iota(jnp.int32, (tile, 1), 0) + (
         scalar_ref[0] * scalar_ref[1] + (chunk * pl.num_programs(0) + step) * tile
     )
     valid = (at < scalar_ref[2]).astype(F32)
     unit, scale = norm_parts(resid)
     n2 = (unit * row_ref[3:4, :] + row_ref[4:5, :]).astype(BF)
-    n2_ref[...] = n2
+    send_ref[:, :depth] = n2
     cot = cot_ref[...]
     dm = cot.astype(BF)
     mlp = None
-    hid = late_own_ref.shape[1] // 2
+    hid = (late_own_ref.shape[1] - 512) // 2
     for half, late in enumerate((late_own_ref, late_sib_ref)):
-        up, down = late.at[:, :hid], late.at[:, hid:]
-        cols = slice(half * hid, (half + 1) * hid)
+        up, down = late.at[:, 512 : 512 + hid], late.at[:, 512 + hid :]
         u = dot(n2, up[...]) + bias_ref[half : half + 1, :]
         square = u * u
         t = jnp.tanh(gelu_scale * (u + gelu_cubic * square * u))
@@ -431,15 +405,29 @@
         g = (u * plus).astype(BF)
         slope = plus + (0.5 * gelu_scale) * u * (1.0 - t * t) * (1.0 + 3.0 * gelu_cubic * square)
         du_wide = (dot(dm, down[...]) * slope).astype(BF)
-        g_ref[:, cols] = g
-        du_ref[:, cols] = du_wide
+        if half == 0:
+            g_ref[...] = g
+            du_ref[...] = du_wide
+        else:
+            send_ref[:, depth : depth + hid] = g
+            send_ref[:, depth + hid :] = du_wide
         up_sum_ref[half : half + 1, :] += jnp.sum(du_wide.astype(F32), axis=0, keepdims=True)
         m = dot(g, down[...], NT)
         d = dot(du_wide, up[...], NT)
         mlp, dn2 = (m, d) if mlp is None else (mlp + m, dn2 + d)
-    mlp_ref[...] = mlp.astype(BF)
+    mlp = mlp.astype(BF)
+    start = 0
+    for ref in mlp_refs:
+        stop = start + ref.shape[0]
+        for k in range(start // tile, (stop - 1) // tile + 1):
+            low, high = max(start, k * tile), min(stop, (k + 1) * tile)
+
+            @pl.when(step == k)
+            def _(ref=ref, at=low - start, low=low - k * tile, size=high - low):
+                ref[at : at + size, :] = mlp[low : low + size, :]
+
+        start = stop
     dr = norm_back(dn2, unit, scale, row_ref[3:4, :]) + 0.5 * cot
-    dr_ref[...] = dr
     da = dr.astype(BF)
     da_ref[...] = da
     do = dot(da, out_w[...]).astype(BF)
@@ -451,24 +439,22 @@
         sum_ref[k : k + 1, :] += jnp.sum(x, axis=0, keepdims=True)
 
 
-def middle(chunk, chunks, scalars, heads_in, tokens, cotangent, weights, row_vectors, up_bias, before):
+def middle(scalars, heads_in, tokens, cotangent, weights, row_vectors, up_bias, pieces):
     depth = tokens.shape[1]
     half = tokens.shape[0] // 2
     tile = 256
-    steps = half // chunks // tile
-    hidden = weights[2].shape[1]
+    chunk, chunks = 0, 1
+    steps = half // tile
+    hidden = weights[0].shape[1] - 512
     own = lambda i, s: (chunk * steps + i, 0)
     absolute = lambda i, s: (s[0] * (half // tile) + chunk * steps + i, 0)
     part = lambda i, s: (i, 0)
-    kept = [(depth, F32), (depth, BF), (hidden, BF), (hidden, BF), (depth, BF), (depth, F32)]
-    n_in = 10
+    parts = [(depth, BF), (depth + hidden, BF), (hidden // 2, BF), (hidden // 2, BF), (depth, BF)]
     return pl.pallas_call(
         functools.partial(middle_kernel, chunk=chunk),
-        out_shape=[jax.ShapeDtypeStruct((half, w), t) for w, t in kept]
-        + [
-            jax.ShapeDtypeStruct((half // chunks, depth), BF),
-            jax.ShapeDtypeStruct((4, half // chunks, 256), BF),
-        ]
+        out_shape=[jax.ShapeDtypeStruct((rows, depth), BF) for rows in pieces]
+        + [jax.ShapeDtypeStruct((half // chunks, w), t) for w, t in parts]
+        + [jax.ShapeDtypeStruct((4, half // chunks, 256), BF)]
         + [jax.ShapeDtypeStruct((8, depth), F32), jax.ShapeDtypeStruct((2, hidden // 2), F32)],
         grid_spec=pltpu.PrefetchScalarGridSpec(
             num_scalar_prefetch=1,
@@ -476,29 +462,28 @@
             in_specs=[pl.BlockSpec((4, tile, 128), lambda i, s: (0, *own(i, s)))] * 2
             + [pl.BlockSpec((tile, depth), absolute)] * 2
             + [whole(w.shape) for w in weights]
-            + [whole(row_vectors.shape), whole(up_bias.shape)]
-            + [pl.BlockSpec(memory_space=pl.ANY)] * len(before),
-            out_specs=[pl.BlockSpec((tile, w), own) for w, _ in kept]
-            + [
-                pl.BlockSpec((tile, depth), part),
-                pl.BlockSpec((4, tile, 256), lambda i, s: (0, i, 0)),
-            ]
+            + [whole(row_vectors.shape), whole(up_bias.shape)],
+            out_specs=[whole((rows, depth)) for rows in pieces]
+            + [pl.BlockSpec((tile, w), part) for w, _ in parts]
+            + [pl.BlockSpec((4, tile, 256), lambda i, s: (0, i, 0))]
             + [whole((8, depth)), whole((2, hidden // 2))],
             scratch_shapes=[
                 pltpu.VMEM((depth, 1024), BF),
             ],
         ),
-        input_output_aliases={n_in + 1 + k: k for k in range(len(before))},
         compiler_params=pltpu.CompilerParams(vmem_limit_bytes=56 * MIB),
         cost_estimate=cost(21e9 / chunks, 24 * MIB),
         name="middle",
-    )(scalars, *heads_in, tokens, cotangent, *weights, row_vectors, up_bias, *before)
+    )(scalars, *heads_in, tokens, cotangent, *weights, row_vectors, up_bias)
 
 
 def last_kernel(
-    scalar_ref, o0_ref, o1_ref, s0_ref, s1_ref, w_own_ref, w_sib_ref, tokens_ref, dr_ref, row_ref, ig_ref, sum_ref,
+    scalar_ref, o0_ref, o1_ref, s0_ref, s1_ref, w_own_ref, w_sib_ref, tokens_ref, *refs
 ):
-    @pl.when(pl.program_id(0) == 0)
+    da_ref, row_ref, *ig_refs, sum_ref = refs
+    step = pl.program_id(0)
+
+    @pl.when(step == 0)
     def _():
         sum_ref[...] = jnp.zeros_like(sum_ref)
 
@@ -507,124 +492,218 @@
 
     dn1 = dot(side(o0_ref, o1_ref), w_own_ref[...], NT) + dot(side(s0_ref, s1_ref), w_sib_ref[...], NT)
     unit, scale = norm_parts(tokens_ref[...].astype(F32))
-    ig_ref[...] = (dr_ref[...] + norm_back(dn1, unit, scale, row_ref[0:1, :])).astype(BF)
+    ig = (da_ref[...].astype(F32) + norm_back(dn1, unit, scale, row_ref[0:1, :])).astype(BF)
+    for k, ref in enumerate(ig_refs):
+
+        @pl.when(step == k)
+        def _(ref=ref):
+            ref[...] = ig
+
     sum_ref[0:1, :] += jnp.sum(dn1 * unit, axis=0, keepdims=True)
     sum_ref[1:2, :] += jnp.sum(dn1, axis=0, keepdims=True)
 
 
-def last(chunk, chunks, scalars, own, sibling, w_own, w_sib, tokens, dr, row_vectors):
+def last(scalars, own, sibling, w_own, w_sib, tokens, da, row_vectors):
     depth = tokens.shape[1]
     half = tokens.shape[0] // 2
-    tile = 256
-    steps = half // chunks // tile
-    absolute = lambda i, s: (s[0] * (half // tile) + chunk * steps + i, 0)
+    steps = 4
+    tile = half // steps
+    absolute = lambda i, s: (s[0] * steps + i, 0)
     return pl.pallas_call(
         last_kernel,
-        out_shape=[
-            jax.ShapeDtypeStruct((half // chunks, depth), BF),
-            jax.ShapeDtypeStruct((8, depth), F32),
-        ],
+        out_shape=[jax.ShapeDtypeStruct((tile, depth), BF)] * steps + [jax.ShapeDtypeStruct((8, depth), F32)],
         grid_spec=pltpu.PrefetchScalarGridSpec(
             num_scalar_prefetch=1,
             grid=(steps,),
-            in_specs=[pl.BlockSpec((3, tile, 128), lambda i, s: (0,) + absolute(i, s))] * 2
-            + [pl.BlockSpec((3, tile, 128), lambda i, s: (0, chunk * steps + i, 0))] * 2
-            + [whole(w_own.shape), whole(w_sib.shape)]
-            + [
-                pl.BlockSpec((tile, depth), absolute),
-                pl.BlockSpec((tile, depth), lambda i, s: (chunk * steps + i, 0)),
-                whole(row_vectors.shape),
+            in_specs=[pl.BlockSpec((3, tile, 128), lambda i, s: (0, *absolute(i, s)))] * 2
+            + [pl.BlockSpec((3, tile, 128), lambda i, s: (0, i, 0))] * 2
+            + [whole(w_own.shape), whole(w_sib.shape), pl.BlockSpec((tile, depth), absolute)]
+            + [pl.BlockSpec((tile, depth), lambda i, s: (i, 0))]
+            + [whole(row_vectors.shape)],
+            out_specs=[
+                *[whole((tile, depth))] * steps,
+                whole((8, depth)),
             ],
-            out_specs=[pl.BlockSpec((tile, depth), lambda i, s: (i, 0)), whole((8, depth))],
         ),
         compiler_params=pltpu.CompilerParams(vmem_limit_bytes=40 * MIB),
-        cost_estimate=cost(3.2e9 / chunks, 10 * MIB),
+        cost_estimate=cost(3.2e9, 20 * MIB),
         name="last",
-    )(scalars, *own, *sibling, w_own, w_sib, tokens, dr, row_vectors)
-
-
-def weight_grads_kernel(half_ref, n2_ref, cot_ref, da_ref, du_ref, g_ref, a0_ref, a1_ref, b0_ref, b1_ref, *refs):
-    out_ref = refs[-1]
-    o_refs = [r.at[0] for r in (a0_ref, a1_ref, b0_ref, b1_ref)]
-    hidden = du_ref.shape[1]
-    parts = [
-        (n2_ref[...], [du_ref]),
-        (cot_ref[...].astype(BF), [g_ref]),
-        (da_ref[...], o_refs),
+    )(scalars, *own, *sibling, w_own, w_sib, tokens, da, row_vectors)
+
+
+def out_grads_kernel(*refs, chunks):
+    das, heads, out_ref = refs[1 : 1 + chunks], refs[1 + chunks : -1], refs[-1]
+    out_ref[...] = sum_over_chunks(das, heads).astype(BF)
+
+
+def sum_over_chunks(das, heads):
+    rows = das[0].shape[0]
+    total = 0.0
+    for c, da in enumerate(das):
+        right = jnp.concatenate([h[0, c * rows : (c + 1) * rows, :] for h in heads], axis=1)
+        total = total + dot(da[...], right, TN)
+    return total
+
+
+def head_specs(half, side):
+    return [
+        pl.BlockSpec((1, half, 128), lambda i, s, flip=flip: (s[3] ^ flip, 0, 0), pipeline_mode=pl.Buffered(1))
+        for flip in (side, side, side + 2, side + 2)
     ]
-    at = 0
-    for left, rights in parts:
-        right = jnp.concatenate([r[...] for r in rights], axis=1) if len(rights) > 1 else rights[0][...]
-        cols = slice(at, at + right.shape[1])
-        at += right.shape[1]
-        value = dot(left, right, TN)
-        if len(refs) > 1:
-            value = value + refs[0][:, cols].astype(F32)
-        out_ref[:, cols] = value.astype(BF)
-
-
-def weight_grads(side, scalars, n2, cotangent, da, du, g, heads_in, more=()):
-    half, depth = n2.shape
-    hidden = du.shape[1] // 2
-    cols = 2 * hidden + 4 * 128
+
+
+def out_grads(scalars, das, heads_in):
+    rows, depth = das[0].shape
     tile = 256
-    left = pl.BlockSpec((half, tile), lambda i, s: (0, i))
-    right = lambda w: pl.BlockSpec((half, w), lambda i, s: (0, side), pipeline_mode=pl.Buffered(1))
-    rows = pl.BlockSpec((tile, cols), lambda i, s: (i, 0))
     return pl.pallas_call(
-        weight_grads_kernel,
-        out_shape=jax.ShapeDtypeStruct((depth, cols), BF),
+        functools.partial(out_grads_kernel, chunks=len(das)),
+        out_shape=jax.ShapeDtypeStruct((depth, 512), BF),
         grid_spec=pltpu.PrefetchScalarGridSpec(
             num_scalar_prefetch=1,
             grid=(depth // tile,),
-            in_specs=[left, pl.BlockSpec((half, tile), lambda i, s: (s[0], i)), left]
-            + [right(hidden), right(hidden)]
-            + [
-                pl.BlockSpec((1, half, 128), lambda i, s, flip=flip: (s[3] ^ flip, 0, 0), pipeline_mode=pl.Buffered(1))
-                for flip in (side, side, side + 2, side + 2)
-            ]
-            + [rows] * len(more),
-            out_specs=rows,
+            in_specs=[pl.BlockSpec((rows, tile), lambda i, s: (0, i))] * len(das)
+            + head_specs(rows * len(das), 1),
+            out_specs=pl.BlockSpec((tile, 512), lambda i, s: (i, 0)),
+        ),
+        compiler_params=pltpu.CompilerParams(vmem_limit_bytes=24 * MIB),
+        name="out_grads",
+    )(scalars, *das, *heads_in, *heads_in)
+
+
+def weight_grads_kernel(scalar_ref, cot_ref, *refs, chunks):
+    *refs, out_ref = refs
+    groups = [refs[3 * k : 3 * k + 3] for k in range(2 * chunks)]
+    das, heads, got_ref = refs[6 * chunks : 7 * chunks], refs[7 * chunks : -1], refs[-1]
+    rows = groups[0][0].shape[0]
+    up = down = 0.0
+    for k, (n2, g, du) in enumerate(groups):
+        side = scalar_ref[0] if k < chunks else 1 - scalar_ref[0]
+        at = pl.multiple_of((side * chunks + k % chunks) * rows, rows)
+        up = up + dot(n2[...], du[...], TN)
+        down = down + dot(cot_ref[pl.ds(at, rows), :].astype(BF), g[...], TN)
+    hidden = up.shape[1]
+    out_ref[:, :hidden] = up.astype(BF)
+    out_ref[:, hidden : 2 * hidden] = down.astype(BF)
+    out_ref[:, 2 * hidden :] = (sum_over_chunks(das, heads) + got_ref[...].astype(F32)).astype(BF)
+
+
+def weight_grads(scalars, cotangent, own, got, das, heads_in, got_out):
+    span, depth = cotangent.shape
+    chunks = len(own)
+    rows, hidden = own[0][1].shape
+    tile = 256
+    block = lambda r, at: pl.BlockSpec((r, tile), lambda i, s: (0, i))
+    fixed = lambda at: pl.BlockSpec((rows, hidden), lambda i, s: (0, at), pipeline_mode=pl.Buffered(1))
+    at = depth // hidden
+    specs = ([block(rows, 0), fixed(0), fixed(0)] * chunks) + ([block(rows, 0), fixed(at), fixed(at + 1)] * chunks)
+    return pl.pallas_call(
+        functools.partial(weight_grads_kernel, chunks=chunks),
+        out_shape=jax.ShapeDtypeStruct((depth, 2 * hidden + 512), BF),
+        grid_spec=pltpu.PrefetchScalarGridSpec(
+            num_scalar_prefetch=1,
+            grid=(depth // tile,),
+            in_specs=[block(span, 0)]
+            + specs
+            + [block(rows, 0)] * chunks
+            + head_specs(rows * chunks, 0)
+            + [pl.BlockSpec((tile, 512), lambda i, s: (i, 0))],
+            out_specs=pl.BlockSpec((tile, 2 * hidden + 512), lambda i, s: (i, 0)),
         ),
         compiler_params=pltpu.CompilerParams(vmem_limit_bytes=50 * MIB),
-        cost_estimate=cost(2 * half * depth * cols, 18 * MIB),
+        cost_estimate=cost(2 * span * depth * (2 * hidden + 256), 30 * MIB),
         name="weight_grads",
-    )(scalars, n2, cotangent, da, du, g, *heads_in, *heads_in, *more)
-
-
-def finish_kernel(half_ref, *refs, steps):
-    out_ref = refs[-1]
-    for k, ref in enumerate(refs[:-1]):
-
-        @pl.when(pl.program_id(0) // steps == k)
-        def _():
-            out_ref[...] = ref[...].astype(F32)
-
-
-def finish(scalars, own, other):
-    chunks = len(own)
-    rows, depth = own[0].shape
+    )(
+        scalars,
+        cotangent,
+        *[x for group in own for x in group],
+        *[x for group in got for x in (group,) * 3],
+        *das,
+        *heads_in,
+        *heads_in,
+        got_out,
+    )
+
+
+def qkv_grads_kernel(n_ref, p0_ref, p1_ref, out_ref):
+    right = jnp.concatenate([p[k] for k in range(3) for p in (p0_ref, p1_ref)], axis=1)
+    out_ref[...] = dot(n_ref[...], right, TN).astype(BF)
+
+
+def qkv_grads(normed, parts):
+    span, depth = normed.shape
+    tile = 256
+    return pl.pallas_call(
+        qkv_grads_kernel,
+        out_shape=jax.ShapeDtypeStruct((depth, 768), BF),
+        grid=(depth // tile,),
+        in_specs=[pl.BlockSpec((span, tile), lambda i: (0, i))] + [whole(p.shape) for p in parts],
+        out_specs=pl.BlockSpec((tile, 768), lambda i: (i, 0)),
+        compiler_params=pltpu.CompilerParams(vmem_limit_bytes=32 * MIB),
+        cost_estimate=cost(2 * span * depth * 768, 10 * MIB),
+        name="qkv_grads",
+    )(normed, *parts)
+
+
+def finish_kernel(scalar_ref, *refs, terms):
+    total = refs[0][...].astype(F32)
+    for ref in refs[1:terms]:
+        total = total + ref[...].astype(F32)
+    refs[-1][...] = total
+
+
+def finish(scalars, side, terms, before=(), piece=0, pieces=1):
+    rows, depth = terms[0].shape
     tile = 256
     steps = rows // tile
-    span = lambda k: pl.BlockSpec((tile, depth), lambda i, s: (jnp.clip(i - k * steps, 0, steps - 1), 0))
-
-    def out_index(i, s):
-        first = i < chunks * steps
-        return (jnp.where(first, s[0], 1 - s[0]) * chunks * steps + i - jnp.where(first, 0, chunks * steps), 0)
-
-    return pl.pallas_call(
-        functools.partial(finish_kernel, steps=steps),
-        out_shape=jax.ShapeDtypeStruct((2 * chunks * rows, depth), F32),
+    out = pl.pallas_call(
+        functools.partial(finish_kernel, terms=len(terms)),
+        out_shape=[jax.ShapeDtypeStruct((2 * pieces * rows, depth), F32)],
         grid_spec=pltpu.PrefetchScalarGridSpec(
             num_scalar_prefetch=1,
-            grid=(2 * chunks * steps,),
-            in_specs=[span(k) for k in range(2 * chunks)],
-            out_specs=pl.BlockSpec((tile, depth), out_index),
+            grid=(steps,),
+            in_specs=[pl.BlockSpec((tile, depth), lambda i, s: (i, 0))] * len(terms)
+            + [pl.BlockSpec(memory_space=pl.ANY)] * len(before),
+            out_specs=[pl.BlockSpec((tile, depth), lambda i, s: (((s[0] ^ side) * pieces + piece) * steps + i, 0))],
         ),
+        input_output_aliases={1 + len(terms): 0} if before else {},
         compiler_params=pltpu.CompilerParams(vmem_limit_bytes=24 * MIB),
-        cost_estimate=cost(0, 12 * chunks * rows * depth),
+        cost_estimate=cost(0, 8 * rows * depth),
         name="finish",
-    )(scalars, *own, *other)
+    )(scalars, *terms, *before)
+    return out[0]
+
+
+def adam_rows_kernel(g_ref, w_ref, m_ref, v_ref, nm_ref, nv_ref, nw_ref):
+    kinds, width = w_ref.shape[1:]
+    for k in range(kinds):
+        grad = g_ref[:, k * width : (k + 1) * width]
+        new = adamw(w_ref[:, k, :], m_ref[:, k, :], v_ref[:, k, :], grad, matrix_rate, weight_decay)
+        nm_ref[:, k, :], nv_ref[:, k, :], nw_ref[:, k, :] = new
+
+
+def adam_turned_kernel(g_ref, w_ref, m_ref, v_ref, nm_ref, nv_ref, nw_ref):
+    new = adamw(w_ref[...], m_ref[...], v_ref[...], g_ref[...].T, matrix_rate, weight_decay)
+    nm_ref[...], nv_ref[...], nw_ref[...] = new
+
+
+def adam(kernel, grad, *state):
+    return pl.pallas_call(
+        kernel,
+        out_shape=[jax.ShapeDtypeStruct(state[0].shape, F32)] * 3,
+        grid=(1,),
+        in_specs=[whole(x.shape) for x in (grad, *state)],
+        out_specs=[whole(state[0].shape)] * 3,
+        compiler_params=pltpu.CompilerParams(vmem_limit_bytes=24 * MIB),
+        cost_estimate=cost(0, 28 * grad.size),
+        name="adam",
+    )(grad, *state)
+
+
+def adam_turned(grad, *state):
+    if grad.shape[0] % 128:
+        return adamw(*state, grad.T.reshape(state[0].shape), matrix_rate, weight_decay)
+    flat = [x.reshape(-1, x.shape[-1]) for x in state]
+    return [x.reshape(state[0].shape) for x in adam(adam_turned_kernel, grad, *flat)]
 
 
 def body(
@@ -667,110 +746,99 @@
     out_piece = out_weight.astype(BF).T
     out_piece = jnp.concatenate([out_piece, to_chip(out_piece)], axis=1)
     qkv_ring = Gather(qkv_weight.astype(BF).reshape(share, 3 * width))
-    out_ring = Gather(out_piece)
-    up_ring = Gather(up_weight.astype(BF).reshape(share, hidden))
-    down_ring = Gather(down_weight.astype(BF).reshape(hidden, share).T)
-    gate = []
-    for _ in range(n_dp // 2):
-        gate.append(qkv_ring.up)
-        qkv_ring.hop()
-        out_ring.hop()
+    up_piece = up_weight.astype(BF).reshape(share, hidden)
+    down_piece = down_weight.astype(BF).reshape(hidden, share).T
+    late_piece = jnp.concatenate([out_piece, up_piece, down_piece], axis=1)
+    late_w = lax.all_gather(late_piece, "dp", axis=0, tiled=True)
     up_bias = col_bias[2:].reshape(1, hidden)
     up_bias = jnp.concatenate([up_bias, to_core(up_bias)], axis=0)
-    up_ring.hop(gate[-1])
-    down_ring.hop(qkv_ring.up)
+    for _ in range(n_dp // 2):
+        qkv_ring.hop()
 
     unit_one, _ = norm_parts(tokens.astype(F32))
     normed = (unit_one * row_vectors[0] + row_vectors[1]).astype(BF)
-    normed = after(normed, out_ring.up, out_ring.down, up_bias)
-    q, k, v, qkv_w = project(normed, index, qkv_ring.finish(), col_bias, slopes, lengths)
+    q, k, v, qkv_w = project(after(normed, up_bias), index, qkv_ring.finish(), col_bias, slopes, lengths)
     outs, heads_in = [], []
     for pair in range(2):
-        ready = (up_ring.up,) if pair == 0 else (up_ring.up, down_ring.up)
-        if pair == 0:
-            up_ring.hop(q)
-        q = after(q, *ready)
         o, qb, send = attend_forward(q, k, v, pair)
         outs.append((o, qb))
-        heads_in.append(to_all(send))
-        down_ring.hop(send)
-        up_ring.hop(send)
+        heads_in.append(to_all(after(send, *heads_in)))
     qkv_sib = to_core(qkv_w)
-    out_w = assemble(index, out_ring.finish())
-    late_w = assemble(index, up_ring.finish(), down_ring.finish())
-    out_sib, late_sib = to_core(out_w), to_core(late_w)
-
-    weights = (out_w, out_sib, late_w, late_sib)
-    chunks = 2
-    before, mlps, partials, sums, up_sums = (), [], [], 0.0, 0.0
-    for chunk in range(chunks):
-        got = middle(
-            chunk,
-            chunks,
-            scalars,
-            heads_in,
-            tokens,
-            cotangent,
-            weights,
-            row_vectors,
-            up_bias,
-            before,
-        )
-        before = got[:6]
-        mlps.append(got[6])
-        partials.append(to_all(got[7]))
-        sums, up_sums = sums + got[8], up_sums + got[9]
-    resid, n2, g, du, da, dr = before
-    mlp_far = [to_chip(after(m, partials[-1])) for m in mlps]
-    grad_args = (scalars, n2, cotangent, da, du, g)
-    other_grads = weight_grads(1, *grad_args, heads_in)
-    got_grads = to_core(other_grads)
+    late_w = after(late_w, heads_in[1])
+    late_sib = to_core(late_w)
+
+    weights = (late_w, after(late_sib, qkv_sib))
+    chunks = 1
+    pieces = [half * 3 // 8, half * 3 // 8, half // 4]
+    *mlps, resid, send, g, du, da, do, sums, up_sums = middle(
+        scalars, heads_in, tokens, cotangent, weights, row_vectors, up_bias, pieces
+    )
+    resids, das = [resid], [da]
+    got_send = to_core(send)
+    got_out = to_core(out_grads(scalars, das, heads_in))
+    partials = [to_all(do)]
+    total = weight_grads(scalars, cotangent, [(send, g, du)], [got_send], das, heads_in, got_out)
+    total = after(total, *partials)
+    mlp_far = [to_chip(after(mlps[0], total))]
+    shard = lax.psum_scatter(total, "dp", scatter_dimension=0, tiled=True)
 
     parts, part_sums, siblings = [], [], []
     for pair in range(2):
         o, qb = outs[pair]
-        d, d_sib, s = attend_backward(scalars, after(qb, other_grads), k, v, o, partials, pair)
+        qb = after(qb, total)
+        d, d_sib, s = attend_backward(scalars, qb, k, v, o, partials, pair)
         parts.append(d)
         part_sums.append(s)
+        d_sib = after(d_sib, mlp_far[pair])
+        if pair == 0:
+            outs[1] = (outs[1][0], after(outs[1][1], mlp_far[0], s))
+        mlp_far.append(to_chip(after(mlps[pair + 1], mlp_far[pair])))
         siblings.append(to_core(d_sib))
-        if pair == 0:
-            total = weight_grads(0, *grad_args, heads_in, (after(got_grads, s),))
-            middle_ring = Reduce(total, index)
-            middle_ring.hop()
-            outs[1] = (outs[1][0], after(outs[1][1], total))
-    middle_ring.hop(part_sums[1])
-    lasts = [
-        last(c, chunks, scalars, parts, siblings, qkv_w, qkv_sib, tokens, dr, row_vectors)
-        for c in range(chunks)
-    ]
-    last_sums = sum(x[1] for x in lasts)
-    last_far = [to_chip(x[0]) for x in lasts]
-    mlp_far = [after(f, lasts[-1][1]) for f in mlp_far]
-    middle_ring.hop(lasts[-1][1])
-
-    qkv_grad = jnp.concatenate([parts[p][kind] for kind in range(3) for p in range(2)], axis=1)
-    qkv_wgrad = dot(normed, after(qkv_grad, lasts[-1][1]), TN).astype(BF)
-    qkv_shard = Reduce(qkv_wgrad, index).finish().reshape(qkv_weight.shape)
-    mid_shard = middle_ring.finish()
-    up_shard = mid_shard[:, :hidden].reshape(up_weight.shape)
-    down_shard = mid_shard[:, hidden : 2 * hidden].T.reshape(down_weight.shape)
-    out_mine = mid_shard[:, 2 * hidden : 2 * hidden + width]
-    out_theirs = to_chip(mid_shard[:, 2 * hidden + width :].astype(BF))
-    out_shard = (out_mine + out_theirs.astype(F32)).T
+    *igs, last_sums = last(scalars, parts, siblings, qkv_w, qkv_sib, tokens, das[0], row_vectors)
+    igs[0] = after(igs[0], mlp_far[2])
+    ig_far = [to_chip(igs[0])]
+
+    qkv_wgrad = after(qkv_grads(after(normed, last_sums), parts), ig_far[0])
+    ig_sib = [to_core(after(x, qkv_wgrad)) for x in igs]
+    qkv_ring = Reduce(qkv_wgrad, index, -1)
+    for hop in range(4):
+        qkv_ring.hop(*ig_far[hop : hop + 1][: 3 - hop])
+        if hop < 3:
+            ig_far.append(to_chip(after(igs[hop + 1], ig_far[hop])))
+    qkv_shard = qkv_ring.finish()
+    up_shard = shard[:, :hidden].astype(F32)
+    down_shard = shard[:, hidden : 2 * hidden].astype(F32)
+    out_mine = shard[:, 2 * hidden : 2 * hidden + width]
+    out_theirs = to_chip(shard[:, 2 * hidden + width :])
+    out_shard = out_mine.astype(F32) + out_theirs.astype(F32)
 
     valid = ((core * half + jnp.arange(half)) < lengths[0]).astype(F32)[:, None]
     stat_out, stat_m, own_low = 0.0, 0.0, []
-    for chunk, (m, f) in enumerate(zip(mlps, mlp_far)):
-        rows = slice(chunk * half // chunks, (chunk + 1) * half // chunks)
-        branch_m = m.astype(F32) + f.astype(F32) + row_vectors[5]
-        outputs_own = resid[rows] + branch_m
+    at = 0
+    for m, f in zip(mlps, mlp_far):
+        rows = slice(at, at + m.shape[0])
+        at += m.shape[0]
+        branch_m = m.astype(F32) + after(f, qkv_wgrad).astype(F32) + row_vectors[5]
+        outputs_own = resid[rows].astype(F32) + branch_m
         stat_out += jnp.sum(valid[rows] * outputs_own * outputs_own)
         stat_m += jnp.sum(valid[rows] * branch_m * branch_m)
-        own_low.append(outputs_own.astype(BF))
-    outputs = finish(scalars, own_low, [to_core(x) for x in own_low])
-
-    summed = [(x[0].astype(F32) + f.astype(F32)).astype(BF) for x, f in zip(lasts, last_far)]
-    input_grad = finish(scalars, summed, [to_core(x) for x in summed])
+        own_low.append(after(outputs_own.astype(BF), ig_far[1]))
+    own_low = jnp.concatenate(own_low, axis=0)
+    outputs = after(finish(scalars, 0, [own_low]), ig_far[2])
+    outputs = finish(scalars, 1, [to_core(own_low)], (outputs,))
+    stat_out, stat_m = after(stat_out, ig_far[1]), after(stat_m, ig_far[1])
+    qkv_new = adam(adam_rows_kernel, qkv_shard, qkv_weight, qkv_first, qkv_second)
+    out_new = adam_turned(out_shard, out_weight, out_first, out_second)
+    up_new = adam(adam_rows_kernel, up_shard, up_weight, up_first, up_second)
+    down_new = adam_turned(down_shard, down_weight, down_first, down_second)
+    input_grad = ()
+    for k in range(4):
+        if k == 2:
+            input_grad = (after(input_grad[0], ig_far[3]),)
+            ig_far[3] = after(ig_far[3], up_new[0], down_new[0], outputs)
+        input_grad = (finish(scalars, 0, [igs[k], ig_far[k]], input_grad, k, 4),)
+        input_grad = (finish(scalars, 1, [ig_sib[k], to_core(ig_far[k])], input_grad, k, 4),)
+    input_grad = input_grad[0]
 
     stats = jnp.stack([stat_out, jnp.sum(sums[4]), stat_m, jnp.sum(valid)])
     small = jnp.concatenate(
@@ -788,22 +856,23 @@
         ],
         axis=0,
     )
-    every = lax.all_gather(small, ("dp", "mp"), axis=0, tiled=False)
-    every = every.reshape(n_dp, -1, *small.shape)
-    row_stat = jnp.sum(every[:, :, :7], axis=(0, 1))
-    row_total, stat_total = row_stat[:6], row_stat[6]
-    col_all = jnp.sum(every[:, :, 7:], axis=0)
-    mine = lax.dynamic_index_in_dim(col_all, device, 0, keepdims=False)
-    theirs = lax.dynamic_index_in_dim(col_all, device ^ 1, 0, keepdims=False)
+    rows, columns = small[:7], small[7:9]
+    other = to_core(small)
+    rows = rows + other[:7]
+    columns = jnp.concatenate([columns[:1], columns[1:] + other[9:]], axis=0)
+    small = jnp.concatenate([rows, columns], axis=0)
+    step = 1
+    while step < n_dp:
+        small = small + lax.ppermute(small, "dp", [(i, i ^ step) for i in range(n_dp)])
+        step *= 2
+    rows = small[:7] + to_chip(after(small[:7], ig_far[3]))
+    small = jnp.concatenate([rows, small[7:]], axis=0)
+    row_total, stat_total = small[:6], small[6]
     col_total = jnp.concatenate(
-        [mine[0, : 2 * width].reshape(2, width), (mine[1] + theirs[2]).reshape(-1, width)], axis=0
+        [small[7, : 2 * width].reshape(2, width), small[8].reshape(-1, width)], axis=0
     )
     rms_stats = jnp.sqrt(stat_total[:3] / (stat_total[3] * depth))
 
-    qkv_new = adamw(qkv_weight, qkv_first, qkv_second, qkv_shard, matrix_rate, weight_decay)
-    out_new = adamw(out_weight, out_first, out_second, out_shard, matrix_rate, weight_decay)
-    up_new = adamw(up_weight, up_first, up_second, up_shard, matrix_rate, weight_decay)
-    down_new = adamw(down_weight, down_first, down_second, down_shard, matrix_rate, weight_decay)
     row_new = adamw(row_vectors, row_first, row_second, row_total, vector_rate, 0.0)
     col_new = adamw(col_bias, col_first, col_second, col_total, vector_rate, 0.0)
     return (

time: 456 us -> 396 us (0.87)
  waiting for transfers between devices: 82.5 us -> 58.9 us
  starting transfers between devices: 71.2 us -> 51.9 us
  other arithmetic: 42.9 us -> 30.8 us
  Pallas kernels: 160 us -> 170 us
  local copies, waits for them, and re-layouts: 44.2 us -> 35.7 us
  matrix products: 5.74 us -> 0 us
    all_to_all x3 -> x2, waiting for transfers between devices: 30.8 us -> 11.3 us  [to_all(): return lax.all_to_all(x, 'mp', split_axis=0, concat_axis=0, tiled=True)]
    pallas_call x8 -> x18, Pallas kernels: 53.1 us -> 71.8 us  [the longest x10 28.9 us: finish(): pl.pallas_call(functools.partial(finish_kernel, terms=len(terms)), out_sh...]
    ppermute x11 -> x17, waiting for transfers between devices: 0.03 us -> 10.4 us  [to_core(): lax.ppermute(x, 'mp', [(i, i ^ 1) for i in range(lax.axis_size('mp'))])]
    ppermute x16 -> x4, starting transfers between devices: 27 us -> 17.5 us  [hop(): lax.ppermute(after(self.up, *gates), 'dp', self.perms[0])]
    ppermute x8 -> x4, starting transfers between devices: 12.7 us -> 3.33 us  [hop(): self.up = lax.ppermute(up, 'dp', self.perms[0])]
    pallas_call x2 -> x1, Pallas kernels: 45 us -> 35.9 us  [middle(): pl.pallas_call(functools.partial(middle_kernel, chunk=chunk), out_shape=[...]
    ppermute x8 -> x4, waiting for transfers between devices: 15.7 us -> 7.68 us  [hop(): self.up = lax.ppermute(up, 'dp', self.perms[0])]
    ppermute x16 -> x4, waiting for transfers between devices: 14.7 us -> 8.64 us  [hop(): lax.ppermute(after(self.up, *gates), 'dp', self.perms[0])]
  transfers between devices with their start and end apart: 63 -> 48, of which waited for: 17 -> 16; matrix products, arithmetic and copies ran while one was open for 15% -> 11% of each run, Pallas kernels for 22% -> 34%
where the time goes in v2:
time: 396 us; the launch traced here: 391 us
  Pallas kernels  170 us (43%)
  waiting for transfers between devices  58.9 us (15%)
  starting transfers between devices  51.9 us (13%)
  local copies, waits for them, and re-layouts  35.7 us (9%)
  other arithmetic  30.8 us (8%)
  between operations  25.6 us (6%)
  blocking collectives  17.8 us (4%)
    pallas_call x1, Pallas kernels, middle(): pl.pallas_call(functools.partial(middle_kernel, chunk=chunk), out_shape=[...  35.9 us
    pallas_call x2, Pallas kernels, attend_backward(): pl.pallas_call(functools.partial(attend_backward_kernel, bk=min(256, span...  33.1 us
    unnamed x137, local copies, waits for them, and re-layouts  29.3 us
    pallas_call x10, Pallas kernels, finish(): pl.pallas_call(functools.partial(finish_kernel, terms=len(terms)), out_sh...  28.9 us
    pallas_call x2, Pallas kernels, attend_forward(): pl.pallas_call(functools.partial(attend_forward_kernel, bq=min(512, span)...  21.1 us
    all_to_all x1, blocking collectives, to_all(): return lax.all_to_all(x, 'mp', split_axis=0, concat_axis=0, tiled=True)  17.8 us
    pallas_call x1, Pallas kernels, weight_grads(): pl.pallas_call(functools.partial(weight_grads_kernel, chunks=chunks), out...  17.5 us
    ppermute x4, starting transfers between devices, hop(): lax.ppermute(after(self.up, *gates), 'dp', self.perms[0])  17.5 us
  transfers between devices with their start and end apart: 48, of which 16 were waited for; matrix products, arithmetic and copies ran while one was open for 11% of the time, Pallas kernels for 34%

profile of v2, /device:TPU:0, one launch (start us, length us, event | category | flops | bytes accessed | tf_op | source)
XLA Modules:
  0.0 391.0 jit_solution(16559624779892994292)
XLA Ops:
  8.2 3.0 collective-permute-start.8
  15.0 1.9 collective-permute-start.4
  17.2 3.0 convert_reduce_fusion
  21.1 1.4 fusion.2
  22.5 1.9 collective-permute-start.5
  24.4 3.0 fusion.5.n_ref
  28.1 5.2 %collective-permute-done.5.refs_6_ = bf16[128,768]{1,0:T(8,128)(2,1)S(1)} collective-permute-done((bf16[128,768]{1,0:T(8,128)(2,1)S(1)}, bf16[128,768]{1,0:T(8,128)(2,1)S(1)}, u32[]{:S(2)}, u32[]{:S(2)}) %collective-permute-start.5) | collective-permute-done | bytes 196640 | tf_op jit(solution)/shard_map/ppermute | solution.py:88
  33.3 4.7 %collective-permute-start.6 = (bf16[128,768]{1,0:T(8,128)(2,1)S(1)}, bf16[128,768]{1,0:T(8,128)(2,1)S(1)}, u32[]{:S(2)}, u32[]{:S(2)}) collective-permute-start(bf16[128,768]{1,0:T(8,128)(2,1)S(1)} %collective-permute-done.5.refs_6_), channel_id=1, source_target_pairs={{0,8},{8,16},{16,24},{24,28},{28,20},{20,12},{12,4},{4,0},{1,9},{9... | collective-permute-start | bytes 589832 | tf_op jit(solution)/shard_map/ppermute | solution.py:88
  38.7 5.6 %collective-permute-done.2.refs_2_ = bf16[128,768]{1,0:T(8,128)(2,1)S(1)} collective-permute-done((bf16[128,768]{1,0:T(8,128)(2,1)S(1)}, bf16[128,768]{1,0:T(8,128)(2,1)S(1)}, u32[]{:S(2)}, u32[]{:S(2)}) %collective-permute-start.2) | collective-permute-done | bytes 196640 | tf_op jit(solution)/shard_map/ppermute | solution.py:90
  44.2 2.1 collective-permute-done.6.refs_5_
  46.4 8.9 %collective-permute-start.7 = (bf16[128,768]{1,0:T(8,128)(2,1)S(1)}, bf16[128,768]{1,0:T(8,128)(2,1)S(1)}, u32[]{:S(2)}, u32[]{:S(2)}) collective-permute-start(bf16[128,768]{1,0:T(8,128)(2,1)S(1)} %collective-permute-done.6.refs_5_), channel_id=1, source_target_pairs={{0,8},{8,16},{16,24},{24,28},{28,20},{20,12},{12,4},{4,0},{1,9},{9... | collective-permute-start | bytes 589832 | tf_op jit(solution)/shard_map/ppermute | solution.py:88
  57.2 1.4 collective-permute-done.7.refs_4_
  58.6 2.2 copy-done.6
  60.8 8.4 %project.1 = (bf16[4,2048,128]{2,1,0:T(8,128)(2,1)S(1)}, bf16[4,2048,128]{2,1,0:T(8,128)(2,1)S(1)}, bf16[4,2048,128]{2,1,0:T(8,128)(2,1)S(1)}, bf16[1024,768]{1,0:T(8,128)(2,1)}) custom-call(s32[8]{0:T(128)S(1)} %gather_fusion, f32[4]{0:T(128)S(1)} %multiply_exponential_fusion.slope_ref, s32[1]{0:T(128)} %copy.86.length_ref, ...), custom_call_target="tpu_custom_call" | custom-call | flops 3221225472 | bytes 12582912 | tf_op jit(solution)/shard_map/project/pallas_call | solution.py:202
  70.5 1.4 copy-done.29
  71.8 1.3 copy-done.30
  73.2 11.0 %attend_forward.2 = (bf16[2048,128]{1,0:T(8,128)(2,1)S(1)}, bf16[2,2048,128]{2,1,0:T(8,128)(2,1)S(1)}, bf16[4,1024,128]{2,1,0:T(8,128)(2,1)}) custom-call(bf16[4,2048,128]{2,1,0:T(8,128)(2,1)} %copy-done.30, bf16[4,2048,128]{2,1,0:T(8,128)(2,1)} %copy-done.28, bf16[4,2048,128]{2,1,0:T(8,128)(2,1)} %copy-done.29), custom_call_target="tpu_custom_call" | custom-call | flops 12000000000 | bytes 5242880 | tf_op jit(solution)/shard_map/attend_forward/pallas_call | solution.py:252
  86.0 3.7 all-to-all-start
  89.7 10.0 %attend_forward.3 = (bf16[2048,128]{1,0:T(8,128)(2,1)S(1)}, bf16[2,2048,128]{2,1,0:T(8,128)(2,1)S(1)}, bf16[4,1024,128]{2,1,0:T(8,128)(2,1)S(1)}) custom-call(bf16[4,2048,128]{2,1,0:T(8,128)(2,1)} %copy-done.30, bf16[4,2048,128]{2,1,0:T(8,128)(2,1)} %copy-done.28, bf16[4,2048,128]{2,1,0:T(8,128)(2,1)} %copy-done.29), custom_call_target="tpu_custom_call" | custom-call | flops 12000000000 | bytes 5242880 | tf_op jit(solution)/shard_map/attend_forward/pallas_call | solution.py:252
  100.7 3.4 all-to-all-done.o0_ref.refs_2_.refs_4_.refs_7_.refs_9_
  104.1 17.8 %all_to_all.15.o1_ref.refs_3_.refs_5_.refs_8_.refs_10_ = bf16[4,1024,128]{2,1,0:T(8,128)(2,1)} all-to-all(bf16[4,1024,128]{2,1,0:T(8,128)(2,1)S(1)} %get-tuple-element.112), channel_id=1, replica_groups=mesh['dp'=8,'mp'=4] {'mp'}, dimensions={0} | all-to-all | bytes 2097152 | tf_op jit(solution)/shard_map/all_to_all | solution.py:55
  123.0 10.1 %collective-permute-done.10.w_sib_ref = bf16[1024,768]{1,0:T(8,128)(2,1)} collective-permute-done((bf16[1024,768]{1,0:T(8,128)(2,1)}, bf16[1024,768]{1,0:T(8,128)(2,1)}, u32[]{:S(2)}, u32[]{:S(2)}) %collective-permute-start.10) | collective-permute-done | bytes 1572896 | tf_op jit(solution)/shard_map/ppermute | solution.py:47
  133.1 35.9 %middle.1 = (bf16[384,1024]{1,0:T(8,128)(2,1)}, bf16[384,1024]{1,0:T(8,128)(2,1)}, bf16[256,1024]{1,0:T(8,128)(2,1)}, bf16[1024,1024]{1,0:T(8,128)(2,1)}, bf16[1...) custom-call(s32[4]{0:T(128)} %pad_add_fusion.scalar_ref.refs_0_.half, ...), custom_call_target="tpu_custom_call" | custom-call | flops 20999999488 | bytes 25165824 | tf_op jit(solution)/shard_map/middle/pallas_call | solution.py:453
  170.5 1.6 copy-done.4
  172.1 3.6 out_grads.1
  176.1 4.6 %all-to-all-start.2 = ((bf16[4,1024,256]{2,1,0:T(8,128)(2,1)}), bf16[4,1024,256]{2,1,0:T(8,128)(2,1)}, u32[]{:S(2)}, u32[]{:S(2)}) async-start(bf16[4,1024,256]{2,1,0:T(8,128)(2,1)} %get-tuple-element.122), calls=%async_computation.2 | async-start | bytes 4194304 | tf_op jit(solution)/shard_map/all_to_all | solution.py:55
  181.0 17.5 %weight_grads.1 = bf16[1024,2560]{1,0:T(8,128)(2,1)} custom-call(s32[4]{0:T(128)S(1)} %copy-done.26, f32[2048,1024]{1,0:T(8,128)} %cot_ref.3, bf16[1024,3072]{1,0:T(8,128)(2,1)} %get-tuple-element.118.refs_0_, bf16[1024,1024]{1,0:T(8,128)(2,1)} %get-tuple-element.119.refs_1_, bf16[1024,1024]{1,0:T(8,128)(2,1)} %get-tuple-element.120.refs_2_, ...), custom_call_target="tpu_custom_call" | custom-call | flops 9663676416 | bytes 31457280 | tf_op jit(solution)/shard_map/weight_grads/pallas_call | solution.py:599
  198.5 7.9 %all-to-all-done.2.refs_0_ = bf16[4,1024,256]{2,1,0:T(8,128)(2,1)} async-done(((bf16[4,1024,256]{2,1,0:T(8,128)(2,1)}), bf16[4,1024,256]{2,1,0:T(8,128)(2,1)}, u32[]{:S(2)}, u32[]{:S(2)}) %all-to-all-start.2) | async-done | bytes 2097184 | tf_op jit(solution)/shard_map/all_to_all | solution.py:55
  206.9 16.5 %attend_backward.2 = (bf16[3,2048,128]{2,1,0:T(8,128)(2,1)S(1)}, bf16[3,1024,128]{2,1,0:T(8,128)(2,1)}, f32[2,128]{1,0:T(2,128)S(1)}) custom-call(s32[4]{0:T(128)S(1)} %copy-done.26, bf16[2,2048,128]{2,1,0:T(8,128)(2,1)S(1)} %copy-done.34, bf16[4,2048,128]{2,1,0:T(8,128)(2,1)} %copy-done.28, bf16[4,2048,128]{2,1,0:T(8,128)(2,1)} %copy-done.29, ...), custom_call_target="tpu_custom_call" | custom-call | flops 17999998976 | bytes 6291456 | tf_op jit(solution)/shard_map/attend_backward/pallas_call | solution.py:317
  226.4 16.6 %attend_backward.3 = (bf16[3,2048,128]{2,1,0:T(8,128)(2,1)S(1)}, bf16[3,1024,128]{2,1,0:T(8,128)(2,1)}, f32[2,128]{1,0:T(2,128)S(1)}) custom-call(s32[4]{0:T(128)S(1)} %copy-done.26, bf16[2,2048,128]{2,1,0:T(8,128)(2,1)S(1)} %copy-done.32, bf16[4,2048,128]{2,1,0:T(8,128)(2,1)} %copy-done.28, bf16[4,2048,128]{2,1,0:T(8,128)(2,1)} %copy-done.29, ...), custom_call_target="tpu_custom_call" | custom-call | flops 17999998976 | bytes 6291456 | tf_op jit(solution)/shard_map/attend_backward/pallas_call | solution.py:317
  248.1 1.4 collective-permute-start.17
  250.1 1.4 copy-done.13
  251.6 1.4 copy-done.15
  253.0 10.8 %last.1 = (bf16[256,1024]{1,0:T(8,128)(2,1)}, bf16[256,1024]{1,0:T(8,128)(2,1)}, bf16[256,1024]{1,0:T(8,128)(2,1)}, bf16[256,1024]{1,0:T(8,128)(2,1)S(1)}, f32[8,1024]{1,0:T(8,128)S(1)}) custom-call(s32[4]{0:T(128)S(1)} %copy-done.26, bf16[3,2048,128]{2,1,0:T(8,128)(2,1)S(1)} %copy-done.13, bf16[3,2048,128]{2,1,0:T(8,128)(2,1)S(1)} %copy-done.15, ...), custom_call_target="tpu_custom_call" | custom-call | flops 3200000000 | bytes 20971520 | tf_op jit(solution)/shard_map/last/pallas_call | solution.py:512
  264.6 4.7 %qkv_grads.1 = bf16[1024,768]{1,0:T(8,128)(2,1)S(1)} custom-call(bf16[2048,1024]{1,0:T(8,128)(2,1)S(1)} %copy-done.7, bf16[3,2048,128]{2,1,0:T(8,128)(2,1)S(1)} %copy-done.13, bf16[3,2048,128]{2,1,0:T(8,128)(2,1)S(1)} %copy-done.15), custom_call_target="tpu_custom_call" | custom-call | flops 3221225472 | bytes 10485760 | tf_op jit(solution)/shard_map/qkv_grads/pallas_call | solution.py:635
  269.4 8.4 %collective-permute-done.18.refs_1_ = bf16[256,1024]{1,0:T(8,128)(2,1)} collective-permute-done((bf16[256,1024]{1,0:T(8,128)(2,1)}, bf16[256,1024]{1,0:T(8,128)(2,1)}, u32[]{:S(2)}, u32[]{:S(2)}) %collective-permute-start.18) | collective-permute-done | bytes 524320 | tf_op jit(solution)/shard_map/ppermute | solution.py:51
  278.5 2.9 fusion.7
  282.7 2.9 fusion.10
  288.8 2.0 collective-permute-done.19.refs_1_
  290.8 1.4 select_maximum_fusion.3
  294.3 2.5 collective-permute-start.32
  296.8 1.7 constant_dynamic-slice_fusion.1
  299.1 2.1 collective-permute-start.33
  306.7 2.1 copy.69.v_ref
  308.8 2.8 finish.12.refs_2_
  311.6 2.7 collective-permute-done.33
  314.4 1.5 collective-permute-start.21
  316.3 1.7 add_convert_fusion.4
  318.0 3.0 finish.10.refs_1_
  321.0 2.8 finish.13.refs_2_
  323.8 2.8 finish.14.refs_2_
  326.6 1.7 collective-permute-start.37
  329.1 6.9 %collective-permute-done.37 = bf16[128,768]{1,0:T(8,128)(2,1)} collective-permute-done((bf16[128,768]{1,0:T(8,128)(2,1)}, bf16[128,768]{1,0:T(8,128)(2,1)}, u32[]{:S(2)}, u32[]{:S(2)}) %collective-permute-start.37) | collective-permute-done | bytes 196640 | tf_op jit(solution)/shard_map/ppermute | solution.py:124
  337.3 1.8 collective-permute-start.41
  340.7 2.8 finish.15.refs_2_
  344.8 1.9 add_convert_fusion.2
  348.9 4.7 %finish.11 = f32[2048,1024]{1,0:T(8,128)} custom-call(s32[4]{0:T(128)S(1)} %copy-done.26, bf16[1024,1024]{1,0:T(8,128)(2,1)} %collective-permute-done.20.refs_0_, f32[2048,1024]{1,0:T(8,128)} %finish.10.refs_1_), custom_call_target="tpu_custom_call", output_to_operand_aliasing={{}: (2, {})} | custom-call | bytes 8388608 | tf_op jit(solution)/shard_map/finish/pallas_call | solution.py:658
  357.0 2.5 adam.4
  359.5 1.6 adam.5
  366.7 2.8 finish.16.refs_2_
  369.5 2.8 finish.17.refs_2_
  372.6 2.7 finish.18.refs_2_
  376.1 1.4 collective-permute-start.43
  382.2 1.6 finish.19
  (254 shorter events, 51.6 us)
Async XLA Ops:
  7.2 114.7 %all-gather.2.cloned.1.call-start = ((), (), s32[]{:S(2)}) async-start(), calls=%async_computation.4 | async-start | bytes 5898240 | tf_op jit(solution)/shard_map/all_gather | solution.py:752
  8.2 5.5 %collective-permute-start.8 = (bf16[128,256]{1,0:T(8,128)(2,1)S(1)}, bf16[128,256]{1,0:T(8,128)(2,1)S(1)}, u32[]{:S(2)}, u32[]{:S(2)}) collective-permute-start(bf16[128,256]{1,0:T(8,128)(2,1)S(1)} %bitcast.62), channel_id=1, source_target_pairs={{0,2},{1,3},{2,0},{3,1},{4,6},{5,7},{6,4},{7,5},{8,10},{9,11},{10,... | collective-permute-start | bytes 196616 | tf_op jit(solution)/shard_map/ppermute | solution.py:51
  15.0 7.5 %collective-permute-start.4 = (bf16[128,768]{1,0:T(8,128)(2,1)S(1)}, bf16[128,768]{1,0:T(8,128)(2,1)S(1)}, u32[]{:S(2)}, u32[]{:S(2)}) collective-permute-start(bf16[128,768]{1,0:T(8,128)(2,1)S(1)} %copy.64.refs_0_), channel_id=1, source_target_pairs={{0,8},{8,16},{16,24},{24,28},{28,20},{20,12},{12,4},{4,0},{1,9},{9... | collective-permute-start | bytes 589832 | tf_op jit(solution)/shard_map/ppermute | solution.py:88
  16.9 11.0 %collective-permute-start.1 = (bf16[128,768]{1,0:T(8,128)(2,1)S(1)}, bf16[128,768]{1,0:T(8,128)(2,1)S(1)}, u32[]{:S(2)}, u32[]{:S(2)}) collective-permute-start(bf16[128,768]{1,0:T(8,128)(2,1)S(1)} %copy.64.refs_0_), channel_id=1, source_target_pairs={{0,4},{8,0},{16,8},{24,16},{28,24},{20,28},{12,20},{4,12},{1,5},{9... | collective-permute-start | bytes 589832 | tf_op jit(solution)/shard_map/ppermute | solution.py:90
  17.1 39.5 %collective-permute-start = (f32[1,1024]{1,0:T(1,128)S(1)}, f32[1,1024]{1,0:T(1,128)S(1)}, u32[]{:S(2)}, u32[]{:S(2)}) collective-permute-start(f32[1,1024]{1,0:T(1,128)S(1)} %bitcast.73), channel_id=1, source_target_pairs={{0,1},{1,0},{2,3},{3,2},{4,5},{5,4},{6,7},{7,6},{8,9},{9,8},{10,11... | collective-permute-start | bytes 12296 | tf_op jit(solution)/shard_map/ppermute | solution.py:47
  22.5 10.8 %collective-permute-start.5 = (bf16[128,768]{1,0:T(8,128)(2,1)S(1)}, bf16[128,768]{1,0:T(8,128)(2,1)S(1)}, u32[]{:S(2)}, u32[]{:S(2)}) collective-permute-start(bf16[128,768]{1,0:T(8,128)(2,1)S(1)} %collective-permute-done.4.refs_7_), channel_id=1, source_target_pairs={{0,8},{8,16},{16,24},{24,28},{28,20},{20,12},{12,4},{4,0},{1,9},{9... | collective-permute-start | bytes 589832 | tf_op jit(solution)/shard_map/ppermute | solution.py:88
  24.4 31.5 %copy-start.39 = (s32[8]{0:T(128)S(1)}, s32[8]{0:T(128)}, u32[]{:S(2)}) copy-start(s32[8]{0:T(128)} %constant.99.clone) | copy-start | bytes 100
  28.0 16.3 %collective-permute-start.2 = (bf16[128,768]{1,0:T(8,128)(2,1)S(1)}, bf16[128,768]{1,0:T(8,128)(2,1)S(1)}, u32[]{:S(2)}, u32[]{:S(2)}) collective-permute-start(bf16[128,768]{1,0:T(8,128)(2,1)S(1)} %collective-permute-done.1.refs_1_), channel_id=1, source_target_pairs={{0,4},{8,0},{16,8},{24,16},{28,24},{20,28},{12,20},{4,12},{1,5},{9... | collective-permute-start | bytes 589832 | tf_op jit(solution)/shard_map/ppermute | solution.py:90
  33.3 13.1 %collective-permute-start.6 = (bf16[128,768]{1,0:T(8,128)(2,1)S(1)}, bf16[128,768]{1,0:T(8,128)(2,1)S(1)}, u32[]{:S(2)}, u32[]{:S(2)}) collective-permute-start(bf16[128,768]{1,0:T(8,128)(2,1)S(1)} %collective-permute-done.5.refs_6_), channel_id=1, source_target_pairs={{0,8},{8,16},{16,24},{24,28},{28,20},{20,12},{12,4},{4,0},{1,9},{9... | collective-permute-start | bytes 589832 | tf_op jit(solution)/shard_map/ppermute | solution.py:88
  44.2 13.0 %collective-permute-start.3 = (bf16[128,768]{1,0:T(8,128)(2,1)S(1)}, bf16[128,768]{1,0:T(8,128)(2,1)S(1)}, u32[]{:S(2)}, u32[]{:S(2)}) collective-permute-start(bf16[128,768]{1,0:T(8,128)(2,1)S(1)} %collective-permute-done.2.refs_2_), channel_id=1, source_target_pairs={{0,4},{8,0},{16,8},{24,16},{28,24},{20,28},{12,20},{4,12},{1,5},{9... | collective-permute-start | bytes 589832 | tf_op jit(solution)/shard_map/ppermute | solution.py:90
  46.4 12.2 %collective-permute-start.7 = (bf16[128,768]{1,0:T(8,128)(2,1)S(1)}, bf16[128,768]{1,0:T(8,128)(2,1)S(1)}, u32[]{:S(2)}, u32[]{:S(2)}) collective-permute-start(bf16[128,768]{1,0:T(8,128)(2,1)S(1)} %collective-permute-done.6.refs_5_), channel_id=1, source_target_pairs={{0,8},{8,16},{16,24},{24,28},{28,20},{20,12},{12,4},{4,0},{1,9},{9... | collective-permute-start | bytes 589832 | tf_op jit(solution)/shard_map/ppermute | solution.py:88
  86.0 18.1 %all-to-all-start = ((bf16[4,1024,128]{2,1,0:T(8,128)(2,1)}), bf16[4,1024,128]{2,1,0:T(8,128)(2,1)S(1)}, u32[]{:S(2)}, u32[]{:S(2)}) async-start(bf16[4,1024,128]{2,1,0:T(8,128)(2,1)} %get-tuple-element.110), calls=%async_computation | async-start | bytes 2097152 | tf_op jit(solution)/shard_map/all_to_all | solution.py:55
  100.7 68.3 %copy-start.35 = (bf16[2048,128]{1,0:T(8,128)(2,1)}, bf16[2048,128]{1,0:T(8,128)(2,1)S(1)}, u32[]{:S(2)}) copy-start(bf16[2048,128]{1,0:T(8,128)(2,1)S(1)} %get-tuple-element.133.o_ref) | copy-start | bytes 1572868
  104.1 29.1 %copy-start = (bf16[4,1024,128]{2,1,0:T(8,128)(2,1)}, bf16[4,1024,128]{2,1,0:T(8,128)(2,1)S(1)}, u32[]{:S(2)}) copy-start(bf16[4,1024,128]{2,1,0:T(8,128)(2,1)S(1)} %all-to-all-done.o0_ref.refs_2_.refs_4_.refs_7_.refs_9_) | copy-start | bytes 3145732
  121.9 11.3 %collective-permute-start.9 = (bf16[1024,2560]{1,0:T(8,128)(2,1)}, bf16[1024,2560]{1,0:T(8,128)(2,1)}, u32[]{:S(2)}, u32[]{:S(2)}) collective-permute-start(bf16[1024,2560]{1,0:T(8,128)(2,1)} %all-gather.2.cloned.1.call-done.late_own_ref), channel_id=1, source_target_pairs={{0,1},{1,0},{2,3},{3,2},{4,5},{5,4},{6,7},{7,6},{8,9},{9,8},{10,11... | collective-permute-start | bytes 15728648 | tf_op jit(solution)/shard_map/ppermute | solution.py:47
  121.9 11.2 %collective-permute-start.10 = (bf16[1024,768]{1,0:T(8,128)(2,1)}, bf16[1024,768]{1,0:T(8,128)(2,1)}, u32[]{:S(2)}, u32[]{:S(2)}) collective-permute-start(bf16[1024,768]{1,0:T(8,128)(2,1)} %get-tuple-element.114.w_own_ref), channel_id=1, source_target_pairs={{0,1},{1,0},{2,3},{3,2},{4,5},{5,4},{6,7},{7,6},{8,9},{9,8},{10,11... | collective-permute-start | bytes 4718600 | tf_op jit(solution)/shard_map/ppermute | solution.py:47
  123.0 46.3 %copy-start.3 = (bf16[4,1024,128]{2,1,0:T(8,128)(2,1)S(1)}, bf16[4,1024,128]{2,1,0:T(8,128)(2,1)}, u32[]{:S(2)}) copy-start(bf16[4,1024,128]{2,1,0:T(8,128)(2,1)} %all_to_all.15.o1_ref.refs_3_.refs_5_.refs_8_.refs_10_) | copy-start | bytes 3145732
  123.0 46.3 %copy-start.26 = (s32[4]{0:T(128)S(1)}, s32[4]{0:T(128)}, u32[]{:S(2)}) copy-start(s32[4]{0:T(128)} %pad_add_fusion.scalar_ref.refs_0_.half_ref) | copy-start | bytes 52
  169.1 11.9 %collective-permute-start.11 = (bf16[1024,3072]{1,0:T(8,128)(2,1)}, bf16[1024,3072]{1,0:T(8,128)(2,1)}, u32[]{:S(2)}, u32[]{:S(2)}) collective-permute-start(bf16[1024,3072]{1,0:T(8,128)(2,1)} %get-tuple-element.118.refs_0_), channel_id=1, source_target_pairs={{0,1},{1,0},{2,3},{3,2},{4,5},{5,4},{6,7},{7,6},{8,9},{9,8},{10,11... | collective-permute-start | bytes 18874376 | tf_op jit(solution)/shard_map/ppermute | solution.py:47
  175.7 5.3 %collective-permute-start.12 = (bf16[1024,512]{1,0:T(8,128)(2,1)}, bf16[1024,512]{1,0:T(8,128)(2,1)S(1)}, u32[]{:S(2)}, u32[]{:S(2)}) collective-permute-start(bf16[1024,512]{1,0:T(8,128)(2,1)} %out_grads.1), channel_id=1, source_target_pairs={{0,1},{1,0},{2,3},{3,2},{4,5},{5,4},{6,7},{7,6},{8,9},{9,8},{10,11... | collective-permute-start | bytes 3145736 | tf_op jit(solution)/shard_map/ppermute | solution.py:47
  176.1 30.4 %all-to-all-start.2 = ((bf16[4,1024,256]{2,1,0:T(8,128)(2,1)}), bf16[4,1024,256]{2,1,0:T(8,128)(2,1)}, u32[]{:S(2)}, u32[]{:S(2)}) async-start(bf16[4,1024,256]{2,1,0:T(8,128)(2,1)} %get-tuple-element.122), calls=%async_computation.2 | async-start | bytes 4194304 | tf_op jit(solution)/shard_map/all_to_all | solution.py:55
  180.7 173.0 %reduce-scatter.2.cloned.1.call-start = ((), (), s32[]{:S(2)}) async-start(), calls=%async_computation.5 | async-start | bytes 5898240 | tf_op jit(solution)/shard_map/reduce_scatter | solution.py:783
  206.5 19.1 %collective-permute-start.13 = (bf16[384,1024]{1,0:T(8,128)(2,1)S(1)}, bf16[384,1024]{1,0:T(8,128)(2,1)S(1)}, u32[]{:S(2)}, u32[]{:S(2)}) collective-permute-start(bf16[384,1024]{1,0:T(8,128)(2,1)S(1)} %copy-done.45), channel_id=1, source_target_pairs={{0,2},{1,3},{2,0},{3,1},{4,6},{5,7},{6,4},{7,5},{8,10},{9,11},{10,... | collective-permute-start | bytes 2359304 | tf_op jit(solution)/shard_map/ppermute | solution.py:51
  206.9 18.7 %copy-start.47 = (bf16[384,1024]{1,0:T(8,128)(2,1)S(1)}, bf16[384,1024]{1,0:T(8,128)(2,1)}, u32[]{:S(2)}) copy-start(bf16[384,1024]{1,0:T(8,128)(2,1)} %get-tuple-element.139) | copy-start | bytes 2359300
  206.9 19.4 %copy-start.32 = (bf16[2,2048,128]{2,1,0:T(8,128)(2,1)S(1)}, bf16[2,2048,128]{2,1,0:T(8,128)(2,1)}, u32[]{:S(2)}) copy-start(bf16[2,2048,128]{2,1,0:T(8,128)(2,1)} %copy-done.31) | copy-start | bytes 3145732
  206.9 19.4 %copy-start.36 = (bf16[2048,128]{1,0:T(8,128)(2,1)S(1)}, bf16[2048,128]{1,0:T(8,128)(2,1)}, u32[]{:S(2)}) copy-start(bf16[2048,128]{1,0:T(8,128)(2,1)} %copy-done.35) | copy-start | bytes 1572868
  225.6 17.3 %copy-start.49 = (bf16[384,1024]{1,0:T(8,128)(2,1)}, bf16[384,1024]{1,0:T(8,128)(2,1)S(1)}, u32[]{:S(2)}) copy-start(bf16[384,1024]{1,0:T(8,128)(2,1)S(1)} %collective-permute-done.13) | copy-start | bytes 2359300
  225.6 18.5 %collective-permute-start.15 = (bf16[384,1024]{1,0:T(8,128)(2,1)S(1)}, bf16[384,1024]{1,0:T(8,128)(2,1)S(1)}, u32[]{:S(2)}, u32[]{:S(2)}) collective-permute-start(bf16[384,1024]{1,0:T(8,128)(2,1)S(1)} %copy-done.47), channel_id=1, source_target_pairs={{0,2},{1,3},{2,0},{3,1},{4,6},{5,7},{6,4},{7,5},{8,10},{9,11},{10,... | collective-permute-start | bytes 2359304 | tf_op jit(solution)/shard_map/ppermute | solution.py:51
  226.3 23.8 %collective-permute-start.14 = (bf16[3,1024,128]{2,1,0:T(8,128)(2,1)}, bf16[3,1024,128]{2,1,0:T(8,128)(2,1)S(1)}, u32[]{:S(2)}, u32[]{:S(2)}) collective-permute-start(bf16[3,1024,128]{2,1,0:T(8,128)(2,1)} %get-tuple-element.136), channel_id=1, source_target_pairs={{0,1},{1,0},{2,3},{3,2},{4,5},{5,4},{6,7},{7,6},{8,9},{9,8},{10,11... | collective-permute-start | bytes 2359304 | tf_op jit(solution)/shard_map/ppermute | solution.py:47
  226.3 21.8 %copy-start.58 = (f32[8,1024]{1,0:T(8,128)S(1)}, f32[8,1024]{1,0:T(8,128)}, u32[]{:S(2)}) copy-start(f32[8,1024]{1,0:T(8,128)} %get-tuple-element.169) | copy-start | bytes 98308
  226.4 23.7 %copy-start.5 = (bf16[1024,1024]{1,0:T(8,128)(2,1)S(1)}, bf16[1024,1024]{1,0:T(8,128)(2,1)}, u32[]{:S(2)}) copy-start(bf16[1024,1024]{1,0:T(8,128)(2,1)} %get-tuple-element.121.refs_1_.refs_6_.refs_0_) | copy-start | bytes 6291460
  226.4 23.7 %copy-start.23 = (f32[6,1024]{1,0:T(8,128)S(1)}, f32[6,1024]{1,0:T(8,128)}, u32[]{:S(2)}) copy-start(f32[6,1024]{1,0:T(8,128)} %refs_1_.1) | copy-start | bytes 73732
  245.0 5.1 %collective-permute-start.16 = (bf16[3,1024,128]{2,1,0:T(8,128)(2,1)}, bf16[3,1024,128]{2,1,0:T(8,128)(2,1)}, u32[]{:S(2)}, u32[]{:S(2)}) collective-permute-start(bf16[3,1024,128]{2,1,0:T(8,128)(2,1)} %get-tuple-element.140), channel_id=1, source_target_pairs={{0,1},{1,0},{2,3},{3,2},{4,5},{5,4},{6,7},{7,6},{8,9},{9,8},{10,11... | collective-permute-start | bytes 2359304 | tf_op jit(solution)/shard_map/ppermute | solution.py:47
  248.1 15.7 %collective-permute-start.17 = (bf16[256,1024]{1,0:T(8,128)(2,1)}, bf16[256,1024]{1,0:T(8,128)(2,1)S(1)}, u32[]{:S(2)}, u32[]{:S(2)}) collective-permute-start(bf16[256,1024]{1,0:T(8,128)(2,1)} %get-tuple-element.145), channel_id=1, source_target_pairs={{0,2},{1,3},{2,0},{3,1},{4,6},{5,7},{6,4},{7,5},{8,10},{9,11},{10,... | collective-permute-start | bytes 1572872 | tf_op jit(solution)/shard_map/ppermute | solution.py:51
  263.8 14.0 %collective-permute-start.18 = (bf16[256,1024]{1,0:T(8,128)(2,1)}, bf16[256,1024]{1,0:T(8,128)(2,1)}, u32[]{:S(2)}, u32[]{:S(2)}) collective-permute-start(bf16[256,1024]{1,0:T(8,128)(2,1)} %get-tuple-element.167.refs_0_), channel_id=1, source_target_pairs={{0,2},{1,3},{2,0},{3,1},{4,6},{5,7},{6,4},{7,5},{8,10},{9,11},{10,... | collective-permute-start | bytes 1572872 | tf_op jit(solution)/shard_map/ppermute | solution.py:51
  264.6 13.9 %copy-start.42 = (bf16[1024,1024]{1,0:T(8,128)(2,1)S(1)}, bf16[1024,1024]{1,0:T(8,128)(2,1)}, u32[]{:S(2)}) copy-start(bf16[1024,1024]{1,0:T(8,128)(2,1)} %get-tuple-element.116) | copy-start | bytes 6291460
  264.6 13.9 %copy-start.46 = (bf16[384,1024]{1,0:T(8,128)(2,1)S(1)}, bf16[384,1024]{1,0:T(8,128)(2,1)}, u32[]{:S(2)}) copy-start(bf16[384,1024]{1,0:T(8,128)(2,1)} %get-tuple-element.124) | copy-start | bytes 2359300
  277.7 13.0 %collective-permute-start.19 = (bf16[256,1024]{1,0:T(8,128)(2,1)}, bf16[256,1024]{1,0:T(8,128)(2,1)}, u32[]{:S(2)}, u32[]{:S(2)}) collective-permute-start(bf16[256,1024]{1,0:T(8,128)(2,1)} %get-tuple-element.166.refs_0_), channel_id=1, source_target_pairs={{0,2},{1,3},{2,0},{3,1},{4,6},{5,7},{6,4},{7,5},{8,10},{9,11},{10,... | collective-permute-start | bytes 1572872 | tf_op jit(solution)/shard_map/ppermute | solution.py:51
  278.4 36.0 %collective-permute-start.29 = (bf16[256,1024]{1,0:T(8,128)(2,1)}, bf16[256,1024]{1,0:T(8,128)(2,1)}, u32[]{:S(2)}, u32[]{:S(2)}) collective-permute-start(bf16[256,1024]{1,0:T(8,128)(2,1)} %get-tuple-element.167.refs_0_), channel_id=1, source_target_pairs={{0,1},{1,0},{2,3},{3,2},{4,5},{5,4},{6,7},{7,6},{8,9},{9,8},{10,11... | collective-permute-start | bytes 1572872 | tf_op jit(solution)/shard_map/ppermute | solution.py:47
  288.2 27.7 %collective-permute-start.30 = (bf16[256,1024]{1,0:T(8,128)(2,1)}, bf16[256,1024]{1,0:T(8,128)(2,1)}, u32[]{:S(2)}, u32[]{:S(2)}) collective-permute-start(bf16[256,1024]{1,0:T(8,128)(2,1)} %collective-permute-done.18.refs_1_), channel_id=1, source_target_pairs={{0,1},{1,0},{2,3},{3,2},{4,5},{5,4},{6,7},{7,6},{8,9},{9,8},{10,11... | collective-permute-start | bytes 1572872 | tf_op jit(solution)/shard_map/ppermute | solution.py:47
  292.2 2.0 collective-permute-start.31
  293.7 53.9 %collective-permute-start.20 = (bf16[1024,1024]{1,0:T(8,128)(2,1)S(1)}, bf16[1024,1024]{1,0:T(8,128)(2,1)}, u32[]{:S(2)}, u32[]{:S(2)}) collective-permute-start(bf16[1024,1024]{1,0:T(8,128)(2,1)S(1)} %constant_dynamic-update-slice_fusion.refs_0_), channel_id=1, source_target_pairs={{0,1},{1,0},{2,3},{3,2},{4,5},{5,4},{6,7},{7,6},{8,9},{9,8},{10,11... | collective-permute-start | bytes 6291464 | tf_op jit(solution)/shard_map/ppermute | solution.py:47
  294.3 4.9 %collective-permute-start.32 = (f32[9,1024]{1,0:T(8,128)S(1)}, f32[9,1024]{1,0:T(8,128)S(1)}, u32[]{:S(2)}, u32[]{:S(2)}) collective-permute-start(f32[9,1024]{1,0:T(8,128)S(1)} %pad_maximum_fusion.1), channel_id=1, source_target_pairs={{0,4},{4,0},{8,12},{12,8},{16,20},{20,16},{24,28},{28,24},{1,5},{5... | collective-permute-start | bytes 110600 | tf_op jit(solution)/shard_map/ppermute | solution.py:866
  298.5 15.8 %collective-permute-start.36 = (bf16[128,768]{1,0:T(8,128)(2,1)}, bf16[128,768]{1,0:T(8,128)(2,1)}, u32[]{:S(2)}, u32[]{:S(2)}) collective-permute-start(bf16[128,768]{1,0:T(8,128)(2,1)} %get-tuple-element.175), channel_id=1, source_target_pairs={{0,4},{8,0},{16,8},{24,16},{28,24},{20,28},{12,20},{4,12},{1,5},{9... | collective-permute-start | bytes 589832 | tf_op jit(solution)/shard_map/ppermute | solution.py:124
  299.1 15.2 %collective-permute-start.33 = (f32[9,1024]{1,0:T(8,128)S(1)}, f32[9,1024]{1,0:T(8,128)S(1)}, u32[]{:S(2)}, u32[]{:S(2)}) collective-permute-start(f32[9,1024]{1,0:T(8,128)S(1)} %fusion.23), channel_id=1, source_target_pairs={{0,8},{4,12},{8,0},{12,4},{16,24},{20,28},{24,16},{28,20},{1,9},{5... | collective-permute-start | bytes 110600 | tf_op jit(solution)/shard_map/ppermute | solution.py:866
  314.3 14.1 %collective-permute-start.40 = (bf16[128,768]{1,0:T(8,128)(2,1)S(1)}, bf16[128,768]{1,0:T(8,128)(2,1)S(1)}, u32[]{:S(2)}, u32[]{:S(2)}) collective-permute-start(bf16[128,768]{1,0:T(8,128)(2,1)S(1)} %get-tuple-element.178), channel_id=1, source_target_pairs={{0,8},{8,16},{16,24},{24,28},{28,20},{20,12},{12,4},{4,0},{1,9},{9... | collective-permute-start | bytes 589832 | tf_op jit(solution)/shard_map/ppermute | solution.py:123
  314.3 25.1 %collective-permute-start.27 = (bf16[256,1024]{1,0:T(8,128)(2,1)}, bf16[256,1024]{1,0:T(8,128)(2,1)}, u32[]{:S(2)}, u32[]{:S(2)}) collective-permute-start(bf16[256,1024]{1,0:T(8,128)(2,1)} %get-tuple-element.166.refs_0_), channel_id=1, source_target_pairs={{0,1},{1,0},{2,3},{3,2},{4,5},{5,4},{6,7},{7,6},{8,9},{9,8},{10,11... | collective-permute-start | bytes 1572872 | tf_op jit(solution)/shard_map/ppermute | solution.py:47
  314.4 24.7 %collective-permute-start.21 = (bf16[256,1024]{1,0:T(8,128)(2,1)}, bf16[256,1024]{1,0:T(8,128)(2,1)}, u32[]{:S(2)}, u32[]{:S(2)}) collective-permute-start(bf16[256,1024]{1,0:T(8,128)(2,1)} %get-tuple-element.165.refs_0_), channel_id=1, source_target_pairs={{0,2},{1,3},{2,0},{3,1},{4,6},{5,7},{6,4},{7,5},{8,10},{9,11},{10,... | collective-permute-start | bytes 1572872 | tf_op jit(solution)/shard_map/ppermute | solution.py:51
  316.0 10.7 %collective-permute-start.34 = (f32[9,1024]{1,0:T(8,128)S(1)}, f32[9,1024]{1,0:T(8,128)S(1)}, u32[]{:S(2)}, u32[]{:S(2)}) collective-permute-start(f32[9,1024]{1,0:T(8,128)S(1)} %add.272), channel_id=1, source_target_pairs={{0,16},{4,20},{8,24},{12,28},{16,0},{20,4},{24,8},{28,12},{1,17},{... | collective-permute-start | bytes 110600 | tf_op jit(solution)/shard_map/ppermute | solution.py:866
  323.8 16.1 %copy-start.59 = (f32[6,256]{1,0:T(8,128)S(1)}, f32[6,256]{1,0:T(8,128)}, u32[]{:S(2)}) copy-start(f32[6,256]{1,0:T(8,128)} %param.43) | copy-start | bytes 18436
  323.8 16.1 %copy-start.60 = (f32[6,256]{1,0:T(8,128)S(1)}, f32[6,256]{1,0:T(8,128)}, u32[]{:S(2)}) copy-start(f32[6,256]{1,0:T(8,128)} %param.42) | copy-start | bytes 18436
  326.6 9.4 %collective-permute-start.37 = (bf16[128,768]{1,0:T(8,128)(2,1)}, bf16[128,768]{1,0:T(8,128)(2,1)}, u32[]{:S(2)}, u32[]{:S(2)}) collective-permute-start(bf16[128,768]{1,0:T(8,128)(2,1)} %add_convert_fusion.4), channel_id=1, source_target_pairs={{0,4},{8,0},{16,8},{24,16},{28,24},{20,28},{12,20},{4,12},{1,5},{9... | collective-permute-start | bytes 589832 | tf_op jit(solution)/shard_map/ppermute | solution.py:124
  329.1 11.5 %collective-permute-start.28 = (bf16[256,1024]{1,0:T(8,128)(2,1)}, bf16[256,1024]{1,0:T(8,128)(2,1)}, u32[]{:S(2)}, u32[]{:S(2)}) collective-permute-start(bf16[256,1024]{1,0:T(8,128)(2,1)} %collective-permute-done.19.refs_1_), channel_id=1, source_target_pairs={{0,1},{1,0},{2,3},{3,2},{4,5},{5,4},{6,7},{7,6},{8,9},{9,8},{10,11... | collective-permute-start | bytes 1572872 | tf_op jit(solution)/shard_map/ppermute | solution.py:47
  337.3 6.2 %collective-permute-start.41 = (bf16[128,768]{1,0:T(8,128)(2,1)S(1)}, bf16[128,768]{1,0:T(8,128)(2,1)S(1)}, u32[]{:S(2)}, u32[]{:S(2)}) collective-permute-start(bf16[128,768]{1,0:T(8,128)(2,1)S(1)} %get-tuple-element.179), channel_id=1, source_target_pairs={{0,8},{8,16},{16,24},{24,28},{28,20},{20,12},{12,4},{4,0},{1,9},{9... | collective-permute-start | bytes 589832 | tf_op jit(solution)/shard_map/ppermute | solution.py:123
  339.1 5.7 %collective-permute-start.38 = (bf16[128,768]{1,0:T(8,128)(2,1)S(1)}, bf16[128,768]{1,0:T(8,128)(2,1)S(1)}, u32[]{:S(2)}, u32[]{:S(2)}) collective-permute-start(bf16[128,768]{1,0:T(8,128)(2,1)S(1)} %get-tuple-element.177), channel_id=1, source_target_pairs={{0,4},{8,0},{16,8},{24,16},{28,24},{20,28},{12,20},{4,12},{1,5},{9... | collective-permute-start | bytes 589832 | tf_op jit(solution)/shard_map/ppermute | solution.py:124
  339.4 21.7 %collective-permute-start.23 = (bf16[256,1024]{1,0:T(8,128)(2,1)}, bf16[256,1024]{1,0:T(8,128)(2,1)}, u32[]{:S(2)}, u32[]{:S(2)}) collective-permute-start(bf16[256,1024]{1,0:T(8,128)(2,1)} %copy-done.16), channel_id=1, source_target_pairs={{0,2},{1,3},{2,0},{3,1},{4,6},{5,7},{6,4},{7,5},{8,10},{9,11},{10,... | collective-permute-start | bytes 1572872 | tf_op jit(solution)/shard_map/ppermute | solution.py:51
  340.6 28.9 %collective-permute-start.25 = (bf16[256,1024]{1,0:T(8,128)(2,1)}, bf16[256,1024]{1,0:T(8,128)(2,1)}, u32[]{:S(2)}, u32[]{:S(2)}) collective-permute-start(bf16[256,1024]{1,0:T(8,128)(2,1)} %get-tuple-element.165.refs_0_), channel_id=1, source_target_pairs={{0,1},{1,0},{2,3},{3,2},{4,5},{5,4},{6,7},{7,6},{8,9},{9,8},{10,11... | collective-permute-start | bytes 1572872 | tf_op jit(solution)/shard_map/ppermute | solution.py:47
  343.5 26.0 %collective-permute-start.26 = (bf16[256,1024]{1,0:T(8,128)(2,1)}, bf16[256,1024]{1,0:T(8,128)(2,1)}, u32[]{:S(2)}, u32[]{:S(2)}) collective-permute-start(bf16[256,1024]{1,0:T(8,128)(2,1)} %collective-permute-done.21.refs_1_), channel_id=1, source_target_pairs={{0,1},{1,0},{2,3},{3,2},{4,5},{5,4},{6,7},{7,6},{8,9},{9,8},{10,11... | collective-permute-start | bytes 1572872 | tf_op jit(solution)/shard_map/ppermute | solution.py:47
  346.6 14.5 %collective-permute-start.42 = (bf16[128,768]{1,0:T(8,128)(2,1)}, bf16[128,768]{1,0:T(8,128)(2,1)S(1)}, u32[]{:S(2)}, u32[]{:S(2)}) collective-permute-start(bf16[128,768]{1,0:T(8,128)(2,1)} %get-tuple-element.180), channel_id=1, source_target_pairs={{0,8},{8,16},{16,24},{24,28},{28,20},{20,12},{12,4},{4,0},{1,9},{9... | collective-permute-start | bytes 589832 | tf_op jit(solution)/shard_map/ppermute | solution.py:123
  347.6 14.3 %collective-permute-start.39 = (bf16[128,768]{1,0:T(8,128)(2,1)}, bf16[128,768]{1,0:T(8,128)(2,1)}, u32[]{:S(2)}, u32[]{:S(2)}) collective-permute-start(bf16[128,768]{1,0:T(8,128)(2,1)} %get-tuple-element.248), channel_id=1, source_target_pairs={{0,4},{8,0},{16,8},{24,16},{28,24},{20,28},{12,20},{4,12},{1,5},{9... | collective-permute-start | bytes 589832 | tf_op jit(solution)/shard_map/ppermute | solution.py:124
  361.1 21.1 %collective-permute-start.22 = (bf16[256,1024]{1,0:T(8,128)(2,1)S(1)}, bf16[256,1024]{1,0:T(8,128)(2,1)S(1)}, u32[]{:S(2)}, u32[]{:S(2)}) collective-permute-start(bf16[256,1024]{1,0:T(8,128)(2,1)S(1)} %copy-done.17), channel_id=1, source_target_pairs={{0,1},{1,0},{2,3},{3,2},{4,5},{5,4},{6,7},{7,6},{8,9},{9,8},{10,11... | collective-permute-start | bytes 1572872 | tf_op jit(solution)/shard_map/ppermute | solution.py:47
  361.1 16.3 %collective-permute-start.35 = (f32[7,1024]{1,0:T(8,128)S(1)}, f32[7,1024]{1,0:T(8,128)S(1)}, u32[]{:S(2)}, u32[]{:S(2)}) collective-permute-start(f32[7,1024]{1,0:T(8,128)S(1)} %slice.191), channel_id=1, source_target_pairs={{0,2},{1,3},{2,0},{3,1},{4,6},{5,7},{6,4},{7,5},{8,10},{9,11},{10,... | collective-permute-start | bytes 86024 | tf_op jit(solution)/shard_map/ppermute | solution.py:51
  372.4 9.9 %collective-permute-start.24 = (bf16[256,1024]{1,0:T(8,128)(2,1)}, bf16[256,1024]{1,0:T(8,128)(2,1)S(1)}, u32[]{:S(2)}, u32[]{:S(2)}) collective-permute-start(bf16[256,1024]{1,0:T(8,128)(2,1)} %collective-permute-done.23.refs_1_), channel_id=1, source_target_pairs={{0,1},{1,0},{2,3},{3,2},{4,5},{5,4},{6,7},{7,6},{8,9},{9,8},{10,11... | collective-permute-start | bytes 1572872 | tf_op jit(solution)/shard_map/ppermute | solution.py:47
  376.1 4.3 %collective-permute-start.43 = (bf16[128,256]{1,0:T(8,128)(2,1)S(1)}, bf16[128,256]{1,0:T(8,128)(2,1)S(1)}, u32[]{:S(2)}, u32[]{:S(2)}) collective-permute-start(bf16[128,256]{1,0:T(8,128)(2,1)S(1)} %slice.195), channel_id=1, source_target_pairs={{0,2},{1,3},{2,0},{3,1},{4,6},{5,7},{6,4},{7,5},{8,10},{9,11},{10,... | collective-permute-start | bytes 196616 | tf_op jit(solution)/shard_map/ppermute | solution.py:51
  (46 other events, 236.3 us)
Sparse Core Ops, SparseCore 0:
  14.8 98.8 all-gather.1
  206.6 106.5 reduce-scatter.1

commit v3 on v2

--- a/solution.py
+++ b/solution.py
@@ -644,30 +644,37 @@
     )(normed, *parts)
 
 
-def finish_kernel(scalar_ref, *refs, terms):
-    total = refs[0][...].astype(F32)
-    for ref in refs[1:terms]:
-        total = total + ref[...].astype(F32)
-    refs[-1][...] = total
-
-
-def finish(scalars, side, terms, before=(), piece=0, pieces=1):
-    rows, depth = terms[0].shape
-    tile = 256
-    steps = rows // tile
+def finish_kernel(scalar_ref, *refs, pieces, terms, cuts):
+    for k in range(pieces):
+
+        @pl.when(pl.program_id(0) // cuts == k)
+        def _():
+            total = refs[k * terms][...].astype(F32)
+            for ref in refs[k * terms + 1 : (k + 1) * terms]:
+                total = total + ref[...].astype(F32)
+            refs[-1][...] = total
+
+
+def finish(scalars, side, pieces, before=(), first=0, whole_pieces=4):
+    rows, depth = pieces[0][0].shape
+    terms = [x for piece in pieces for x in piece]
+    cuts = 4 if len(pieces) == 1 else 1
+    tile = rows // cuts
+    spec = whole((rows, depth)) if cuts == 1 else pl.BlockSpec((tile, depth), lambda i, s: (i, 0))
     out = pl.pallas_call(
-        functools.partial(finish_kernel, terms=len(terms)),
-        out_shape=[jax.ShapeDtypeStruct((2 * pieces * rows, depth), F32)],
+        functools.partial(finish_kernel, pieces=len(pieces), terms=len(pieces[0]), cuts=cuts),
+        out_shape=[jax.ShapeDtypeStruct((2 * whole_pieces * rows, depth), F32)],
         grid_spec=pltpu.PrefetchScalarGridSpec(
             num_scalar_prefetch=1,
-            grid=(steps,),
-            in_specs=[pl.BlockSpec((tile, depth), lambda i, s: (i, 0))] * len(terms)
-            + [pl.BlockSpec(memory_space=pl.ANY)] * len(before),
-            out_specs=[pl.BlockSpec((tile, depth), lambda i, s: (((s[0] ^ side) * pieces + piece) * steps + i, 0))],
+            grid=(len(pieces) * cuts,),
+            in_specs=[spec] * len(terms) + [pl.BlockSpec(memory_space=pl.ANY)] * len(before),
+            out_specs=[
+                pl.BlockSpec((tile, depth), lambda i, s: ((s[0] ^ side) * whole_pieces * cuts + first + i, 0))
+            ],
         ),
         input_output_aliases={1 + len(terms): 0} if before else {},
         compiler_params=pltpu.CompilerParams(vmem_limit_bytes=24 * MIB),
-        cost_estimate=cost(0, 8 * rows * depth),
+        cost_estimate=cost(0, 8 * rows * depth * len(pieces)),
         name="finish",
     )(scalars, *terms, *before)
     return out[0]
@@ -794,51 +801,32 @@
             outs[1] = (outs[1][0], after(outs[1][1], mlp_far[0], s))
         mlp_far.append(to_chip(after(mlps[pair + 1], mlp_far[pair])))
         siblings.append(to_core(d_sib))
-    *igs, last_sums = last(scalars, parts, siblings, qkv_w, qkv_sib, tokens, das[0], row_vectors)
-    igs[0] = after(igs[0], mlp_far[2])
+    qkv_wgrad = after(qkv_grads(normed, parts), *siblings)
+    qkv_ring = Reduce(qkv_wgrad, index, -1)
+    qkv_ring.hop()
+
+    *igs, last_sums = last(
+        scalars, parts, siblings, qkv_w, qkv_sib, after(tokens, qkv_wgrad), das[0], row_vectors
+    )
+    first_gates = (mlp_far[2], qkv_ring.up, qkv_ring.down)
+    igs[0], last_sums = after(igs[0], *first_gates), after(last_sums, *first_gates)
     ig_far = [to_chip(igs[0])]
-
-    qkv_wgrad = after(qkv_grads(after(normed, last_sums), parts), ig_far[0])
-    ig_sib = [to_core(after(x, qkv_wgrad)) for x in igs]
-    qkv_ring = Reduce(qkv_wgrad, index, -1)
-    for hop in range(4):
-        qkv_ring.hop(*ig_far[hop : hop + 1][: 3 - hop])
-        if hop < 3:
-            ig_far.append(to_chip(after(igs[hop + 1], ig_far[hop])))
-    qkv_shard = qkv_ring.finish()
-    up_shard = shard[:, :hidden].astype(F32)
-    down_shard = shard[:, hidden : 2 * hidden].astype(F32)
-    out_mine = shard[:, 2 * hidden : 2 * hidden + width]
-    out_theirs = to_chip(shard[:, 2 * hidden + width :])
-    out_shard = out_mine.astype(F32) + out_theirs.astype(F32)
-
+    ig_sib = [to_core(after(x, last_sums)) for x in igs]
+    qkv_ring.hop(last_sums)
     valid = ((core * half + jnp.arange(half)) < lengths[0]).astype(F32)[:, None]
     stat_out, stat_m, own_low = 0.0, 0.0, []
     at = 0
     for m, f in zip(mlps, mlp_far):
         rows = slice(at, at + m.shape[0])
         at += m.shape[0]
-        branch_m = m.astype(F32) + after(f, qkv_wgrad).astype(F32) + row_vectors[5]
+        branch_m = m.astype(F32) + after(f, last_sums).astype(F32) + row_vectors[5]
         outputs_own = resid[rows].astype(F32) + branch_m
         stat_out += jnp.sum(valid[rows] * outputs_own * outputs_own)
         stat_m += jnp.sum(valid[rows] * branch_m * branch_m)
-        own_low.append(after(outputs_own.astype(BF), ig_far[1]))
+        own_low.append(outputs_own.astype(BF))
     own_low = jnp.concatenate(own_low, axis=0)
-    outputs = after(finish(scalars, 0, [own_low]), ig_far[2])
-    outputs = finish(scalars, 1, [to_core(own_low)], (outputs,))
-    stat_out, stat_m = after(stat_out, ig_far[1]), after(stat_m, ig_far[1])
-    qkv_new = adam(adam_rows_kernel, qkv_shard, qkv_weight, qkv_first, qkv_second)
-    out_new = adam_turned(out_shard, out_weight, out_first, out_second)
-    up_new = adam(adam_rows_kernel, up_shard, up_weight, up_first, up_second)
-    down_new = adam_turned(down_shard, down_weight, down_first, down_second)
-    input_grad = ()
-    for k in range(4):
-        if k == 2:
-            input_grad = (after(input_grad[0], ig_far[3]),)
-            ig_far[3] = after(ig_far[3], up_new[0], down_new[0], outputs)
-        input_grad = (finish(scalars, 0, [igs[k], ig_far[k]], input_grad, k, 4),)
-        input_grad = (finish(scalars, 1, [ig_sib[k], to_core(ig_far[k])], input_grad, k, 4),)
-    input_grad = input_grad[0]
+    ig_far.append(to_chip(after(igs[1], ig_far[0], own_low, stat_out, stat_m)))
+    qkv_ring.hop(ig_far[0])
 
     stats = jnp.stack([stat_out, jnp.sum(sums[4]), stat_m, jnp.sum(valid)])
     small = jnp.concatenate(
@@ -861,10 +849,36 @@
     rows = rows + other[:7]
     columns = jnp.concatenate([columns[:1], columns[1:] + other[9:]], axis=0)
     small = jnp.concatenate([rows, columns], axis=0)
-    step = 1
+    meet = lambda x, step: x + lax.ppermute(x, "dp", [(i, i ^ step) for i in range(n_dp)])
+    outputs = finish(scalars, 0, [[own_low]], (), 0, 1)
+    ig_far.append(to_chip(after(igs[2], ig_far[1], outputs, small)))
+    qkv_ring.hop(ig_far[1])
+    small = meet(after(small, ig_far[1]), 1)
+    outputs = finish(scalars, 1, [[to_core(own_low)]], (outputs,), 0, 1)
+    ig_cross = [to_core(x) for x in ig_far[:2]]
+    front, back = slice(0, 2), slice(2, 4)
+    input_grad = finish(scalars, 0, list(zip(igs, ig_far))[front])
+    ig_far.append(to_chip(after(igs[3], ig_far[2], outputs, input_grad, small)))
+    qkv_shard = after(qkv_ring.finish(), ig_far[2])
+    step = 2
     while step < n_dp:
-        small = small + lax.ppermute(small, "dp", [(i, i ^ step) for i in range(n_dp)])
+        small = meet(after(small, *ig_far[2 : step]), step)
         step *= 2
+    input_grad = finish(scalars, 1, list(zip(ig_sib, ig_cross))[front], (input_grad,))
+    up_shard = shard[:, :hidden].astype(F32)
+    down_shard = shard[:, hidden : 2 * hidden].astype(F32)
+    out_mine = shard[:, 2 * hidden : 2 * hidden + width]
+    out_theirs = to_chip(shard[:, 2 * hidden + width :])
+    out_shard = out_mine.astype(F32) + out_theirs.astype(F32)
+
+    qkv_new = adam(adam_rows_kernel, qkv_shard, qkv_weight, qkv_first, qkv_second)
+    out_new = adam_turned(out_shard, out_weight, out_first, out_second)
+    up_new = adam(adam_rows_kernel, up_shard, up_weight, up_first, up_second)
+    down_new = adam_turned(down_shard, down_weight, down_first, down_second)
+    ig_cross += [to_core(x) for x in ig_far[2:]]
+    input_grad = after(input_grad, ig_far[3], up_new[0], down_new[0], qkv_new[0])
+    input_grad = finish(scalars, 0, list(zip(igs, ig_far))[back], (input_grad,), 2)
+    input_grad = finish(scalars, 1, list(zip(ig_sib, ig_cross))[back], (input_grad,), 2)
     rows = small[:7] + to_chip(after(small[:7], ig_far[3]))
     small = jnp.concatenate([rows, small[7:]], axis=0)
     row_total, stat_total = small[:6], small[6]

time: 396 us -> 388 us (0.980)
  Pallas kernels: 170 us -> 162 us
  local copies, waits for them, and re-layouts: 35.7 us -> 28.3 us
  starting transfers between devices: 51.9 us -> 57 us
    ppermute x10, waiting for transfers between devices: 12 us -> 21.9 us  [to_chip(): lax.ppermute(x, 'mp', [(i, i ^ 2) for i in range(lax.axis_size('mp'))])]
    pallas_call x10 -> x6, Pallas kernels: 28.9 us -> 21.2 us  [finish(): pl.pallas_call(functools.partial(finish_kernel, pieces=len(pieces), terms...]
    unnamed x137 -> x127, local copies, waits for them, and re-layouts: 29.3 us -> 23.4 us
    ppermute x4, waiting for transfers between devices: 7.68 us -> 2.19 us  [hop(): self.up = lax.ppermute(up, 'dp', self.perms[0])]
  transfers between devices with their start and end apart: 48 -> 48, of which waited for: 16 -> 17; matrix products, arithmetic and copies ran while one was open for 11% -> 10% of each run, Pallas kernels for 34% -> 33%
where the time goes in v3:
time: 388 us; the launch traced here: 383 us
  Pallas kernels  162 us (42%)
  waiting for transfers between devices  62.5 us (16%)
  starting transfers between devices  57 us (15%)
  other arithmetic  29.3 us (8%)
  local copies, waits for them, and re-layouts  28.3 us (7%)
  between operations  25.5 us (7%)
  blocking collectives  17.8 us (5%)
    pallas_call x1, Pallas kernels, middle(): pl.pallas_call(functools.partial(middle_kernel, chunk=chunk), out_shape=[...  35.9 us
    pallas_call x2, Pallas kernels, attend_backward(): pl.pallas_call(functools.partial(attend_backward_kernel, bk=min(256, span...  33 us
    unnamed x127, local copies, waits for them, and re-layouts  23.4 us
    ppermute x10, waiting for transfers between devices, to_chip(): lax.ppermute(x, 'mp', [(i, i ^ 2) for i in range(lax.axis_size('mp'))])  21.9 us
    pallas_call x6, Pallas kernels, finish(): pl.pallas_call(functools.partial(finish_kernel, pieces=len(pieces), terms...  21.2 us
    pallas_call x2, Pallas kernels, attend_forward(): pl.pallas_call(functools.partial(attend_forward_kernel, bq=min(512, span)...  21 us
    all_to_all x1, blocking collectives, to_all(): return lax.all_to_all(x, 'mp', split_axis=0, concat_axis=0, tiled=True)  17.8 us
    pallas_call x1, Pallas kernels, weight_grads(): pl.pallas_call(functools.partial(weight_grads_kernel, chunks=chunks), out...  17.5 us
  transfers between devices with their start and end apart: 48, of which 17 were waited for; matrix products, arithmetic and copies ran while one was open for 10% of the time, Pallas kernels for 33%

profile of v3, /device:TPU:0, one launch (start us, length us, event | category | flops | bytes accessed | tf_op | source)
XLA Modules:
  0.0 382.9 jit_solution(10495910191208005715)
XLA Ops:
  8.2 3.0 collective-permute-start.8
  15.0 1.9 collective-permute-start.4
  17.1 3.0 convert_reduce_fusion
  21.0 1.4 fusion.2
  22.4 1.9 collective-permute-start.5
  24.4 3.0 fusion.5.n_ref
  28.1 5.2 %collective-permute-done.5.refs_6_ = bf16[128,768]{1,0:T(8,128)(2,1)S(1)} collective-permute-done((bf16[128,768]{1,0:T(8,128)(2,1)S(1)}, bf16[128,768]{1,0:T(8,128)(2,1)S(1)}, u32[]{:S(2)}, u32[]{:S(2)}) %collective-permute-start.5) | collective-permute-done | bytes 196640 | tf_op jit(solution)/shard_map/ppermute | solution.py:88
  33.2 4.7 %collective-permute-start.6 = (bf16[128,768]{1,0:T(8,128)(2,1)S(1)}, bf16[128,768]{1,0:T(8,128)(2,1)S(1)}, u32[]{:S(2)}, u32[]{:S(2)}) collective-permute-start(bf16[128,768]{1,0:T(8,128)(2,1)S(1)} %collective-permute-done.5.refs_6_), channel_id=1, source_target_pairs={{0,8},{8,16},{16,24},{24,28},{28,20},{20,12},{12,4},{4,0},{1,9},{9... | collective-permute-start | bytes 589832 | tf_op jit(solution)/shard_map/ppermute | solution.py:88
  38.6 5.5 %collective-permute-done.2.refs_2_ = bf16[128,768]{1,0:T(8,128)(2,1)S(1)} collective-permute-done((bf16[128,768]{1,0:T(8,128)(2,1)S(1)}, bf16[128,768]{1,0:T(8,128)(2,1)S(1)}, u32[]{:S(2)}, u32[]{:S(2)}) %collective-permute-start.2) | collective-permute-done | bytes 196640 | tf_op jit(solution)/shard_map/ppermute | solution.py:90
  44.2 2.1 collective-permute-done.6.refs_5_
  46.3 8.9 %collective-permute-start.7 = (bf16[128,768]{1,0:T(8,128)(2,1)S(1)}, bf16[128,768]{1,0:T(8,128)(2,1)S(1)}, u32[]{:S(2)}, u32[]{:S(2)}) collective-permute-start(bf16[128,768]{1,0:T(8,128)(2,1)S(1)} %collective-permute-done.6.refs_5_), channel_id=1, source_target_pairs={{0,8},{8,16},{16,24},{24,28},{28,20},{20,12},{12,4},{4,0},{1,9},{9... | collective-permute-start | bytes 589832 | tf_op jit(solution)/shard_map/ppermute | solution.py:88
  57.2 1.4 collective-permute-done.7.refs_4_
  58.5 2.2 copy-done.6
  60.7 8.4 %project.1 = (bf16[4,2048,128]{2,1,0:T(8,128)(2,1)S(1)}, bf16[4,2048,128]{2,1,0:T(8,128)(2,1)S(1)}, bf16[4,2048,128]{2,1,0:T(8,128)(2,1)S(1)}, bf16[1024,768]{1,0:T(8,128)(2,1)}) custom-call(s32[8]{0:T(128)S(1)} %gather_fusion, f32[4]{0:T(128)S(1)} %multiply_exponential_fusion.slope_ref, s32[1]{0:T(128)} %copy.76.length_ref, ...), custom_call_target="tpu_custom_call" | custom-call | flops 3221225472 | bytes 12582912 | tf_op jit(solution)/shard_map/project/pallas_call | solution.py:202
  69.1 1.3 copy-done.25
  70.5 1.3 copy-done.26
  71.8 1.3 copy-done.27
  73.1 11.0 %attend_forward.2 = (bf16[2048,128]{1,0:T(8,128)(2,1)S(1)}, bf16[2,2048,128]{2,1,0:T(8,128)(2,1)S(1)}, bf16[4,1024,128]{2,1,0:T(8,128)(2,1)}) custom-call(bf16[4,2048,128]{2,1,0:T(8,128)(2,1)} %copy-done.27, bf16[4,2048,128]{2,1,0:T(8,128)(2,1)} %copy-done.25, bf16[4,2048,128]{2,1,0:T(8,128)(2,1)} %copy-done.26), custom_call_target="tpu_custom_call" | custom-call | flops 12000000000 | bytes 5242880 | tf_op jit(solution)/shard_map/attend_forward/pallas_call | solution.py:252
  85.9 3.7 all-to-all-start
  89.6 10.0 %attend_forward.3 = (bf16[2048,128]{1,0:T(8,128)(2,1)S(1)}, bf16[2,2048,128]{2,1,0:T(8,128)(2,1)S(1)}, bf16[4,1024,128]{2,1,0:T(8,128)(2,1)S(1)}) custom-call(bf16[4,2048,128]{2,1,0:T(8,128)(2,1)} %copy-done.27, bf16[4,2048,128]{2,1,0:T(8,128)(2,1)} %copy-done.25, bf16[4,2048,128]{2,1,0:T(8,128)(2,1)} %copy-done.26), custom_call_target="tpu_custom_call" | custom-call | flops 12000000000 | bytes 5242880 | tf_op jit(solution)/shard_map/attend_forward/pallas_call | solution.py:252
  100.4 3.6 all-to-all-done.o0_ref.refs_2_.refs_4_.refs_7_.refs_9_
  104.0 17.8 %all_to_all.15.o1_ref.refs_3_.refs_5_.refs_8_.refs_10_ = bf16[4,1024,128]{2,1,0:T(8,128)(2,1)} all-to-all(bf16[4,1024,128]{2,1,0:T(8,128)(2,1)S(1)} %get-tuple-element.108), channel_id=1, replica_groups=mesh['dp'=8,'mp'=4] {'mp'}, dimensions={0} | all-to-all | bytes 2097152 | tf_op jit(solution)/shard_map/all_to_all | solution.py:55
  122.9 10.1 %collective-permute-done.10.w_sib_ref = bf16[1024,768]{1,0:T(8,128)(2,1)} collective-permute-done((bf16[1024,768]{1,0:T(8,128)(2,1)}, bf16[1024,768]{1,0:T(8,128)(2,1)}, u32[]{:S(2)}, u32[]{:S(2)}) %collective-permute-start.10) | collective-permute-done | bytes 1572896 | tf_op jit(solution)/shard_map/ppermute | solution.py:47
  133.0 35.9 %middle.1 = (bf16[384,1024]{1,0:T(8,128)(2,1)}, bf16[384,1024]{1,0:T(8,128)(2,1)}, bf16[256,1024]{1,0:T(8,128)(2,1)}, bf16[1024,1024]{1,0:T(8,128)(2,1)}, bf16[1...) custom-call(s32[4]{0:T(128)} %pad_add_fusion.scalar_ref.refs_0_.half, ...), custom_call_target="tpu_custom_call" | custom-call | flops 20999999488 | bytes 25165824 | tf_op jit(solution)/shard_map/middle/pallas_call | solution.py:453
  169.2 1.2 copy-done.1
  170.4 1.6 copy-done.4
  172.0 3.6 out_grads.1
  176.0 4.6 %all-to-all-start.2 = ((bf16[4,1024,256]{2,1,0:T(8,128)(2,1)}), bf16[4,1024,256]{2,1,0:T(8,128)(2,1)}, u32[]{:S(2)}, u32[]{:S(2)}) async-start(bf16[4,1024,256]{2,1,0:T(8,128)(2,1)} %get-tuple-element.118), calls=%async_computation.2 | async-start | bytes 4194304 | tf_op jit(solution)/shard_map/all_to_all | solution.py:55
  180.9 17.5 %weight_grads.1 = bf16[1024,2560]{1,0:T(8,128)(2,1)} custom-call(s32[4]{0:T(128)S(1)} %copy-done.23, f32[2048,1024]{1,0:T(8,128)} %cot_ref.3, bf16[1024,3072]{1,0:T(8,128)(2,1)} %get-tuple-element.114.refs_0_, bf16[1024,1024]{1,0:T(8,128)(2,1)} %get-tuple-element.115.refs_1_, bf16[1024,1024]{1,0:T(8,128)(2,1)} %get-tuple-element.116.refs_2_, ...), custom_call_target="tpu_custom_call" | custom-call | flops 9663676416 | bytes 31457280 | tf_op jit(solution)/shard_map/weight_grads/pallas_call | solution.py:599
  198.5 7.9 %all-to-all-done.2.refs_0_ = bf16[4,1024,256]{2,1,0:T(8,128)(2,1)} async-done(((bf16[4,1024,256]{2,1,0:T(8,128)(2,1)}), bf16[4,1024,256]{2,1,0:T(8,128)(2,1)}, u32[]{:S(2)}, u32[]{:S(2)}) %all-to-all-start.2) | async-done | bytes 2097184 | tf_op jit(solution)/shard_map/all_to_all | solution.py:55
  206.8 16.5 %attend_backward.2 = (bf16[3,2048,128]{2,1,0:T(8,128)(2,1)S(1)}, bf16[3,1024,128]{2,1,0:T(8,128)(2,1)}, f32[2,128]{1,0:T(2,128)S(1)}) custom-call(s32[4]{0:T(128)S(1)} %copy-done.23, bf16[2,2048,128]{2,1,0:T(8,128)(2,1)S(1)} %copy-done.31, bf16[4,2048,128]{2,1,0:T(8,128)(2,1)} %copy-done.25, bf16[4,2048,128]{2,1,0:T(8,128)(2,1)} %copy-done.26, ...), custom_call_target="tpu_custom_call" | custom-call | flops 17999998976 | bytes 6291456 | tf_op jit(solution)/shard_map/attend_backward/pallas_call | solution.py:317
  223.3 2.4 collective-permute-done.13
  226.4 16.5 %attend_backward.3 = (bf16[3,2048,128]{2,1,0:T(8,128)(2,1)S(1)}, bf16[3,1024,128]{2,1,0:T(8,128)(2,1)}, f32[2,128]{1,0:T(2,128)S(1)}) custom-call(s32[4]{0:T(128)S(1)} %copy-done.23, bf16[2,2048,128]{2,1,0:T(8,128)(2,1)S(1)} %copy-done.29, bf16[4,2048,128]{2,1,0:T(8,128)(2,1)} %copy-done.25, bf16[4,2048,128]{2,1,0:T(8,128)(2,1)} %copy-done.26, ...), custom_call_target="tpu_custom_call" | custom-call | flops 17999998976 | bytes 6291456 | tf_op jit(solution)/shard_map/attend_backward/pallas_call | solution.py:317
  247.3 2.2 copy-done.7
  249.5 4.7 %qkv_grads.1 = bf16[1024,768]{1,0:T(8,128)(2,1)S(1)} custom-call(bf16[2048,1024]{1,0:T(8,128)(2,1)S(1)} %copy-done.7, bf16[3,2048,128]{2,1,0:T(8,128)(2,1)S(1)} %get-tuple-element.124.p0_ref.o0_ref, bf16[3,2048,128]{2,1,0:T(8,128)(2,1)S(1)} %get-tuple-element.130.p1_ref.o1_ref), custom_call_target="tpu_custom_call" | custom-call | flops 3221225472 | bytes 10485760 | tf_op jit(solution)/shard_map/qkv_grads/pallas_call | solution.py:635
  255.4 2.5 collective-permute-start.18
  258.0 10.7 %last.1 = (bf16[256,1024]{1,0:T(8,128)(2,1)}, bf16[256,1024]{1,0:T(8,128)(2,1)}, bf16[256,1024]{1,0:T(8,128)(2,1)S(1)}, bf16[256,1024]{1,0:T(8,128)(2,1)S(1)}, f32[8,1024]{1,0:T(8,128)S(1)}) custom-call(s32[4]{0:T(128)S(1)} %copy-done.23, bf16[3,2048,128]{2,1,0:T(8,128)(2,1)S(1)} %get-tuple-element.124.p0_ref.o0_ref, ...), custom_call_target="tpu_custom_call" | custom-call | flops 3200000000 | bytes 20971520 | tf_op jit(solution)/shard_map/last/pallas_call | solution.py:512
  269.5 1.2 fusion.11
  270.8 3.2 fusion.7
  281.1 1.4 select_maximum_fusion.3
  283.9 3.0 finish.6.refs_1_
  286.9 1.6 collective-permute-start.35
  288.5 2.2 collective-permute-done.22.refs_1_
  291.9 12.7 %collective-permute-done.23.refs_3_ = bf16[256,1024]{1,0:T(8,128)(2,1)} collective-permute-done((bf16[256,1024]{1,0:T(8,128)(2,1)}, bf16[256,1024]{1,0:T(8,128)(2,1)}, u32[]{:S(2)}, u32[]{:S(2)}) %collective-permute-start.23) | collective-permute-done | bytes 524320 | tf_op jit(solution)/shard_map/ppermute | solution.py:51
  307.0 1.9 add_convert_fusion.3
  308.9 2.1 collective-permute-start.38
  311.0 1.6 collective-permute-start.28
  312.6 3.5 finish.8.refs_4_
  316.2 4.8 %finish.7 = f32[2048,1024]{1,0:T(8,128)} custom-call(s32[4]{0:T(128)S(1)} %copy-done.23, bf16[1024,1024]{1,0:T(8,128)(2,1)} %collective-permute-done.20.refs_0_, f32[2048,1024]{1,0:T(8,128)} %finish.6.refs_1_), custom_call_target="tpu_custom_call", output_to_operand_aliasing={{}: (2, {})} | custom-call | bytes 8388608 | tf_op jit(solution)/shard_map/finish/pallas_call | solution.py:664
  323.2 2.0 add_convert_fusion.2
  325.2 1.5 collective-permute-start.39
  326.7 1.5 collective-permute-start.40
  328.7 2.2 collective-permute-done.39
  332.6 1.9 collective-permute-start.37
  335.7 1.3 copy.65.v_ref
  337.0 2.2 collective-permute-done.37
  339.2 3.0 collective-permute-start.41
  343.3 1.3 adam.6
  347.7 3.5 finish.9.refs_4_
  353.6 2.2 collective-permute-done.42
  363.5 2.5 adam.4
  366.0 1.6 adam.5
  367.5 3.0 finish.10.refs_4_
  370.6 3.4 finish.11
  (240 shorter events, 44.7 us)
Async XLA Ops:
  7.2 114.6 %all-gather.2.cloned.1.call-start = ((), (), s32[]{:S(2)}) async-start(), calls=%async_computation.4 | async-start | bytes 5898240 | tf_op jit(solution)/shard_map/all_gather | solution.py:759
  8.2 5.5 %collective-permute-start.8 = (bf16[128,256]{1,0:T(8,128)(2,1)S(1)}, bf16[128,256]{1,0:T(8,128)(2,1)S(1)}, u32[]{:S(2)}, u32[]{:S(2)}) collective-permute-start(bf16[128,256]{1,0:T(8,128)(2,1)S(1)} %bitcast.62), channel_id=1, source_target_pairs={{0,2},{1,3},{2,0},{3,1},{4,6},{5,7},{6,4},{7,5},{8,10},{9,11},{10,... | collective-permute-start | bytes 196616 | tf_op jit(solution)/shard_map/ppermute | solution.py:51
  15.0 7.5 %collective-permute-start.4 = (bf16[128,768]{1,0:T(8,128)(2,1)S(1)}, bf16[128,768]{1,0:T(8,128)(2,1)S(1)}, u32[]{:S(2)}, u32[]{:S(2)}) collective-permute-start(bf16[128,768]{1,0:T(8,128)(2,1)S(1)} %copy.60.refs_0_), channel_id=1, source_target_pairs={{0,8},{8,16},{16,24},{24,28},{28,20},{20,12},{12,4},{4,0},{1,9},{9... | collective-permute-start | bytes 589832 | tf_op jit(solution)/shard_map/ppermute | solution.py:88
  16.9 11.0 %collective-permute-start.1 = (bf16[128,768]{1,0:T(8,128)(2,1)S(1)}, bf16[128,768]{1,0:T(8,128)(2,1)S(1)}, u32[]{:S(2)}, u32[]{:S(2)}) collective-permute-start(bf16[128,768]{1,0:T(8,128)(2,1)S(1)} %copy.60.refs_0_), channel_id=1, source_target_pairs={{0,4},{8,0},{16,8},{24,16},{28,24},{20,28},{12,20},{4,12},{1,5},{9... | collective-permute-start | bytes 589832 | tf_op jit(solution)/shard_map/ppermute | solution.py:90
  17.1 39.5 %collective-permute-start = (f32[1,1024]{1,0:T(1,128)S(1)}, f32[1,1024]{1,0:T(1,128)S(1)}, u32[]{:S(2)}, u32[]{:S(2)}) collective-permute-start(f32[1,1024]{1,0:T(1,128)S(1)} %bitcast.72), channel_id=1, source_target_pairs={{0,1},{1,0},{2,3},{3,2},{4,5},{5,4},{6,7},{7,6},{8,9},{9,8},{10,11... | collective-permute-start | bytes 12296 | tf_op jit(solution)/shard_map/ppermute | solution.py:47
  22.4 10.8 %collective-permute-start.5 = (bf16[128,768]{1,0:T(8,128)(2,1)S(1)}, bf16[128,768]{1,0:T(8,128)(2,1)S(1)}, u32[]{:S(2)}, u32[]{:S(2)}) collective-permute-start(bf16[128,768]{1,0:T(8,128)(2,1)S(1)} %collective-permute-done.4.refs_7_), channel_id=1, source_target_pairs={{0,8},{8,16},{16,24},{24,28},{28,20},{20,12},{12,4},{4,0},{1,9},{9... | collective-permute-start | bytes 589832 | tf_op jit(solution)/shard_map/ppermute | solution.py:88
  24.4 31.5 %copy-start.36 = (s32[8]{0:T(128)S(1)}, s32[8]{0:T(128)}, u32[]{:S(2)}) copy-start(s32[8]{0:T(128)} %constant.99.clone) | copy-start | bytes 100
  27.9 16.2 %collective-permute-start.2 = (bf16[128,768]{1,0:T(8,128)(2,1)S(1)}, bf16[128,768]{1,0:T(8,128)(2,1)S(1)}, u32[]{:S(2)}, u32[]{:S(2)}) collective-permute-start(bf16[128,768]{1,0:T(8,128)(2,1)S(1)} %collective-permute-done.1.refs_1_), channel_id=1, source_target_pairs={{0,4},{8,0},{16,8},{24,16},{28,24},{20,28},{12,20},{4,12},{1,5},{9... | collective-permute-start | bytes 589832 | tf_op jit(solution)/shard_map/ppermute | solution.py:90
  33.2 13.1 %collective-permute-start.6 = (bf16[128,768]{1,0:T(8,128)(2,1)S(1)}, bf16[128,768]{1,0:T(8,128)(2,1)S(1)}, u32[]{:S(2)}, u32[]{:S(2)}) collective-permute-start(bf16[128,768]{1,0:T(8,128)(2,1)S(1)} %collective-permute-done.5.refs_6_), channel_id=1, source_target_pairs={{0,8},{8,16},{16,24},{24,28},{28,20},{20,12},{12,4},{4,0},{1,9},{9... | collective-permute-start | bytes 589832 | tf_op jit(solution)/shard_map/ppermute | solution.py:88
  44.2 13.0 %collective-permute-start.3 = (bf16[128,768]{1,0:T(8,128)(2,1)S(1)}, bf16[128,768]{1,0:T(8,128)(2,1)S(1)}, u32[]{:S(2)}, u32[]{:S(2)}) collective-permute-start(bf16[128,768]{1,0:T(8,128)(2,1)S(1)} %collective-permute-done.2.refs_2_), channel_id=1, source_target_pairs={{0,4},{8,0},{16,8},{24,16},{28,24},{20,28},{12,20},{4,12},{1,5},{9... | collective-permute-start | bytes 589832 | tf_op jit(solution)/shard_map/ppermute | solution.py:90
  46.3 12.2 %collective-permute-start.7 = (bf16[128,768]{1,0:T(8,128)(2,1)S(1)}, bf16[128,768]{1,0:T(8,128)(2,1)S(1)}, u32[]{:S(2)}, u32[]{:S(2)}) collective-permute-start(bf16[128,768]{1,0:T(8,128)(2,1)S(1)} %collective-permute-done.6.refs_5_), channel_id=1, source_target_pairs={{0,8},{8,16},{16,24},{24,28},{28,20},{20,12},{12,4},{4,0},{1,9},{9... | collective-permute-start | bytes 589832 | tf_op jit(solution)/shard_map/ppermute | solution.py:88
  85.9 18.1 %all-to-all-start = ((bf16[4,1024,128]{2,1,0:T(8,128)(2,1)}), bf16[4,1024,128]{2,1,0:T(8,128)(2,1)S(1)}, u32[]{:S(2)}, u32[]{:S(2)}) async-start(bf16[4,1024,128]{2,1,0:T(8,128)(2,1)} %get-tuple-element.106), calls=%async_computation | async-start | bytes 2097152 | tf_op jit(solution)/shard_map/all_to_all | solution.py:55
  100.4 68.6 %copy-start.28 = (bf16[2,2048,128]{2,1,0:T(8,128)(2,1)}, bf16[2,2048,128]{2,1,0:T(8,128)(2,1)S(1)}, u32[]{:S(2)}) copy-start(bf16[2,2048,128]{2,1,0:T(8,128)(2,1)S(1)} %get-tuple-element.128.q_ref) | copy-start | bytes 3145732
  104.0 29.1 %copy-start = (bf16[4,1024,128]{2,1,0:T(8,128)(2,1)}, bf16[4,1024,128]{2,1,0:T(8,128)(2,1)S(1)}, u32[]{:S(2)}) copy-start(bf16[4,1024,128]{2,1,0:T(8,128)(2,1)S(1)} %all-to-all-done.o0_ref.refs_2_.refs_4_.refs_7_.refs_9_) | copy-start | bytes 3145732
  121.8 11.3 %collective-permute-start.9 = (bf16[1024,2560]{1,0:T(8,128)(2,1)}, bf16[1024,2560]{1,0:T(8,128)(2,1)}, u32[]{:S(2)}, u32[]{:S(2)}) collective-permute-start(bf16[1024,2560]{1,0:T(8,128)(2,1)} %all-gather.2.cloned.1.call-done.late_own_ref), channel_id=1, source_target_pairs={{0,1},{1,0},{2,3},{3,2},{4,5},{5,4},{6,7},{7,6},{8,9},{9,8},{10,11... | collective-permute-start | bytes 15728648 | tf_op jit(solution)/shard_map/ppermute | solution.py:47
  121.8 11.2 %collective-permute-start.10 = (bf16[1024,768]{1,0:T(8,128)(2,1)}, bf16[1024,768]{1,0:T(8,128)(2,1)}, u32[]{:S(2)}, u32[]{:S(2)}) collective-permute-start(bf16[1024,768]{1,0:T(8,128)(2,1)} %get-tuple-element.110.w_own_ref), channel_id=1, source_target_pairs={{0,1},{1,0},{2,3},{3,2},{4,5},{5,4},{6,7},{7,6},{8,9},{9,8},{10,11... | collective-permute-start | bytes 4718600 | tf_op jit(solution)/shard_map/ppermute | solution.py:47
  122.9 46.3 %copy-start.3 = (bf16[4,1024,128]{2,1,0:T(8,128)(2,1)S(1)}, bf16[4,1024,128]{2,1,0:T(8,128)(2,1)}, u32[]{:S(2)}) copy-start(bf16[4,1024,128]{2,1,0:T(8,128)(2,1)} %all_to_all.15.o1_ref.refs_3_.refs_5_.refs_8_.refs_10_) | copy-start | bytes 3145732
  122.9 46.3 %copy-start.23 = (s32[4]{0:T(128)S(1)}, s32[4]{0:T(128)}, u32[]{:S(2)}) copy-start(s32[4]{0:T(128)} %pad_add_fusion.scalar_ref.refs_0_.half_ref) | copy-start | bytes 52
  169.0 11.9 %collective-permute-start.11 = (bf16[1024,3072]{1,0:T(8,128)(2,1)}, bf16[1024,3072]{1,0:T(8,128)(2,1)}, u32[]{:S(2)}, u32[]{:S(2)}) collective-permute-start(bf16[1024,3072]{1,0:T(8,128)(2,1)} %get-tuple-element.114.refs_0_), channel_id=1, source_target_pairs={{0,1},{1,0},{2,3},{3,2},{4,5},{5,4},{6,7},{7,6},{8,9},{9,8},{10,11... | collective-permute-start | bytes 18874376 | tf_op jit(solution)/shard_map/ppermute | solution.py:47
  175.6 5.3 %collective-permute-start.12 = (bf16[1024,512]{1,0:T(8,128)(2,1)}, bf16[1024,512]{1,0:T(8,128)(2,1)S(1)}, u32[]{:S(2)}, u32[]{:S(2)}) collective-permute-start(bf16[1024,512]{1,0:T(8,128)(2,1)} %out_grads.1), channel_id=1, source_target_pairs={{0,1},{1,0},{2,3},{3,2},{4,5},{5,4},{6,7},{7,6},{8,9},{9,8},{10,11... | collective-permute-start | bytes 3145736 | tf_op jit(solution)/shard_map/ppermute | solution.py:47
  176.0 30.4 %all-to-all-start.2 = ((bf16[4,1024,256]{2,1,0:T(8,128)(2,1)}), bf16[4,1024,256]{2,1,0:T(8,128)(2,1)}, u32[]{:S(2)}, u32[]{:S(2)}) async-start(bf16[4,1024,256]{2,1,0:T(8,128)(2,1)} %get-tuple-element.118), calls=%async_computation.2 | async-start | bytes 4194304 | tf_op jit(solution)/shard_map/all_to_all | solution.py:55
  180.6 177.6 %reduce-scatter.2.cloned.1.call-start = ((), (), s32[]{:S(2)}) async-start(), calls=%async_computation.5 | async-start | bytes 5898240 | tf_op jit(solution)/shard_map/reduce_scatter | solution.py:790
  206.4 19.4 %collective-permute-start.13 = (bf16[384,1024]{1,0:T(8,128)(2,1)}, bf16[384,1024]{1,0:T(8,128)(2,1)S(1)}, u32[]{:S(2)}, u32[]{:S(2)}) collective-permute-start(bf16[384,1024]{1,0:T(8,128)(2,1)} %get-tuple-element.120), channel_id=1, source_target_pairs={{0,2},{1,3},{2,0},{3,1},{4,6},{5,7},{6,4},{7,5},{8,10},{9,11},{10,... | collective-permute-start | bytes 2359304 | tf_op jit(solution)/shard_map/ppermute | solution.py:51
  206.8 18.9 %copy-start.41 = (bf16[384,1024]{1,0:T(8,128)(2,1)S(1)}, bf16[384,1024]{1,0:T(8,128)(2,1)}, u32[]{:S(2)}) copy-start(bf16[384,1024]{1,0:T(8,128)(2,1)} %get-tuple-element.135) | copy-start | bytes 2359300
  206.8 19.6 %copy-start.29 = (bf16[2,2048,128]{2,1,0:T(8,128)(2,1)S(1)}, bf16[2,2048,128]{2,1,0:T(8,128)(2,1)}, u32[]{:S(2)}) copy-start(bf16[2,2048,128]{2,1,0:T(8,128)(2,1)} %copy-done.28) | copy-start | bytes 3145732
  206.8 19.6 %copy-start.33 = (bf16[2048,128]{1,0:T(8,128)(2,1)S(1)}, bf16[2048,128]{1,0:T(8,128)(2,1)}, u32[]{:S(2)}) copy-start(bf16[2048,128]{1,0:T(8,128)(2,1)} %copy-done.32) | copy-start | bytes 1572868
  225.7 17.1 %copy-start.43 = (bf16[384,1024]{1,0:T(8,128)(2,1)}, bf16[384,1024]{1,0:T(8,128)(2,1)S(1)}, u32[]{:S(2)}) copy-start(bf16[384,1024]{1,0:T(8,128)(2,1)S(1)} %collective-permute-done.13) | copy-start | bytes 2359300
  225.7 18.3 %collective-permute-start.15 = (bf16[384,1024]{1,0:T(8,128)(2,1)S(1)}, bf16[384,1024]{1,0:T(8,128)(2,1)S(1)}, u32[]{:S(2)}, u32[]{:S(2)}) collective-permute-start(bf16[384,1024]{1,0:T(8,128)(2,1)S(1)} %copy-done.41), channel_id=1, source_target_pairs={{0,2},{1,3},{2,0},{3,1},{4,6},{5,7},{6,4},{7,5},{8,10},{9,11},{10,... | collective-permute-start | bytes 2359304 | tf_op jit(solution)/shard_map/ppermute | solution.py:51
  226.4 27.9 %collective-permute-start.14 = (bf16[3,1024,128]{2,1,0:T(8,128)(2,1)}, bf16[3,1024,128]{2,1,0:T(8,128)(2,1)}, u32[]{:S(2)}, u32[]{:S(2)}) collective-permute-start(bf16[3,1024,128]{2,1,0:T(8,128)(2,1)} %get-tuple-element.132), channel_id=1, source_target_pairs={{0,1},{1,0},{2,3},{3,2},{4,5},{5,4},{6,7},{7,6},{8,9},{9,8},{10,11... | collective-permute-start | bytes 2359304 | tf_op jit(solution)/shard_map/ppermute | solution.py:47
  244.0 10.2 %collective-permute-start.16 = (bf16[3,1024,128]{2,1,0:T(8,128)(2,1)}, bf16[3,1024,128]{2,1,0:T(8,128)(2,1)}, u32[]{:S(2)}, u32[]{:S(2)}) collective-permute-start(bf16[3,1024,128]{2,1,0:T(8,128)(2,1)} %get-tuple-element.136), channel_id=1, source_target_pairs={{0,1},{1,0},{2,3},{3,2},{4,5},{5,4},{6,7},{7,6},{8,9},{9,8},{10,11... | collective-permute-start | bytes 2359304 | tf_op jit(solution)/shard_map/ppermute | solution.py:47
  246.3 22.5 %collective-permute-start.17 = (bf16[256,1024]{1,0:T(8,128)(2,1)}, bf16[256,1024]{1,0:T(8,128)(2,1)S(1)}, u32[]{:S(2)}, u32[]{:S(2)}) collective-permute-start(bf16[256,1024]{1,0:T(8,128)(2,1)} %get-tuple-element.141), channel_id=1, source_target_pairs={{0,2},{1,3},{2,0},{3,1},{4,6},{5,7},{6,4},{7,5},{8,10},{9,11},{10,... | collective-permute-start | bytes 1572872 | tf_op jit(solution)/shard_map/ppermute | solution.py:51
  255.4 13.4 %collective-permute-start.18 = (bf16[128,768]{1,0:T(8,128)(2,1)S(1)}, bf16[128,768]{1,0:T(8,128)(2,1)S(1)}, u32[]{:S(2)}, u32[]{:S(2)}) collective-permute-start(bf16[128,768]{1,0:T(8,128)(2,1)S(1)} %get-tuple-element.245), channel_id=1, source_target_pairs={{0,4},{8,0},{16,8},{24,16},{28,24},{20,28},{12,20},{4,12},{1,5},{9... | collective-permute-start | bytes 589832 | tf_op jit(solution)/shard_map/ppermute | solution.py:124
  257.9 11.6 %copy-start.47 = (bf16[256,1024]{1,0:T(8,128)(2,1)S(1)}, bf16[256,1024]{1,0:T(8,128)(2,1)}, u32[]{:S(2)}) copy-start(bf16[256,1024]{1,0:T(8,128)(2,1)} %get-tuple-element.141) | copy-start | bytes 1572868
  257.9 10.9 %collective-permute-start.19 = (bf16[128,768]{1,0:T(8,128)(2,1)S(1)}, bf16[128,768]{1,0:T(8,128)(2,1)S(1)}, u32[]{:S(2)}, u32[]{:S(2)}) collective-permute-start(bf16[128,768]{1,0:T(8,128)(2,1)S(1)} %get-tuple-element.244), channel_id=1, source_target_pairs={{0,8},{8,16},{16,24},{24,28},{28,20},{20,12},{12,4},{4,0},{1,9},{9... | collective-permute-start | bytes 589832 | tf_op jit(solution)/shard_map/ppermute | solution.py:123
  258.0 12.7 %copy-start.46 = (bf16[384,1024]{1,0:T(8,128)(2,1)S(1)}, bf16[384,1024]{1,0:T(8,128)(2,1)}, u32[]{:S(2)}) copy-start(bf16[384,1024]{1,0:T(8,128)(2,1)} %copy-done.45) | copy-start | bytes 2359300
  274.1 42.0 %collective-permute-start.20 = (bf16[1024,1024]{1,0:T(8,128)(2,1)S(1)}, bf16[1024,1024]{1,0:T(8,128)(2,1)}, u32[]{:S(2)}, u32[]{:S(2)}) collective-permute-start(bf16[1024,1024]{1,0:T(8,128)(2,1)S(1)} %pad_maximum_fusion.refs_0_), channel_id=1, source_target_pairs={{0,1},{1,0},{2,3},{3,2},{4,5},{5,4},{6,7},{7,6},{8,9},{9,8},{10,11... | collective-permute-start | bytes 6291464 | tf_op jit(solution)/shard_map/ppermute | solution.py:47
  276.1 14.6 %collective-permute-start.22 = (bf16[256,1024]{1,0:T(8,128)(2,1)}, bf16[256,1024]{1,0:T(8,128)(2,1)}, u32[]{:S(2)}, u32[]{:S(2)}) collective-permute-start(bf16[256,1024]{1,0:T(8,128)(2,1)} %get-tuple-element.160.refs_0_), channel_id=1, source_target_pairs={{0,2},{1,3},{2,0},{3,1},{4,6},{5,7},{6,4},{7,5},{8,10},{9,11},{10,... | collective-permute-start | bytes 1572872 | tf_op jit(solution)/shard_map/ppermute | solution.py:51
  282.5 9.3 %collective-permute-start.24 = (f32[10,1024]{1,0:T(8,128)S(1)}, f32[10,1024]{1,0:T(8,128)S(1)}, u32[]{:S(2)}, u32[]{:S(2)}) collective-permute-start(f32[10,1024]{1,0:T(8,128)S(1)} %concatenate.30), channel_id=1, source_target_pairs={{0,1},{1,0},{2,3},{3,2},{4,5},{5,4},{6,7},{7,6},{8,9},{9,8},{10,11... | collective-permute-start | bytes 122888 | tf_op jit(solution)/shard_map/ppermute | solution.py:47
  283.9 20.7 %copy-start.12 = (bf16[256,1024]{1,0:T(8,128)(2,1)S(1)}, bf16[256,1024]{1,0:T(8,128)(2,1)}, u32[]{:S(2)}) copy-start(bf16[256,1024]{1,0:T(8,128)(2,1)} %copy-done.11) | copy-start | bytes 1572868
  283.9 23.1 %copy-start.50 = (bf16[128,768]{1,0:T(8,128)(2,1)S(1)}, bf16[128,768]{1,0:T(8,128)(2,1)}, u32[]{:S(2)}) copy-start(bf16[128,768]{1,0:T(8,128)(2,1)} %copy-done.49) | copy-start | bytes 589828
  286.9 20.1 %collective-permute-start.35 = (bf16[128,768]{1,0:T(8,128)(2,1)S(1)}, bf16[128,768]{1,0:T(8,128)(2,1)}, u32[]{:S(2)}, u32[]{:S(2)}) collective-permute-start(bf16[128,768]{1,0:T(8,128)(2,1)S(1)} %add_convert_fusion.4), channel_id=1, source_target_pairs={{0,4},{8,0},{16,8},{24,16},{28,24},{20,28},{12,20},{4,12},{1,5},{9... | collective-permute-start | bytes 589832 | tf_op jit(solution)/shard_map/ppermute | solution.py:124
  290.7 13.9 %collective-permute-start.23 = (bf16[256,1024]{1,0:T(8,128)(2,1)}, bf16[256,1024]{1,0:T(8,128)(2,1)}, u32[]{:S(2)}, u32[]{:S(2)}) collective-permute-start(bf16[256,1024]{1,0:T(8,128)(2,1)} %get-tuple-element.161.refs_2_), channel_id=1, source_target_pairs={{0,2},{1,3},{2,0},{3,1},{4,6},{5,7},{6,4},{7,5},{8,10},{9,11},{10,... | collective-permute-start | bytes 1572872 | tf_op jit(solution)/shard_map/ppermute | solution.py:51
  304.6 16.3 %collective-permute-start.25 = (bf16[256,1024]{1,0:T(8,128)(2,1)S(1)}, bf16[256,1024]{1,0:T(8,128)(2,1)}, u32[]{:S(2)}, u32[]{:S(2)}) collective-permute-start(bf16[256,1024]{1,0:T(8,128)(2,1)S(1)} %copy-done.12), channel_id=1, source_target_pairs={{0,2},{1,3},{2,0},{3,1},{4,6},{5,7},{6,4},{7,5},{8,10},{9,11},{10,... | collective-permute-start | bytes 1572872 | tf_op jit(solution)/shard_map/ppermute | solution.py:51
  308.9 14.2 %collective-permute-start.38 = (bf16[128,768]{1,0:T(8,128)(2,1)}, bf16[128,768]{1,0:T(8,128)(2,1)}, u32[]{:S(2)}, u32[]{:S(2)}) collective-permute-start(bf16[128,768]{1,0:T(8,128)(2,1)} %get-tuple-element.167), channel_id=1, source_target_pairs={{0,8},{8,16},{16,24},{24,28},{28,20},{20,12},{12,4},{4,0},{1,9},{9... | collective-permute-start | bytes 589832 | tf_op jit(solution)/shard_map/ppermute | solution.py:123
  311.0 12.1 %collective-permute-start.36 = (bf16[128,768]{1,0:T(8,128)(2,1)S(1)}, bf16[128,768]{1,0:T(8,128)(2,1)}, u32[]{:S(2)}, u32[]{:S(2)}) collective-permute-start(bf16[128,768]{1,0:T(8,128)(2,1)S(1)} %get-tuple-element.165), channel_id=1, source_target_pairs={{0,4},{8,0},{16,8},{24,16},{28,24},{20,28},{12,20},{4,12},{1,5},{9... | collective-permute-start | bytes 589832 | tf_op jit(solution)/shard_map/ppermute | solution.py:124
  311.0 5.1 %collective-permute-start.28 = (f32[9,1024]{1,0:T(8,128)S(1)}, f32[9,1024]{1,0:T(8,128)S(1)}, u32[]{:S(2)}, u32[]{:S(2)}) collective-permute-start(f32[9,1024]{1,0:T(8,128)S(1)} %pad_maximum_fusion.2), channel_id=1, source_target_pairs={{0,4},{4,0},{8,12},{12,8},{16,20},{20,16},{24,28},{28,24},{1,5},{5... | collective-permute-start | bytes 110600 | tf_op jit(solution)/shard_map/ppermute | solution.py:852
  316.1 19.0 %copy-start.40 = (f32[128,3,256]{2,0,1:T(8,128)S(1)}, f32[128,3,256]{2,0,1:T(8,128)}, u32[]{:S(2)}) copy-start(f32[128,3,256]{2,0,1:T(8,128)} %param.26) | copy-start | bytes 1179652
  320.9 14.5 %copy-start.48 = (f32[128,3,256]{2,0,1:T(8,128)S(1)}, f32[128,3,256]{2,0,1:T(8,128)}, u32[]{:S(2)}) copy-start(f32[128,3,256]{2,0,1:T(8,128)} %param.27) | copy-start | bytes 1179652
  320.9 11.6 %collective-permute-start.29 = (bf16[256,1024]{1,0:T(8,128)(2,1)S(1)}, bf16[256,1024]{1,0:T(8,128)(2,1)S(1)}, u32[]{:S(2)}, u32[]{:S(2)}) collective-permute-start(bf16[256,1024]{1,0:T(8,128)(2,1)S(1)} %copy-done.14), channel_id=1, source_target_pairs={{0,2},{1,3},{2,0},{3,1},{4,6},{5,7},{6,4},{7,5},{8,10},{9,11},{10,... | collective-permute-start | bytes 1572872 | tf_op jit(solution)/shard_map/ppermute | solution.py:51
  325.2 5.7 %collective-permute-start.39 = (bf16[128,768]{1,0:T(8,128)(2,1)S(1)}, bf16[128,768]{1,0:T(8,128)(2,1)S(1)}, u32[]{:S(2)}, u32[]{:S(2)}) collective-permute-start(bf16[128,768]{1,0:T(8,128)(2,1)S(1)} %get-tuple-element.168), channel_id=1, source_target_pairs={{0,8},{8,16},{16,24},{24,28},{28,20},{20,12},{12,4},{4,0},{1,9},{9... | collective-permute-start | bytes 589832 | tf_op jit(solution)/shard_map/ppermute | solution.py:123
  326.7 4.3 %collective-permute-start.40 = (f32[9,1024]{1,0:T(8,128)S(1)}, f32[9,1024]{1,0:T(8,128)S(1)}, u32[]{:S(2)}, u32[]{:S(2)}) collective-permute-start(f32[9,1024]{1,0:T(8,128)S(1)} %add.273), channel_id=1, source_target_pairs={{0,8},{4,12},{8,0},{12,4},{16,24},{20,28},{24,16},{28,20},{1,9},{5... | collective-permute-start | bytes 110600 | tf_op jit(solution)/shard_map/ppermute | solution.py:852
  328.2 18.9 %collective-permute-start.33 = (bf16[256,1024]{1,0:T(8,128)(2,1)}, bf16[256,1024]{1,0:T(8,128)(2,1)}, u32[]{:S(2)}, u32[]{:S(2)}) collective-permute-start(bf16[256,1024]{1,0:T(8,128)(2,1)} %get-tuple-element.161.refs_2_), channel_id=1, source_target_pairs={{0,1},{1,0},{2,3},{3,2},{4,5},{5,4},{6,7},{7,6},{8,9},{9,8},{10,11... | collective-permute-start | bytes 1572872 | tf_op jit(solution)/shard_map/ppermute | solution.py:47
  328.2 19.0 %collective-permute-start.31 = (bf16[256,1024]{1,0:T(8,128)(2,1)}, bf16[256,1024]{1,0:T(8,128)(2,1)}, u32[]{:S(2)}, u32[]{:S(2)}) collective-permute-start(bf16[256,1024]{1,0:T(8,128)(2,1)} %get-tuple-element.160.refs_0_), channel_id=1, source_target_pairs={{0,1},{1,0},{2,3},{3,2},{4,5},{5,4},{6,7},{7,6},{8,9},{9,8},{10,11... | collective-permute-start | bytes 1572872 | tf_op jit(solution)/shard_map/ppermute | solution.py:47
  330.8 16.8 %collective-permute-start.32 = (bf16[256,1024]{1,0:T(8,128)(2,1)}, bf16[256,1024]{1,0:T(8,128)(2,1)}, u32[]{:S(2)}, u32[]{:S(2)}) collective-permute-start(bf16[256,1024]{1,0:T(8,128)(2,1)} %collective-permute-done.22.refs_1_), channel_id=1, source_target_pairs={{0,1},{1,0},{2,3},{3,2},{4,5},{5,4},{6,7},{7,6},{8,9},{9,8},{10,11... | collective-permute-start | bytes 1572872 | tf_op jit(solution)/shard_map/ppermute | solution.py:47
  331.0 16.7 %collective-permute-start.34 = (bf16[256,1024]{1,0:T(8,128)(2,1)}, bf16[256,1024]{1,0:T(8,128)(2,1)}, u32[]{:S(2)}, u32[]{:S(2)}) collective-permute-start(bf16[256,1024]{1,0:T(8,128)(2,1)} %collective-permute-done.23.refs_3_), channel_id=1, source_target_pairs={{0,1},{1,0},{2,3},{3,2},{4,5},{5,4},{6,7},{7,6},{8,9},{9,8},{10,11... | collective-permute-start | bytes 1572872 | tf_op jit(solution)/shard_map/ppermute | solution.py:47
  332.6 6.7 %collective-permute-start.37 = (bf16[128,768]{1,0:T(8,128)(2,1)}, bf16[128,768]{1,0:T(8,128)(2,1)}, u32[]{:S(2)}, u32[]{:S(2)}) collective-permute-start(bf16[128,768]{1,0:T(8,128)(2,1)} %get-tuple-element.166), channel_id=1, source_target_pairs={{0,4},{8,0},{16,8},{24,16},{28,24},{20,28},{12,20},{4,12},{1,5},{9... | collective-permute-start | bytes 589832 | tf_op jit(solution)/shard_map/ppermute | solution.py:124
  339.2 12.5 %collective-permute-start.41 = (f32[9,1024]{1,0:T(8,128)S(1)}, f32[9,1024]{1,0:T(8,128)S(1)}, u32[]{:S(2)}, u32[]{:S(2)}) collective-permute-start(f32[9,1024]{1,0:T(8,128)S(1)} %add.287), channel_id=1, source_target_pairs={{0,16},{4,20},{8,24},{12,28},{16,0},{20,4},{24,8},{28,12},{1,17},{... | collective-permute-start | bytes 110600 | tf_op jit(solution)/shard_map/ppermute | solution.py:852
  347.0 23.5 %collective-permute-start.27 = (bf16[256,1024]{1,0:T(8,128)(2,1)S(1)}, bf16[256,1024]{1,0:T(8,128)(2,1)S(1)}, u32[]{:S(2)}, u32[]{:S(2)}) collective-permute-start(bf16[256,1024]{1,0:T(8,128)(2,1)S(1)} %copy-done.14), channel_id=1, source_target_pairs={{0,1},{1,0},{2,3},{3,2},{4,5},{5,4},{6,7},{7,6},{8,9},{9,8},{10,11... | collective-permute-start | bytes 1572872 | tf_op jit(solution)/shard_map/ppermute | solution.py:47
  347.1 23.5 %collective-permute-start.21 = (bf16[256,1024]{1,0:T(8,128)(2,1)S(1)}, bf16[256,1024]{1,0:T(8,128)(2,1)}, u32[]{:S(2)}, u32[]{:S(2)}) collective-permute-start(bf16[256,1024]{1,0:T(8,128)(2,1)S(1)} %copy-done.12), channel_id=1, source_target_pairs={{0,1},{1,0},{2,3},{3,2},{4,5},{5,4},{6,7},{7,6},{8,9},{9,8},{10,11... | collective-permute-start | bytes 1572872 | tf_op jit(solution)/shard_map/ppermute | solution.py:47
  347.6 23.0 %collective-permute-start.26 = (bf16[256,1024]{1,0:T(8,128)(2,1)}, bf16[256,1024]{1,0:T(8,128)(2,1)}, u32[]{:S(2)}, u32[]{:S(2)}) collective-permute-start(bf16[256,1024]{1,0:T(8,128)(2,1)} %collective-permute-done.25.refs_1_), channel_id=1, source_target_pairs={{0,1},{1,0},{2,3},{3,2},{4,5},{5,4},{6,7},{7,6},{8,9},{9,8},{10,11... | collective-permute-start | bytes 1572872 | tf_op jit(solution)/shard_map/ppermute | solution.py:47
  351.2 19.4 %collective-permute-start.30 = (bf16[256,1024]{1,0:T(8,128)(2,1)S(1)}, bf16[256,1024]{1,0:T(8,128)(2,1)}, u32[]{:S(2)}, u32[]{:S(2)}) collective-permute-start(bf16[256,1024]{1,0:T(8,128)(2,1)S(1)} %collective-permute-done.29.refs_3_), channel_id=1, source_target_pairs={{0,1},{1,0},{2,3},{3,2},{4,5},{5,4},{6,7},{7,6},{8,9},{9,8},{10,11... | collective-permute-start | bytes 1572872 | tf_op jit(solution)/shard_map/ppermute | solution.py:47
  351.8 14.2 %copy-start.9 = (f32[4,256,128]{2,1,0:T(8,128)S(1)}, f32[4,256,128]{2,1,0:T(8,128)}, u32[]{:S(2)}) copy-start(f32[4,256,128]{2,1,0:T(8,128)} %param.35) | copy-start | bytes 1572868
  351.8 4.0 %collective-permute-start.42 = (f32[7,1024]{1,0:T(8,128)S(1)}, f32[7,1024]{1,0:T(8,128)S(1)}, u32[]{:S(2)}, u32[]{:S(2)}) collective-permute-start(f32[7,1024]{1,0:T(8,128)S(1)} %slice.191), channel_id=1, source_target_pairs={{0,2},{1,3},{2,0},{3,1},{4,6},{5,7},{6,4},{7,5},{8,10},{9,11},{10,... | collective-permute-start | bytes 86024 | tf_op jit(solution)/shard_map/ppermute | solution.py:51
  359.1 14.9 %collective-permute-start.43 = (bf16[128,256]{1,0:T(8,128)(2,1)S(1)}, bf16[128,256]{1,0:T(8,128)(2,1)S(1)}, u32[]{:S(2)}, u32[]{:S(2)}) collective-permute-start(bf16[128,256]{1,0:T(8,128)(2,1)S(1)} %slice.195), channel_id=1, source_target_pairs={{0,2},{1,3},{2,0},{3,1},{4,6},{5,7},{6,4},{7,5},{8,10},{9,11},{10,... | collective-permute-start | bytes 196616 | tf_op jit(solution)/shard_map/ppermute | solution.py:51
  (42 other events, 183.1 us)
Sparse Core Ops, SparseCore 0:
  14.8 98.8 all-gather.1
  206.5 111.1 reduce-scatter.1

commit v4 on v3

--- a/solution.py
+++ b/solution.py
@@ -851,20 +851,20 @@
     small = jnp.concatenate([rows, columns], axis=0)
     meet = lambda x, step: x + lax.ppermute(x, "dp", [(i, i ^ step) for i in range(n_dp)])
     outputs = finish(scalars, 0, [[own_low]], (), 0, 1)
+    outputs = finish(scalars, 1, [[to_core(own_low)]], (outputs,), 0, 1)
     ig_far.append(to_chip(after(igs[2], ig_far[1], outputs, small)))
     qkv_ring.hop(ig_far[1])
     small = meet(after(small, ig_far[1]), 1)
-    outputs = finish(scalars, 1, [[to_core(own_low)]], (outputs,), 0, 1)
     ig_cross = [to_core(x) for x in ig_far[:2]]
     front, back = slice(0, 2), slice(2, 4)
     input_grad = finish(scalars, 0, list(zip(igs, ig_far))[front])
-    ig_far.append(to_chip(after(igs[3], ig_far[2], outputs, input_grad, small)))
+    input_grad = finish(scalars, 1, list(zip(ig_sib, ig_cross))[front], (input_grad,))
+    ig_far.append(to_chip(after(igs[3], ig_far[2], input_grad, small)))
     qkv_shard = after(qkv_ring.finish(), ig_far[2])
     step = 2
     while step < n_dp:
         small = meet(after(small, *ig_far[2 : step]), step)
         step *= 2
-    input_grad = finish(scalars, 1, list(zip(ig_sib, ig_cross))[front], (input_grad,))
     up_shard = shard[:, :hidden].astype(F32)
     down_shard = shard[:, hidden : 2 * hidden].astype(F32)
     out_mine = shard[:, 2 * hidden : 2 * hidden + width]
@@ -879,7 +879,7 @@
     input_grad = after(input_grad, ig_far[3], up_new[0], down_new[0], qkv_new[0])
     input_grad = finish(scalars, 0, list(zip(igs, ig_far))[back], (input_grad,), 2)
     input_grad = finish(scalars, 1, list(zip(ig_sib, ig_cross))[back], (input_grad,), 2)
-    rows = small[:7] + to_chip(after(small[:7], ig_far[3]))
+    rows = small[:7] + to_chip(after(small[:7], ig_far[3], up_new[0], down_new[0], qkv_new[0]))
     small = jnp.concatenate([rows, small[7:]], axis=0)
     row_total, stat_total = small[:6], small[6]
     col_total = jnp.concatenate(

time: 388 us -> 380 us (0.979)
  waiting for transfers between devices: 62.5 us -> 58.4 us
  transfers between devices with their start and end apart: 48 -> 48, of which waited for: 17 -> 14; matrix products, arithmetic and copies ran while one was open for 10% -> 10% of each run, Pallas kernels for 33% -> 33%
where the time goes in v4:
time: 380 us; the launch traced here: 375 us
  Pallas kernels  162 us (43%)
  waiting for transfers between devices  58.4 us (15%)
  starting transfers between devices  53.8 us (14%)
  other arithmetic  29.5 us (8%)
  local copies, waits for them, and re-layouts  28.3 us (7%)
  between operations  25.5 us (7%)
  blocking collectives  17.8 us (5%)
    pallas_call x1, Pallas kernels, middle(): pl.pallas_call(functools.partial(middle_kernel, chunk=chunk), out_shape=[...  35.9 us
    pallas_call x2, Pallas kernels, attend_backward(): pl.pallas_call(functools.partial(attend_backward_kernel, bk=min(256, span...  33 us
    unnamed x127, local copies, waits for them, and re-layouts  23.4 us
    pallas_call x2, Pallas kernels, attend_forward(): pl.pallas_call(functools.partial(attend_forward_kernel, bq=min(512, span)...  21 us
    pallas_call x6, Pallas kernels, finish(): pl.pallas_call(functools.partial(finish_kernel, pieces=len(pieces), terms...  21 us
    ppermute x10, waiting for transfers between devices, to_chip(): lax.ppermute(x, 'mp', [(i, i ^ 2) for i in range(lax.axis_size('mp'))])  20 us
    all_to_all x1, blocking collectives, to_all(): return lax.all_to_all(x, 'mp', split_axis=0, concat_axis=0, tiled=True)  17.8 us
    pallas_call x1, Pallas kernels, weight_grads(): pl.pallas_call(functools.partial(weight_grads_kernel, chunks=chunks), out...  17.5 us
  transfers between devices with their start and end apart: 48, of which 14 were waited for; matrix products, arithmetic and copies ran while one was open for 10% of the time, Pallas kernels for 33%

profile of v4, /device:TPU:0, one launch (start us, length us, event | category | flops | bytes accessed | tf_op | source)
XLA Modules:
  0.0 375.4 jit_solution(17981124907288798944)
XLA Ops:
  8.2 3.0 collective-permute-start.8
  15.0 1.9 collective-permute-start.4
  17.1 3.0 convert_reduce_fusion
  21.0 1.4 fusion.2
  22.4 1.9 collective-permute-start.5
  24.4 3.0 fusion.5.n_ref
  28.1 5.2 %collective-permute-done.5.refs_6_ = bf16[128,768]{1,0:T(8,128)(2,1)S(1)} collective-permute-done((bf16[128,768]{1,0:T(8,128)(2,1)S(1)}, bf16[128,768]{1,0:T(8,128)(2,1)S(1)}, u32[]{:S(2)}, u32[]{:S(2)}) %collective-permute-start.5) | collective-permute-done | bytes 196640 | tf_op jit(solution)/shard_map/ppermute | solution.py:88
  33.2 4.7 %collective-permute-start.6 = (bf16[128,768]{1,0:T(8,128)(2,1)S(1)}, bf16[128,768]{1,0:T(8,128)(2,1)S(1)}, u32[]{:S(2)}, u32[]{:S(2)}) collective-permute-start(bf16[128,768]{1,0:T(8,128)(2,1)S(1)} %collective-permute-done.5.refs_6_), channel_id=1, source_target_pairs={{0,8},{8,16},{16,24},{24,28},{28,20},{20,12},{12,4},{4,0},{1,9},{9... | collective-permute-start | bytes 589832 | tf_op jit(solution)/shard_map/ppermute | solution.py:88
  38.6 5.5 %collective-permute-done.2.refs_2_ = bf16[128,768]{1,0:T(8,128)(2,1)S(1)} collective-permute-done((bf16[128,768]{1,0:T(8,128)(2,1)S(1)}, bf16[128,768]{1,0:T(8,128)(2,1)S(1)}, u32[]{:S(2)}, u32[]{:S(2)}) %collective-permute-start.2) | collective-permute-done | bytes 196640 | tf_op jit(solution)/shard_map/ppermute | solution.py:90
  44.2 2.1 collective-permute-done.6.refs_5_
  46.3 8.9 %collective-permute-start.7 = (bf16[128,768]{1,0:T(8,128)(2,1)S(1)}, bf16[128,768]{1,0:T(8,128)(2,1)S(1)}, u32[]{:S(2)}, u32[]{:S(2)}) collective-permute-start(bf16[128,768]{1,0:T(8,128)(2,1)S(1)} %collective-permute-done.6.refs_5_), channel_id=1, source_target_pairs={{0,8},{8,16},{16,24},{24,28},{28,20},{20,12},{12,4},{4,0},{1,9},{9... | collective-permute-start | bytes 589832 | tf_op jit(solution)/shard_map/ppermute | solution.py:88
  57.2 1.4 collective-permute-done.7.refs_4_
  58.5 2.2 copy-done.6
  60.7 8.4 %project.1 = (bf16[4,2048,128]{2,1,0:T(8,128)(2,1)S(1)}, bf16[4,2048,128]{2,1,0:T(8,128)(2,1)S(1)}, bf16[4,2048,128]{2,1,0:T(8,128)(2,1)S(1)}, bf16[1024,768]{1,0:T(8,128)(2,1)}) custom-call(s32[8]{0:T(128)S(1)} %gather_fusion, f32[4]{0:T(128)S(1)} %multiply_exponential_fusion.slope_ref, s32[1]{0:T(128)} %copy.76.length_ref, ...), custom_call_target="tpu_custom_call" | custom-call | flops 3221225472 | bytes 12582912 | tf_op jit(solution)/shard_map/project/pallas_call | solution.py:202
  69.1 1.3 copy-done.25
  70.5 1.3 copy-done.26
  71.8 1.3 copy-done.27
  73.1 11.0 %attend_forward.2 = (bf16[2048,128]{1,0:T(8,128)(2,1)S(1)}, bf16[2,2048,128]{2,1,0:T(8,128)(2,1)S(1)}, bf16[4,1024,128]{2,1,0:T(8,128)(2,1)}) custom-call(bf16[4,2048,128]{2,1,0:T(8,128)(2,1)} %copy-done.27, bf16[4,2048,128]{2,1,0:T(8,128)(2,1)} %copy-done.25, bf16[4,2048,128]{2,1,0:T(8,128)(2,1)} %copy-done.26), custom_call_target="tpu_custom_call" | custom-call | flops 12000000000 | bytes 5242880 | tf_op jit(solution)/shard_map/attend_forward/pallas_call | solution.py:252
  85.9 3.7 all-to-all-start
  89.6 10.0 %attend_forward.3 = (bf16[2048,128]{1,0:T(8,128)(2,1)S(1)}, bf16[2,2048,128]{2,1,0:T(8,128)(2,1)S(1)}, bf16[4,1024,128]{2,1,0:T(8,128)(2,1)S(1)}) custom-call(bf16[4,2048,128]{2,1,0:T(8,128)(2,1)} %copy-done.27, bf16[4,2048,128]{2,1,0:T(8,128)(2,1)} %copy-done.25, bf16[4,2048,128]{2,1,0:T(8,128)(2,1)} %copy-done.26), custom_call_target="tpu_custom_call" | custom-call | flops 12000000000 | bytes 5242880 | tf_op jit(solution)/shard_map/attend_forward/pallas_call | solution.py:252
  100.4 3.6 all-to-all-done.o0_ref.refs_2_.refs_4_.refs_7_.refs_9_
  104.0 17.8 %all_to_all.15.o1_ref.refs_3_.refs_5_.refs_8_.refs_10_ = bf16[4,1024,128]{2,1,0:T(8,128)(2,1)} all-to-all(bf16[4,1024,128]{2,1,0:T(8,128)(2,1)S(1)} %get-tuple-element.108), channel_id=1, replica_groups=mesh['dp'=8,'mp'=4] {'mp'}, dimensions={0} | all-to-all | bytes 2097152 | tf_op jit(solution)/shard_map/all_to_all | solution.py:55
  122.9 10.1 %collective-permute-done.10.w_sib_ref = bf16[1024,768]{1,0:T(8,128)(2,1)} collective-permute-done((bf16[1024,768]{1,0:T(8,128)(2,1)}, bf16[1024,768]{1,0:T(8,128)(2,1)}, u32[]{:S(2)}, u32[]{:S(2)}) %collective-permute-start.10) | collective-permute-done | bytes 1572896 | tf_op jit(solution)/shard_map/ppermute | solution.py:47
  133.0 35.9 %middle.1 = (bf16[384,1024]{1,0:T(8,128)(2,1)}, bf16[384,1024]{1,0:T(8,128)(2,1)}, bf16[256,1024]{1,0:T(8,128)(2,1)}, bf16[1024,1024]{1,0:T(8,128)(2,1)}, bf16[1...) custom-call(s32[4]{0:T(128)} %pad_add_fusion.scalar_ref.refs_0_.half, ...), custom_call_target="tpu_custom_call" | custom-call | flops 20999999488 | bytes 25165824 | tf_op jit(solution)/shard_map/middle/pallas_call | solution.py:453
  169.2 1.2 copy-done.1
  170.4 1.6 copy-done.4
  172.0 3.6 out_grads.1
  176.0 4.6 %all-to-all-start.2 = ((bf16[4,1024,256]{2,1,0:T(8,128)(2,1)}), bf16[4,1024,256]{2,1,0:T(8,128)(2,1)}, u32[]{:S(2)}, u32[]{:S(2)}) async-start(bf16[4,1024,256]{2,1,0:T(8,128)(2,1)} %get-tuple-element.118), calls=%async_computation.2 | async-start | bytes 4194304 | tf_op jit(solution)/shard_map/all_to_all | solution.py:55
  180.9 17.5 %weight_grads.1 = bf16[1024,2560]{1,0:T(8,128)(2,1)} custom-call(s32[4]{0:T(128)S(1)} %copy-done.23, f32[2048,1024]{1,0:T(8,128)} %cot_ref.3, bf16[1024,3072]{1,0:T(8,128)(2,1)} %get-tuple-element.114.refs_0_, bf16[1024,1024]{1,0:T(8,128)(2,1)} %get-tuple-element.115.refs_1_, bf16[1024,1024]{1,0:T(8,128)(2,1)} %get-tuple-element.116.refs_2_, ...), custom_call_target="tpu_custom_call" | custom-call | flops 9663676416 | bytes 31457280 | tf_op jit(solution)/shard_map/weight_grads/pallas_call | solution.py:599
  198.5 7.9 %all-to-all-done.2.refs_0_ = bf16[4,1024,256]{2,1,0:T(8,128)(2,1)} async-done(((bf16[4,1024,256]{2,1,0:T(8,128)(2,1)}), bf16[4,1024,256]{2,1,0:T(8,128)(2,1)}, u32[]{:S(2)}, u32[]{:S(2)}) %all-to-all-start.2) | async-done | bytes 2097184 | tf_op jit(solution)/shard_map/all_to_all | solution.py:55
  206.8 16.5 %attend_backward.2 = (bf16[3,2048,128]{2,1,0:T(8,128)(2,1)S(1)}, bf16[3,1024,128]{2,1,0:T(8,128)(2,1)}, f32[2,128]{1,0:T(2,128)S(1)}) custom-call(s32[4]{0:T(128)S(1)} %copy-done.23, bf16[2,2048,128]{2,1,0:T(8,128)(2,1)S(1)} %copy-done.31, bf16[4,2048,128]{2,1,0:T(8,128)(2,1)} %copy-done.25, bf16[4,2048,128]{2,1,0:T(8,128)(2,1)} %copy-done.26, ...), custom_call_target="tpu_custom_call" | custom-call | flops 17999998976 | bytes 6291456 | tf_op jit(solution)/shard_map/attend_backward/pallas_call | solution.py:317
  223.3 2.4 collective-permute-done.13
  226.4 16.5 %attend_backward.3 = (bf16[3,2048,128]{2,1,0:T(8,128)(2,1)S(1)}, bf16[3,1024,128]{2,1,0:T(8,128)(2,1)}, f32[2,128]{1,0:T(2,128)S(1)}) custom-call(s32[4]{0:T(128)S(1)} %copy-done.23, bf16[2,2048,128]{2,1,0:T(8,128)(2,1)S(1)} %copy-done.29, bf16[4,2048,128]{2,1,0:T(8,128)(2,1)} %copy-done.25, bf16[4,2048,128]{2,1,0:T(8,128)(2,1)} %copy-done.26, ...), custom_call_target="tpu_custom_call" | custom-call | flops 17999998976 | bytes 6291456 | tf_op jit(solution)/shard_map/attend_backward/pallas_call | solution.py:317
  242.8 1.2 collective-permute-done.15
  247.3 2.2 copy-done.7
  249.5 4.7 %qkv_grads.1 = bf16[1024,768]{1,0:T(8,128)(2,1)S(1)} custom-call(bf16[2048,1024]{1,0:T(8,128)(2,1)S(1)} %copy-done.7, bf16[3,2048,128]{2,1,0:T(8,128)(2,1)S(1)} %get-tuple-element.124.p0_ref.o0_ref, bf16[3,2048,128]{2,1,0:T(8,128)(2,1)S(1)} %get-tuple-element.130.p1_ref.o1_ref), custom_call_target="tpu_custom_call" | custom-call | flops 3221225472 | bytes 10485760 | tf_op jit(solution)/shard_map/qkv_grads/pallas_call | solution.py:635
  255.4 2.5 collective-permute-start.18
  258.0 10.7 %last.1 = (bf16[256,1024]{1,0:T(8,128)(2,1)}, bf16[256,1024]{1,0:T(8,128)(2,1)}, bf16[256,1024]{1,0:T(8,128)(2,1)S(1)}, bf16[256,1024]{1,0:T(8,128)(2,1)S(1)}, f32[8,1024]{1,0:T(8,128)S(1)}) custom-call(s32[4]{0:T(128)S(1)} %copy-done.23, bf16[3,2048,128]{2,1,0:T(8,128)(2,1)S(1)} %get-tuple-element.124.p0_ref.o0_ref, ...), custom_call_target="tpu_custom_call" | custom-call | flops 3200000000 | bytes 20971520 | tf_op jit(solution)/shard_map/last/pallas_call | solution.py:512
  269.5 1.2 fusion.11
  270.8 3.2 fusion.7
  277.2 3.0 finish.6.refs_1_
  284.1 1.4 select_maximum_fusion.3
  287.4 3.3 collective-permute-done.22.refs_1_
  290.7 1.6 collective-permute-start.35
  292.3 1.2 collective-permute-start.23
  293.5 12.4 %collective-permute-done.23.refs_3_ = bf16[256,1024]{1,0:T(8,128)(2,1)} collective-permute-done((bf16[256,1024]{1,0:T(8,128)(2,1)}, bf16[256,1024]{1,0:T(8,128)(2,1)}, u32[]{:S(2)}, u32[]{:S(2)}) %collective-permute-start.23) | collective-permute-done | bytes 524320 | tf_op jit(solution)/shard_map/ppermute | solution.py:51
  306.4 4.8 %finish.7 = f32[2048,1024]{1,0:T(8,128)} custom-call(s32[4]{0:T(128)S(1)} %copy-done.23, bf16[1024,1024]{1,0:T(8,128)(2,1)} %collective-permute-done.20.refs_0_, f32[2048,1024]{1,0:T(8,128)} %finish.6.refs_1_), custom_call_target="tpu_custom_call", output_to_operand_aliasing={{}: (2, {})} | custom-call | bytes 8388608 | tf_op jit(solution)/shard_map/finish/pallas_call | solution.py:664
  311.2 1.2 collective-permute-start.25
  313.6 1.5 collective-permute-start.32
  315.1 2.0 add_convert_fusion.3
  318.0 1.4 collective-permute-start.36
  319.4 3.5 finish.8.refs_4_
  323.0 3.4 finish.9.refs_4_
  328.7 2.0 add_convert_fusion.2
  331.2 1.7 collective-permute-start.37
  334.7 1.3 copy.65.v_ref
  336.0 2.2 collective-permute-done.40
  338.9 2.2 collective-permute-start.41
  342.2 1.3 adam.6
  346.6 1.2 slice_convert_fusion
  350.0 2.5 adam.4
  352.5 1.6 adam.5
  356.6 3.0 finish.10.refs_4_
  360.7 3.4 finish.11
  (240 shorter events, 41.0 us)
Async XLA Ops:
  7.2 114.6 %all-gather.2.cloned.1.call-start = ((), (), s32[]{:S(2)}) async-start(), calls=%async_computation.4 | async-start | bytes 5898240 | tf_op jit(solution)/shard_map/all_gather | solution.py:759
  8.2 5.5 %collective-permute-start.8 = (bf16[128,256]{1,0:T(8,128)(2,1)S(1)}, bf16[128,256]{1,0:T(8,128)(2,1)S(1)}, u32[]{:S(2)}, u32[]{:S(2)}) collective-permute-start(bf16[128,256]{1,0:T(8,128)(2,1)S(1)} %bitcast.62), channel_id=1, source_target_pairs={{0,2},{1,3},{2,0},{3,1},{4,6},{5,7},{6,4},{7,5},{8,10},{9,11},{10,... | collective-permute-start | bytes 196616 | tf_op jit(solution)/shard_map/ppermute | solution.py:51
  15.0 7.5 %collective-permute-start.4 = (bf16[128,768]{1,0:T(8,128)(2,1)S(1)}, bf16[128,768]{1,0:T(8,128)(2,1)S(1)}, u32[]{:S(2)}, u32[]{:S(2)}) collective-permute-start(bf16[128,768]{1,0:T(8,128)(2,1)S(1)} %copy.60.refs_0_), channel_id=1, source_target_pairs={{0,8},{8,16},{16,24},{24,28},{28,20},{20,12},{12,4},{4,0},{1,9},{9... | collective-permute-start | bytes 589832 | tf_op jit(solution)/shard_map/ppermute | solution.py:88
  16.9 11.0 %collective-permute-start.1 = (bf16[128,768]{1,0:T(8,128)(2,1)S(1)}, bf16[128,768]{1,0:T(8,128)(2,1)S(1)}, u32[]{:S(2)}, u32[]{:S(2)}) collective-permute-start(bf16[128,768]{1,0:T(8,128)(2,1)S(1)} %copy.60.refs_0_), channel_id=1, source_target_pairs={{0,4},{8,0},{16,8},{24,16},{28,24},{20,28},{12,20},{4,12},{1,5},{9... | collective-permute-start | bytes 589832 | tf_op jit(solution)/shard_map/ppermute | solution.py:90
  17.1 39.5 %collective-permute-start = (f32[1,1024]{1,0:T(1,128)S(1)}, f32[1,1024]{1,0:T(1,128)S(1)}, u32[]{:S(2)}, u32[]{:S(2)}) collective-permute-start(f32[1,1024]{1,0:T(1,128)S(1)} %bitcast.72), channel_id=1, source_target_pairs={{0,1},{1,0},{2,3},{3,2},{4,5},{5,4},{6,7},{7,6},{8,9},{9,8},{10,11... | collective-permute-start | bytes 12296 | tf_op jit(solution)/shard_map/ppermute | solution.py:47
  22.4 10.8 %collective-permute-start.5 = (bf16[128,768]{1,0:T(8,128)(2,1)S(1)}, bf16[128,768]{1,0:T(8,128)(2,1)S(1)}, u32[]{:S(2)}, u32[]{:S(2)}) collective-permute-start(bf16[128,768]{1,0:T(8,128)(2,1)S(1)} %collective-permute-done.4.refs_7_), channel_id=1, source_target_pairs={{0,8},{8,16},{16,24},{24,28},{28,20},{20,12},{12,4},{4,0},{1,9},{9... | collective-permute-start | bytes 589832 | tf_op jit(solution)/shard_map/ppermute | solution.py:88
  24.4 31.5 %copy-start.36 = (s32[8]{0:T(128)S(1)}, s32[8]{0:T(128)}, u32[]{:S(2)}) copy-start(s32[8]{0:T(128)} %constant.99.clone) | copy-start | bytes 100
  27.9 16.2 %collective-permute-start.2 = (bf16[128,768]{1,0:T(8,128)(2,1)S(1)}, bf16[128,768]{1,0:T(8,128)(2,1)S(1)}, u32[]{:S(2)}, u32[]{:S(2)}) collective-permute-start(bf16[128,768]{1,0:T(8,128)(2,1)S(1)} %collective-permute-done.1.refs_1_), channel_id=1, source_target_pairs={{0,4},{8,0},{16,8},{24,16},{28,24},{20,28},{12,20},{4,12},{1,5},{9... | collective-permute-start | bytes 589832 | tf_op jit(solution)/shard_map/ppermute | solution.py:90
  33.2 13.1 %collective-permute-start.6 = (bf16[128,768]{1,0:T(8,128)(2,1)S(1)}, bf16[128,768]{1,0:T(8,128)(2,1)S(1)}, u32[]{:S(2)}, u32[]{:S(2)}) collective-permute-start(bf16[128,768]{1,0:T(8,128)(2,1)S(1)} %collective-permute-done.5.refs_6_), channel_id=1, source_target_pairs={{0,8},{8,16},{16,24},{24,28},{28,20},{20,12},{12,4},{4,0},{1,9},{9... | collective-permute-start | bytes 589832 | tf_op jit(solution)/shard_map/ppermute | solution.py:88
  44.2 13.0 %collective-permute-start.3 = (bf16[128,768]{1,0:T(8,128)(2,1)S(1)}, bf16[128,768]{1,0:T(8,128)(2,1)S(1)}, u32[]{:S(2)}, u32[]{:S(2)}) collective-permute-start(bf16[128,768]{1,0:T(8,128)(2,1)S(1)} %collective-permute-done.2.refs_2_), channel_id=1, source_target_pairs={{0,4},{8,0},{16,8},{24,16},{28,24},{20,28},{12,20},{4,12},{1,5},{9... | collective-permute-start | bytes 589832 | tf_op jit(solution)/shard_map/ppermute | solution.py:90
  46.3 12.2 %collective-permute-start.7 = (bf16[128,768]{1,0:T(8,128)(2,1)S(1)}, bf16[128,768]{1,0:T(8,128)(2,1)S(1)}, u32[]{:S(2)}, u32[]{:S(2)}) collective-permute-start(bf16[128,768]{1,0:T(8,128)(2,1)S(1)} %collective-permute-done.6.refs_5_), channel_id=1, source_target_pairs={{0,8},{8,16},{16,24},{24,28},{28,20},{20,12},{12,4},{4,0},{1,9},{9... | collective-permute-start | bytes 589832 | tf_op jit(solution)/shard_map/ppermute | solution.py:88
  85.9 18.1 %all-to-all-start = ((bf16[4,1024,128]{2,1,0:T(8,128)(2,1)}), bf16[4,1024,128]{2,1,0:T(8,128)(2,1)S(1)}, u32[]{:S(2)}, u32[]{:S(2)}) async-start(bf16[4,1024,128]{2,1,0:T(8,128)(2,1)} %get-tuple-element.106), calls=%async_computation | async-start | bytes 2097152 | tf_op jit(solution)/shard_map/all_to_all | solution.py:55
  100.4 68.6 %copy-start.28 = (bf16[2,2048,128]{2,1,0:T(8,128)(2,1)}, bf16[2,2048,128]{2,1,0:T(8,128)(2,1)S(1)}, u32[]{:S(2)}) copy-start(bf16[2,2048,128]{2,1,0:T(8,128)(2,1)S(1)} %get-tuple-element.128.q_ref) | copy-start | bytes 3145732
  104.0 29.1 %copy-start = (bf16[4,1024,128]{2,1,0:T(8,128)(2,1)}, bf16[4,1024,128]{2,1,0:T(8,128)(2,1)S(1)}, u32[]{:S(2)}) copy-start(bf16[4,1024,128]{2,1,0:T(8,128)(2,1)S(1)} %all-to-all-done.o0_ref.refs_2_.refs_4_.refs_7_.refs_9_) | copy-start | bytes 3145732
  121.8 11.3 %collective-permute-start.9 = (bf16[1024,2560]{1,0:T(8,128)(2,1)}, bf16[1024,2560]{1,0:T(8,128)(2,1)}, u32[]{:S(2)}, u32[]{:S(2)}) collective-permute-start(bf16[1024,2560]{1,0:T(8,128)(2,1)} %all-gather.2.cloned.1.call-done.late_own_ref), channel_id=1, source_target_pairs={{0,1},{1,0},{2,3},{3,2},{4,5},{5,4},{6,7},{7,6},{8,9},{9,8},{10,11... | collective-permute-start | bytes 15728648 | tf_op jit(solution)/shard_map/ppermute | solution.py:47
  121.8 11.2 %collective-permute-start.10 = (bf16[1024,768]{1,0:T(8,128)(2,1)}, bf16[1024,768]{1,0:T(8,128)(2,1)}, u32[]{:S(2)}, u32[]{:S(2)}) collective-permute-start(bf16[1024,768]{1,0:T(8,128)(2,1)} %get-tuple-element.110.w_own_ref), channel_id=1, source_target_pairs={{0,1},{1,0},{2,3},{3,2},{4,5},{5,4},{6,7},{7,6},{8,9},{9,8},{10,11... | collective-permute-start | bytes 4718600 | tf_op jit(solution)/shard_map/ppermute | solution.py:47
  122.9 46.3 %copy-start.3 = (bf16[4,1024,128]{2,1,0:T(8,128)(2,1)S(1)}, bf16[4,1024,128]{2,1,0:T(8,128)(2,1)}, u32[]{:S(2)}) copy-start(bf16[4,1024,128]{2,1,0:T(8,128)(2,1)} %all_to_all.15.o1_ref.refs_3_.refs_5_.refs_8_.refs_10_) | copy-start | bytes 3145732
  122.9 46.3 %copy-start.23 = (s32[4]{0:T(128)S(1)}, s32[4]{0:T(128)}, u32[]{:S(2)}) copy-start(s32[4]{0:T(128)} %pad_add_fusion.scalar_ref.refs_0_.half_ref) | copy-start | bytes 52
  169.0 11.9 %collective-permute-start.11 = (bf16[1024,3072]{1,0:T(8,128)(2,1)}, bf16[1024,3072]{1,0:T(8,128)(2,1)}, u32[]{:S(2)}, u32[]{:S(2)}) collective-permute-start(bf16[1024,3072]{1,0:T(8,128)(2,1)} %get-tuple-element.114.refs_0_), channel_id=1, source_target_pairs={{0,1},{1,0},{2,3},{3,2},{4,5},{5,4},{6,7},{7,6},{8,9},{9,8},{10,11... | collective-permute-start | bytes 18874376 | tf_op jit(solution)/shard_map/ppermute | solution.py:47
  175.6 5.3 %collective-permute-start.12 = (bf16[1024,512]{1,0:T(8,128)(2,1)}, bf16[1024,512]{1,0:T(8,128)(2,1)S(1)}, u32[]{:S(2)}, u32[]{:S(2)}) collective-permute-start(bf16[1024,512]{1,0:T(8,128)(2,1)} %out_grads.1), channel_id=1, source_target_pairs={{0,1},{1,0},{2,3},{3,2},{4,5},{5,4},{6,7},{7,6},{8,9},{9,8},{10,11... | collective-permute-start | bytes 3145736 | tf_op jit(solution)/shard_map/ppermute | solution.py:47
  176.0 30.4 %all-to-all-start.2 = ((bf16[4,1024,256]{2,1,0:T(8,128)(2,1)}), bf16[4,1024,256]{2,1,0:T(8,128)(2,1)}, u32[]{:S(2)}, u32[]{:S(2)}) async-start(bf16[4,1024,256]{2,1,0:T(8,128)(2,1)} %get-tuple-element.118), calls=%async_computation.2 | async-start | bytes 4194304 | tf_op jit(solution)/shard_map/all_to_all | solution.py:55
  180.6 166.0 %reduce-scatter.2.cloned.1.call-start = ((), (), s32[]{:S(2)}) async-start(), calls=%async_computation.5 | async-start | bytes 5898240 | tf_op jit(solution)/shard_map/reduce_scatter | solution.py:790
  206.4 19.4 %collective-permute-start.13 = (bf16[384,1024]{1,0:T(8,128)(2,1)}, bf16[384,1024]{1,0:T(8,128)(2,1)S(1)}, u32[]{:S(2)}, u32[]{:S(2)}) collective-permute-start(bf16[384,1024]{1,0:T(8,128)(2,1)} %get-tuple-element.120), channel_id=1, source_target_pairs={{0,2},{1,3},{2,0},{3,1},{4,6},{5,7},{6,4},{7,5},{8,10},{9,11},{10,... | collective-permute-start | bytes 2359304 | tf_op jit(solution)/shard_map/ppermute | solution.py:51
  206.8 18.9 %copy-start.41 = (bf16[384,1024]{1,0:T(8,128)(2,1)S(1)}, bf16[384,1024]{1,0:T(8,128)(2,1)}, u32[]{:S(2)}) copy-start(bf16[384,1024]{1,0:T(8,128)(2,1)} %get-tuple-element.135) | copy-start | bytes 2359300
  206.8 19.6 %copy-start.29 = (bf16[2,2048,128]{2,1,0:T(8,128)(2,1)S(1)}, bf16[2,2048,128]{2,1,0:T(8,128)(2,1)}, u32[]{:S(2)}) copy-start(bf16[2,2048,128]{2,1,0:T(8,128)(2,1)} %copy-done.28) | copy-start | bytes 3145732
  206.8 19.6 %copy-start.33 = (bf16[2048,128]{1,0:T(8,128)(2,1)S(1)}, bf16[2048,128]{1,0:T(8,128)(2,1)}, u32[]{:S(2)}) copy-start(bf16[2048,128]{1,0:T(8,128)(2,1)} %copy-done.32) | copy-start | bytes 1572868
  225.7 17.1 %copy-start.43 = (bf16[384,1024]{1,0:T(8,128)(2,1)}, bf16[384,1024]{1,0:T(8,128)(2,1)S(1)}, u32[]{:S(2)}) copy-start(bf16[384,1024]{1,0:T(8,128)(2,1)S(1)} %collective-permute-done.13) | copy-start | bytes 2359300
  225.7 18.3 %collective-permute-start.15 = (bf16[384,1024]{1,0:T(8,128)(2,1)S(1)}, bf16[384,1024]{1,0:T(8,128)(2,1)S(1)}, u32[]{:S(2)}, u32[]{:S(2)}) collective-permute-start(bf16[384,1024]{1,0:T(8,128)(2,1)S(1)} %copy-done.41), channel_id=1, source_target_pairs={{0,2},{1,3},{2,0},{3,1},{4,6},{5,7},{6,4},{7,5},{8,10},{9,11},{10,... | collective-permute-start | bytes 2359304 | tf_op jit(solution)/shard_map/ppermute | solution.py:51
  226.4 27.9 %collective-permute-start.14 = (bf16[3,1024,128]{2,1,0:T(8,128)(2,1)}, bf16[3,1024,128]{2,1,0:T(8,128)(2,1)}, u32[]{:S(2)}, u32[]{:S(2)}) collective-permute-start(bf16[3,1024,128]{2,1,0:T(8,128)(2,1)} %get-tuple-element.132), channel_id=1, source_target_pairs={{0,1},{1,0},{2,3},{3,2},{4,5},{5,4},{6,7},{7,6},{8,9},{9,8},{10,11... | collective-permute-start | bytes 2359304 | tf_op jit(solution)/shard_map/ppermute | solution.py:47
  244.0 10.2 %collective-permute-start.16 = (bf16[3,1024,128]{2,1,0:T(8,128)(2,1)}, bf16[3,1024,128]{2,1,0:T(8,128)(2,1)}, u32[]{:S(2)}, u32[]{:S(2)}) collective-permute-start(bf16[3,1024,128]{2,1,0:T(8,128)(2,1)} %get-tuple-element.136), channel_id=1, source_target_pairs={{0,1},{1,0},{2,3},{3,2},{4,5},{5,4},{6,7},{7,6},{8,9},{9,8},{10,11... | collective-permute-start | bytes 2359304 | tf_op jit(solution)/shard_map/ppermute | solution.py:47
  246.3 22.5 %collective-permute-start.17 = (bf16[256,1024]{1,0:T(8,128)(2,1)}, bf16[256,1024]{1,0:T(8,128)(2,1)S(1)}, u32[]{:S(2)}, u32[]{:S(2)}) collective-permute-start(bf16[256,1024]{1,0:T(8,128)(2,1)} %get-tuple-element.141), channel_id=1, source_target_pairs={{0,2},{1,3},{2,0},{3,1},{4,6},{5,7},{6,4},{7,5},{8,10},{9,11},{10,... | collective-permute-start | bytes 1572872 | tf_op jit(solution)/shard_map/ppermute | solution.py:51
  249.5 8.5 %copy-start.20 = (f32[6,1024]{1,0:T(8,128)S(1)}, f32[6,1024]{1,0:T(8,128)}, u32[]{:S(2)}) copy-start(f32[6,1024]{1,0:T(8,128)} %refs_1_.1) | copy-start | bytes 73732
  255.4 13.4 %collective-permute-start.18 = (bf16[128,768]{1,0:T(8,128)(2,1)S(1)}, bf16[128,768]{1,0:T(8,128)(2,1)S(1)}, u32[]{:S(2)}, u32[]{:S(2)}) collective-permute-start(bf16[128,768]{1,0:T(8,128)(2,1)S(1)} %get-tuple-element.245), channel_id=1, source_target_pairs={{0,4},{8,0},{16,8},{24,16},{28,24},{20,28},{12,20},{4,12},{1,5},{9... | collective-permute-start | bytes 589832 | tf_op jit(solution)/shard_map/ppermute | solution.py:124
  257.9 11.6 %copy-start.38 = (bf16[1024,1024]{1,0:T(8,128)(2,1)S(1)}, bf16[1024,1024]{1,0:T(8,128)(2,1)}, u32[]{:S(2)}) copy-start(bf16[1024,1024]{1,0:T(8,128)(2,1)} %get-tuple-element.112) | copy-start | bytes 6291460
  257.9 11.6 %copy-start.47 = (bf16[256,1024]{1,0:T(8,128)(2,1)S(1)}, bf16[256,1024]{1,0:T(8,128)(2,1)}, u32[]{:S(2)}) copy-start(bf16[256,1024]{1,0:T(8,128)(2,1)} %get-tuple-element.141) | copy-start | bytes 1572868
  257.9 10.9 %collective-permute-start.19 = (bf16[128,768]{1,0:T(8,128)(2,1)S(1)}, bf16[128,768]{1,0:T(8,128)(2,1)S(1)}, u32[]{:S(2)}, u32[]{:S(2)}) collective-permute-start(bf16[128,768]{1,0:T(8,128)(2,1)S(1)} %get-tuple-element.244), channel_id=1, source_target_pairs={{0,8},{8,16},{16,24},{24,28},{28,20},{20,12},{12,4},{4,0},{1,9},{9... | collective-permute-start | bytes 589832 | tf_op jit(solution)/shard_map/ppermute | solution.py:123
  258.0 12.7 %copy-start.46 = (bf16[384,1024]{1,0:T(8,128)(2,1)S(1)}, bf16[384,1024]{1,0:T(8,128)(2,1)}, u32[]{:S(2)}) copy-start(bf16[384,1024]{1,0:T(8,128)(2,1)} %copy-done.45) | copy-start | bytes 2359300
  274.1 31.8 %collective-permute-start.20 = (bf16[1024,1024]{1,0:T(8,128)(2,1)S(1)}, bf16[1024,1024]{1,0:T(8,128)(2,1)}, u32[]{:S(2)}, u32[]{:S(2)}) collective-permute-start(bf16[1024,1024]{1,0:T(8,128)(2,1)S(1)} %pad_maximum_fusion.refs_0_), channel_id=1, source_target_pairs={{0,1},{1,0},{2,3},{3,2},{4,5},{5,4},{6,7},{7,6},{8,9},{9,8},{10,11... | collective-permute-start | bytes 6291464 | tf_op jit(solution)/shard_map/ppermute | solution.py:47
  276.1 14.6 %collective-permute-start.22 = (bf16[256,1024]{1,0:T(8,128)(2,1)}, bf16[256,1024]{1,0:T(8,128)(2,1)}, u32[]{:S(2)}, u32[]{:S(2)}) collective-permute-start(bf16[256,1024]{1,0:T(8,128)(2,1)} %get-tuple-element.158.refs_0_), channel_id=1, source_target_pairs={{0,2},{1,3},{2,0},{3,1},{4,6},{5,7},{6,4},{7,5},{8,10},{9,11},{10,... | collective-permute-start | bytes 1572872 | tf_op jit(solution)/shard_map/ppermute | solution.py:51
  285.6 6.7 %collective-permute-start.24 = (f32[10,1024]{1,0:T(8,128)S(1)}, f32[10,1024]{1,0:T(8,128)S(1)}, u32[]{:S(2)}, u32[]{:S(2)}) collective-permute-start(f32[10,1024]{1,0:T(8,128)S(1)} %concatenate.30), channel_id=1, source_target_pairs={{0,1},{1,0},{2,3},{3,2},{4,5},{5,4},{6,7},{7,6},{8,9},{9,8},{10,11... | collective-permute-start | bytes 122888 | tf_op jit(solution)/shard_map/ppermute | solution.py:47
  285.9 27.8 %collective-permute-start.30 = (bf16[256,1024]{1,0:T(8,128)(2,1)}, bf16[256,1024]{1,0:T(8,128)(2,1)}, u32[]{:S(2)}, u32[]{:S(2)}) collective-permute-start(bf16[256,1024]{1,0:T(8,128)(2,1)} %get-tuple-element.159.refs_2_), channel_id=1, source_target_pairs={{0,1},{1,0},{2,3},{3,2},{4,5},{5,4},{6,7},{7,6},{8,9},{9,8},{10,11... | collective-permute-start | bytes 1572872 | tf_op jit(solution)/shard_map/ppermute | solution.py:47
  286.2 30.9 %collective-permute-start.28 = (bf16[256,1024]{1,0:T(8,128)(2,1)}, bf16[256,1024]{1,0:T(8,128)(2,1)}, u32[]{:S(2)}, u32[]{:S(2)}) collective-permute-start(bf16[256,1024]{1,0:T(8,128)(2,1)} %get-tuple-element.158.refs_0_), channel_id=1, source_target_pairs={{0,1},{1,0},{2,3},{3,2},{4,5},{5,4},{6,7},{7,6},{8,9},{9,8},{10,11... | collective-permute-start | bytes 1572872 | tf_op jit(solution)/shard_map/ppermute | solution.py:47
  290.7 20.5 %collective-permute-start.35 = (bf16[128,768]{1,0:T(8,128)(2,1)S(1)}, bf16[128,768]{1,0:T(8,128)(2,1)}, u32[]{:S(2)}, u32[]{:S(2)}) collective-permute-start(bf16[128,768]{1,0:T(8,128)(2,1)S(1)} %add_convert_fusion.4), channel_id=1, source_target_pairs={{0,4},{8,0},{16,8},{24,16},{28,24},{20,28},{12,20},{4,12},{1,5},{9... | collective-permute-start | bytes 589832 | tf_op jit(solution)/shard_map/ppermute | solution.py:124
  292.3 13.6 %collective-permute-start.23 = (bf16[256,1024]{1,0:T(8,128)(2,1)}, bf16[256,1024]{1,0:T(8,128)(2,1)}, u32[]{:S(2)}, u32[]{:S(2)}) collective-permute-start(bf16[256,1024]{1,0:T(8,128)(2,1)} %get-tuple-element.159.refs_2_), channel_id=1, source_target_pairs={{0,2},{1,3},{2,0},{3,1},{4,6},{5,7},{6,4},{7,5},{8,10},{9,11},{10,... | collective-permute-start | bytes 1572872 | tf_op jit(solution)/shard_map/ppermute | solution.py:51
  293.5 17.7 %copy-start.12 = (bf16[256,1024]{1,0:T(8,128)(2,1)S(1)}, bf16[256,1024]{1,0:T(8,128)(2,1)}, u32[]{:S(2)}) copy-start(bf16[256,1024]{1,0:T(8,128)(2,1)} %copy-done.11) | copy-start | bytes 1572868
  293.5 21.6 %copy-start.50 = (bf16[128,768]{1,0:T(8,128)(2,1)S(1)}, bf16[128,768]{1,0:T(8,128)(2,1)}, u32[]{:S(2)}) copy-start(bf16[128,768]{1,0:T(8,128)(2,1)} %copy-done.49) | copy-start | bytes 589828
  305.9 17.1 %collective-permute-start.29 = (bf16[256,1024]{1,0:T(8,128)(2,1)}, bf16[256,1024]{1,0:T(8,128)(2,1)}, u32[]{:S(2)}, u32[]{:S(2)}) collective-permute-start(bf16[256,1024]{1,0:T(8,128)(2,1)} %collective-permute-done.22.refs_1_), channel_id=1, source_target_pairs={{0,1},{1,0},{2,3},{3,2},{4,5},{5,4},{6,7},{7,6},{8,9},{9,8},{10,11... | collective-permute-start | bytes 1572872 | tf_op jit(solution)/shard_map/ppermute | solution.py:47
  305.9 17.1 %collective-permute-start.31 = (bf16[256,1024]{1,0:T(8,128)(2,1)}, bf16[256,1024]{1,0:T(8,128)(2,1)S(1)}, u32[]{:S(2)}, u32[]{:S(2)}) collective-permute-start(bf16[256,1024]{1,0:T(8,128)(2,1)} %collective-permute-done.23.refs_3_), channel_id=1, source_target_pairs={{0,1},{1,0},{2,3},{3,2},{4,5},{5,4},{6,7},{7,6},{8,9},{9,8},{10,11... | collective-permute-start | bytes 1572872 | tf_op jit(solution)/shard_map/ppermute | solution.py:47
  311.2 15.1 %collective-permute-start.25 = (bf16[256,1024]{1,0:T(8,128)(2,1)S(1)}, bf16[256,1024]{1,0:T(8,128)(2,1)S(1)}, u32[]{:S(2)}, u32[]{:S(2)}) collective-permute-start(bf16[256,1024]{1,0:T(8,128)(2,1)S(1)} %copy-done.12), channel_id=1, source_target_pairs={{0,2},{1,3},{2,0},{3,1},{4,6},{5,7},{6,4},{7,5},{8,10},{9,11},{10,... | collective-permute-start | bytes 1572872 | tf_op jit(solution)/shard_map/ppermute | solution.py:51
  313.6 4.4 %collective-permute-start.32 = (f32[9,1024]{1,0:T(8,128)S(1)}, f32[9,1024]{1,0:T(8,128)S(1)}, u32[]{:S(2)}, u32[]{:S(2)}) collective-permute-start(f32[9,1024]{1,0:T(8,128)S(1)} %pad_maximum_fusion.2), channel_id=1, source_target_pairs={{0,4},{4,0},{8,12},{12,8},{16,20},{20,16},{24,28},{28,24},{1,5},{5... | collective-permute-start | bytes 110600 | tf_op jit(solution)/shard_map/ppermute | solution.py:852
  317.1 11.5 %collective-permute-start.38 = (bf16[128,768]{1,0:T(8,128)(2,1)}, bf16[128,768]{1,0:T(8,128)(2,1)S(1)}, u32[]{:S(2)}, u32[]{:S(2)}) collective-permute-start(bf16[128,768]{1,0:T(8,128)(2,1)} %get-tuple-element.167), channel_id=1, source_target_pairs={{0,8},{8,16},{16,24},{24,28},{28,20},{20,12},{12,4},{4,0},{1,9},{9... | collective-permute-start | bytes 589832 | tf_op jit(solution)/shard_map/ppermute | solution.py:123
  318.0 10.6 %collective-permute-start.36 = (bf16[128,768]{1,0:T(8,128)(2,1)}, bf16[128,768]{1,0:T(8,128)(2,1)}, u32[]{:S(2)}, u32[]{:S(2)}) collective-permute-start(bf16[128,768]{1,0:T(8,128)(2,1)} %get-tuple-element.165), channel_id=1, source_target_pairs={{0,4},{8,0},{16,8},{24,16},{28,24},{20,28},{12,20},{4,12},{1,5},{9... | collective-permute-start | bytes 589832 | tf_op jit(solution)/shard_map/ppermute | solution.py:124
  322.9 11.2 %copy-start.40 = (f32[128,3,256]{2,0,1:T(8,128)S(1)}, f32[128,3,256]{2,0,1:T(8,128)}, u32[]{:S(2)}) copy-start(f32[128,3,256]{2,0,1:T(8,128)} %param.26) | copy-start | bytes 1179652
  326.3 12.6 %collective-permute-start.33 = (bf16[256,1024]{1,0:T(8,128)(2,1)S(1)}, bf16[256,1024]{1,0:T(8,128)(2,1)}, u32[]{:S(2)}, u32[]{:S(2)}) collective-permute-start(bf16[256,1024]{1,0:T(8,128)(2,1)S(1)} %copy-done.14), channel_id=1, source_target_pairs={{0,2},{1,3},{2,0},{3,1},{4,6},{5,7},{6,4},{7,5},{8,10},{9,11},{10,... | collective-permute-start | bytes 1572872 | tf_op jit(solution)/shard_map/ppermute | solution.py:51
  330.6 10.5 %collective-permute-start.39 = (bf16[128,768]{1,0:T(8,128)(2,1)}, bf16[128,768]{1,0:T(8,128)(2,1)S(1)}, u32[]{:S(2)}, u32[]{:S(2)}) collective-permute-start(bf16[128,768]{1,0:T(8,128)(2,1)} %get-tuple-element.168), channel_id=1, source_target_pairs={{0,8},{8,16},{16,24},{24,28},{28,20},{20,12},{12,4},{4,0},{1,9},{9... | collective-permute-start | bytes 589832 | tf_op jit(solution)/shard_map/ppermute | solution.py:123
  331.2 9.9 %collective-permute-start.37 = (bf16[128,768]{1,0:T(8,128)(2,1)}, bf16[128,768]{1,0:T(8,128)(2,1)}, u32[]{:S(2)}, u32[]{:S(2)}) collective-permute-start(bf16[128,768]{1,0:T(8,128)(2,1)} %get-tuple-element.166), channel_id=1, source_target_pairs={{0,4},{8,0},{16,8},{24,16},{28,24},{20,28},{12,20},{4,12},{1,5},{9... | collective-permute-start | bytes 589832 | tf_op jit(solution)/shard_map/ppermute | solution.py:124
  332.9 5.3 %collective-permute-start.40 = (f32[9,1024]{1,0:T(8,128)S(1)}, f32[9,1024]{1,0:T(8,128)S(1)}, u32[]{:S(2)}, u32[]{:S(2)}) collective-permute-start(f32[9,1024]{1,0:T(8,128)S(1)} %add.273), channel_id=1, source_target_pairs={{0,8},{4,12},{8,0},{12,4},{16,24},{20,28},{24,16},{28,20},{1,9},{5... | collective-permute-start | bytes 110600 | tf_op jit(solution)/shard_map/ppermute | solution.py:852
  335.9 23.7 %collective-permute-start.27 = (bf16[256,1024]{1,0:T(8,128)(2,1)S(1)}, bf16[256,1024]{1,0:T(8,128)(2,1)}, u32[]{:S(2)}, u32[]{:S(2)}) collective-permute-start(bf16[256,1024]{1,0:T(8,128)(2,1)S(1)} %copy-done.14), channel_id=1, source_target_pairs={{0,1},{1,0},{2,3},{3,2},{4,5},{5,4},{6,7},{7,6},{8,9},{9,8},{10,11... | collective-permute-start | bytes 1572872 | tf_op jit(solution)/shard_map/ppermute | solution.py:47
  338.2 22.5 %collective-permute-start.21 = (bf16[256,1024]{1,0:T(8,128)(2,1)S(1)}, bf16[256,1024]{1,0:T(8,128)(2,1)}, u32[]{:S(2)}, u32[]{:S(2)}) collective-permute-start(bf16[256,1024]{1,0:T(8,128)(2,1)S(1)} %copy-done.12), channel_id=1, source_target_pairs={{0,1},{1,0},{2,3},{3,2},{4,5},{5,4},{6,7},{7,6},{8,9},{9,8},{10,11... | collective-permute-start | bytes 1572872 | tf_op jit(solution)/shard_map/ppermute | solution.py:47
  338.9 7.5 %collective-permute-start.41 = (f32[9,1024]{1,0:T(8,128)S(1)}, f32[9,1024]{1,0:T(8,128)S(1)}, u32[]{:S(2)}, u32[]{:S(2)}) collective-permute-start(f32[9,1024]{1,0:T(8,128)S(1)} %add.287), channel_id=1, source_target_pairs={{0,16},{4,20},{8,24},{12,28},{16,0},{20,4},{24,8},{28,12},{1,17},{... | collective-permute-start | bytes 110600 | tf_op jit(solution)/shard_map/ppermute | solution.py:852
  346.0 14.7 %collective-permute-start.26 = (bf16[256,1024]{1,0:T(8,128)(2,1)S(1)}, bf16[256,1024]{1,0:T(8,128)(2,1)S(1)}, u32[]{:S(2)}, u32[]{:S(2)}) collective-permute-start(bf16[256,1024]{1,0:T(8,128)(2,1)S(1)} %collective-permute-done.25.refs_1_), channel_id=1, source_target_pairs={{0,1},{1,0},{2,3},{3,2},{4,5},{5,4},{6,7},{7,6},{8,9},{9,8},{10,11... | collective-permute-start | bytes 1572872 | tf_op jit(solution)/shard_map/ppermute | solution.py:47
  346.2 14.5 %collective-permute-start.34 = (bf16[256,1024]{1,0:T(8,128)(2,1)}, bf16[256,1024]{1,0:T(8,128)(2,1)}, u32[]{:S(2)}, u32[]{:S(2)}) collective-permute-start(bf16[256,1024]{1,0:T(8,128)(2,1)} %collective-permute-done.33.refs_3_), channel_id=1, source_target_pairs={{0,1},{1,0},{2,3},{3,2},{4,5},{5,4},{6,7},{7,6},{8,9},{9,8},{10,11... | collective-permute-start | bytes 1572872 | tf_op jit(solution)/shard_map/ppermute | solution.py:47
  354.1 10.0 %collective-permute-start.42 = (f32[7,1024]{1,0:T(8,128)S(1)}, f32[7,1024]{1,0:T(8,128)S(1)}, u32[]{:S(2)}, u32[]{:S(2)}) collective-permute-start(f32[7,1024]{1,0:T(8,128)S(1)} %slice.191), channel_id=1, source_target_pairs={{0,2},{1,3},{2,0},{3,1},{4,6},{5,7},{6,4},{7,5},{8,10},{9,11},{10,... | collective-permute-start | bytes 86024 | tf_op jit(solution)/shard_map/ppermute | solution.py:51
  359.7 6.8 %collective-permute-start.43 = (bf16[128,256]{1,0:T(8,128)(2,1)S(1)}, bf16[128,256]{1,0:T(8,128)(2,1)S(1)}, u32[]{:S(2)}, u32[]{:S(2)}) collective-permute-start(bf16[128,256]{1,0:T(8,128)(2,1)S(1)} %slice.195), channel_id=1, source_target_pairs={{0,2},{1,3},{2,0},{3,1},{4,6},{5,7},{6,4},{7,5},{8,10},{9,11},{10,... | collective-permute-start | bytes 196616 | tf_op jit(solution)/shard_map/ppermute | solution.py:51
  (42 other events, 164.1 us)
Sparse Core Ops, SparseCore 0:
  14.8 98.8 all-gather.1
  206.5 111.0 reduce-scatter.1

commit v5 on v4

--- a/solution.py
+++ b/solution.py
@@ -255,7 +255,7 @@
         grid=(1,),
         in_specs=[pair_spec(span, pair)] * 3,
         out_specs=[whole(x) for x in shapes],
-        compiler_params=pltpu.CompilerParams(vmem_limit_bytes=50 * MIB),
+        compiler_params=pltpu.CompilerParams(vmem_limit_bytes=60 * MIB),
         cost_estimate=cost(12e9, 5 * MIB),
         name="attend_forward",
     )(q, k, v)
@@ -332,7 +332,7 @@
             pltpu.VMEM((2, span, 128), BF),
             pltpu.VMEM((2, 64, span), F32),
         ],
-        compiler_params=pltpu.CompilerParams(vmem_limit_bytes=50 * MIB),
+        compiler_params=pltpu.CompilerParams(vmem_limit_bytes=60 * MIB),
         cost_estimate=cost(18e9, 6 * MIB),
         name="attend_backward",
     )(scalars, qb, k, v, o, *partials)
@@ -609,7 +609,7 @@
             + [pl.BlockSpec((tile, 512), lambda i, s: (i, 0))],
             out_specs=pl.BlockSpec((tile, 2 * hidden + 512), lambda i, s: (i, 0)),
         ),
-        compiler_params=pltpu.CompilerParams(vmem_limit_bytes=50 * MIB),
+        compiler_params=pltpu.CompilerParams(vmem_limit_bytes=60 * MIB),
         cost_estimate=cost(2 * span * depth * (2 * hidden + 256), 30 * MIB),
         name="weight_grads",
     )(

time: 380 us -> 381 us (level)
    unnamed x127 -> x123, local copies, waits for them, and re-layouts: 23.4 us -> 23.5 us
  transfers between devices with their start and end apart: 48 -> 48, of which waited for: 14 -> 15; matrix products, arithmetic and copies ran while one was open for 10% -> 10% of each run, Pallas kernels for 33% -> 34%
where the time goes in v5:
time: 381 us; the launch traced here: 376 us
  Pallas kernels  164 us (43%)
  waiting for transfers between devices  55.7 us (15%)
  starting transfers between devices  54.3 us (14%)
  other arithmetic  29.9 us (8%)
  local copies, waits for them, and re-layouts  28.2 us (7%)
  between operations  25.4 us (7%)
  blocking collectives  19 us (5%)
    pallas_call x1, Pallas kernels, middle(): pl.pallas_call(functools.partial(middle_kernel, chunk=chunk), out_shape=[...  35.9 us
    pallas_call x2, Pallas kernels, attend_backward(): pl.pallas_call(functools.partial(attend_backward_kernel, bk=min(256, span...  34.7 us
    unnamed x123, local copies, waits for them, and re-layouts  23.5 us
    pallas_call x2, Pallas kernels, attend_forward(): pl.pallas_call(functools.partial(attend_forward_kernel, bq=min(512, span)...  23 us
    pallas_call x6, Pallas kernels, finish(): pl.pallas_call(functools.partial(finish_kernel, pieces=len(pieces), terms...  21 us
    all_to_all x1, blocking collectives, to_all(): return lax.all_to_all(x, 'mp', split_axis=0, concat_axis=0, tiled=True)  19 us
    ppermute x10, waiting for transfers between devices, to_chip(): lax.ppermute(x, 'mp', [(i, i ^ 2) for i in range(lax.axis_size('mp'))])  18.6 us
    pallas_call x1, Pallas kernels, weight_grads(): pl.pallas_call(functools.partial(weight_grads_kernel, chunks=chunks), out...  18.2 us
  transfers between devices with their start and end apart: 48, of which 15 were waited for; matrix products, arithmetic and copies ran while one was open for 10% of the time, Pallas kernels for 34%

profile of v5, /device:TPU:0, one launch (start us, length us, event | category | flops | bytes accessed | tf_op | source)
XLA Modules:
  0.0 376.5 jit_solution(16778840534774220802)
XLA Ops:
  8.2 3.0 collective-permute-start.8
  15.0 1.9 collective-permute-start.4
  17.2 3.0 convert_reduce_fusion
  21.1 1.4 fusion.2
  22.5 1.9 collective-permute-start.5
  24.4 3.0 fusion.5.n_ref
  28.2 5.1 %collective-permute-done.5.refs_6_ = bf16[128,768]{1,0:T(8,128)(2,1)S(1)} collective-permute-done((bf16[128,768]{1,0:T(8,128)(2,1)S(1)}, bf16[128,768]{1,0:T(8,128)(2,1)S(1)}, u32[]{:S(2)}, u32[]{:S(2)}) %collective-permute-start.5) | collective-permute-done | bytes 196640 | tf_op jit(solution)/shard_map/ppermute | solution.py:88
  33.3 4.7 %collective-permute-start.6 = (bf16[128,768]{1,0:T(8,128)(2,1)S(1)}, bf16[128,768]{1,0:T(8,128)(2,1)S(1)}, u32[]{:S(2)}, u32[]{:S(2)}) collective-permute-start(bf16[128,768]{1,0:T(8,128)(2,1)S(1)} %collective-permute-done.5.refs_6_), channel_id=1, source_target_pairs={{0,8},{8,16},{16,24},{24,28},{28,20},{20,12},{12,4},{4,0},{1,9},{9... | collective-permute-start | bytes 589832 | tf_op jit(solution)/shard_map/ppermute | solution.py:88
  38.7 5.5 %collective-permute-done.2.refs_2_ = bf16[128,768]{1,0:T(8,128)(2,1)S(1)} collective-permute-done((bf16[128,768]{1,0:T(8,128)(2,1)S(1)}, bf16[128,768]{1,0:T(8,128)(2,1)S(1)}, u32[]{:S(2)}, u32[]{:S(2)}) %collective-permute-start.2) | collective-permute-done | bytes 196640 | tf_op jit(solution)/shard_map/ppermute | solution.py:90
  44.3 2.1 collective-permute-done.6.refs_5_
  46.4 8.9 %collective-permute-start.7 = (bf16[128,768]{1,0:T(8,128)(2,1)S(1)}, bf16[128,768]{1,0:T(8,128)(2,1)S(1)}, u32[]{:S(2)}, u32[]{:S(2)}) collective-permute-start(bf16[128,768]{1,0:T(8,128)(2,1)S(1)} %collective-permute-done.6.refs_5_), channel_id=1, source_target_pairs={{0,8},{8,16},{16,24},{24,28},{28,20},{20,12},{12,4},{4,0},{1,9},{9... | collective-permute-start | bytes 589832 | tf_op jit(solution)/shard_map/ppermute | solution.py:88
  57.2 1.4 collective-permute-done.7.refs_4_
  58.6 2.2 copy-done.5
  60.8 7.3 %project.1 = (bf16[4,2048,128]{2,1,0:T(8,128)(2,1)S(1)}, bf16[4,2048,128]{2,1,0:T(8,128)(2,1)S(1)}, bf16[4,2048,128]{2,1,0:T(8,128)(2,1)S(1)}, bf16[1024,768]{1,0:T(8,128)(2,1)S(1)}) custom-call(s32[8]{0:T(128)S(1)} %gather_fusion, f32[4]{0:T(128)S(1)} %multiply_exponential_fusion.slope_ref, s32[1]{0:T(128)} %copy.76.length_ref, ...), custom_call_target="tpu_custom_call" | custom-call | flops 3221225472 | bytes 12582912 | tf_op jit(solution)/shard_map/project/pallas_call | solution.py:202
  68.1 1.3 copy-done.29
  69.4 1.3 copy-done.30
  70.7 1.3 copy-done.31
  72.0 11.6 %attend_forward.2 = (bf16[2048,128]{1,0:T(8,128)(2,1)}, bf16[2,2048,128]{2,1,0:T(8,128)(2,1)}, bf16[4,1024,128]{2,1,0:T(8,128)(2,1)}) custom-call(bf16[4,2048,128]{2,1,0:T(8,128)(2,1)} %copy-done.31, bf16[4,2048,128]{2,1,0:T(8,128)(2,1)} %copy-done.29, bf16[4,2048,128]{2,1,0:T(8,128)(2,1)} %copy-done.30), custom_call_target="tpu_custom_call" | custom-call | flops 12000000000 | bytes 5242880 | tf_op jit(solution)/shard_map/attend_forward/pallas_call | solution.py:252
  83.6 3.7 all-to-all-start
  87.3 11.4 %attend_forward.3 = (bf16[2048,128]{1,0:T(8,128)(2,1)}, bf16[2,2048,128]{2,1,0:T(8,128)(2,1)}, bf16[4,1024,128]{2,1,0:T(8,128)(2,1)}) custom-call(bf16[4,2048,128]{2,1,0:T(8,128)(2,1)} %copy-done.31, bf16[4,2048,128]{2,1,0:T(8,128)(2,1)} %copy-done.29, bf16[4,2048,128]{2,1,0:T(8,128)(2,1)} %copy-done.30), custom_call_target="tpu_custom_call" | custom-call | flops 12000000000 | bytes 5242880 | tf_op jit(solution)/shard_map/attend_forward/pallas_call | solution.py:252
  98.7 3.0 all-to-all-done.o0_ref.refs_2_.refs_4_.refs_7_.refs_9_
  101.7 19.0 %all_to_all.15.o1_ref.refs_3_.refs_5_.refs_8_.refs_10_ = bf16[4,1024,128]{2,1,0:T(8,128)(2,1)} all-to-all(bf16[4,1024,128]{2,1,0:T(8,128)(2,1)} %get-tuple-element.108), channel_id=1, replica_groups=mesh['dp'=8,'mp'=4] {'mp'}, dimensions={0} | all-to-all | bytes 2097152 | tf_op jit(solution)/shard_map/all_to_all | solution.py:55
  121.8 9.4 %collective-permute-done.10.w_sib_ref = bf16[1024,768]{1,0:T(8,128)(2,1)} collective-permute-done((bf16[1024,768]{1,0:T(8,128)(2,1)S(1)}, bf16[1024,768]{1,0:T(8,128)(2,1)}, u32[]{:S(2)}, u32[]{:S(2)}) %collective-permute-start.10) | collective-permute-done | bytes 1572896 | tf_op jit(solution)/shard_map/ppermute | solution.py:47
  131.9 35.9 %middle.1 = (bf16[384,1024]{1,0:T(8,128)(2,1)}, bf16[384,1024]{1,0:T(8,128)(2,1)}, bf16[256,1024]{1,0:T(8,128)(2,1)}, bf16[1024,1024]{1,0:T(8,128)(2,1)}, bf16[1...) custom-call(s32[4]{0:T(128)} %pad_add_fusion.scalar_ref.refs_0_.half, ...), custom_call_target="tpu_custom_call" | custom-call | flops 20999999488 | bytes 25165824 | tf_op jit(solution)/shard_map/middle/pallas_call | solution.py:453
  169.3 1.6 copy-done.3
  170.9 2.8 out_grads.1
  174.1 4.5 %all-to-all-start.2 = ((bf16[4,1024,256]{2,1,0:T(8,128)(2,1)}), bf16[4,1024,256]{2,1,0:T(8,128)(2,1)}, u32[]{:S(2)}, u32[]{:S(2)}) async-start(bf16[4,1024,256]{2,1,0:T(8,128)(2,1)} %get-tuple-element.118), calls=%async_computation.2 | async-start | bytes 4194304 | tf_op jit(solution)/shard_map/all_to_all | solution.py:55
  179.7 18.2 %weight_grads.1 = bf16[1024,2560]{1,0:T(8,128)(2,1)} custom-call(s32[4]{0:T(128)} %pad_add_fusion.scalar_ref.refs_0_.half_ref, f32[2048,1024]{1,0:T(8,128)} %cot_ref.3, bf16[1024,3072]{1,0:T(8,128)(2,1)} %get-tuple-element.114.refs_0_, bf16[1024,1024]{1,0:T(8,128)(2,1)} %get-tuple-element.115.refs_1_, bf16[1024,1024]{1,0:T(8,128)(2,1)} %get-tuple-element.116.refs_2_, ...), custom_call_target="tpu_custom_call" | custom-call | flops 9663676416 | bytes 31457280 | tf_op jit(solution)/shard_map/weight_grads/pallas_call | solution.py:599
  197.9 6.4 %all-to-all-done.2.refs_0_ = bf16[4,1024,256]{2,1,0:T(8,128)(2,1)} async-done(((bf16[4,1024,256]{2,1,0:T(8,128)(2,1)}), bf16[4,1024,256]{2,1,0:T(8,128)(2,1)}, u32[]{:S(2)}, u32[]{:S(2)}) %all-to-all-start.2) | async-done | bytes 2097184 | tf_op jit(solution)/shard_map/all_to_all | solution.py:55
  204.8 17.3 %attend_backward.2 = (bf16[3,2048,128]{2,1,0:T(8,128)(2,1)}, bf16[3,1024,128]{2,1,0:T(8,128)(2,1)}, f32[2,128]{1,0:T(2,128)}) custom-call(s32[4]{0:T(128)} %pad_add_fusion.scalar_ref.refs_0_.half_ref, bf16[2,2048,128]{2,1,0:T(8,128)(2,1)} %get-tuple-element.122.q_ref, bf16[4,2048,128]{2,1,0:T(8,128)(2,1)} %copy-done.29, bf16[4,2048,128]{2,1,0:T(8,128)(2,1)} %copy-done.30, ...), custom_call_target="tpu_custom_call" | custom-call | flops 17999998976 | bytes 6291456 | tf_op jit(solution)/shard_map/attend_backward/pallas_call | solution.py:317
  222.1 1.5 collective-permute-done.13
  224.2 17.4 %attend_backward.3 = (bf16[3,2048,128]{2,1,0:T(8,128)(2,1)}, bf16[3,1024,128]{2,1,0:T(8,128)(2,1)}, f32[2,128]{1,0:T(2,128)}) custom-call(s32[4]{0:T(128)} %pad_add_fusion.scalar_ref.refs_0_.half_ref, bf16[2,2048,128]{2,1,0:T(8,128)(2,1)} %get-tuple-element.128.q_ref, bf16[4,2048,128]{2,1,0:T(8,128)(2,1)} %copy-done.29, bf16[4,2048,128]{2,1,0:T(8,128)(2,1)} %copy-done.30, ...), custom_call_target="tpu_custom_call" | custom-call | flops 17999998976 | bytes 6291456 | tf_op jit(solution)/shard_map/attend_backward/pallas_call | solution.py:317
  244.1 1.5 collective-permute-start.17
  245.6 2.2 copy-done.6
  247.9 1.4 copy-done.10
  249.3 1.4 copy-done.12
  250.8 4.8 %qkv_grads.1 = bf16[1024,768]{1,0:T(8,128)(2,1)S(1)} custom-call(bf16[2048,1024]{1,0:T(8,128)(2,1)S(1)} %copy-done.6, bf16[3,2048,128]{2,1,0:T(8,128)(2,1)S(1)} %copy-done.10, bf16[3,2048,128]{2,1,0:T(8,128)(2,1)S(1)} %copy-done.12), custom_call_target="tpu_custom_call" | custom-call | flops 3221225472 | bytes 10485760 | tf_op jit(solution)/shard_map/qkv_grads/pallas_call | solution.py:635
  256.8 2.4 collective-permute-start.18
  259.5 9.8 %last.1 = (bf16[256,1024]{1,0:T(8,128)(2,1)}, bf16[256,1024]{1,0:T(8,128)(2,1)}, bf16[256,1024]{1,0:T(8,128)(2,1)S(1)}, bf16[256,1024]{1,0:T(8,128)(2,1)S(1)}, f32[8,1024]{1,0:T(8,128)S(1)}) custom-call(s32[4]{0:T(128)S(1)} %copy-done.27, bf16[3,2048,128]{2,1,0:T(8,128)(2,1)S(1)} %copy-done.11, bf16[3,2048,128]{2,1,0:T(8,128)(2,1)S(1)} %copy-done.13, ...), custom_call_target="tpu_custom_call" | custom-call | flops 3200000000 | bytes 20971520 | tf_op jit(solution)/shard_map/last/pallas_call | solution.py:512
  269.4 1.2 fusion.11
  271.2 3.5 fusion.7
  277.5 3.0 finish.6.refs_1_
  284.4 1.4 select_maximum_fusion.3
  287.7 3.8 %collective-permute-done.22.refs_1_ = bf16[256,1024]{1,0:T(8,128)(2,1)} collective-permute-done((bf16[256,1024]{1,0:T(8,128)(2,1)}, bf16[256,1024]{1,0:T(8,128)(2,1)}, u32[]{:S(2)}, u32[]{:S(2)}) %collective-permute-start.22) | collective-permute-done | bytes 524320 | tf_op jit(solution)/shard_map/ppermute | solution.py:51
  291.5 1.8 collective-permute-start.35
  294.1 12.8 %collective-permute-done.23.refs_3_ = bf16[256,1024]{1,0:T(8,128)(2,1)} collective-permute-done((bf16[256,1024]{1,0:T(8,128)(2,1)}, bf16[256,1024]{1,0:T(8,128)(2,1)}, u32[]{:S(2)}, u32[]{:S(2)}) %collective-permute-start.23) | collective-permute-done | bytes 524320 | tf_op jit(solution)/shard_map/ppermute | solution.py:51
  307.4 4.8 %finish.7 = f32[2048,1024]{1,0:T(8,128)} custom-call(s32[4]{0:T(128)S(1)} %copy-done.27, bf16[1024,1024]{1,0:T(8,128)(2,1)} %collective-permute-done.20.refs_0_, f32[2048,1024]{1,0:T(8,128)} %finish.6.refs_1_), custom_call_target="tpu_custom_call", output_to_operand_aliasing={{}: (2, {})} | custom-call | bytes 8388608 | tf_op jit(solution)/shard_map/finish/pallas_call | solution.py:664
  314.2 1.5 collective-permute-start.32
  315.7 1.8 add_convert_fusion.3
  318.5 1.5 collective-permute-start.36
  320.0 3.5 finish.8.refs_4_
  323.6 3.4 finish.9.refs_4_
  326.9 1.5 collective-permute-start.33
  329.6 2.1 add_convert_fusion.2
  332.2 1.7 collective-permute-start.37
  335.7 1.3 copy.65.v_ref
  337.1 2.1 collective-permute-done.40
  339.5 2.6 collective-permute-start.41
  343.2 1.3 adam.6
  351.0 2.5 adam.4
  353.5 1.6 adam.5
  357.4 3.0 finish.10.refs_4_
  360.4 1.3 collective-permute-start.43
  361.8 3.4 finish.11
  (236 shorter events, 40.1 us)
Async XLA Ops:
  7.2 113.5 %all-gather.2.cloned.1.call-start = ((), (), s32[]{:S(2)}) async-start(), calls=%async_computation.4 | async-start | bytes 5898240 | tf_op jit(solution)/shard_map/all_gather | solution.py:759
  8.2 5.5 %collective-permute-start.8 = (bf16[128,256]{1,0:T(8,128)(2,1)S(1)}, bf16[128,256]{1,0:T(8,128)(2,1)S(1)}, u32[]{:S(2)}, u32[]{:S(2)}) collective-permute-start(bf16[128,256]{1,0:T(8,128)(2,1)S(1)} %bitcast.62), channel_id=1, source_target_pairs={{0,2},{1,3},{2,0},{3,1},{4,6},{5,7},{6,4},{7,5},{8,10},{9,11},{10,... | collective-permute-start | bytes 196616 | tf_op jit(solution)/shard_map/ppermute | solution.py:51
  15.0 7.5 %collective-permute-start.4 = (bf16[128,768]{1,0:T(8,128)(2,1)S(1)}, bf16[128,768]{1,0:T(8,128)(2,1)S(1)}, u32[]{:S(2)}, u32[]{:S(2)}) collective-permute-start(bf16[128,768]{1,0:T(8,128)(2,1)S(1)} %copy.60.refs_0_), channel_id=1, source_target_pairs={{0,8},{8,16},{16,24},{24,28},{28,20},{20,12},{12,4},{4,0},{1,9},{9... | collective-permute-start | bytes 589832 | tf_op jit(solution)/shard_map/ppermute | solution.py:88
  17.0 11.1 %collective-permute-start.1 = (bf16[128,768]{1,0:T(8,128)(2,1)S(1)}, bf16[128,768]{1,0:T(8,128)(2,1)S(1)}, u32[]{:S(2)}, u32[]{:S(2)}) collective-permute-start(bf16[128,768]{1,0:T(8,128)(2,1)S(1)} %copy.60.refs_0_), channel_id=1, source_target_pairs={{0,4},{8,0},{16,8},{24,16},{28,24},{20,28},{12,20},{4,12},{1,5},{9... | collective-permute-start | bytes 589832 | tf_op jit(solution)/shard_map/ppermute | solution.py:90
  17.1 39.5 %collective-permute-start = (f32[1,1024]{1,0:T(1,128)S(1)}, f32[1,1024]{1,0:T(1,128)S(1)}, u32[]{:S(2)}, u32[]{:S(2)}) collective-permute-start(f32[1,1024]{1,0:T(1,128)S(1)} %bitcast.72), channel_id=1, source_target_pairs={{0,1},{1,0},{2,3},{3,2},{4,5},{5,4},{6,7},{7,6},{8,9},{9,8},{10,11... | collective-permute-start | bytes 12296 | tf_op jit(solution)/shard_map/ppermute | solution.py:47
  22.5 10.8 %collective-permute-start.5 = (bf16[128,768]{1,0:T(8,128)(2,1)S(1)}, bf16[128,768]{1,0:T(8,128)(2,1)S(1)}, u32[]{:S(2)}, u32[]{:S(2)}) collective-permute-start(bf16[128,768]{1,0:T(8,128)(2,1)S(1)} %collective-permute-done.4.refs_7_), channel_id=1, source_target_pairs={{0,8},{8,16},{16,24},{24,28},{28,20},{20,12},{12,4},{4,0},{1,9},{9... | collective-permute-start | bytes 589832 | tf_op jit(solution)/shard_map/ppermute | solution.py:88
  24.4 31.5 %copy-start.32 = (s32[8]{0:T(128)S(1)}, s32[8]{0:T(128)}, u32[]{:S(2)}) copy-start(s32[8]{0:T(128)} %constant.99.clone) | copy-start | bytes 100
  28.0 16.2 %collective-permute-start.2 = (bf16[128,768]{1,0:T(8,128)(2,1)S(1)}, bf16[128,768]{1,0:T(8,128)(2,1)S(1)}, u32[]{:S(2)}, u32[]{:S(2)}) collective-permute-start(bf16[128,768]{1,0:T(8,128)(2,1)S(1)} %collective-permute-done.1.refs_1_), channel_id=1, source_target_pairs={{0,4},{8,0},{16,8},{24,16},{28,24},{20,28},{12,20},{4,12},{1,5},{9... | collective-permute-start | bytes 589832 | tf_op jit(solution)/shard_map/ppermute | solution.py:90
  33.3 13.1 %collective-permute-start.6 = (bf16[128,768]{1,0:T(8,128)(2,1)S(1)}, bf16[128,768]{1,0:T(8,128)(2,1)S(1)}, u32[]{:S(2)}, u32[]{:S(2)}) collective-permute-start(bf16[128,768]{1,0:T(8,128)(2,1)S(1)} %collective-permute-done.5.refs_6_), channel_id=1, source_target_pairs={{0,8},{8,16},{16,24},{24,28},{28,20},{20,12},{12,4},{4,0},{1,9},{9... | collective-permute-start | bytes 589832 | tf_op jit(solution)/shard_map/ppermute | solution.py:88
  44.3 13.0 %collective-permute-start.3 = (bf16[128,768]{1,0:T(8,128)(2,1)S(1)}, bf16[128,768]{1,0:T(8,128)(2,1)S(1)}, u32[]{:S(2)}, u32[]{:S(2)}) collective-permute-start(bf16[128,768]{1,0:T(8,128)(2,1)S(1)} %collective-permute-done.2.refs_2_), channel_id=1, source_target_pairs={{0,4},{8,0},{16,8},{24,16},{28,24},{20,28},{12,20},{4,12},{1,5},{9... | collective-permute-start | bytes 589832 | tf_op jit(solution)/shard_map/ppermute | solution.py:90
  46.4 12.2 %collective-permute-start.7 = (bf16[128,768]{1,0:T(8,128)(2,1)S(1)}, bf16[128,768]{1,0:T(8,128)(2,1)S(1)}, u32[]{:S(2)}, u32[]{:S(2)}) collective-permute-start(bf16[128,768]{1,0:T(8,128)(2,1)S(1)} %collective-permute-done.6.refs_5_), channel_id=1, source_target_pairs={{0,8},{8,16},{16,24},{24,28},{28,20},{20,12},{12,4},{4,0},{1,9},{9... | collective-permute-start | bytes 589832 | tf_op jit(solution)/shard_map/ppermute | solution.py:88
  83.6 18.1 %all-to-all-start = ((bf16[4,1024,128]{2,1,0:T(8,128)(2,1)}), bf16[4,1024,128]{2,1,0:T(8,128)(2,1)S(1)}, u32[]{:S(2)}, u32[]{:S(2)}) async-start(bf16[4,1024,128]{2,1,0:T(8,128)(2,1)} %get-tuple-element.106), calls=%async_computation | async-start | bytes 2097152 | tf_op jit(solution)/shard_map/all_to_all | solution.py:55
  101.7 30.2 %copy-start = (bf16[4,1024,128]{2,1,0:T(8,128)(2,1)}, bf16[4,1024,128]{2,1,0:T(8,128)(2,1)S(1)}, u32[]{:S(2)}) copy-start(bf16[4,1024,128]{2,1,0:T(8,128)(2,1)S(1)} %all-to-all-done.o0_ref.refs_2_.refs_4_.refs_7_.refs_9_) | copy-start | bytes 3145732
  120.7 11.3 %collective-permute-start.9 = (bf16[1024,2560]{1,0:T(8,128)(2,1)}, bf16[1024,2560]{1,0:T(8,128)(2,1)}, u32[]{:S(2)}, u32[]{:S(2)}) collective-permute-start(bf16[1024,2560]{1,0:T(8,128)(2,1)} %all-gather.2.cloned.1.call-done.late_own_ref), channel_id=1, source_target_pairs={{0,1},{1,0},{2,3},{3,2},{4,5},{5,4},{6,7},{7,6},{8,9},{9,8},{10,11... | collective-permute-start | bytes 15728648 | tf_op jit(solution)/shard_map/ppermute | solution.py:47
  120.7 10.5 %collective-permute-start.10 = (bf16[1024,768]{1,0:T(8,128)(2,1)S(1)}, bf16[1024,768]{1,0:T(8,128)(2,1)}, u32[]{:S(2)}, u32[]{:S(2)}) collective-permute-start(bf16[1024,768]{1,0:T(8,128)(2,1)S(1)} %get-tuple-element.110.w_own_ref), channel_id=1, source_target_pairs={{0,1},{1,0},{2,3},{3,2},{4,5},{5,4},{6,7},{7,6},{8,9},{9,8},{10,11... | collective-permute-start | bytes 4718600 | tf_op jit(solution)/shard_map/ppermute | solution.py:47
  121.8 46.3 %copy-start.2 = (bf16[4,1024,128]{2,1,0:T(8,128)(2,1)S(1)}, bf16[4,1024,128]{2,1,0:T(8,128)(2,1)}, u32[]{:S(2)}) copy-start(bf16[4,1024,128]{2,1,0:T(8,128)(2,1)} %all_to_all.15.o1_ref.refs_3_.refs_5_.refs_8_.refs_10_) | copy-start | bytes 3145732
  121.8 46.3 %copy-start.26 = (s32[4]{0:T(128)S(1)}, s32[4]{0:T(128)}, u32[]{:S(2)}) copy-start(s32[4]{0:T(128)} %pad_add_fusion.scalar_ref.refs_0_.half_ref) | copy-start | bytes 52
  167.8 11.9 %collective-permute-start.11 = (bf16[1024,3072]{1,0:T(8,128)(2,1)}, bf16[1024,3072]{1,0:T(8,128)(2,1)}, u32[]{:S(2)}, u32[]{:S(2)}) collective-permute-start(bf16[1024,3072]{1,0:T(8,128)(2,1)} %get-tuple-element.114.refs_0_), channel_id=1, source_target_pairs={{0,1},{1,0},{2,3},{3,2},{4,5},{5,4},{6,7},{7,6},{8,9},{9,8},{10,11... | collective-permute-start | bytes 18874376 | tf_op jit(solution)/shard_map/ppermute | solution.py:47
  173.7 6.0 %collective-permute-start.12 = (bf16[1024,512]{1,0:T(8,128)(2,1)S(1)}, bf16[1024,512]{1,0:T(8,128)(2,1)}, u32[]{:S(2)}, u32[]{:S(2)}) collective-permute-start(bf16[1024,512]{1,0:T(8,128)(2,1)S(1)} %out_grads.1), channel_id=1, source_target_pairs={{0,1},{1,0},{2,3},{3,2},{4,5},{5,4},{6,7},{7,6},{8,9},{9,8},{10,11... | collective-permute-start | bytes 3145736 | tf_op jit(solution)/shard_map/ppermute | solution.py:47
  174.1 30.2 %all-to-all-start.2 = ((bf16[4,1024,256]{2,1,0:T(8,128)(2,1)}), bf16[4,1024,256]{2,1,0:T(8,128)(2,1)}, u32[]{:S(2)}, u32[]{:S(2)}) async-start(bf16[4,1024,256]{2,1,0:T(8,128)(2,1)} %get-tuple-element.118), calls=%async_computation.2 | async-start | bytes 4194304 | tf_op jit(solution)/shard_map/all_to_all | solution.py:55
  178.6 169.1 %reduce-scatter.2.cloned.1.call-start = ((), (), s32[]{:S(2)}) async-start(), calls=%async_computation.5 | async-start | bytes 5898240 | tf_op jit(solution)/shard_map/reduce_scatter | solution.py:790
  204.4 19.3 %collective-permute-start.13 = (bf16[384,1024]{1,0:T(8,128)(2,1)S(1)}, bf16[384,1024]{1,0:T(8,128)(2,1)}, u32[]{:S(2)}, u32[]{:S(2)}) collective-permute-start(bf16[384,1024]{1,0:T(8,128)(2,1)S(1)} %copy-done.37), channel_id=1, source_target_pairs={{0,2},{1,3},{2,0},{3,1},{4,6},{5,7},{6,4},{7,5},{8,10},{9,11},{10,... | collective-permute-start | bytes 2359304 | tf_op jit(solution)/shard_map/ppermute | solution.py:51
  204.8 18.8 %copy-start.39 = (bf16[384,1024]{1,0:T(8,128)(2,1)S(1)}, bf16[384,1024]{1,0:T(8,128)(2,1)}, u32[]{:S(2)}) copy-start(bf16[384,1024]{1,0:T(8,128)(2,1)} %get-tuple-element.135) | copy-start | bytes 2359300
  223.6 18.3 %collective-permute-start.15 = (bf16[384,1024]{1,0:T(8,128)(2,1)S(1)}, bf16[384,1024]{1,0:T(8,128)(2,1)}, u32[]{:S(2)}, u32[]{:S(2)}) collective-permute-start(bf16[384,1024]{1,0:T(8,128)(2,1)S(1)} %copy-done.39), channel_id=1, source_target_pairs={{0,2},{1,3},{2,0},{3,1},{4,6},{5,7},{6,4},{7,5},{8,10},{9,11},{10,... | collective-permute-start | bytes 2359304 | tf_op jit(solution)/shard_map/ppermute | solution.py:51
  224.2 31.4 %collective-permute-start.14 = (bf16[3,1024,128]{2,1,0:T(8,128)(2,1)}, bf16[3,1024,128]{2,1,0:T(8,128)(2,1)S(1)}, u32[]{:S(2)}, u32[]{:S(2)}) collective-permute-start(bf16[3,1024,128]{2,1,0:T(8,128)(2,1)} %get-tuple-element.132), channel_id=1, source_target_pairs={{0,1},{1,0},{2,3},{3,2},{4,5},{5,4},{6,7},{7,6},{8,9},{9,8},{10,11... | collective-permute-start | bytes 2359304 | tf_op jit(solution)/shard_map/ppermute | solution.py:47
  241.9 13.7 %collective-permute-start.16 = (bf16[3,1024,128]{2,1,0:T(8,128)(2,1)}, bf16[3,1024,128]{2,1,0:T(8,128)(2,1)S(1)}, u32[]{:S(2)}, u32[]{:S(2)}) collective-permute-start(bf16[3,1024,128]{2,1,0:T(8,128)(2,1)} %get-tuple-element.136), channel_id=1, source_target_pairs={{0,1},{1,0},{2,3},{3,2},{4,5},{5,4},{6,7},{7,6},{8,9},{9,8},{10,11... | collective-permute-start | bytes 2359304 | tf_op jit(solution)/shard_map/ppermute | solution.py:47
  244.1 25.2 %collective-permute-start.17 = (bf16[256,1024]{1,0:T(8,128)(2,1)}, bf16[256,1024]{1,0:T(8,128)(2,1)S(1)}, u32[]{:S(2)}, u32[]{:S(2)}) collective-permute-start(bf16[256,1024]{1,0:T(8,128)(2,1)} %get-tuple-element.141), channel_id=1, source_target_pairs={{0,2},{1,3},{2,0},{3,1},{4,6},{5,7},{6,4},{7,5},{8,10},{9,11},{10,... | collective-permute-start | bytes 1572872 | tf_op jit(solution)/shard_map/ppermute | solution.py:51
  250.7 8.7 %copy-start.4 = (bf16[1024,1024]{1,0:T(8,128)(2,1)S(1)}, bf16[1024,1024]{1,0:T(8,128)(2,1)}, u32[]{:S(2)}) copy-start(bf16[1024,1024]{1,0:T(8,128)(2,1)} %get-tuple-element.117.refs_1_.refs_6_.refs_0_) | copy-start | bytes 6291460
  250.7 8.7 %copy-start.11 = (bf16[3,2048,128]{2,1,0:T(8,128)(2,1)S(1)}, bf16[3,2048,128]{2,1,0:T(8,128)(2,1)}, u32[]{:S(2)}) copy-start(bf16[3,2048,128]{2,1,0:T(8,128)(2,1)} %get-tuple-element.124.p0_ref.o0_ref) | copy-start | bytes 4718596
  250.7 8.7 %copy-start.13 = (bf16[3,2048,128]{2,1,0:T(8,128)(2,1)S(1)}, bf16[3,2048,128]{2,1,0:T(8,128)(2,1)}, u32[]{:S(2)}) copy-start(bf16[3,2048,128]{2,1,0:T(8,128)(2,1)} %get-tuple-element.130.p1_ref.o1_ref) | copy-start | bytes 4718596
  250.7 8.7 %copy-start.23 = (f32[6,1024]{1,0:T(8,128)S(1)}, f32[6,1024]{1,0:T(8,128)}, u32[]{:S(2)}) copy-start(f32[6,1024]{1,0:T(8,128)} %refs_1_.1) | copy-start | bytes 73732
  250.7 8.7 %copy-start.27 = (s32[4]{0:T(128)S(1)}, s32[4]{0:T(128)}, u32[]{:S(2)}) copy-start(s32[4]{0:T(128)} %pad_add_fusion.scalar_ref.refs_0_.half_ref) | copy-start | bytes 52
  256.8 12.5 %collective-permute-start.18 = (bf16[128,768]{1,0:T(8,128)(2,1)S(1)}, bf16[128,768]{1,0:T(8,128)(2,1)S(1)}, u32[]{:S(2)}, u32[]{:S(2)}) collective-permute-start(bf16[128,768]{1,0:T(8,128)(2,1)S(1)} %get-tuple-element.245), channel_id=1, source_target_pairs={{0,4},{8,0},{16,8},{24,16},{28,24},{20,28},{12,20},{4,12},{1,5},{9... | collective-permute-start | bytes 589832 | tf_op jit(solution)/shard_map/ppermute | solution.py:124
  259.2 10.1 %copy-start.34 = (bf16[1024,1024]{1,0:T(8,128)(2,1)S(1)}, bf16[1024,1024]{1,0:T(8,128)(2,1)}, u32[]{:S(2)}) copy-start(bf16[1024,1024]{1,0:T(8,128)(2,1)} %get-tuple-element.112) | copy-start | bytes 6291460
  259.2 10.2 %copy-start.41 = (bf16[256,1024]{1,0:T(8,128)(2,1)S(1)}, bf16[256,1024]{1,0:T(8,128)(2,1)}, u32[]{:S(2)}) copy-start(bf16[256,1024]{1,0:T(8,128)(2,1)} %get-tuple-element.141) | copy-start | bytes 1572868
  259.2 10.1 %collective-permute-start.19 = (bf16[128,768]{1,0:T(8,128)(2,1)S(1)}, bf16[128,768]{1,0:T(8,128)(2,1)S(1)}, u32[]{:S(2)}, u32[]{:S(2)}) collective-permute-start(bf16[128,768]{1,0:T(8,128)(2,1)S(1)} %get-tuple-element.244), channel_id=1, source_target_pairs={{0,8},{8,16},{16,24},{24,28},{28,20},{20,12},{12,4},{4,0},{1,9},{9... | collective-permute-start | bytes 589832 | tf_op jit(solution)/shard_map/ppermute | solution.py:123
  274.9 32.0 %collective-permute-start.20 = (bf16[1024,1024]{1,0:T(8,128)(2,1)S(1)}, bf16[1024,1024]{1,0:T(8,128)(2,1)}, u32[]{:S(2)}, u32[]{:S(2)}) collective-permute-start(bf16[1024,1024]{1,0:T(8,128)(2,1)S(1)} %pad_maximum_fusion.refs_0_), channel_id=1, source_target_pairs={{0,1},{1,0},{2,3},{3,2},{4,5},{5,4},{6,7},{7,6},{8,9},{9,8},{10,11... | collective-permute-start | bytes 6291464 | tf_op jit(solution)/shard_map/ppermute | solution.py:47
  276.9 14.6 %collective-permute-start.22 = (bf16[256,1024]{1,0:T(8,128)(2,1)}, bf16[256,1024]{1,0:T(8,128)(2,1)}, u32[]{:S(2)}, u32[]{:S(2)}) collective-permute-start(bf16[256,1024]{1,0:T(8,128)(2,1)} %get-tuple-element.158.refs_0_), channel_id=1, source_target_pairs={{0,2},{1,3},{2,0},{3,1},{4,6},{5,7},{6,4},{7,5},{8,10},{9,11},{10,... | collective-permute-start | bytes 1572872 | tf_op jit(solution)/shard_map/ppermute | solution.py:51
  277.5 9.2 %copy-start.44 = (bf16[128,768]{1,0:T(8,128)(2,1)S(1)}, bf16[128,768]{1,0:T(8,128)(2,1)}, u32[]{:S(2)}) copy-start(bf16[128,768]{1,0:T(8,128)(2,1)} %copy-done.43) | copy-start | bytes 589828
  285.9 7.4 %collective-permute-start.24 = (f32[10,1024]{1,0:T(8,128)S(1)}, f32[10,1024]{1,0:T(8,128)S(1)}, u32[]{:S(2)}, u32[]{:S(2)}) collective-permute-start(f32[10,1024]{1,0:T(8,128)S(1)} %concatenate.30), channel_id=1, source_target_pairs={{0,1},{1,0},{2,3},{3,2},{4,5},{5,4},{6,7},{7,6},{8,9},{9,8},{10,11... | collective-permute-start | bytes 122888 | tf_op jit(solution)/shard_map/ppermute | solution.py:47
  286.2 28.0 %collective-permute-start.30 = (bf16[256,1024]{1,0:T(8,128)(2,1)}, bf16[256,1024]{1,0:T(8,128)(2,1)}, u32[]{:S(2)}, u32[]{:S(2)}) collective-permute-start(bf16[256,1024]{1,0:T(8,128)(2,1)} %get-tuple-element.159.refs_2_), channel_id=1, source_target_pairs={{0,1},{1,0},{2,3},{3,2},{4,5},{5,4},{6,7},{7,6},{8,9},{9,8},{10,11... | collective-permute-start | bytes 1572872 | tf_op jit(solution)/shard_map/ppermute | solution.py:47
  286.5 31.0 %collective-permute-start.28 = (bf16[256,1024]{1,0:T(8,128)(2,1)}, bf16[256,1024]{1,0:T(8,128)(2,1)}, u32[]{:S(2)}, u32[]{:S(2)}) collective-permute-start(bf16[256,1024]{1,0:T(8,128)(2,1)} %get-tuple-element.158.refs_0_), channel_id=1, source_target_pairs={{0,1},{1,0},{2,3},{3,2},{4,5},{5,4},{6,7},{7,6},{8,9},{9,8},{10,11... | collective-permute-start | bytes 1572872 | tf_op jit(solution)/shard_map/ppermute | solution.py:47
  291.5 20.7 %collective-permute-start.35 = (bf16[128,768]{1,0:T(8,128)(2,1)S(1)}, bf16[128,768]{1,0:T(8,128)(2,1)S(1)}, u32[]{:S(2)}, u32[]{:S(2)}) collective-permute-start(bf16[128,768]{1,0:T(8,128)(2,1)S(1)} %add_convert_fusion.4), channel_id=1, source_target_pairs={{0,4},{8,0},{16,8},{24,16},{28,24},{20,28},{12,20},{4,12},{1,5},{9... | collective-permute-start | bytes 589832 | tf_op jit(solution)/shard_map/ppermute | solution.py:124
  293.3 13.6 %collective-permute-start.23 = (bf16[256,1024]{1,0:T(8,128)(2,1)}, bf16[256,1024]{1,0:T(8,128)(2,1)}, u32[]{:S(2)}, u32[]{:S(2)}) collective-permute-start(bf16[256,1024]{1,0:T(8,128)(2,1)} %get-tuple-element.159.refs_2_), channel_id=1, source_target_pairs={{0,2},{1,3},{2,0},{3,1},{4,6},{5,7},{6,4},{7,5},{8,10},{9,11},{10,... | collective-permute-start | bytes 1572872 | tf_op jit(solution)/shard_map/ppermute | solution.py:51
  294.1 18.1 %copy-start.15 = (bf16[256,1024]{1,0:T(8,128)(2,1)S(1)}, bf16[256,1024]{1,0:T(8,128)(2,1)}, u32[]{:S(2)}) copy-start(bf16[256,1024]{1,0:T(8,128)(2,1)} %copy-done.14) | copy-start | bytes 1572868
  294.1 21.6 %copy-start.46 = (bf16[128,768]{1,0:T(8,128)(2,1)S(1)}, bf16[128,768]{1,0:T(8,128)(2,1)}, u32[]{:S(2)}) copy-start(bf16[128,768]{1,0:T(8,128)(2,1)} %copy-done.45) | copy-start | bytes 589828
  306.9 16.6 %collective-permute-start.29 = (bf16[256,1024]{1,0:T(8,128)(2,1)}, bf16[256,1024]{1,0:T(8,128)(2,1)}, u32[]{:S(2)}, u32[]{:S(2)}) collective-permute-start(bf16[256,1024]{1,0:T(8,128)(2,1)} %collective-permute-done.22.refs_1_), channel_id=1, source_target_pairs={{0,1},{1,0},{2,3},{3,2},{4,5},{5,4},{6,7},{7,6},{8,9},{9,8},{10,11... | collective-permute-start | bytes 1572872 | tf_op jit(solution)/shard_map/ppermute | solution.py:47
  306.9 16.6 %collective-permute-start.31 = (bf16[256,1024]{1,0:T(8,128)(2,1)}, bf16[256,1024]{1,0:T(8,128)(2,1)S(1)}, u32[]{:S(2)}, u32[]{:S(2)}) collective-permute-start(bf16[256,1024]{1,0:T(8,128)(2,1)} %collective-permute-done.23.refs_3_), channel_id=1, source_target_pairs={{0,1},{1,0},{2,3},{3,2},{4,5},{5,4},{6,7},{7,6},{8,9},{9,8},{10,11... | collective-permute-start | bytes 1572872 | tf_op jit(solution)/shard_map/ppermute | solution.py:47
  312.2 14.7 %collective-permute-start.25 = (bf16[256,1024]{1,0:T(8,128)(2,1)S(1)}, bf16[256,1024]{1,0:T(8,128)(2,1)S(1)}, u32[]{:S(2)}, u32[]{:S(2)}) collective-permute-start(bf16[256,1024]{1,0:T(8,128)(2,1)S(1)} %copy-done.15), channel_id=1, source_target_pairs={{0,2},{1,3},{2,0},{3,1},{4,6},{5,7},{6,4},{7,5},{8,10},{9,11},{10,... | collective-permute-start | bytes 1572872 | tf_op jit(solution)/shard_map/ppermute | solution.py:51
  314.2 4.3 %collective-permute-start.32 = (f32[9,1024]{1,0:T(8,128)S(1)}, f32[9,1024]{1,0:T(8,128)S(1)}, u32[]{:S(2)}, u32[]{:S(2)}) collective-permute-start(f32[9,1024]{1,0:T(8,128)S(1)} %pad_maximum_fusion.2), channel_id=1, source_target_pairs={{0,4},{4,0},{8,12},{12,8},{16,20},{20,16},{24,28},{28,24},{1,5},{5... | collective-permute-start | bytes 110600 | tf_op jit(solution)/shard_map/ppermute | solution.py:852
  317.5 12.1 %collective-permute-start.38 = (bf16[128,768]{1,0:T(8,128)(2,1)}, bf16[128,768]{1,0:T(8,128)(2,1)}, u32[]{:S(2)}, u32[]{:S(2)}) collective-permute-start(bf16[128,768]{1,0:T(8,128)(2,1)} %get-tuple-element.167), channel_id=1, source_target_pairs={{0,8},{8,16},{16,24},{24,28},{28,20},{20,12},{12,4},{4,0},{1,9},{9... | collective-permute-start | bytes 589832 | tf_op jit(solution)/shard_map/ppermute | solution.py:123
  318.5 11.1 %collective-permute-start.36 = (bf16[128,768]{1,0:T(8,128)(2,1)S(1)}, bf16[128,768]{1,0:T(8,128)(2,1)}, u32[]{:S(2)}, u32[]{:S(2)}) collective-permute-start(bf16[128,768]{1,0:T(8,128)(2,1)S(1)} %get-tuple-element.165), channel_id=1, source_target_pairs={{0,4},{8,0},{16,8},{24,16},{28,24},{20,28},{12,20},{4,12},{1,5},{9... | collective-permute-start | bytes 589832 | tf_op jit(solution)/shard_map/ppermute | solution.py:124
  323.5 11.6 %copy-start.36 = (f32[128,3,256]{2,0,1:T(8,128)S(1)}, f32[128,3,256]{2,0,1:T(8,128)}, u32[]{:S(2)}) copy-start(f32[128,3,256]{2,0,1:T(8,128)} %param.26) | copy-start | bytes 1179652
  326.9 12.6 %collective-permute-start.33 = (bf16[256,1024]{1,0:T(8,128)(2,1)S(1)}, bf16[256,1024]{1,0:T(8,128)(2,1)}, u32[]{:S(2)}, u32[]{:S(2)}) collective-permute-start(bf16[256,1024]{1,0:T(8,128)(2,1)S(1)} %copy-done.17), channel_id=1, source_target_pairs={{0,2},{1,3},{2,0},{3,1},{4,6},{5,7},{6,4},{7,5},{8,10},{9,11},{10,... | collective-permute-start | bytes 1572872 | tf_op jit(solution)/shard_map/ppermute | solution.py:51
  331.7 10.4 %collective-permute-start.39 = (bf16[128,768]{1,0:T(8,128)(2,1)}, bf16[128,768]{1,0:T(8,128)(2,1)S(1)}, u32[]{:S(2)}, u32[]{:S(2)}) collective-permute-start(bf16[128,768]{1,0:T(8,128)(2,1)} %get-tuple-element.168), channel_id=1, source_target_pairs={{0,8},{8,16},{16,24},{24,28},{28,20},{20,12},{12,4},{4,0},{1,9},{9... | collective-permute-start | bytes 589832 | tf_op jit(solution)/shard_map/ppermute | solution.py:123
  332.2 9.9 %collective-permute-start.37 = (bf16[128,768]{1,0:T(8,128)(2,1)}, bf16[128,768]{1,0:T(8,128)(2,1)}, u32[]{:S(2)}, u32[]{:S(2)}) collective-permute-start(bf16[128,768]{1,0:T(8,128)(2,1)} %get-tuple-element.166), channel_id=1, source_target_pairs={{0,4},{8,0},{16,8},{24,16},{28,24},{20,28},{12,20},{4,12},{1,5},{9... | collective-permute-start | bytes 589832 | tf_op jit(solution)/shard_map/ppermute | solution.py:124
  334.0 5.3 %collective-permute-start.40 = (f32[9,1024]{1,0:T(8,128)S(1)}, f32[9,1024]{1,0:T(8,128)S(1)}, u32[]{:S(2)}, u32[]{:S(2)}) collective-permute-start(f32[9,1024]{1,0:T(8,128)S(1)} %add.273), channel_id=1, source_target_pairs={{0,8},{4,12},{8,0},{12,4},{16,24},{20,28},{24,16},{28,20},{1,9},{5... | collective-permute-start | bytes 110600 | tf_op jit(solution)/shard_map/ppermute | solution.py:852
  337.0 23.4 %collective-permute-start.27 = (bf16[256,1024]{1,0:T(8,128)(2,1)S(1)}, bf16[256,1024]{1,0:T(8,128)(2,1)}, u32[]{:S(2)}, u32[]{:S(2)}) collective-permute-start(bf16[256,1024]{1,0:T(8,128)(2,1)S(1)} %copy-done.17), channel_id=1, source_target_pairs={{0,1},{1,0},{2,3},{3,2},{4,5},{5,4},{6,7},{7,6},{8,9},{9,8},{10,11... | collective-permute-start | bytes 1572872 | tf_op jit(solution)/shard_map/ppermute | solution.py:47
  339.2 22.6 %collective-permute-start.21 = (bf16[256,1024]{1,0:T(8,128)(2,1)S(1)}, bf16[256,1024]{1,0:T(8,128)(2,1)}, u32[]{:S(2)}, u32[]{:S(2)}) collective-permute-start(bf16[256,1024]{1,0:T(8,128)(2,1)S(1)} %copy-done.15), channel_id=1, source_target_pairs={{0,1},{1,0},{2,3},{3,2},{4,5},{5,4},{6,7},{7,6},{8,9},{9,8},{10,11... | collective-permute-start | bytes 1572872 | tf_op jit(solution)/shard_map/ppermute | solution.py:47
  339.5 8.0 %collective-permute-start.41 = (f32[9,1024]{1,0:T(8,128)S(1)}, f32[9,1024]{1,0:T(8,128)S(1)}, u32[]{:S(2)}, u32[]{:S(2)}) collective-permute-start(f32[9,1024]{1,0:T(8,128)S(1)} %add.287), channel_id=1, source_target_pairs={{0,16},{4,20},{8,24},{12,28},{16,0},{20,4},{24,8},{28,12},{1,17},{... | collective-permute-start | bytes 110600 | tf_op jit(solution)/shard_map/ppermute | solution.py:852
  347.0 14.8 %collective-permute-start.26 = (bf16[256,1024]{1,0:T(8,128)(2,1)S(1)}, bf16[256,1024]{1,0:T(8,128)(2,1)S(1)}, u32[]{:S(2)}, u32[]{:S(2)}) collective-permute-start(bf16[256,1024]{1,0:T(8,128)(2,1)S(1)} %collective-permute-done.25.refs_1_), channel_id=1, source_target_pairs={{0,1},{1,0},{2,3},{3,2},{4,5},{5,4},{6,7},{7,6},{8,9},{9,8},{10,11... | collective-permute-start | bytes 1572872 | tf_op jit(solution)/shard_map/ppermute | solution.py:47
  347.2 14.5 %collective-permute-start.34 = (bf16[256,1024]{1,0:T(8,128)(2,1)}, bf16[256,1024]{1,0:T(8,128)(2,1)}, u32[]{:S(2)}, u32[]{:S(2)}) collective-permute-start(bf16[256,1024]{1,0:T(8,128)(2,1)} %collective-permute-done.33.refs_3_), channel_id=1, source_target_pairs={{0,1},{1,0},{2,3},{3,2},{4,5},{5,4},{6,7},{7,6},{8,9},{9,8},{10,11... | collective-permute-start | bytes 1572872 | tf_op jit(solution)/shard_map/ppermute | solution.py:47
  355.1 10.0 %collective-permute-start.42 = (f32[7,1024]{1,0:T(8,128)S(1)}, f32[7,1024]{1,0:T(8,128)S(1)}, u32[]{:S(2)}, u32[]{:S(2)}) collective-permute-start(f32[7,1024]{1,0:T(8,128)S(1)} %slice.191), channel_id=1, source_target_pairs={{0,2},{1,3},{2,0},{3,1},{4,6},{5,7},{6,4},{7,5},{8,10},{9,11},{10,... | collective-permute-start | bytes 86024 | tf_op jit(solution)/shard_map/ppermute | solution.py:51
  360.4 7.2 %collective-permute-start.43 = (bf16[128,256]{1,0:T(8,128)(2,1)S(1)}, bf16[128,256]{1,0:T(8,128)(2,1)S(1)}, u32[]{:S(2)}, u32[]{:S(2)}) collective-permute-start(bf16[128,256]{1,0:T(8,128)(2,1)S(1)} %slice.195), channel_id=1, source_target_pairs={{0,2},{1,3},{2,0},{3,1},{4,6},{5,7},{6,4},{7,5},{8,10},{9,11},{10,... | collective-permute-start | bytes 196616 | tf_op jit(solution)/shard_map/ppermute | solution.py:51
  (40 other events, 157.5 us)
Sparse Core Ops, SparseCore 0:
  14.8 98.8 all-gather.1
  204.5 107.6 reduce-scatter.1
